TPU v7x, 32 devices: a whole 2x2x4 slice. The times are simulated.
32 devices in a mesh: visit: 2 (over x), py: 4 (over y, core), px: 4 (over z).
Axes of the slice: x: 2, y: 2, z: 4, core: 2. Of those that a mesh axis runs over, the one named last changes fastest.
Arguments:
- images: bfloat16 [768, 256, 256], P(('visit', 'py', 'px')), may hold values from -6 to 6
- inv_var: bfloat16 [768, 256, 256], P(('visit', 'py', 'px')), may hold values from 0.25 to 4
- good_columns: int32 [16, 256], P('visit'), may hold values 0 or 1
- warp_rows: bfloat16 [16, 256, 256], P('visit'), may hold values from -0.4 to 1.4, as said below
- warp_cols: bfloat16 [16, 256, 256], P('visit'), may hold values from -0.4 to 1.4, as said below
- block_visit: int32 [768], P(('visit', 'py', 'px')), may hold values from 0 to 7
- dest_tile: int32 [768, 1], P(('visit', 'py', 'px')), may hold values from 0 to 15; in each aligned block of 24 rows (0 to 23, 24 to 47, ...) at most 2 rows name the same one
- offsets: int32 [768, 2], P(('visit', 'py', 'px')), may hold values from 0 to 6
- psf_taps: float32 [7], replicated, may hold values from 0.1 to 1
Outputs:
- detection: float32 [4096, 4096], P('py', 'px')
- local_variance: float32 [4096, 4096], P('py', 'px')
Inputs may be any that keep to these rules, and one draw needn't show every extreme that they name: `dest_tile`: among the rows of one device no tile is named more than 2 times, a bound that some block reaches. `warp_rows`: lanczos interpolation weights of each visit. `warp_cols`: lanczos interpolation weights of each visit.
All inputs are finite; a program needn't handle non-finite values. No bound on the sum of `good_columns` on one device may be relied on, other than what follows from the above.
Results may differ from a plain program's by a relative error of at most 0.0057.
Values may be sent and summed in bfloat16 or wider, within the bound.
No kernel may reach another device: no remote copies, remote signals or barrier semaphores. Data moves between devices by JAX's collectives and lax.ppermute only.
A program may use at most 128 MiB of HBM per device.

v0:
```python
import jax
import jax.numpy as jnp
from jax import lax
from jax.sharding import PartitionSpec as P

TY = 1024
TX = 1024
STEP = 128
CAP = 2


def with_halo(shard, sides, width):
    for axis, dim in sides:
        count, length = (lax.axis_size(axis), shard.shape[dim])
        up = [(i, (i + 1) % count) for i in range(count - 1)]
        down = [(j, i) for i, j in up]
        last = lax.slice_in_dim(shard, length - width, length, axis=dim)
        initial = lax.slice_in_dim(shard, 0, width, axis=dim)
        before = lax.ppermute(last, axis, up)
        after = lax.ppermute(initial, axis, down)
        shard = jnp.concatenate([before, shard, after], axis=dim)
    return shard


def box_sum(field, span, height, breadth):
    vertical = sum((field[offset : offset + height, :] for offset in range(span)))
    return sum((vertical[:, offset : offset + breadth] for offset in range(span)))


def filters(padded, taps, height, breadth):
    smooth = box_sum(padded, 3, height + 8, breadth + 8) / 9.0
    resid = padded[1:-1, 1:-1] - smooth
    local_var = box_sum(resid * resid, 9, height, breadth) / 81.0 + 1e-05
    rowwise = sum(
        (
            taps[offset] * padded[2 + offset : 2 + offset + height, :]
            for offset in range(taps.shape[0])
        )
    )
    blurred = sum(
        (
            taps[offset] * rowwise[:, 2 + offset : 2 + offset + breadth]
            for offset in range(taps.shape[0])
        )
    )
    return (blurred / jnp.sqrt(local_var), local_var)


def unit_table(starts, lanes, cells):
    grid = jnp.arange(cells, dtype=jnp.int32)[:, None, None]
    within = jnp.arange(lanes, dtype=jnp.int32)[None, None, :]
    return (starts[None, :, None] + within == grid).astype(jnp.bfloat16)


def per_device(
    images, inv_var, good_columns, warp_rows, warp_cols, block_visit, dest_tile, offsets, psf_taps
):
    count_rows = lax.axis_size("py")
    count_cols = lax.axis_size("px")
    tiles = count_rows * count_cols
    side = images.shape[1]
    lanes = side // STEP
    row_sel = jnp.take(warp_rows, block_visit, axis=0)
    col_sel = jnp.take(warp_cols, block_visit, axis=0)
    good = jnp.take(good_columns, block_visit, axis=0).astype(jnp.float32)
    weight = inv_var.astype(jnp.float32) * good[:, None, :]
    planes = jnp.stack(
        [(weight * images.astype(jnp.float32)).astype(jnp.bfloat16), weight.astype(jnp.bfloat16)],
        axis=1,
    )
    halves = jnp.einsum(
        "bij,bpjk->bpik", row_sel, planes, preferred_element_type=jnp.float32
    ).astype(jnp.bfloat16)
    warped = jnp.einsum(
        "bpik,blk->bpil", halves, col_sel, preferred_element_type=jnp.float32
    ).astype(jnp.bfloat16)
    target = dest_tile[:, 0]
    one_hot = (target[:, None] == jnp.arange(tiles, dtype=jnp.int32)[None, :]).astype(jnp.int32)
    earlier = jnp.cumsum(one_hot, axis=0) - one_hot
    slot_rank = jnp.sum(earlier * one_hot, axis=1)
    height = TY
    breadth = TX
    columns_wide = breadth // STEP
    rows_high = height // STEP
    position = target * CAP + slot_rank
    outgoing = jnp.zeros((tiles * CAP, 2, side, side), jnp.bfloat16).at[position].set(warped)
    out_offsets = (
        jnp.zeros((tiles * CAP, 2), jnp.bfloat16).at[position].set(offsets.astype(jnp.bfloat16))
    )
    incoming, in_offsets = (
        lax.all_to_all(outgoing, ("py", "px"), split_axis=0, concat_axis=0, tiled=True),
        lax.all_to_all(out_offsets, ("py", "px"), split_axis=0, concat_axis=0, tiled=True),
    )
    row_units = in_offsets[:, 0].astype(jnp.float32).astype(jnp.int32)
    col_units = in_offsets[:, 1].astype(jnp.float32).astype(jnp.int32)
    quarters = incoming.reshape(tiles * CAP, 2, lanes, STEP, lanes, STEP)
    row_table = unit_table(row_units, lanes, rows_high)
    column_table = unit_table(col_units, lanes, columns_wide)
    placement = row_table[:, None, :, :, None] * column_table[None, :, :, None, :]
    totals = jnp.einsum(
        "yxsac,sparcq->pyrxq", placement, quarters, preferred_element_type=jnp.float32
    )
    totals = totals.reshape(2, height, breadth)
    data_sum, weight_sum = lax.psum((totals[0], totals[1]), "visit")
    coadd = data_sum / jnp.maximum(weight_sum, 1.0)
    padded = with_halo(coadd, (("py", 0), ("px", 1)), 5)
    detection, local_variance = filters(padded, psf_taps, height, breadth)
    return (detection, local_variance)


def solution(mesh):
    in_specs = (
        P(("visit", "py", "px"), None, None),
        P(("visit", "py", "px"), None, None),
        P("visit", None),
        P("visit", None, None),
        P("visit", None, None),
        P(("visit", "py", "px")),
        P(("visit", "py", "px"), None),
        P(("visit", "py", "px"), None),
        P(),
    )
    out_specs = (P("py", "px"), P("py", "px"))
    return jax.shard_map(
        per_device, mesh=mesh, in_specs=in_specs, out_specs=out_specs, check_vma=False
    )
```

profile of v0, /device:TPU:0, one launch (start us, length us, event | category | flops | bytes accessed | tf_op | source)
XLA Modules:
  0.0 627.0 jit_solution(5337293225645826475)
XLA Ops:
  11.8 7.4 %all-to-all-start.1 = ((bf16[16,2,2]{1,2,0:T(2,128)(2,1)}), bf16[16,2,2]{1,2,0:T(2,128)(2,1)S(1)}, u32[]{:S(2)}, u32[]{:S(2)}) async-start(bf16[16,2,2]{1,2,0:T(2,128)(2,1)} %copy.22), calls=%async_computation.1 | async-start | bytes 16384 | tf_op jit(solution)/shard_map/all_to_all | solution.py:92
  20.5 4.6 copy.16
  25.1 4.6 copy.17
  30.4 2.5 gather_fusion.1
  32.9 2.6 gather_fusion.2
  35.5 5.4 fusion.41
  40.9 8.5 %fusion.32 = bf16[24,2,256,256]{3,2,1,0:T(8,128)(2,1)} fusion(bf16[24,1,256,256]{2,3,1,0:T(8,128)(2,1)} %get-tuple-element.14, bf16[24,1,256,256]{2,3,1,0:T(8,128)(2,1)} %get-tuple-element.13, bf16[24,256,256]{2,1,0:T(8,128)(2,1)} %gather_fusion.2, bf16[24,256,256]{2,1,0:T(8,128)(2,1)} %gather_fusion.1, pred[24]{0:T(512)(128)(4,1)S(1)} %compare_and_fusion), kind=kOutput, calls=%fused_computation.72 | convolution fusion | flops 3233808384 | bytes 18874392 | tf_op jit(solution)/shard_map/bpik,blk->bpil/dot_general | solution.py:74
  49.4 4.3 broadcast_in_dim.25
  53.6 16.2 %scatter_fusion = bf16[32,2,256,256]{3,2,1,0:T(8,128)(2,1)} fusion(bf16[32,2,256,256]{3,2,1,0:T(8,128)(2,1)} %broadcast_in_dim.25, s32[24]{0:T(128)S(1)} %fusion.60, bf16[24,2,256,256]{3,2,1,0:T(8,128)(2,1)} %fusion.32), kind=kCustom, calls=%fused_computation.3 | custom fusion | bytes 18874464 | tf_op jit(solution)/shard_map/scatter | solution.py:86
  69.8 6.1 all-to-all-start
  76.2 183.9 %all-to-all-done = bf16[32,2,256,256]{3,2,1,0:T(8,128)(2,1)} async-done(((bf16[32,2,256,256]{3,2,1,0:T(8,128)(2,1)}), bf16[32,2,256,256]{3,2,1,0:T(8,128)(2,1)}, u32[]{:S(2)}, u32[]{:S(2)}) %all-to-all-start) | async-done | bytes 8388640 | tf_op jit(solution)/shard_map/all_to_all | solution.py:91
  260.2 12.5 %reshape.109 = bf16[32,2,2,128,2,128]{5,4,3,2,1,0:T(2,128)(2,1)} reshape(bf16[32,2,256,256]{3,2,1,0:T(8,128)(2,1)} %all-to-all-done) | data formatting | bytes 16777216 | tf_op jit(solution)/shard_map/reshape | solution.py:96
  272.7 9.7 %fusion.37 = f32[2,8,128,8,128]{4,3,1,2,0:T(8,128)S(1)} fusion(bf16[32,2,2,128,2,128,1]{5,4,3,2,1,0,6:T(2,128)(2,1)} %bitcast.67, bf16[8,32,2]{1,0,2:T(8,128)(2,1)S(1)} %fusion.57, bf16[8,32,2]{1,2,0:T(2,128)(2,1)S(1)} %compare_convert_fusion), kind=kOutput, calls=%fused_computation.73 | convolution fusion | flops 536903680 | bytes 16779264 | tf_op jit(solution)/shard_map/yxsac,sparcq->pyrxq/dot_general | solution.py:100
  282.4 1.7 fusion.66
  284.3 3.0 copy.49
  287.6 3.0 copy.50
  290.7 197.4 %all-reduce.3.cloned.1.call-done = (f32[1024,1024]{1,0:T(8,128)}, f32[1024,1024]{1,0:T(8,128)}) async-done(((f32[1024,1024]{1,0:T(8,128)}, f32[1024,1024]{1,0:T(8,128)}), (f32[1024,1024]{1,0:T(8,128)}, f32[1024,1024]{1,0:T(8,128)})) %all-reduce.3.cloned.1.call-update) | async-done | bytes 8388624 | tf_op jit(solution)/shard_map/psum | solution.py:104
  488.1 4.4 maximum_divide_fusion
  492.5 2.0 copy-done.3
  494.5 1.7 collective-permute-start
  497.6 3.0 collective-permute-done.1
  500.7 13.6 %concatenate.6 = f32[1034,1024]{1,0:T(8,128)} concatenate(f32[5,1024]{1,0:T(8,128)S(1)} %collective-permute-done, f32[1024,1024]{1,0:T(8,128)} %copy-done.3, f32[5,1024]{1,0:T(8,128)S(1)} %collective-permute-done.1), dimensions={0} | concatenate | bytes 8470528 | tf_op jit(solution)/shard_map/concatenate | solution.py:21
  514.3 1.4 fusion.67
  515.9 3.4 collective-permute-start.2
  519.5 1.5 collective-permute-start.3
  522.0 3.4 collective-permute-done.3
  525.6 6.7 %concatenate.7 = f32[1034,1034]{1,0:T(8,128)} concatenate(f32[1034,5]{1,0:T(8,128)S(1)} %copy.29, f32[1034,1024]{1,0:T(8,128)} %concatenate.6, f32[1034,5]{1,0:T(8,128)S(1)} %copy.30), dimensions={1} | concatenate | bytes 8553248 | tf_op jit(solution)/shard_map/concatenate | solution.py:21
  532.3 6.2 slice_add_fusion.2
  538.8 5.5 fusion.12
  544.2 18.4 %slice_add_fusion.4 = f32[1024,1032]{1,0:T(8,128)} fusion(f32[1032,1032]{1,0:T(8,128)} %fusion.12), kind=kLoop, calls=%fused_computation.24 | loop fusion | flops 8454144 | bytes 42270720 | tf_op jit(solution)/shard_map/add | solution.py:26
  562.6 9.5 %fusion.13 = f32[1024,1034]{1,0:T(8,128)} fusion(f32[1034,1034]{1,0:T(8,128)S(1)} %copy-done.2, f32[]{:T(128)} %bitcast.28, f32[]{:T(128)} %bitcast.27, f32[]{:T(128)} %bitcast.26, f32[]{:T(128)} %bitcast.25, f32[]{:T(128)} %bitcast.24, f32[]{:T(128)} %bitcast.23, f32[]{:T(128)} %bitcast), kind=kLoop, calls=%fused_computation.33 | loop fusion | flops 13764608 | bytes 33882140 | tf_op jit(solution)/shard_map/add | solution.py:34
  572.1 48.1 %fusion.22 = (f32[1024,1024]{1,0:T(8,128)}, f32[1024,1024]{1,0:T(8,128)}) fusion(f32[1024,1034]{1,0:T(8,128)} %fusion.13, f32[]{:T(128)} %bitcast.28, f32[]{:T(128)} %bitcast.27, f32[]{:T(128)} %bitcast.26, f32[]{:T(128)} %bitcast.25, f32[]{:T(128)} %bitcast.24, f32[]{:T(128)} %bitcast.23, f32[]{:T(128)} %bitcast, f32[1024,1032]{1,0:T(8,128)} %slice_add_fusion.4), kind=kLoop, calls=%fused_computation.59 | loop fusion | flops 25165824 | bytes 75497504 | tf_op jit(solution)/shard_map/div | solution.py:46
  (46 shorter events, 10.6 us)
Async XLA Ops:
  7.2 23.2 %copy-start = (bf16[8,256,256]{2,1,0:T(8,128)(2,1)S(1)}, bf16[8,256,256]{2,1,0:T(8,128)(2,1)}, u32[]{:S(2)}) copy-start(bf16[8,256,256]{2,1,0:T(8,128)(2,1)} %param.14) | copy-start | bytes 3145732
  11.8 58.0 %all-to-all-start.1 = ((bf16[16,2,2]{1,2,0:T(2,128)(2,1)}), bf16[16,2,2]{1,2,0:T(2,128)(2,1)S(1)}, u32[]{:S(2)}, u32[]{:S(2)}) async-start(bf16[16,2,2]{1,2,0:T(2,128)(2,1)} %copy.22), calls=%async_computation.1 | async-start | bytes 16384 | tf_op jit(solution)/shard_map/all_to_all | solution.py:92
  25.1 4.6 copy-start.5
  29.8 3.1 copy-start.4
  69.8 190.4 %all-to-all-start = ((bf16[32,2,256,256]{3,2,1,0:T(8,128)(2,1)}), bf16[32,2,256,256]{3,2,1,0:T(8,128)(2,1)}, u32[]{:S(2)}, u32[]{:S(2)}) async-start(bf16[32,2,256,256]{3,2,1,0:T(8,128)(2,1)} %scatter_fusion), calls=%async_computation | async-start | bytes 16777216 | tf_op jit(solution)/shard_map/all_to_all | solution.py:91
  75.8 412.2 %all-reduce.3.cloned.1.call-start = ((), (), s32[]{:S(2)}) async-start(), calls=%async_computation.2 | async-start | bytes 16777216 | tf_op jit(solution)/shard_map/psum | solution.py:104
  492.5 2.0 copy-start.3
  494.5 3.1 collective-permute-start
  496.3 24.8 %copy-start.6 = (f32[7]{0:T(128)S(1)}, f32[7]{0:T(128)}, u32[]{:S(2)}) copy-start(f32[7]{0:T(128)} %param.19) | copy-start | bytes 88
  496.3 4.4 collective-permute-start.1
  515.9 5.8 collective-permute-start.2
  519.5 5.9 collective-permute-start.3
  532.3 6.5 %copy-start.2 = (f32[1034,1034]{1,0:T(8,128)S(1)}, f32[1034,1034]{1,0:T(8,128)}, u32[]{:S(2)}) copy-start(f32[1034,1034]{1,0:T(8,128)} %concatenate.7) | copy-start | bytes 12829876
  572.1 48.1 %copy-start.1 = (bf16[8,256,256]{2,1,0:T(8,128)(2,1)S(1)}, bf16[8,256,256]{2,1,0:T(8,128)(2,1)}, u32[]{:S(2)}) copy-start(bf16[8,256,256]{2,1,0:T(8,128)(2,1)} %param.14) | copy-start | bytes 3145732
Sparse Core Ops, SparseCore 0:
  290.8 197.2 all-reduce.2
where the time goes:
time: 629 us; the launch traced here: 627 us
  waiting for transfers between devices  388 us (62%)
  other arithmetic  102 us (16%)
  local copies, waits for them, and re-layouts  83.3 us (13%)
  starting transfers between devices  21.6 us (3%)
  matrix products  18.2 us (3%)
  between operations  14.3 us (2%)
    psum x1, waiting for transfers between devices, per_device(): data_sum, weight_sum = lax.psum((totals[0], totals[1]), 'visit')  197 us
    all_to_all x1, waiting for transfers between devices, per_device(): lax.all_to_all(outgoing, ('py', 'px'), split_axis=0, concat_axis=0, tiled...  184 us
    div x1, other arithmetic, filters(): return (blurred / jnp.sqrt(local_var), local_var)  48.1 us
    add x2, other arithmetic, box_sum(): vertical = sum((field[offset:offset + height, :] for offset in range(span)))  24.6 us
    concatenate x2, local copies, waits for them, and re-layouts, with_halo(): shard = jnp.concatenate([before, shard, after], axis=dim)  20.3 us
    unnamed x18, local copies, waits for them, and re-layouts  17.6 us
    scatter x1, local copies, waits for them, and re-layouts, per_device(): jnp.zeros((tiles * CAP, 2, side, side), jnp.bfloat16).at[position]  16.2 us
  transfers between devices with their start and end apart: 7, of which 4 were waited for; matrix products, arithmetic and copies ran while one was open for 8% of the time, Pallas kernels for 0%

commit v1 on v0

v1 whole, which is shorter than its diff:
```python
import functools

import jax
import jax.numpy as jnp
from jax import lax
from jax.experimental import pallas as pl
from jax.experimental.pallas import tpu as pltpu
from jax.sharding import PartitionSpec as P

TY = 1024
TX = 1024
STEP = 128
CAP = 2
EDGE = 16
HALO = 8
SIDE = 128
ROWS = 64
MIB = 1 << 20


def warp_kernel(
    tiles,
    visit_ref,
    tile_ref,
    offset_ref,
    good_ref,
    rows_hbm,
    cols_hbm,
    var_hbm,
    *refs,
):
    more = (len(refs) - 9) // 2
    image_hbm, refs = refs[:more], refs[more:]
    out_hbm, code_ref, rows, cols, var = refs[:5]
    image = refs[5 : 5 + more]
    done, count, sems, out_sems = refs[5 + more :]
    blocks = var.shape[0]
    loads = [
        pltpu.make_async_copy(rows_hbm, rows, sems.at[0]),
        pltpu.make_async_copy(cols_hbm, cols, sems.at[1]),
    ]
    half = blocks // 2
    for part in range(2):
        span = pl.ds(part * half, half)
        loads.append(
            pltpu.make_async_copy(var_hbm.at[span], var.at[span], sems.at[2 + 2 * part])
        )
        if image:
            loads.append(
                pltpu.make_async_copy(
                    image_hbm[0].at[span], image[0].at[span], sems.at[3 + 2 * part]
                )
            )
    for load in loads:
        load.start()

    @pl.loop(0, tiles)
    def _(tile):
        count[tile] = 0
        for slot in range(CAP):
            code_ref[tile * CAP + slot] = -1

    per_part = 1 + len(image)
    for load in loads[: 2 + per_part]:
        load.wait()

    def one(block):
        visit = visit_ref[block]
        tile = tile_ref[block]
        rank = count[tile]
        count[tile] = rank + 1
        slot = tile * CAP + rank
        code_ref[slot] = offset_ref[2 * block] * 8 + offset_ref[2 * block + 1]
        good = good_ref[pl.ds(visit, 1), :].astype(jnp.float32)
        plane = var[block].astype(jnp.float32) * good
        if image:
            plane = plane * image[0][block].astype(jnp.float32)
        plane = plane.astype(jnp.bfloat16)
        turned = jnp.dot(rows[visit], plane, preferred_element_type=jnp.float32)
        warped = lax.dot_general(
            turned.astype(jnp.bfloat16),
            cols[visit],
            (((1,), (1,)), ((), ())),
            preferred_element_type=jnp.float32,
        )
        done[block] = warped.astype(jnp.bfloat16)
        pltpu.make_async_copy(done.at[block], out_hbm.at[slot], out_sems.at[block]).start()

    unroll = 4 if half % 4 == 0 else 1
    for part in range(2):
        if part:
            for load in loads[2 + per_part :]:
                load.wait()

        @pl.loop(part * half, (part + 1) * half, step=unroll)
        def _(block):
            for ahead in range(unroll):
                one(block + ahead)

    @pl.loop(0, blocks)
    def _(block):
        pltpu.make_async_copy(done.at[block], out_hbm.at[0], out_sems.at[block]).wait()


def warp(tiles, visit, tile, offset, good, rows, cols, var, *image):
    blocks, side, _ = var.shape
    smem = pl.BlockSpec(memory_space=pltpu.SMEM)
    anywhere = pl.BlockSpec(memory_space=pl.ANY)
    plane = pltpu.VMEM(var.shape, jnp.bfloat16)
    return pl.pallas_call(
        functools.partial(warp_kernel, tiles),
        out_shape=(
            jax.ShapeDtypeStruct((tiles * CAP, side, side), jnp.bfloat16),
            jax.ShapeDtypeStruct((tiles * CAP,), jnp.int32),
        ),
        in_specs=[smem, smem, smem, pl.BlockSpec(memory_space=pltpu.VMEM)]
        + [anywhere] * (3 + len(image)),
        out_specs=(anywhere, smem),
        scratch_shapes=[
            pltpu.VMEM(rows.shape, jnp.bfloat16),
            pltpu.VMEM(cols.shape, jnp.bfloat16),
            *[plane] * (1 + len(image)),
            plane,
            pltpu.SMEM((tiles,), jnp.int32),
            pltpu.SemaphoreType.DMA((6,)),
            pltpu.SemaphoreType.DMA((blocks,)),
        ],
        compiler_params=pltpu.CompilerParams(vmem_limit_bytes=32 * MIB),
        cost_estimate=pl.CostEstimate(
            flops=4 * blocks * side**3, bytes_accessed=4 * blocks * side**2 * 2, transcendentals=0
        ),
        name="warp_data" if image else "warp_weight",
    )(visit, tile, offset, good, rows, cols, var, *image)


def place_kernel(code_ref, blocks_ref, out_ref, edge_ref, total):
    step = pl.program_id(0)
    some, side, _ = blocks_ref.shape
    height, breadth = total.shape

    @pl.when(step == 0)
    def _():
        total[...] = jnp.zeros_like(total)

    for block in range(some):
        code = code_ref[step * some + block]

        @pl.when(code >= 0)
        def _():
            row = pl.multiple_of((code // 8) * STEP, STEP)
            col = pl.multiple_of((code % 8) * STEP, STEP)
            total[pl.ds(row, side), pl.ds(col, side)] += blocks_ref[block].astype(jnp.float32)

    @pl.when(step == pl.num_programs(0) - 1)
    def _():
        out_ref[...] = total[...].astype(jnp.bfloat16)
        edge_ref[:EDGE] = total[:EDGE].astype(jnp.bfloat16)
        edge_ref[EDGE : 2 * EDGE] = total[height - EDGE :].astype(jnp.bfloat16)
        edge_ref[2 * EDGE : 3 * EDGE] = total[:, :SIDE].T[:EDGE].astype(jnp.bfloat16)
        edge_ref[3 * EDGE :] = total[:, breadth - SIDE :].T[SIDE - EDGE :].astype(jnp.bfloat16)


def place(code, blocks):
    count, side, _ = blocks.shape
    some = 4
    return pl.pallas_call(
        place_kernel,
        grid_spec=pltpu.PrefetchScalarGridSpec(
            num_scalar_prefetch=1,
            grid=(count // some,),
            in_specs=[pl.BlockSpec((some, side, side), lambda step, code: (step, 0, 0))],
            out_specs=(
                pl.BlockSpec((TY, TX), lambda step, code: (0, 0)),
                pl.BlockSpec((4 * EDGE, TX), lambda step, code: (0, 0)),
            ),
            scratch_shapes=[pltpu.VMEM((TY, TX), jnp.float32)],
        ),
        out_shape=(
            jax.ShapeDtypeStruct((TY, TX), jnp.bfloat16),
            jax.ShapeDtypeStruct((4 * EDGE, TX), jnp.bfloat16),
        ),
        compiler_params=pltpu.CompilerParams(vmem_limit_bytes=32 * MIB),
        cost_estimate=pl.CostEstimate(
            flops=count * side**2, bytes_accessed=count * side**2 * 2 + TY * TX * 2, transcendentals=0
        ),
        name="place",
    )(code, blocks)


def visit_parts(shard):
    count = lax.axis_size("visit")
    if count == 1:
        return (shard,)
    if count == 2:
        return (shard, lax.ppermute(shard, "visit", [(0, 1), (1, 0)]))
    return (lax.psum(shard.astype(jnp.float32), "visit"),)


def ratio(data, weight):
    top = sum(part.astype(jnp.float32) for part in data)
    below = sum(part.astype(jnp.float32) for part in weight)
    return top / jnp.maximum(below, 1.0)


def neighbours(first, last, axis):
    count = lax.axis_size(axis)
    up = [(i, i + 1) for i in range(count - 1)]
    down = [(j, i) for i, j in up]
    return lax.ppermute(last, axis, up), lax.ppermute(first, axis, down)


def filter_kernel(parts, taps_ref, *refs):
    data, weight = refs[:parts], refs[parts : 2 * parts]
    above, below, left, right, detection_ref, variance_ref, coadd = refs[2 * parts :]
    height, breadth = detection_ref.shape
    wide = breadth + SIDE

    coadd[:HALO, :] = above[...]
    coadd[HALO + height :, :] = below[...]
    lanes = jnp.concatenate(
        [right[...], jnp.zeros((SIDE - 2 * HALO, height), jnp.float32), left[...]], axis=0
    )
    coadd[HALO : HALO + height, breadth:] = lanes.T

    @pl.loop(0, height, step=ROWS)
    def _(start):
        start = pl.multiple_of(start, ROWS)
        rows = pl.ds(start, ROWS)
        coadd[pl.ds(pl.multiple_of(start + HALO, HALO), ROWS), :breadth] = ratio(
            [ref[rows, :] for ref in data], [ref[rows, :] for ref in weight]
        )

    taps = [taps_ref[tap] for tap in range(7)]
    tall = ROWS + 2 * HALO

    def down(field, by):
        return field if by == 0 else pltpu.roll(field, by % tall, 0)

    def across(field, by):
        return field if by == 0 else pltpu.roll(field, by % wide, 1)

    def three(field, shift, by):
        return field + shift(field, by) + shift(field, -by)

    @pl.loop(0, height, step=ROWS)
    def _(start):
        start = pl.multiple_of(start, ROWS)
        field = coadd[pl.ds(start, tall), :]
        resid = field - three(three(field, down, 1), across, 1) * (1.0 / 9.0)
        square = resid * resid
        tower = three(three(square, down, 1), down, 3)[HALO : HALO + ROWS]
        box = three(three(tower, across, 1), across, 3)
        variance = box[:, :breadth] * (1.0 / 81.0) + 1e-05
        rowwise = sum(taps[tap] * down(field, 3 - tap) for tap in range(7))[HALO : HALO + ROWS]
        blurred = sum(taps[tap] * across(rowwise, 3 - tap) for tap in range(7))
        rows = pl.ds(start, ROWS)
        variance_ref[rows, :] = variance
        detection_ref[rows, :] = blurred[:, :breadth] * lax.rsqrt(variance)


def filters(taps, data, weight, halos):
    shape = jax.ShapeDtypeStruct((TY, TX), jnp.float32)
    vmem = pl.BlockSpec(memory_space=pltpu.VMEM)
    return pl.pallas_call(
        functools.partial(filter_kernel, len(data)),
        out_shape=(shape, shape),
        in_specs=[pl.BlockSpec(memory_space=pltpu.SMEM)]
        + [vmem] * (2 * len(data) + len(halos)),
        out_specs=(vmem, vmem),
        scratch_shapes=[pltpu.VMEM((TY + 2 * HALO, TX + SIDE), jnp.float32)],
        compiler_params=pltpu.CompilerParams(vmem_limit_bytes=48 * MIB),
        name="filters",
    )(taps, *data, *weight, *halos)


def per_device(
    images, inv_var, good_columns, warp_rows, warp_cols, block_visit, dest_tile, offsets, psf_taps
):
    tiles = lax.axis_size("py") * lax.axis_size("px")
    sky = ("py", "px")
    tile, offset = dest_tile[:, 0], offsets.reshape(-1)
    common = (tiles, block_visit, tile, offset, good_columns, warp_rows, warp_cols)

    def send(blocks):
        return lax.all_to_all(blocks, sky, split_axis=0, concat_axis=0, tiled=True)

    weight_out, code_out = warp(*common, inv_var)
    weight_in = send(weight_out)
    code = send(code_out)
    data_out, _ = warp(*common, inv_var, images)
    weight_in, data_out = lax.optimization_barrier((weight_in, data_out))
    data_in = send(data_out)

    weight_own, weight_edge_own = place(code, weight_in)
    weight_edge = visit_parts(weight_edge_own)
    weight = visit_parts(weight_own)
    data_own, data_edge_own = place(code, data_in)
    data_edge = visit_parts(data_edge_own)
    data = visit_parts(data_own)

    edge = ratio(data_edge, weight_edge)
    first_row, last_row, first_col, last_col = (
        edge[:HALO],
        edge[2 * EDGE - HALO : 2 * EDGE],
        edge[2 * EDGE : 2 * EDGE + HALO],
        edge[4 * EDGE - HALO :],
    )
    above, below = neighbours(first_row, last_row, "py")
    left, right = neighbours(
        jnp.concatenate([first_col, above[:, :SIDE], below[:, :SIDE]], axis=1),
        jnp.concatenate([last_col, above[:, TX - SIDE :], below[:, TX - SIDE :]], axis=1),
        "px",
    )
    from_left = jnp.arange(SIDE, dtype=jnp.int32)[None, :] >= SIDE // 2

    def corners(at):
        span = slice(TY + at * SIDE, TY + (at + 1) * SIDE)
        return jnp.where(from_left, left[:, span], right[:, span])

    above = jnp.concatenate([above, corners(0)], axis=1)
    below = jnp.concatenate([below, corners(1)], axis=1)
    return filters(psf_taps, data, weight, (above, below, left[:, :TY], right[:, :TY]))


def solution(mesh):
    in_specs = (
        P(("visit", "py", "px"), None, None),
        P(("visit", "py", "px"), None, None),
        P("visit", None),
        P("visit", None, None),
        P("visit", None, None),
        P(("visit", "py", "px")),
        P(("visit", "py", "px"), None),
        P(("visit", "py", "px"), None),
        P(),
    )
    out_specs = (P("py", "px"), P("py", "px"))
    return jax.shard_map(
        per_device, mesh=mesh, in_specs=in_specs, out_specs=out_specs, check_vma=False
    )
```

time: 629 us -> 381 us (0.61)
  waiting for transfers between devices: 388 us -> 260 us
  other arithmetic: 102 us -> 0.79 us
  Pallas kernels: 0 us -> 69 us
  local copies, waits for them, and re-layouts: 83.3 us -> 16.9 us
  matrix products: 18.2 us -> 0 us
  between operations: 14.3 us -> 0.88 us
  starting transfers between devices: 21.6 us -> 32.5 us
    psum x1 -> x0, waiting for transfers between devices: 197 us -> none  [per_device(): data_sum, weight_sum = lax.psum((totals[0], totals[1]), 'visit')]
    ppermute x4 -> x8, waiting for transfers between devices: 6.46 us -> 81.1 us  [the longest x4 78.6 us: visit_parts(): return (shard, lax.ppermute(shard, 'visit', [(0, 1), (1, 0)]))]
    pallas_call x0 -> x5, Pallas kernels: none -> 69 us  [the longest x2 28.7 us: warp(): pl.pallas_call(functools.partial(warp_kernel, tiles), out_shape=(jax.Shap...]
    div x2 -> x1, other arithmetic: 52.5 us -> 0.09 us  [ratio(): return top / jnp.maximum(below, 1.0)]
    add x4 -> x0, other arithmetic: 34 us -> none  [the longest x2 24.6 us: box_sum(): vertical = sum((field[offset:offset + height, :] for offset in range(span)))]
    concatenate x2 -> x0, local copies, waits for them, and re-layouts: 20.3 us -> none  [with_halo(): shard = jnp.concatenate([before, shard, after], axis=dim)]
    dot_general x2 -> x0, matrix products: 18.2 us -> none  [the longest x1 9.71 us: per_device(): jnp.einsum('yxsac,sparcq->pyrxq', placement, quarters, preferred_element_...]
    scatter x2 -> x0, local copies, waits for them, and re-layouts: 16.8 us -> none  [the longest x1 16.2 us: per_device(): jnp.zeros((tiles * CAP, 2, side, side), jnp.bfloat16).at[position]]
  transfers between devices with their start and end apart: 7 -> 11, of which waited for: 4 -> 7; matrix products, arithmetic and copies ran while one was open for 8% -> 0% of each run, Pallas kernels for 0% -> 7%
where the time goes in v1:
time: 381 us; the launch traced here: 380 us
  waiting for transfers between devices  260 us (68%)
  Pallas kernels  69 us (18%)
  starting transfers between devices  32.5 us (9%)
  local copies, waits for them, and re-layouts  16.9 us (4%)
    all_to_all x3, waiting for transfers between devices, send(): return lax.all_to_all(blocks, sky, split_axis=0, concat_axis=0, tiled=True)  179 us
    ppermute x4, waiting for transfers between devices, visit_parts(): return (shard, lax.ppermute(shard, 'visit', [(0, 1), (1, 0)]))  78.6 us
    pallas_call x2, Pallas kernels, warp(): pl.pallas_call(functools.partial(warp_kernel, tiles), out_shape=(jax.Shap...  28.7 us
    pallas_call x1, Pallas kernels, filters(): pl.pallas_call(functools.partial(filter_kernel, len(data)), out_shape=(sh...  27.8 us
    all_to_all x3, starting transfers between devices, send(): return lax.all_to_all(blocks, sky, split_axis=0, concat_axis=0, tiled=True)  17.2 us
    unnamed x37, local copies, waits for them, and re-layouts  15.5 us
    pallas_call x2, Pallas kernels, place(): pl.pallas_call(place_kernel, grid_spec=pltpu.PrefetchScalarGridSpec(num_s...  12.5 us
    ppermute x4, starting transfers between devices, neighbours(): return (lax.ppermute(last, axis, up), lax.ppermute(first, axis, down))  10.2 us
  transfers between devices with their start and end apart: 11, of which 7 were waited for; matrix products, arithmetic and copies ran while one was open for 0% of the time, Pallas kernels for 7%

profile of v1, /device:TPU:0, one launch (start us, length us, event | category | flops | bytes accessed | tf_op | source)
XLA Modules:
  0.0 380.2 jit_solution(12064691667899555049)
XLA Ops:
  0.6 0.8 copy.13
  1.5 1.9 copy-done.2
  3.4 1.2 copy-done.6
  4.6 1.2 copy-done.8
  5.8 0.7 copy-done.10
  7.8 14.2 %warp_weight.1 = (bf16[32,256,256]{2,1,0:T(8,128)(2,1)S(1)}, s32[32]{0:T(128)S(1)}) custom-call(s32[24]{0:T(128)S(1)} %copy-done.13, s32[24]{0:T(128)S(1)} %bitcast.3, s32[48]{0:T(128)S(1)} %reshape.14.offset_ref, s32[8,256]{1,0:T(8,128)S(1)} %copy-done.10, bf16[8,256,256]{2,1,0:T(8,128)(2,1)S(1)} %copy-done.6, bf16[8,256,256]{2,1,0:T(8,128)(2,1)S(1)} %copy-done.8, ...), custom_call_target="tpu_custom_call" | custom-call | flops 1610612736 | bytes 12582912 | tf_op jit(solution)/shard_map/warp_weight/pallas_call | solution.py:110
  22.1 2.0 copy-done.1
  24.1 7.7 %all-to-all-start.1 = ((bf16[32,256,256]{2,1,0:T(8,128)(2,1)}), bf16[32,256,256]{2,1,0:T(8,128)(2,1)}, u32[]{:S(2)}, u32[]{:S(2)}) async-start(bf16[32,256,256]{2,1,0:T(8,128)(2,1)} %copy-done.1), calls=%async_computation.1 | async-start | bytes 8388608 | tf_op jit(solution)/shard_map/all_to_all | solution.py:285
  32.5 93.7 %all-to-all-done.1.blocks_ref = bf16[32,256,256]{2,1,0:T(8,128)(2,1)} async-done(((bf16[32,256,256]{2,1,0:T(8,128)(2,1)}), bf16[32,256,256]{2,1,0:T(8,128)(2,1)}, u32[]{:S(2)}, u32[]{:S(2)}) %all-to-all-start.1) | async-done | bytes 4194336 | tf_op jit(solution)/shard_map/all_to_all | solution.py:285
  126.3 3.5 all-to-all-start
  129.8 1.9 copy-done.4
  131.7 1.2 copy-done.7
  132.9 1.2 copy-done.9
  134.1 14.4 %warp_data.1 = (bf16[32,256,256]{2,1,0:T(8,128)(2,1)S(1)}, s32[32]{0:T(128)}) custom-call(s32[24]{0:T(128)S(1)} %copy-done.14, s32[24]{0:T(128)S(1)} %bitcast.4, s32[48]{0:T(128)S(1)} %reshape.14.offset_ref, s32[8,256]{1,0:T(8,128)S(1)} %copy-done.11, bf16[8,256,256]{2,1,0:T(8,128)(2,1)S(1)} %copy-done.7, bf16[8,256,256]{2,1,0:T(8,128)(2,1)S(1)} %copy-done.9, ...), custom_call_target="tpu_custom_call" | custom-call | flops 1610612736 | bytes 12582912 | tf_op jit(solution)/shard_map/warp_data/pallas_call | solution.py:110
  148.6 2.0 copy-done
  150.6 6.0 %all-to-all-start.2 = ((bf16[32,256,256]{2,1,0:T(8,128)(2,1)}), bf16[32,256,256]{2,1,0:T(8,128)(2,1)}, u32[]{:S(2)}, u32[]{:S(2)}) async-start(bf16[32,256,256]{2,1,0:T(8,128)(2,1)} %copy-done), calls=%async_computation.2 | async-start | bytes 8388608 | tf_op jit(solution)/shard_map/all_to_all | solution.py:285
  157.9 6.3 %place.3 = (bf16[1024,1024]{1,0:T(8,128)(2,1)S(1)}, bf16[64,1024]{1,0:T(8,128)(2,1)S(1)}) custom-call(s32[32]{0:T(128)S(1)} %all_to_all.15.code_ref, bf16[32,256,256]{2,1,0:T(8,128)(2,1)} %all-to-all-done.1.blocks_ref), custom_call_target="tpu_custom_call" | custom-call | flops 2097152 | bytes 6291456 | tf_op jit(solution)/shard_map/place/pallas_call | solution.py:166
  164.2 1.6 collective-permute-start.3
  165.7 85.3 %all-to-all-done.2.blocks_ref = bf16[32,256,256]{2,1,0:T(8,128)(2,1)} async-done(((bf16[32,256,256]{2,1,0:T(8,128)(2,1)}), bf16[32,256,256]{2,1,0:T(8,128)(2,1)}, u32[]{:S(2)}, u32[]{:S(2)}) %all-to-all-start.2) | async-done | bytes 4194336 | tf_op jit(solution)/shard_map/all_to_all | solution.py:285
  251.0 6.3 %place.2 = (bf16[1024,1024]{1,0:T(8,128)(2,1)S(1)}, bf16[64,1024]{1,0:T(8,128)(2,1)S(1)}) custom-call(s32[32]{0:T(128)S(1)} %all_to_all.15.code_ref, bf16[32,256,256]{2,1,0:T(8,128)(2,1)} %all-to-all-done.2.blocks_ref), custom_call_target="tpu_custom_call" | custom-call | flops 2097152 | bytes 6291456 | tf_op jit(solution)/shard_map/place/pallas_call | solution.py:166
  257.3 1.6 collective-permute-start.2
  259.4 1.5 collective-permute-start
  260.9 2.9 collective-permute-done.2
  263.9 1.3 collective-permute-start.5
  265.2 3.0 collective-permute-start.4
  268.2 0.8 collective-permute-done.4
  269.1 1.3 collective-permute-start.7
  270.4 4.5 %collective-permute-start.6 = (f32[8,1280]{1,0:T(8,128)S(1)}, f32[8,1280]{1,0:T(8,128)S(1)}, u32[]{:S(2)}, u32[]{:S(2)}) collective-permute-start(f32[8,1280]{1,0:T(8,128)S(1)} %pad_maximum_fusion), channel_id=1, source_target_pairs={{0,1},{1,2},{2,3},{4,5},{5,6},{6,7},{8,9},{9,10},{10,11},{12,13},{... | collective-permute-start | bytes 122888 | tf_op jit(solution)/shard_map/ppermute | solution.py:209
  275.0 1.6 collective-permute-done.6
  276.6 32.1 %collective-permute-done.1.refs_3_ = bf16[1024,1024]{1,0:T(8,128)(2,1)S(1)} collective-permute-done((bf16[1024,1024]{1,0:T(8,128)(2,1)S(1)}, bf16[1024,1024]{1,0:T(8,128)(2,1)S(1)}, u32[]{:S(2)}, u32[]{:S(2)}) %collective-permute-start.1) | collective-permute-done | bytes 2097184 | tf_op jit(solution)/shard_map/ppermute | solution.py:195
  308.7 43.6 %collective-permute-done.refs_1_ = bf16[1024,1024]{1,0:T(8,128)(2,1)S(1)} collective-permute-done((bf16[1024,1024]{1,0:T(8,128)(2,1)S(1)}, bf16[1024,1024]{1,0:T(8,128)(2,1)S(1)}, u32[]{:S(2)}, u32[]{:S(2)}) %collective-permute-start) | collective-permute-done | bytes 2097184 | tf_op jit(solution)/shard_map/ppermute | solution.py:195
  352.3 27.8 %filters.1 = (f32[1024,1024]{1,0:T(8,128)}, f32[1024,1024]{1,0:T(8,128)}) custom-call(f32[7]{0:T(128)S(1)} %copy-done.12, bf16[1024,1024]{1,0:T(8,128)(2,1)S(1)} %get-tuple-element.15.refs_0_, bf16[1024,1024]{1,0:T(8,128)(2,1)S(1)} %collective-permute-done.refs_1_, bf16[1024,1024]{1,0:T(8,128)(2,1)} %copy-done.5, bf16[1024,1024]{1,0:T(8,128)(2,1)} %copy-done.17, ...), custom_call_target="tpu_custom_call" | custom-call | tf_op jit(solution)/shard_map/filters/pallas_call | solution.py:264
  (48 shorter events, 4.1 us)
Async XLA Ops:
  1.5 1.9 copy-start.2
  3.4 1.2 copy-start.6
  4.6 1.2 copy-start.8
  5.8 0.7 copy-start.10
  6.5 0.7 copy-start.13
  7.2 0.7 copy-start.15
  22.1 2.0 copy-start.1
  24.1 105.6 %copy-start.3 = (bf16[24,256,256]{2,1,0:T(8,128)(2,1)S(1)}, bf16[24,256,256]{2,1,0:T(8,128)(2,1)}, u32[]{:S(2)}) copy-start(bf16[24,256,256]{2,1,0:T(8,128)(2,1)} %var_hbm.3) | copy-start | bytes 9437188
  24.1 105.7 %copy-start.11 = (s32[8,256]{1,0:T(8,128)S(1)}, s32[8,256]{1,0:T(8,128)}, u32[]{:S(2)}) copy-start(s32[8,256]{1,0:T(8,128)} %good_ref.3) | copy-start | bytes 24580
  24.1 105.7 %copy-start.14 = (s32[24]{0:T(128)S(1)}, s32[24]{0:T(128)}, u32[]{:S(2)}) copy-start(s32[24]{0:T(128)} %visit_ref.3) | copy-start | bytes 292
  24.1 105.7 %copy-start.16 = (s32[24,1]{0,1:T(1,128)S(1)}, s32[24,1]{0,1:T(1,128)}, u32[]{:S(2)}) copy-start(s32[24,1]{0,1:T(1,128)} %param.15) | copy-start | bytes 292
  24.1 102.2 %all-to-all-start.1 = ((bf16[32,256,256]{2,1,0:T(8,128)(2,1)}), bf16[32,256,256]{2,1,0:T(8,128)(2,1)}, u32[]{:S(2)}, u32[]{:S(2)}) async-start(bf16[32,256,256]{2,1,0:T(8,128)(2,1)} %copy-done.1), calls=%async_computation.1 | async-start | bytes 8388608 | tf_op jit(solution)/shard_map/all_to_all | solution.py:285
  126.3 24.3 %all-to-all-start = ((s32[16,2,1]{1,2,0:T(1,128)}), s32[16,2,1]{1,2,0:T(1,128)S(1)}, u32[]{:S(2)}, u32[]{:S(2)}) async-start(s32[16,2,1]{1,2,0:T(1,128)} %bitcast.1), calls=%async_computation | async-start | bytes 16384 | tf_op jit(solution)/shard_map/all_to_all | solution.py:285
  129.8 1.9 copy-start.4
  131.7 1.2 copy-start.7
  132.9 1.2 copy-start.9
  148.6 2.0 copy-start
  150.6 100.4 %all-to-all-start.2 = ((bf16[32,256,256]{2,1,0:T(8,128)(2,1)}), bf16[32,256,256]{2,1,0:T(8,128)(2,1)}, u32[]{:S(2)}, u32[]{:S(2)}) async-start(bf16[32,256,256]{2,1,0:T(8,128)(2,1)} %copy-done), calls=%async_computation.2 | async-start | bytes 8388608 | tf_op jit(solution)/shard_map/all_to_all | solution.py:285
  157.9 194.5 %copy-start.12 = (f32[7]{0:T(128)S(1)}, f32[7]{0:T(128)}, u32[]{:S(2)}) copy-start(f32[7]{0:T(128)} %taps_ref.1) | copy-start | bytes 88
  164.1 188.2 %copy-start.5 = (bf16[1024,1024]{1,0:T(8,128)(2,1)}, bf16[1024,1024]{1,0:T(8,128)(2,1)S(1)}, u32[]{:S(2)}) copy-start(bf16[1024,1024]{1,0:T(8,128)(2,1)S(1)} %get-tuple-element.17.refs_2_) | copy-start | bytes 6291460
  164.2 96.7 %collective-permute-start.3 = (bf16[64,1024]{1,0:T(8,128)(2,1)S(1)}, bf16[64,1024]{1,0:T(8,128)(2,1)S(1)}, u32[]{:S(2)}, u32[]{:S(2)}) collective-permute-start(bf16[64,1024]{1,0:T(8,128)(2,1)S(1)} %get-tuple-element.19), channel_id=1, source_target_pairs={{0,16},{16,0},{1,17},{17,1},{2,18},{18,2},{3,19},{19,3},{4,20},{20... | collective-permute-start | bytes 393224 | tf_op jit(solution)/shard_map/ppermute | solution.py:195
  257.3 6.5 %collective-permute-start.2 = (bf16[64,1024]{1,0:T(8,128)(2,1)S(1)}, bf16[64,1024]{1,0:T(8,128)(2,1)S(1)}, u32[]{:S(2)}, u32[]{:S(2)}) collective-permute-start(bf16[64,1024]{1,0:T(8,128)(2,1)S(1)} %get-tuple-element.18), channel_id=1, source_target_pairs={{0,16},{16,0},{1,17},{17,1},{2,18},{18,2},{3,19},{19,3},{4,20},{20... | collective-permute-start | bytes 393224 | tf_op jit(solution)/shard_map/ppermute | solution.py:195
  258.8 49.9 %collective-permute-start.1 = (bf16[1024,1024]{1,0:T(8,128)(2,1)S(1)}, bf16[1024,1024]{1,0:T(8,128)(2,1)S(1)}, u32[]{:S(2)}, u32[]{:S(2)}) collective-permute-start(bf16[1024,1024]{1,0:T(8,128)(2,1)S(1)} %get-tuple-element.17.refs_2_), channel_id=1, source_target_pairs={{0,16},{16,0},{1,17},{17,1},{2,18},{18,2},{3,19},{19,3},{4,20},{20... | collective-permute-start | bytes 6291464 | tf_op jit(solution)/shard_map/ppermute | solution.py:195
  259.4 92.9 %collective-permute-start = (bf16[1024,1024]{1,0:T(8,128)(2,1)S(1)}, bf16[1024,1024]{1,0:T(8,128)(2,1)S(1)}, u32[]{:S(2)}, u32[]{:S(2)}) collective-permute-start(bf16[1024,1024]{1,0:T(8,128)(2,1)S(1)} %get-tuple-element.15.refs_0_), channel_id=1, source_target_pairs={{0,16},{16,0},{1,17},{17,1},{2,18},{18,2},{3,19},{19,3},{4,20},{20... | collective-permute-start | bytes 6291464 | tf_op jit(solution)/shard_map/ppermute | solution.py:195
  263.9 4.3 %collective-permute-start.5 = (f32[8,1024]{1,0:T(8,128)S(1)}, f32[8,1024]{1,0:T(8,128)S(1)}, u32[]{:S(2)}, u32[]{:S(2)}) collective-permute-start(f32[8,1024]{1,0:T(8,128)S(1)} %get-tuple-element.22), channel_id=1, source_target_pairs={{4,0},{8,4},{12,8},{5,1},{9,5},{13,9},{6,2},{10,6},{14,10},{7,3},{... | collective-permute-start | bytes 98312 | tf_op jit(solution)/shard_map/ppermute | solution.py:209
  265.2 3.9 %collective-permute-start.4 = (f32[8,1024]{1,0:T(8,128)S(1)}, f32[8,1024]{1,0:T(8,128)S(1)}, u32[]{:S(2)}, u32[]{:S(2)}) collective-permute-start(f32[8,1024]{1,0:T(8,128)S(1)} %get-tuple-element.23), channel_id=1, source_target_pairs={{0,4},{4,8},{8,12},{1,5},{5,9},{9,13},{2,6},{6,10},{10,14},{3,7},{... | collective-permute-start | bytes 98312 | tf_op jit(solution)/shard_map/ppermute | solution.py:209
  269.1 5.9 %collective-permute-start.7 = (f32[8,1280]{1,0:T(8,128)S(1)}, f32[8,1280]{1,0:T(8,128)S(1)}, u32[]{:S(2)}, u32[]{:S(2)}) collective-permute-start(f32[8,1280]{1,0:T(8,128)S(1)} %pad_maximum_fusion.1), channel_id=1, source_target_pairs={{1,0},{2,1},{3,2},{5,4},{6,5},{7,6},{9,8},{10,9},{11,10},{13,12},{... | collective-permute-start | bytes 122888 | tf_op jit(solution)/shard_map/ppermute | solution.py:209
  270.4 6.2 %collective-permute-start.6 = (f32[8,1280]{1,0:T(8,128)S(1)}, f32[8,1280]{1,0:T(8,128)S(1)}, u32[]{:S(2)}, u32[]{:S(2)}) collective-permute-start(f32[8,1280]{1,0:T(8,128)S(1)} %pad_maximum_fusion), channel_id=1, source_target_pairs={{0,1},{1,2},{2,3},{4,5},{5,6},{6,7},{8,9},{9,10},{10,11},{12,13},{... | collective-permute-start | bytes 122888 | tf_op jit(solution)/shard_map/ppermute | solution.py:209
  308.7 43.6 %copy-start.17 = (bf16[1024,1024]{1,0:T(8,128)(2,1)}, bf16[1024,1024]{1,0:T(8,128)(2,1)S(1)}, u32[]{:S(2)}) copy-start(bf16[1024,1024]{1,0:T(8,128)(2,1)S(1)} %collective-permute-done.1.refs_3_) | copy-start | bytes 6291460

commit v2 on v0

v2 whole, which is shorter than its diff:
```python
import functools

import jax
import jax.numpy as jnp
from jax import lax
from jax.experimental import pallas as pl
from jax.experimental.pallas import tpu as pltpu
from jax.sharding import PartitionSpec as P

TY = 1024
TX = 1024
STEP = 128
CAP = 2
UNITS = TY // STEP
HALO = 8
SIDE = 128
WIDE = TX + SIDE
GROUP = 4
MIB = 1 << 20
EVERY = ("visit", "py", "px")
HBM = pl.BlockSpec(memory_space=pltpu.HBM)
SMEM = pl.BlockSpec(memory_space=pltpu.SMEM)
VMEM = pl.BlockSpec(memory_space=pltpu.VMEM)


def shares(visits):
    if visits == 2:
        edge, inner = 48, 16
        return [(edge, (0, STEP - edge)), (inner, (edge, edge + inner))]
    rows = STEP // visits
    return [(rows, tuple(visit * rows for visit in range(visits)))]


def warp_kernel(
    tiles, share, visit_ref, tile_ref, good_ref, rows_hbm, cols_hbm, var_hbm, image_hbm, out_hbm,
    rows, cols, var, image, done, count, table_sems, sems, out_sems,
):
    blocks, side, _ = var.shape
    some, firsts = share
    groups = blocks // GROUP
    tables = [
        pltpu.make_async_copy(rows_hbm, rows, table_sems.at[0]),
        pltpu.make_async_copy(cols_hbm, cols, table_sems.at[1]),
    ]

    def loads(group):
        span = pl.ds(group * GROUP, GROUP)
        return (
            pltpu.make_async_copy(var_hbm.at[span], var.at[span], sems.at[group, 0]),
            pltpu.make_async_copy(image_hbm.at[span], image.at[span], sems.at[group, 1]),
        )

    for load in tables:
        load.start()
    for group in range(groups):
        for load in loads(group):
            load.start()

    @pl.loop(0, tiles)
    def _(tile):
        count[tile] = 0

    for load in tables:
        load.wait()

    strips = [first + strip * STEP for first in firsts for strip in range(side // STEP)]
    tall = some * len(strips)
    part = tall // len(firsts)

    @pl.loop(0, groups)
    def _(group):
        for load in loads(group):
            load.wait()
        visits = [visit_ref[group * GROUP + ahead] for ahead in range(GROUP)]
        planes, turned, warped = [], [], []
        for ahead in range(GROUP):
            block = group * GROUP + ahead
            good = good_ref[pl.ds(visits[ahead], 1), :].astype(jnp.float32)
            weight = var[block].astype(jnp.float32) * good
            data = weight * image[block].astype(jnp.float32)
            planes.append(
                jnp.concatenate([data.astype(jnp.bfloat16), weight.astype(jnp.bfloat16)], axis=1)
            )
        for ahead in range(GROUP):
            matrix = jnp.concatenate(
                [rows[visits[ahead], first : first + some, :] for first in strips], axis=0
            )
            turned.append(
                jnp.dot(matrix, planes[ahead], preferred_element_type=jnp.float32).astype(jnp.bfloat16)
            )
        for ahead in range(GROUP):
            both = jnp.concatenate([turned[ahead][:, :side], turned[ahead][:, side:]], axis=0)
            warped.append(
                lax.dot_general(
                    both,
                    cols[visits[ahead]],
                    (((1,), (1,)), ((), ())),
                    preferred_element_type=jnp.float32,
                ).astype(jnp.bfloat16)
            )
        for ahead in range(GROUP):
            block = group * GROUP + ahead
            for visit in range(len(firsts)):
                for plane in range(2):
                    start = plane * tall + visit * part
                    done[block, visit, plane * part : (plane + 1) * part, :] = warped[ahead][
                        start : start + part
                    ]
        for ahead in range(GROUP):
            block = group * GROUP + ahead
            tile = tile_ref[block]
            rank = count[tile]
            count[tile] = rank + 1
            for visit in range(len(firsts)):
                pltpu.make_async_copy(
                    done.at[block, visit],
                    out_hbm.at[(visit * tiles + tile) * CAP + rank],
                    out_sems.at[block, visit],
                ).start()

    @pl.loop(0, blocks)
    def _(block):
        for visit in range(len(firsts)):
            pltpu.make_async_copy(
                done.at[block, visit], out_hbm.at[0], out_sems.at[block, visit]
            ).wait()


def warp(tiles, share, visit, tile, good, rows, cols, var, image):
    blocks, side, _ = var.shape
    some, firsts = share
    tall = 2 * (side // STEP) * some
    visits = len(firsts)
    return pl.pallas_call(
        functools.partial(warp_kernel, tiles, share),
        out_shape=jax.ShapeDtypeStruct((visits * tiles * CAP, tall, side), jnp.bfloat16),
        in_specs=[SMEM, SMEM, VMEM, HBM, HBM, HBM, HBM],
        out_specs=HBM,
        scratch_shapes=[
            pltpu.VMEM(rows.shape, jnp.bfloat16),
            pltpu.VMEM(cols.shape, jnp.bfloat16),
            pltpu.VMEM(var.shape, jnp.bfloat16),
            pltpu.VMEM(var.shape, jnp.bfloat16),
            pltpu.VMEM((blocks, visits, tall, side), jnp.bfloat16),
            pltpu.SMEM((tiles,), jnp.int32),
            pltpu.SemaphoreType.DMA((2,)),
            pltpu.SemaphoreType.DMA((blocks // GROUP, 2)),
            pltpu.SemaphoreType.DMA((blocks, visits)),
        ],
        compiler_params=pltpu.CompilerParams(vmem_limit_bytes=40 * MIB),
        cost_estimate=pl.CostEstimate(
            flops=8 * blocks * side**3, bytes_accessed=8 * blocks * side**2, transcendentals=0
        ),
        name="warp",
    )(visit, tile, good, rows, cols, var, image)


def place_kernel(code_ref, blocks_ref, coadd_ref, strip_ref, data, weight):
    step = pl.program_id(0)
    some, tall, side = blocks_ref.shape
    part = tall // 2
    lot = data.shape[0] // UNITS

    @pl.when(step == 0)
    def _():
        data[...] = jnp.zeros_like(data)
        weight[...] = jnp.zeros_like(weight)

    for block in range(some):
        code = code_ref[step * some + block]

        @pl.when(code >= 0)
        def _():
            row = pl.multiple_of((code // 8) * lot, lot)
            col = pl.multiple_of((code % 8) * STEP, STEP)
            cells = (pl.ds(row, part), pl.ds(col, side))
            data[cells] += blocks_ref[block, :part].astype(jnp.float32)
            weight[cells] += blocks_ref[block, part:].astype(jnp.float32)

    @pl.when(step == pl.num_programs(0) - 1)
    def _():
        coadd = data[...] / jnp.maximum(weight[...], 1.0)
        coadd_ref[...] = coadd
        strip_ref[:HALO] = coadd[:, :SIDE].T[:HALO]
        strip_ref[HALO:] = coadd[:, TX - SIDE :].T[SIDE - HALO :]


def place(code, blocks):
    count, tall, side = blocks.shape
    some = 8
    height = tall // 4 * UNITS
    return pl.pallas_call(
        place_kernel,
        grid_spec=pltpu.PrefetchScalarGridSpec(
            num_scalar_prefetch=1,
            grid=(count // some,),
            in_specs=[pl.BlockSpec((some, tall, side), lambda step, code: (step, 0, 0))],
            out_specs=(
                pl.BlockSpec((height, TX), lambda step, code: (0, 0)),
                pl.BlockSpec((2 * HALO, height), lambda step, code: (0, 0)),
            ),
            scratch_shapes=[pltpu.VMEM((height, TX), jnp.float32)] * 2,
        ),
        out_shape=(
            jax.ShapeDtypeStruct((height, TX), jnp.float32),
            jax.ShapeDtypeStruct((2 * HALO, height), jnp.float32),
        ),
        compiler_params=pltpu.CompilerParams(vmem_limit_bytes=32 * MIB),
        cost_estimate=pl.CostEstimate(
            flops=count * tall * side, bytes_accessed=count * tall * side * 2, transcendentals=0
        ),
        name="place",
    )(code, blocks)


def beside(axis):
    count = lax.axis_size(axis)
    up = [(i, i + 1) for i in range(count - 1)]
    return up, [(j, i) for i, j in up]


def neighbours(first, last, axis):
    up, down = beside(axis)
    return lax.ppermute(last, axis, up), lax.ppermute(first, axis, down)


def spread(coadd, strip):
    visits = lax.axis_size("visit")
    left, right = neighbours(strip[:HALO], strip[HALO:], "px")
    if visits == 2:
        swap = [(0, 1), (1, 0)]
        count = lax.axis_size("px")
        up, down = beside("px")

        def crossed(pairs):
            return [(v * count + i, (1 - v) * count + j) for v in range(2) for i, j in pairs]

        other_left = lax.ppermute(strip[HALO:], ("visit", "px"), crossed(up))
        other_right = lax.ppermute(strip[:HALO], ("visit", "px"), crossed(down))
        other = lax.ppermute(coadd, "visit", swap)
        return [(coadd, left, right), (other, other_left, other_right)]
    if visits == 1:
        return [(coadd, left, right)]
    every = [lax.all_gather(part, "visit") for part in (coadd, left, right)]
    return [tuple(part[visit] for part in every) for visit in range(visits)]


def rows_between(parts, lot):
    mine = lax.axis_index("visit")
    pair = len(parts) == 2
    top = parts[0][0][:HALO]
    bottom = parts[-1][0][UNITS * lot - HALO :]
    if pair:
        top = jnp.where(mine == 0, top, parts[1][0][:HALO])
        bottom = jnp.where(mine == 1, parts[0][0][UNITS * lot - HALO :], bottom)
    above, below = neighbours(top, bottom, "py")
    both = jnp.concatenate([above, below], axis=0)
    left, right = neighbours(both[:, :SIDE], both[:, TX - SIDE :], "px")
    from_left = jnp.arange(SIDE, dtype=jnp.int32)[None, :] >= SIDE // 2
    return jnp.concatenate([both, jnp.where(from_left, left, right)], axis=1)


def stage_kernel(plan, lots, *refs):
    mine_ref, taps_ref, between_ref = refs[:3]
    fields, copies, outs = plan
    visits = fields["visits"]
    at = 3
    chunks = []
    for lot in lots:
        parts = []
        for _ in range(visits):
            parts.append(refs[at : at + 3])
            at += 3
        chunks.append(parts)
    at += fields["aliased"]
    detection_hbm, variance_hbm = refs[at : at + 2]
    field, detection, variance, sems = refs[at + 2 : at + 6]
    sides = refs[at + 6 :]
    spans, tall, _ = field.shape

    which = 0
    held = []
    for parts in chunks:
        group = []
        for cells, left, right in parts:
            side = sides[which]
            which += 1
            height = cells.shape[0]
            side[...] = jnp.concatenate(
                [right[...], jnp.zeros((SIDE - 2 * HALO, height), jnp.float32), left[...]], axis=0
            ).T
            group.append((cells, side))
        held.append(group)

    def assemble(order):
        for chunk, visit, first, rows, at_row, begin, end, shift in copies:
            cells, side = held[chunk][order[visit]]
            lot = lots[chunk]

            @pl.loop(begin, end)
            def _(unit):
                start = pl.multiple_of(unit * lot + first, HALO)
                into = pl.ds(at_row, rows)
                field[unit + shift, into, :TX] = cells[pl.ds(start, rows), :]
                field[unit + shift, into, TX:] = side[pl.ds(start, rows), :]

    if visits == 2:
        for flip in range(2):

            @pl.when(mine_ref[0] == flip)
            def _():
                assemble((0, 1) if flip == 0 else (1, 0))

    else:
        assemble(tuple(range(visits)))
    if fields["between"]:
        above_at, below_at = fields["between"]
        field[0, above_at : above_at + HALO, :] = between_ref[:HALO, :]
        field[spans - 1, below_at : below_at + HALO, :] = between_ref[HALO:, :]

    taps = [taps_ref[tap] for tap in range(7)]

    def down(value, by):
        return value if by == 0 else pltpu.roll(value, by % tall, 0)

    def across(value, by):
        return value if by == 0 else pltpu.roll(value, by % WIDE, 1)

    def three(value, shift, by):
        return value + shift(value, by) + shift(value, -by)

    def stores(unit, source, rows, target):
        return [
            pltpu.make_async_copy(
                scratch.at[unit, pl.ds(source, rows)], hbm.at[pl.ds(target, rows)], sems.at[unit, at]
            )
            for at, (scratch, hbm) in enumerate(
                ((detection, detection_hbm), (variance, variance_hbm))
            )
        ]

    @pl.loop(0, spans)
    def _(unit):
        value = field[unit]
        resid = value - three(three(value, down, 1), across, 1) * (1.0 / 9.0)
        square = resid * resid
        tower = three(three(square, down, 1), down, 3)[HALO : tall - HALO]
        box = three(three(tower, across, 1), across, 3)
        local = box[:, :TX] * (1.0 / 81.0) + 1e-05
        rowwise = sum(taps[tap] * down(value, 3 - tap) for tap in range(7))[HALO : tall - HALO]
        blurred = sum(taps[tap] * across(rowwise, 3 - tap) for tap in range(7))
        variance[unit] = local
        detection[unit] = blurred[:, :TX] * lax.rsqrt(local)
        for begin, end, source, rows, shift in outs:

            @pl.when((unit >= begin) & (unit < end))
            def _():
                target = pl.multiple_of(unit * STEP + shift, HALO)
                for store in stores(unit, source, rows, target):
                    store.start()

    @pl.loop(0, spans)
    def _(unit):
        for begin, end, source, rows, shift in outs:

            @pl.when((unit >= begin) & (unit < end))
            def _():
                for store in stores(unit, source, rows, 0):
                    store.wait()


def stage(plan, mine, taps, between, chunks, lots, held=()):
    fields, _, _ = plan
    spans, tall = fields["spans"], fields["tall"]
    shape = jax.ShapeDtypeStruct((TY, TX), jnp.float32)
    flat = [array for parts in chunks for part in parts for array in part]
    first = 3 + len(flat)
    return pl.pallas_call(
        functools.partial(stage_kernel, plan, lots),
        out_shape=(shape, shape),
        in_specs=[SMEM, SMEM, VMEM] + [VMEM] * len(flat) + [HBM] * len(held),
        out_specs=(HBM, HBM),
        input_output_aliases={first + at: at for at in range(len(held))},
        scratch_shapes=[
            pltpu.VMEM((spans, tall, WIDE), jnp.float32),
            pltpu.VMEM((spans, tall - 2 * HALO, TX), jnp.float32),
            pltpu.VMEM((spans, tall - 2 * HALO, TX), jnp.float32),
            pltpu.SemaphoreType.DMA((spans, 2)),
        ]
        + [pltpu.VMEM((part[0].shape[0], SIDE), jnp.float32) for parts in chunks for part in parts],
        compiler_params=pltpu.CompilerParams(vmem_limit_bytes=56 * MIB),
        cost_estimate=pl.CostEstimate(
            flops=80 * spans * tall * WIDE, bytes_accessed=12 * spans * tall * WIDE, transcendentals=0
        ),
        name="stage",
    )(mine, taps, between, *flat, *held)


def outer_plan(lot):
    fields = dict(visits=2, aliased=0, spans=UNITS + 1, tall=2 * lot, between=(lot - HALO, lot))
    copies = [(0, 1, 0, lot, 0, 0, UNITS, 1), (0, 0, 0, lot, lot, 0, UNITS, 0)]
    rows = lot - HALO
    outs = [
        (0, 1, rows, rows, 0),
        (1, UNITS, 0, 2 * rows, -rows),
        (UNITS, UNITS + 1, 0, rows, -rows),
    ]
    return fields, copies, outs


def inner_plan(lot, inner):
    edge = 2 * HALO
    tall = 2 * inner + 2 * edge
    fields = dict(visits=2, aliased=2, spans=UNITS, tall=tall, between=None)
    copies = [
        (0, 0, lot - edge, edge, 0, 0, UNITS, 0),
        (1, 0, 0, inner, edge, 0, UNITS, 0),
        (1, 1, 0, inner, edge + inner, 0, UNITS, 0),
        (0, 1, 0, edge, edge + 2 * inner, 0, UNITS, 0),
    ]
    return fields, copies, [(0, UNITS, 0, tall - edge, lot - HALO)]


def whole_plan(lot, visits):
    fields = dict(
        visits=visits, aliased=0, spans=UNITS, tall=STEP + 2 * HALO, between=(0, HALO + STEP)
    )
    copies = [(0, visit, 0, lot, HALO + visit * lot, 0, UNITS, 0) for visit in range(visits)]
    copies.append((0, visits - 1, lot - HALO, HALO, 0, 0, UNITS - 1, 1))
    copies.append((0, 0, 0, HALO, HALO + STEP, 1, UNITS, -1))
    return fields, copies, [(0, UNITS, 0, STEP, 0)]


def slot_codes(tile, offsets):
    note = tile * 64 + offsets[:, 0] * 8 + offsets[:, 1]
    notes = lax.all_gather(note, EVERY)
    mine = (notes // 64) == lax.axis_index("py") * lax.axis_size("px") + lax.axis_index("px")
    blocks = notes.shape[1]
    at = jnp.arange(blocks, dtype=jnp.int32)
    before = mine[:, None, :] & (at[None, None, :] < at[None, :, None])
    rank = jnp.sum(before.astype(jnp.int32), axis=2)
    slot = jnp.arange(CAP, dtype=jnp.int32)[None, :, None]
    chosen = mine[:, None, :] & (rank[:, None, :] == slot)
    return jnp.max(jnp.where(chosen, (notes % 64)[:, None, :], -1), axis=2).reshape(-1)


def per_device(
    images, inv_var, good_columns, warp_rows, warp_cols, block_visit, dest_tile, offsets, psf_taps
):
    tiles = lax.axis_size("py") * lax.axis_size("px")
    visits = lax.axis_size("visit")
    tile = dest_tile[:, 0]
    plan = shares(visits)
    lots = [rows for rows, _ in plan]
    mine = lax.axis_index("visit").astype(jnp.int32).reshape(1)

    def make(share):
        return warp(
            tiles, share, block_visit, tile, good_columns, warp_rows, warp_cols, inv_var, images
        )

    def send(blocks):
        return lax.all_to_all(blocks, EVERY, split_axis=0, concat_axis=0, tiled=True)

    arrived = send(make(plan[0]))
    code = slot_codes(tile, offsets)
    if len(plan) == 1:
        parts = spread(*place(code, arrived))
        between = rows_between(parts, lots[0])
        return stage(whole_plan(lots[0], visits), mine, psf_taps, between, [parts], lots)

    later = make(plan[1])
    arrived, later = lax.optimization_barrier((arrived, later))
    second = send(later)
    parts = spread(*place(code, arrived))
    between = rows_between(parts, lots[0])
    held = stage(outer_plan(lots[0]), mine, psf_taps, between, [parts], lots[:1])
    second, held = lax.optimization_barrier((second, held))
    more = spread(*place(code, second))
    return stage(inner_plan(*lots), mine, psf_taps, between, [parts, more], lots, held)


def solution(mesh):
    in_specs = (
        P(EVERY, None, None),
        P(EVERY, None, None),
        P("visit", None),
        P("visit", None, None),
        P("visit", None, None),
        P(EVERY),
        P(EVERY, None),
        P(EVERY, None),
        P(),
    )
    out_specs = (P("py", "px"), P("py", "px"))
    return jax.shard_map(
        per_device, mesh=mesh, in_specs=in_specs, out_specs=out_specs, check_vma=False
    )
```

time: 629 us -> 356 us (0.57)
  waiting for transfers between devices: 388 us -> 160 us
  other arithmetic: 102 us -> 1.8 us
  blocking collectives: 0 us -> 68.8 us
  local copies, waits for them, and re-layouts: 83.3 us -> 16.2 us
  Pallas kernels: 0 us -> 52.9 us
  starting transfers between devices: 21.6 us -> 53.9 us
  matrix products: 18.2 us -> 0 us
  between operations: 14.3 us -> 1.11 us
    psum x1 -> x0, waiting for transfers between devices: 197 us -> none  [per_device(): data_sum, weight_sum = lax.psum((totals[0], totals[1]), 'visit')]
    unnamed x0 -> x1, blocking collectives: none -> 68.8 us
    all_to_all x2, waiting for transfers between devices: 184 us -> 121 us  [send(): lax.all_to_all(blocks, EVERY, split_axis=0, concat_axis=0, tiled=True)]
    pallas_call x0 -> x6, Pallas kernels: none -> 52.9 us  [the longest x2 29.4 us: stage(): pl.pallas_call(functools.partial(stage_kernel, plan, lots), out_shape=(sh...]
    div x2 -> x0, other arithmetic: 52.5 us -> none  [the longest x1 48.1 us: filters(): return (blurred / jnp.sqrt(local_var), local_var)]
    add x4 -> x0, other arithmetic: 34 us -> none  [the longest x2 24.6 us: box_sum(): vertical = sum((field[offset:offset + height, :] for offset in range(span)))]
    ppermute x4 -> x14, waiting for transfers between devices: 6.46 us -> 38.7 us  [the longest x2 33.4 us: spread(): other = lax.ppermute(coadd, 'visit', swap)]
    ppermute x4 -> x14, starting transfers between devices: 7.96 us -> 37.7 us  [the longest x8 19.1 us: neighbours(): return (lax.ppermute(last, axis, up), lax.ppermute(first, axis, down))]
  transfers between devices with their start and end apart: 7 -> 16, of which waited for: 4 -> 5; matrix products, arithmetic and copies ran while one was open for 8% -> 1% of each run, Pallas kernels for 0% -> 9%
where the time goes in v2:
time: 356 us; the launch traced here: 355 us
  waiting for transfers between devices  160 us (45%)
  blocking collectives  68.8 us (19%)
  starting transfers between devices  53.9 us (15%)
  Pallas kernels  52.9 us (15%)
  local copies, waits for them, and re-layouts  16.2 us (5%)
    all_to_all x2, waiting for transfers between devices, send(): lax.all_to_all(blocks, EVERY, split_axis=0, concat_axis=0, tiled=True)  121 us
    unnamed x1, blocking collectives  68.8 us
    ppermute x2, waiting for transfers between devices, spread(): other = lax.ppermute(coadd, 'visit', swap)  33.4 us
    pallas_call x2, Pallas kernels, stage(): pl.pallas_call(functools.partial(stage_kernel, plan, lots), out_shape=(sh...  29.4 us
    ppermute x8, starting transfers between devices, neighbours(): return (lax.ppermute(last, axis, up), lax.ppermute(first, axis, down))  19.1 us
    all_to_all x2, starting transfers between devices, send(): lax.all_to_all(blocks, EVERY, split_axis=0, concat_axis=0, tiled=True)  16.2 us
    unnamed x54, local copies, waits for them, and re-layouts  15.9 us
    pallas_call x2, Pallas kernels, warp(): pl.pallas_call(functools.partial(warp_kernel, tiles, share), out_shape=ja...  13.9 us
  transfers between devices with their start and end apart: 16, of which 5 were waited for; matrix products, arithmetic and copies ran while one was open for 1% of the time, Pallas kernels for 9%

profile of v2, /device:TPU:0, one launch (start us, length us, event | category | flops | bytes accessed | tf_op | source)
XLA Modules:
  0.0 354.7 jit_solution(7184630582580304296)
XLA Ops:
  0.6 1.9 copy-done
  2.5 1.9 copy-done.2
  8.9 6.5 %warp.2 = bf16[64,192,256]{2,1,0:T(8,128)(2,1)} custom-call(s32[24]{0:T(128)S(1)} %copy-done.14, s32[24]{0:T(128)S(1)} %bitcast.4, s32[8,256]{1,0:T(8,128)S(1)} %copy-done.10, bf16[8,256,256]{2,1,0:T(8,128)(2,1)S(1)} %copy-done.5, bf16[8,256,256]{2,1,0:T(8,128)(2,1)S(1)} %copy-done.7, bf16[24,256,256]{2,1,0:T(8,128)(2,1)S(1)} %copy-done, ...), custom_call_target="tpu_custom_call" | custom-call | flops 3221225472 | bytes 12582912 | tf_op jit(solution)/shard_map/warp/pallas_call | solution.py:134
  15.5 7.4 %all-to-all-start = ((bf16[64,192,256]{2,1,0:T(8,128)(2,1)}), bf16[64,192,256]{2,1,0:T(8,128)(2,1)}, u32[]{:S(2)}, u32[]{:S(2)}) async-start(bf16[64,192,256]{2,1,0:T(8,128)(2,1)} %warp.2), calls=%async_computation | async-start | bytes 12582912 | tf_op jit(solution)/shard_map/all_to_all | solution.py:463
  22.9 1.9 copy-done.3
  26.0 1.2 copy-done.8
  27.3 7.4 %warp.3 = bf16[64,64,256]{2,1,0:T(8,128)(2,1)S(1)} custom-call(s32[24]{0:T(128)S(1)} %copy-done.15, s32[24]{0:T(128)S(1)} %bitcast.5, s32[8,256]{1,0:T(8,128)S(1)} %copy-done.11, bf16[8,256,256]{2,1,0:T(8,128)(2,1)S(1)} %copy-done.6, bf16[8,256,256]{2,1,0:T(8,128)(2,1)S(1)} %copy-done.8, bf16[24,256,256]{2,1,0:T(8,128)(2,1)S(1)} %copy-done.1, ...), custom_call_target="tpu_custom_call" | custom-call | flops 3221225472 | bytes 12582912 | tf_op jit(solution)/shard_map/warp/pallas_call | solution.py:134
  34.6 1.3 copy-done.4
  35.9 121.2 %all-to-all-done.blocks_ref = bf16[64,192,256]{2,1,0:T(8,128)(2,1)} async-done(((bf16[64,192,256]{2,1,0:T(8,128)(2,1)}), bf16[64,192,256]{2,1,0:T(8,128)(2,1)}, u32[]{:S(2)}, u32[]{:S(2)}) %all-to-all-start) | async-done | bytes 6291488 | tf_op jit(solution)/shard_map/all_to_all | solution.py:463
  157.1 8.8 %all-to-all-start.1 = ((bf16[64,64,256]{2,1,0:T(8,128)(2,1)}), bf16[64,64,256]{2,1,0:T(8,128)(2,1)S(1)}, u32[]{:S(2)}, u32[]{:S(2)}) async-start(bf16[64,64,256]{2,1,0:T(8,128)(2,1)} %copy-done.4), calls=%async_computation.1 | async-start | bytes 4194304 | tf_op jit(solution)/shard_map/all_to_all | solution.py:463
  166.1 68.8 %all-reduce = s32[768]{0:T(1024)S(1)} all-reduce(s32[768]{0:T(1024)S(1)} %bitcast_dynamic-update-slice_fusion), channel_id=2, replica_groups=mesh['visit'=2,'py'=4,'px'=4] {'visit','py','px'}, use_global_device_ids=true, to_apply=%add | all-reduce | flops 768 | bytes 6144
  235.5 7.8 %place.2 = (f32[384,1024]{1,0:T(8,128)}, f32[16,384]{1,0:T(8,128)S(1)}) custom-call(s32[64]{0:T(128)S(1)} %reshape.73.code_ref, bf16[64,192,256]{2,1,0:T(8,128)(2,1)} %all-to-all-done.blocks_ref), custom_call_target="tpu_custom_call" | custom-call | flops 3145728 | bytes 6291456 | tf_op jit(solution)/shard_map/place/pallas_call | solution.py:192
  243.4 2.3 collective-permute-start
  245.6 33.4 %collective-permute-done.refs_6_ = f32[384,1024]{1,0:T(8,128)} collective-permute-done((f32[384,1024]{1,0:T(8,128)}, f32[384,1024]{1,0:T(8,128)}, u32[]{:S(2)}, u32[]{:S(2)}) %collective-permute-start) | collective-permute-done | bytes 1572896 | tf_op jit(solution)/shard_map/ppermute | solution.py:240
  279.8 1.3 collective-permute-start.1
  281.1 1.3 collective-permute-start.2
  282.5 3.3 collective-permute-done.2
  285.8 1.3 collective-permute-start.4
  287.1 4.5 %collective-permute-start.3 = (f32[16,128]{1,0:T(8,128)S(1)}, f32[16,128]{1,0:T(8,128)S(1)}, u32[]{:S(2)}, u32[]{:S(2)}) collective-permute-start(f32[16,128]{1,0:T(8,128)S(1)} %get-tuple-element.27), channel_id=1, source_target_pairs={{0,1},{1,2},{2,3},{4,5},{5,6},{6,7},{8,9},{9,10},{10,11},{12,13},{... | collective-permute-start | bytes 24584 | tf_op jit(solution)/shard_map/ppermute | solution.py:224
  291.7 1.3 collective-permute-start.8
  293.0 1.3 collective-permute-start.6
  294.3 6.1 %collective-permute-start.7 = (f32[8,384]{1,0:T(8,128)S(1)}, f32[8,384]{1,0:T(8,128)S(1)}, u32[]{:S(2)}, u32[]{:S(2)}) collective-permute-start(f32[8,384]{1,0:T(8,128)S(1)} %get-tuple-element.29), channel_id=1, source_target_pairs={{0,17},{1,18},{2,19},{16,1},{17,2},{18,3},{4,21},{5,22},{6,23},{20... | collective-permute-start | bytes 36872 | tf_op jit(solution)/shard_map/ppermute | solution.py:238
  300.4 3.9 %collective-permute-start.5 = (f32[8,384]{1,0:T(8,128)S(1)}, f32[8,384]{1,0:T(8,128)S(1)}, u32[]{:S(2)}, u32[]{:S(2)}) collective-permute-start(f32[8,384]{1,0:T(8,128)S(1)} %get-tuple-element.29), channel_id=1, source_target_pairs={{0,1},{1,2},{2,3},{4,5},{5,6},{6,7},{8,9},{9,10},{10,11},{12,13},{... | collective-permute-start | bytes 36872 | tf_op jit(solution)/shard_map/ppermute | solution.py:224
  306.3 17.6 %stage.2 = (f32[1024,1024]{1,0:T(8,128)}, f32[1024,1024]{1,0:T(8,128)}) custom-call(s32[1]{0:T(128)} %bitcast.refs_0_, f32[7]{0:T(128)} %refs_1_.3, f32[16,1152]{1,0:T(8,128)} %pad_maximum_fusion.refs_2_, f32[384,1024]{1,0:T(8,128)} %get-tuple-element.14.refs_3_, f32[8,384]{1,0:T(8,128)} %copy-done.20, f32[8,384]{1,0:T(8,128)} %copy-done.18, ...), custom_call_target="tpu_custom_call" | custom-call | flops 79626240 | bytes 11943936 | tf_op jit(solution)/shard_map/stage/pallas_call | solution.py:378
  323.8 1.8 place.3
  325.6 1.6 collective-permute-start.11
  327.2 1.3 collective-permute-start.13
  328.5 1.3 collective-permute-start.10
  329.8 6.1 %collective-permute-start.12 = (f32[8,128]{1,0:T(8,128)S(1)}, f32[8,128]{1,0:T(8,128)S(1)}, u32[]{:S(2)}, u32[]{:S(2)}) collective-permute-start(f32[8,128]{1,0:T(8,128)S(1)} %get-tuple-element.31), channel_id=1, source_target_pairs={{0,17},{1,18},{2,19},{16,1},{17,2},{18,3},{4,21},{5,22},{6,23},{20... | collective-permute-start | bytes 12296 | tf_op jit(solution)/shard_map/ppermute | solution.py:238
  335.9 4.2 %collective-permute-start.9 = (f32[8,128]{1,0:T(8,128)S(1)}, f32[8,128]{1,0:T(8,128)S(1)}, u32[]{:S(2)}, u32[]{:S(2)}) collective-permute-start(f32[8,128]{1,0:T(8,128)S(1)} %get-tuple-element.31), channel_id=1, source_target_pairs={{0,1},{1,2},{2,3},{4,5},{5,6},{6,7},{8,9},{9,10},{10,11},{12,13},{... | collective-permute-start | bytes 12296 | tf_op jit(solution)/shard_map/ppermute | solution.py:224
  340.1 1.2 collective-permute-done.9.refs_10_
  342.8 11.9 %stage.3 = (f32[1024,1024]{1,0:T(8,128)}, f32[1024,1024]{1,0:T(8,128)}) custom-call(s32[1]{0:T(128)} %bitcast.refs_0_, f32[7]{0:T(128)} %refs_1_.3, f32[16,1152]{1,0:T(8,128)} %pad_maximum_fusion.refs_2_, f32[384,1024]{1,0:T(8,128)} %get-tuple-element.14.refs_3_, f32[8,384]{1,0:T(8,128)} %copy-done.20, ...), custom_call_target="tpu_custom_call", output_to_operand_aliasing={{0}: (15, {}), {1}: (16, {})} | custom-call | flops 47185920 | bytes 7077888 | tf_op jit(solution)/shard_map/stage/pallas_call | solution.py:378
  (79 shorter events, 10.6 us)
Async XLA Ops:
  0.6 1.9 copy-start
  2.5 1.9 copy-start.2
  4.4 1.2 copy-start.5
  5.6 1.2 copy-start.7
  15.4 7.5 %copy-start.1 = (bf16[24,256,256]{2,1,0:T(8,128)(2,1)S(1)}, bf16[24,256,256]{2,1,0:T(8,128)(2,1)}, u32[]{:S(2)}) copy-start(bf16[24,256,256]{2,1,0:T(8,128)(2,1)} %var_hbm.3) | copy-start | bytes 9437188
  15.4 7.5 %copy-start.11 = (s32[8,256]{1,0:T(8,128)S(1)}, s32[8,256]{1,0:T(8,128)}, u32[]{:S(2)}) copy-start(s32[8,256]{1,0:T(8,128)} %good_ref.3) | copy-start | bytes 24580
  15.5 7.5 %copy-start.13 = (s32[24,1]{0,1:T(1,128)S(1)}, s32[24,1]{0,1:T(1,128)}, u32[]{:S(2)}) copy-start(s32[24,1]{0,1:T(1,128)} %param.15) | copy-start | bytes 292
  15.5 7.4 %copy-start.15 = (s32[24]{0:T(128)S(1)}, s32[24]{0:T(128)}, u32[]{:S(2)}) copy-start(s32[24]{0:T(128)} %visit_ref.3) | copy-start | bytes 292
  15.5 141.7 %all-to-all-start = ((bf16[64,192,256]{2,1,0:T(8,128)(2,1)}), bf16[64,192,256]{2,1,0:T(8,128)(2,1)}, u32[]{:S(2)}, u32[]{:S(2)}) async-start(bf16[64,192,256]{2,1,0:T(8,128)(2,1)} %warp.2), calls=%async_computation | async-start | bytes 12582912 | tf_op jit(solution)/shard_map/all_to_all | solution.py:463
  22.9 1.9 copy-start.3
  26.0 1.2 copy-start.8
  34.6 1.3 copy-start.4
  35.9 130.1 %copy-start.25 = (s32[24,2]{0,1:T(2,128)S(1)}, s32[24,2]{0,1:T(2,128)}, u32[]{:S(2)}) copy-start(s32[24,2]{0,1:T(2,128)} %param.16) | copy-start | bytes 580
  157.1 166.7 %all-to-all-start.1 = ((bf16[64,64,256]{2,1,0:T(8,128)(2,1)}), bf16[64,64,256]{2,1,0:T(8,128)(2,1)S(1)}, u32[]{:S(2)}, u32[]{:S(2)}) async-start(bf16[64,64,256]{2,1,0:T(8,128)(2,1)} %copy-done.4), calls=%async_computation.1 | async-start | bytes 4194304 | tf_op jit(solution)/shard_map/all_to_all | solution.py:463
  243.4 35.6 %collective-permute-start = (f32[384,1024]{1,0:T(8,128)}, f32[384,1024]{1,0:T(8,128)}, u32[]{:S(2)}, u32[]{:S(2)}) collective-permute-start(f32[384,1024]{1,0:T(8,128)} %get-tuple-element.14.refs_3_), channel_id=1, source_target_pairs={{0,16},{16,0},{1,17},{17,1},{2,18},{18,2},{3,19},{19,3},{4,20},{20... | collective-permute-start | bytes 4718600 | tf_op jit(solution)/shard_map/ppermute | solution.py:240
  279.8 2.6 collective-permute-start.1
  281.1 4.7 %collective-permute-start.2 = (f32[8,1024]{1,0:T(8,128)S(1)}, f32[8,1024]{1,0:T(8,128)S(1)}, u32[]{:S(2)}, u32[]{:S(2)}) collective-permute-start(f32[8,1024]{1,0:T(8,128)S(1)} %get-tuple-element.24), channel_id=1, source_target_pairs={{4,0},{8,4},{12,8},{5,1},{9,5},{13,9},{6,2},{10,6},{14,10},{7,3},{... | collective-permute-start | bytes 98312 | tf_op jit(solution)/shard_map/ppermute | solution.py:224
  285.8 14.5 %collective-permute-start.4 = (f32[16,128]{1,0:T(8,128)S(1)}, f32[16,128]{1,0:T(8,128)S(1)}, u32[]{:S(2)}, u32[]{:S(2)}) collective-permute-start(f32[16,128]{1,0:T(8,128)S(1)} %get-tuple-element.26), channel_id=1, source_target_pairs={{1,0},{2,1},{3,2},{5,4},{6,5},{7,6},{9,8},{10,9},{11,10},{13,12},{... | collective-permute-start | bytes 24584 | tf_op jit(solution)/shard_map/ppermute | solution.py:224
  287.1 17.2 %collective-permute-start.3 = (f32[16,128]{1,0:T(8,128)S(1)}, f32[16,128]{1,0:T(8,128)S(1)}, u32[]{:S(2)}, u32[]{:S(2)}) collective-permute-start(f32[16,128]{1,0:T(8,128)S(1)} %get-tuple-element.27), channel_id=1, source_target_pairs={{0,1},{1,2},{2,3},{4,5},{5,6},{6,7},{8,9},{9,10},{10,11},{12,13},{... | collective-permute-start | bytes 24584 | tf_op jit(solution)/shard_map/ppermute | solution.py:224
  291.7 13.3 %collective-permute-start.8 = (f32[8,384]{1,0:T(8,128)S(1)}, f32[8,384]{1,0:T(8,128)S(1)}, u32[]{:S(2)}, u32[]{:S(2)}) collective-permute-start(f32[8,384]{1,0:T(8,128)S(1)} %get-tuple-element.28), channel_id=1, source_target_pairs={{1,16},{2,17},{3,18},{17,0},{18,1},{19,2},{5,20},{6,21},{7,22},{21... | collective-permute-start | bytes 36872 | tf_op jit(solution)/shard_map/ppermute | solution.py:239
  293.0 12.0 %collective-permute-start.6 = (f32[8,384]{1,0:T(8,128)S(1)}, f32[8,384]{1,0:T(8,128)S(1)}, u32[]{:S(2)}, u32[]{:S(2)}) collective-permute-start(f32[8,384]{1,0:T(8,128)S(1)} %get-tuple-element.28), channel_id=1, source_target_pairs={{1,0},{2,1},{3,2},{5,4},{6,5},{7,6},{9,8},{10,9},{11,10},{13,12},{... | collective-permute-start | bytes 36872 | tf_op jit(solution)/shard_map/ppermute | solution.py:224
  294.3 10.7 %collective-permute-start.7 = (f32[8,384]{1,0:T(8,128)S(1)}, f32[8,384]{1,0:T(8,128)S(1)}, u32[]{:S(2)}, u32[]{:S(2)}) collective-permute-start(f32[8,384]{1,0:T(8,128)S(1)} %get-tuple-element.29), channel_id=1, source_target_pairs={{0,17},{1,18},{2,19},{16,1},{17,2},{18,3},{4,21},{5,22},{6,23},{20... | collective-permute-start | bytes 36872 | tf_op jit(solution)/shard_map/ppermute | solution.py:238
  300.4 5.3 %collective-permute-start.5 = (f32[8,384]{1,0:T(8,128)S(1)}, f32[8,384]{1,0:T(8,128)S(1)}, u32[]{:S(2)}, u32[]{:S(2)}) collective-permute-start(f32[8,384]{1,0:T(8,128)S(1)} %get-tuple-element.29), channel_id=1, source_target_pairs={{0,1},{1,2},{2,3},{4,5},{5,6},{6,7},{8,9},{9,10},{10,11},{12,13},{... | collective-permute-start | bytes 36872 | tf_op jit(solution)/shard_map/ppermute | solution.py:224
  325.6 15.8 %copy-start.9 = (f32[128,1024]{1,0:T(8,128)}, f32[128,1024]{1,0:T(8,128)S(1)}, u32[]{:S(2)}) copy-start(f32[128,1024]{1,0:T(8,128)S(1)} %get-tuple-element.20.refs_9_) | copy-start | bytes 1572868
  325.6 15.8 %collective-permute-start.11 = (f32[128,1024]{1,0:T(8,128)S(1)}, f32[128,1024]{1,0:T(8,128)S(1)}, u32[]{:S(2)}, u32[]{:S(2)}) collective-permute-start(f32[128,1024]{1,0:T(8,128)S(1)} %get-tuple-element.20.refs_9_), channel_id=1, source_target_pairs={{0,16},{16,0},{1,17},{17,1},{2,18},{18,2},{3,19},{19,3},{4,20},{20... | collective-permute-start | bytes 1572872 | tf_op jit(solution)/shard_map/ppermute | solution.py:240
  327.2 12.9 %collective-permute-start.13 = (f32[8,128]{1,0:T(8,128)S(1)}, f32[8,128]{1,0:T(8,128)S(1)}, u32[]{:S(2)}, u32[]{:S(2)}) collective-permute-start(f32[8,128]{1,0:T(8,128)S(1)} %get-tuple-element.30), channel_id=1, source_target_pairs={{1,16},{2,17},{3,18},{17,0},{18,1},{19,2},{5,20},{6,21},{7,22},{21... | collective-permute-start | bytes 12296 | tf_op jit(solution)/shard_map/ppermute | solution.py:239
  328.5 11.6 %collective-permute-start.10 = (f32[8,128]{1,0:T(8,128)S(1)}, f32[8,128]{1,0:T(8,128)S(1)}, u32[]{:S(2)}, u32[]{:S(2)}) collective-permute-start(f32[8,128]{1,0:T(8,128)S(1)} %get-tuple-element.30), channel_id=1, source_target_pairs={{1,0},{2,1},{3,2},{5,4},{6,5},{7,6},{9,8},{10,9},{11,10},{13,12},{... | collective-permute-start | bytes 12296 | tf_op jit(solution)/shard_map/ppermute | solution.py:224
  329.8 10.3 %collective-permute-start.12 = (f32[8,128]{1,0:T(8,128)S(1)}, f32[8,128]{1,0:T(8,128)S(1)}, u32[]{:S(2)}, u32[]{:S(2)}) collective-permute-start(f32[8,128]{1,0:T(8,128)S(1)} %get-tuple-element.31), channel_id=1, source_target_pairs={{0,17},{1,18},{2,19},{16,1},{17,2},{18,3},{4,21},{5,22},{6,23},{20... | collective-permute-start | bytes 12296 | tf_op jit(solution)/shard_map/ppermute | solution.py:238
  335.9 5.5 %collective-permute-start.9 = (f32[8,128]{1,0:T(8,128)S(1)}, f32[8,128]{1,0:T(8,128)S(1)}, u32[]{:S(2)}, u32[]{:S(2)}) collective-permute-start(f32[8,128]{1,0:T(8,128)S(1)} %get-tuple-element.31), channel_id=1, source_target_pairs={{0,1},{1,2},{2,3},{4,5},{5,6},{6,7},{8,9},{9,10},{10,11},{12,13},{... | collective-permute-start | bytes 12296 | tf_op jit(solution)/shard_map/ppermute | solution.py:224
  340.1 1.3 copy-start.21
  340.1 1.3 copy-start.22
  340.1 1.3 copy-start.23
  (10 other events, 7.4 us)

commit v3 on v2

--- a/solution.py
+++ b/solution.py
@@ -16,6 +16,7 @@
 SIDE = 128
 WIDE = TX + SIDE
 GROUP = 4
+NOTE = 16
 MIB = 1 << 20
 EVERY = ("visit", "py", "px")
 HBM = pl.BlockSpec(memory_space=pltpu.HBM)
@@ -32,12 +33,13 @@
 
 
 def warp_kernel(
-    tiles, share, visit_ref, tile_ref, good_ref, rows_hbm, cols_hbm, var_hbm, image_hbm, out_hbm,
-    rows, cols, var, image, done, count, table_sems, sems, out_sems,
+    tiles, share, noted, visit_ref, tile_ref, offset_ref, good_ref, rows_hbm, cols_hbm, var_hbm,
+    image_hbm, out_hbm, rows, cols, var, image, done, note, count, table_sems, sems, out_sems,
 ):
     blocks, side, _ = var.shape
     some, firsts = share
     groups = blocks // GROUP
+    slot_rows = done.shape[2]
     tables = [
         pltpu.make_async_copy(rows_hbm, rows, table_sems.at[0]),
         pltpu.make_async_copy(cols_hbm, cols, table_sems.at[1]),
@@ -59,6 +61,10 @@
     @pl.loop(0, tiles)
     def _(tile):
         count[tile] = 0
+
+    if noted:
+        note[...] = jnp.full(note.shape, -1, jnp.bfloat16)
+        slot_of_lane = lax.broadcasted_iota(jnp.int32, (NOTE, SIDE), 1) // (SIDE // CAP)
 
     for load in tables:
         load.wait()
@@ -101,65 +107,85 @@
         for ahead in range(GROUP):
             block = group * GROUP + ahead
             for visit in range(len(firsts)):
-                for plane in range(2):
-                    start = plane * tall + visit * part
-                    done[block, visit, plane * part : (plane + 1) * part, :] = warped[ahead][
-                        start : start + part
-                    ]
+                for half in range(side // SIDE):
+                    for plane in range(2):
+                        start = plane * tall + visit * part
+                        into = (2 * half + plane) * part
+                        done[block, visit, into : into + part, :] = warped[ahead][
+                            start : start + part, half * SIDE : (half + 1) * SIDE
+                        ]
         for ahead in range(GROUP):
             block = group * GROUP + ahead
             tile = tile_ref[block]
             rank = count[tile]
             count[tile] = rank + 1
             for visit in range(len(firsts)):
+                target = visit * tiles + tile
                 pltpu.make_async_copy(
                     done.at[block, visit],
-                    out_hbm.at[(visit * tiles + tile) * CAP + rank],
+                    out_hbm.at[target, pl.ds(pl.multiple_of(rank * slot_rows, NOTE), slot_rows)],
                     out_sems.at[block, visit],
                 ).start()
+                if noted:
+                    code = offset_ref[2 * block] * 8 + offset_ref[2 * block + 1]
+                    note[target] = jnp.where(
+                        slot_of_lane == rank, code.astype(jnp.float32), note[target].astype(jnp.float32)
+                    ).astype(jnp.bfloat16)
+
+    if noted:
+        notes = pltpu.make_async_copy(
+            note, out_hbm.at[:, pl.ds(CAP * slot_rows, NOTE)], table_sems.at[0]
+        )
+        notes.start()
 
     @pl.loop(0, blocks)
     def _(block):
         for visit in range(len(firsts)):
             pltpu.make_async_copy(
-                done.at[block, visit], out_hbm.at[0], out_sems.at[block, visit]
+                done.at[block, visit], out_hbm.at[0, pl.ds(0, slot_rows)], out_sems.at[block, visit]
             ).wait()
 
-
-def warp(tiles, share, visit, tile, good, rows, cols, var, image):
+    if noted:
+        notes.wait()
+
+
+def warp(tiles, share, noted, visit, tile, offset, good, rows, cols, var, image):
     blocks, side, _ = var.shape
     some, firsts = share
-    tall = 2 * (side // STEP) * some
+    slot_rows = 2 * (side // STEP) * some * (side // SIDE)
     visits = len(firsts)
     return pl.pallas_call(
-        functools.partial(warp_kernel, tiles, share),
-        out_shape=jax.ShapeDtypeStruct((visits * tiles * CAP, tall, side), jnp.bfloat16),
-        in_specs=[SMEM, SMEM, VMEM, HBM, HBM, HBM, HBM],
+        functools.partial(warp_kernel, tiles, share, noted),
+        out_shape=jax.ShapeDtypeStruct(
+            (visits * tiles, CAP * slot_rows + noted * NOTE, SIDE), jnp.bfloat16
+        ),
+        in_specs=[SMEM, SMEM, SMEM, VMEM, HBM, HBM, HBM, HBM],
         out_specs=HBM,
         scratch_shapes=[
             pltpu.VMEM(rows.shape, jnp.bfloat16),
             pltpu.VMEM(cols.shape, jnp.bfloat16),
             pltpu.VMEM(var.shape, jnp.bfloat16),
             pltpu.VMEM(var.shape, jnp.bfloat16),
-            pltpu.VMEM((blocks, visits, tall, side), jnp.bfloat16),
+            pltpu.VMEM((blocks, visits, slot_rows, SIDE), jnp.bfloat16),
+            pltpu.VMEM((visits * tiles, NOTE, SIDE), jnp.bfloat16),
             pltpu.SMEM((tiles,), jnp.int32),
             pltpu.SemaphoreType.DMA((2,)),
             pltpu.SemaphoreType.DMA((blocks // GROUP, 2)),
             pltpu.SemaphoreType.DMA((blocks, visits)),
         ],
-        compiler_params=pltpu.CompilerParams(vmem_limit_bytes=40 * MIB),
+        compiler_params=pltpu.CompilerParams(vmem_limit_bytes=60 * MIB),
         cost_estimate=pl.CostEstimate(
             flops=8 * blocks * side**3, bytes_accessed=8 * blocks * side**2, transcendentals=0
         ),
         name="warp",
-    )(visit, tile, good, rows, cols, var, image)
-
-
-def place_kernel(code_ref, blocks_ref, coadd_ref, strip_ref, data, weight):
+    )(visit, tile, offset, good, rows, cols, var, image)
+
+
+def place_kernel(part, code_ref, blocks_ref, coadd_ref, strip_ref, edge_ref, data, weight):
     step = pl.program_id(0)
-    some, tall, side = blocks_ref.shape
-    part = tall // 2
-    lot = data.shape[0] // UNITS
+    some = blocks_ref.shape[0]
+    height = data.shape[0]
+    lot = height // UNITS
 
     @pl.when(step == 0)
     def _():
@@ -167,44 +193,46 @@
         weight[...] = jnp.zeros_like(weight)
 
     for block in range(some):
-        code = code_ref[step * some + block]
-
-        @pl.when(code >= 0)
-        def _():
-            row = pl.multiple_of((code // 8) * lot, lot)
-            col = pl.multiple_of((code % 8) * STEP, STEP)
-            cells = (pl.ds(row, part), pl.ds(col, side))
-            data[cells] += blocks_ref[block, :part].astype(jnp.float32)
-            weight[cells] += blocks_ref[block, part:].astype(jnp.float32)
+        for slot in range(CAP):
+            code = code_ref[(step * some + block) * CAP + slot]
+
+            @pl.when(code >= 0)
+            def _():
+                row = pl.multiple_of((code // 8) * lot, lot)
+                for half in range(2):
+                    col = pl.multiple_of((code % 8 + half) * STEP, STEP)
+                    cells = (pl.ds(row, part), pl.ds(col, STEP))
+                    first = (slot * 2 + half) * 2 * part
+                    data[cells] += blocks_ref[block, first : first + part].astype(jnp.float32)
+                    weight[cells] += blocks_ref[block, first + part : first + 2 * part].astype(
+                        jnp.float32
+                    )
 
     @pl.when(step == pl.num_programs(0) - 1)
     def _():
         coadd = data[...] / jnp.maximum(weight[...], 1.0)
-        coadd_ref[...] = coadd
+        coadd_ref[...] = coadd.astype(coadd_ref.dtype)
         strip_ref[:HALO] = coadd[:, :SIDE].T[:HALO]
         strip_ref[HALO:] = coadd[:, TX - SIDE :].T[SIDE - HALO :]
-
-
-def place(code, blocks):
+        edge_ref[:HALO] = coadd[:HALO]
+        edge_ref[HALO:] = coadd[height - HALO :]
+
+
+def place(code, blocks, lot, dtype):
     count, tall, side = blocks.shape
-    some = 8
-    height = tall // 4 * UNITS
+    some = 4
+    height = lot * UNITS
+    shapes = [((height, TX), dtype), ((2 * HALO, height), jnp.float32), ((2 * HALO, TX), jnp.float32)]
     return pl.pallas_call(
-        place_kernel,
+        functools.partial(place_kernel, 2 * lot),
         grid_spec=pltpu.PrefetchScalarGridSpec(
             num_scalar_prefetch=1,
             grid=(count // some,),
             in_specs=[pl.BlockSpec((some, tall, side), lambda step, code: (step, 0, 0))],
-            out_specs=(
-                pl.BlockSpec((height, TX), lambda step, code: (0, 0)),
-                pl.BlockSpec((2 * HALO, height), lambda step, code: (0, 0)),
-            ),
+            out_specs=[pl.BlockSpec(shape, lambda step, code: (0, 0)) for shape, _ in shapes],
             scratch_shapes=[pltpu.VMEM((height, TX), jnp.float32)] * 2,
         ),
-        out_shape=(
-            jax.ShapeDtypeStruct((height, TX), jnp.float32),
-            jax.ShapeDtypeStruct((2 * HALO, height), jnp.float32),
-        ),
+        out_shape=[jax.ShapeDtypeStruct(*shape) for shape in shapes],
         compiler_params=pltpu.CompilerParams(vmem_limit_bytes=32 * MIB),
         cost_estimate=pl.CostEstimate(
             flops=count * tall * side, bytes_accessed=count * tall * side * 2, transcendentals=0
@@ -226,38 +254,51 @@
 
 def spread(coadd, strip):
     visits = lax.axis_size("visit")
-    left, right = neighbours(strip[:HALO], strip[HALO:], "px")
     if visits == 2:
         swap = [(0, 1), (1, 0)]
-        count = lax.axis_size("px")
-        up, down = beside("px")
-
-        def crossed(pairs):
-            return [(v * count + i, (1 - v) * count + j) for v in range(2) for i, j in pairs]
-
-        other_left = lax.ppermute(strip[HALO:], ("visit", "px"), crossed(up))
-        other_right = lax.ppermute(strip[:HALO], ("visit", "px"), crossed(down))
         other = lax.ppermute(coadd, "visit", swap)
-        return [(coadd, left, right), (other, other_left, other_right)]
+        beyond = jnp.concatenate(neighbours(strip[:HALO], strip[HALO:], "px"), axis=0)
+        return [(coadd, beyond), (other, lax.ppermute(beyond, "visit", swap))]
+    beyond = jnp.concatenate(neighbours(strip[:HALO], strip[HALO:], "px"), axis=0)
     if visits == 1:
-        return [(coadd, left, right)]
-    every = [lax.all_gather(part, "visit") for part in (coadd, left, right)]
+        return [(coadd, beyond)]
+    every = [lax.all_gather(part, "visit") for part in (coadd, beyond)]
     return [tuple(part[visit] for part in every) for visit in range(visits)]
 
 
-def rows_between(parts, lot):
-    mine = lax.axis_index("visit")
-    pair = len(parts) == 2
-    top = parts[0][0][:HALO]
-    bottom = parts[-1][0][UNITS * lot - HALO :]
-    if pair:
-        top = jnp.where(mine == 0, top, parts[1][0][:HALO])
-        bottom = jnp.where(mine == 1, parts[0][0][UNITS * lot - HALO :], bottom)
-    above, below = neighbours(top, bottom, "py")
-    both = jnp.concatenate([above, below], axis=0)
-    left, right = neighbours(both[:, :SIDE], both[:, TX - SIDE :], "px")
-    from_left = jnp.arange(SIDE, dtype=jnp.int32)[None, :] >= SIDE // 2
-    return jnp.concatenate([both, jnp.where(from_left, left, right)], axis=1)
+def widened(rows, beyond):
+    corner = beyond.T
+    gap = jnp.zeros((HALO, SIDE - 2 * HALO), jnp.float32)
+    return jnp.concatenate([rows, corner[:, HALO:], gap, corner[:, :HALO]], axis=1)
+
+
+def rows_between(edge, parts):
+    visits = len(parts)
+    height = parts[0][1].shape[1]
+    if visits != 2:
+        last = widened(edge[0][HALO:], parts[-1][1][:, height - HALO :])
+        first = widened(edge[1][:HALO], parts[0][1][:, :HALO])
+        above, below = neighbours(first, last, "py")
+        return jnp.concatenate([above, below], axis=0)
+    lower = lax.axis_index("visit") == 0
+    beyond = parts[0][1]
+    mine = widened(
+        jnp.where(lower, edge[:HALO], edge[HALO:]),
+        jnp.where(lower, beyond[:, :HALO], beyond[:, height - HALO :]),
+    )
+    count = lax.axis_size("py")
+    up, down = beside("py")
+
+    def pairs(cross):
+        return [(i, j + cross * count) for i, j in down] + [
+            (count + i, j + (1 - cross) * count) for i, j in up
+        ]
+
+    straight = lax.ppermute(mine, ("visit", "py"), pairs(0))
+    crossed = lax.ppermute(mine, ("visit", "py"), pairs(1))
+    return jnp.concatenate(
+        [jnp.where(lower, crossed, straight), jnp.where(lower, straight, crossed)], axis=0
+    )
 
 
 def stage_kernel(plan, lots, *refs):
@@ -269,8 +310,8 @@
     for lot in lots:
         parts = []
         for _ in range(visits):
-            parts.append(refs[at : at + 3])
-            at += 3
+            parts.append(refs[at : at + 2])
+            at += 2
         chunks.append(parts)
     at += fields["aliased"]
     detection_hbm, variance_hbm = refs[at : at + 2]
@@ -282,12 +323,17 @@
     held = []
     for parts in chunks:
         group = []
-        for cells, left, right in parts:
+        for cells, beyond in parts:
             side = sides[which]
             which += 1
             height = cells.shape[0]
             side[...] = jnp.concatenate(
-                [right[...], jnp.zeros((SIDE - 2 * HALO, height), jnp.float32), left[...]], axis=0
+                [
+                    beyond[HALO:, :],
+                    jnp.zeros((SIDE - 2 * HALO, height), jnp.float32),
+                    beyond[:HALO, :],
+                ],
+                axis=0,
             ).T
             group.append((cells, side))
         held.append(group)
@@ -301,7 +347,7 @@
             def _(unit):
                 start = pl.multiple_of(unit * lot + first, HALO)
                 into = pl.ds(at_row, rows)
-                field[unit + shift, into, :TX] = cells[pl.ds(start, rows), :]
+                field[unit + shift, into, :TX] = cells[pl.ds(start, rows), :].astype(jnp.float32)
                 field[unit + shift, into, TX:] = side[pl.ds(start, rows), :]
 
     if visits == 2:
@@ -431,53 +477,55 @@
     return fields, copies, [(0, UNITS, 0, STEP, 0)]
 
 
-def slot_codes(tile, offsets):
-    note = tile * 64 + offsets[:, 0] * 8 + offsets[:, 1]
-    notes = lax.all_gather(note, EVERY)
-    mine = (notes // 64) == lax.axis_index("py") * lax.axis_size("px") + lax.axis_index("px")
-    blocks = notes.shape[1]
-    at = jnp.arange(blocks, dtype=jnp.int32)
-    before = mine[:, None, :] & (at[None, None, :] < at[None, :, None])
-    rank = jnp.sum(before.astype(jnp.int32), axis=2)
-    slot = jnp.arange(CAP, dtype=jnp.int32)[None, :, None]
-    chosen = mine[:, None, :] & (rank[:, None, :] == slot)
-    return jnp.max(jnp.where(chosen, (notes % 64)[:, None, :], -1), axis=2).reshape(-1)
-
-
 def per_device(
     images, inv_var, good_columns, warp_rows, warp_cols, block_visit, dest_tile, offsets, psf_taps
 ):
     tiles = lax.axis_size("py") * lax.axis_size("px")
     visits = lax.axis_size("visit")
-    tile = dest_tile[:, 0]
     plan = shares(visits)
     lots = [rows for rows, _ in plan]
     mine = lax.axis_index("visit").astype(jnp.int32).reshape(1)
-
-    def make(share):
+    dtype = jnp.bfloat16 if visits == 2 else jnp.float32
+
+    def make(chunk):
         return warp(
-            tiles, share, block_visit, tile, good_columns, warp_rows, warp_cols, inv_var, images
+            tiles, plan[chunk], chunk == 0, block_visit, dest_tile[:, 0], offsets.reshape(-1),
+            good_columns, warp_rows, warp_cols, inv_var, images,
         )
 
     def send(blocks):
         return lax.all_to_all(blocks, EVERY, split_axis=0, concat_axis=0, tiled=True)
 
-    arrived = send(make(plan[0]))
-    code = slot_codes(tile, offsets)
+    arrived = send(make(0))
     if len(plan) == 1:
-        parts = spread(*place(code, arrived))
-        between = rows_between(parts, lots[0])
+        code = codes(arrived)
+        coadd, strip, edge = place(code, arrived, lots[0], dtype)
+        parts = spread(coadd, strip)
+        if visits > 1:
+            edges = lax.all_gather(edge, "visit")
+            edge = (edges[visits - 1], edges[0])
+        else:
+            edge = (edge, edge)
+        between = rows_between(edge, parts)
         return stage(whole_plan(lots[0], visits), mine, psf_taps, between, [parts], lots)
 
-    later = make(plan[1])
+    later = make(1)
     arrived, later = lax.optimization_barrier((arrived, later))
     second = send(later)
-    parts = spread(*place(code, arrived))
-    between = rows_between(parts, lots[0])
+    code = codes(arrived)
+    coadd, strip, edge = place(code, arrived, lots[0], dtype)
+    parts = spread(coadd, strip)
+    between = rows_between(edge, parts)
     held = stage(outer_plan(lots[0]), mine, psf_taps, between, [parts], lots[:1])
     second, held = lax.optimization_barrier((second, held))
-    more = spread(*place(code, second))
+    coadd, strip, _ = place(code, second, lots[1], dtype)
+    more = spread(coadd, strip)
     return stage(inner_plan(*lots), mine, psf_taps, between, [parts, more], lots, held)
+
+
+def codes(arrived):
+    note = arrived[:, arrived.shape[1] - NOTE, :: SIDE // CAP]
+    return note.astype(jnp.float32).astype(jnp.int32).reshape(-1)
 
 
 def solution(mesh):

time: 356 us -> 269 us (0.76)
  blocking collectives: 68.8 us -> 0 us
  local copies, waits for them, and re-layouts: 16.2 us -> 4.56 us
  starting transfers between devices: 53.9 us -> 49.9 us
    unnamed x1 -> x0, blocking collectives: 68.8 us -> none
    ppermute x2, waiting for transfers between devices: 33.4 us -> 0.01 us  [spread(): other = lax.ppermute(coadd, 'visit', swap)]
    ppermute x8 -> x4, waiting for transfers between devices: 5.29 us -> 23.3 us  [neighbours(): return (lax.ppermute(last, axis, up), lax.ppermute(first, axis, down))]
    unnamed x54 -> x17, local copies, waits for them, and re-layouts: 15.9 us -> 2.63 us
    ppermute x4, starting transfers between devices: 14.7 us -> 6.54 us  [the longest x2 4.59 us: spread(): return [(coadd, beyond), (other, lax.ppermute(beyond, 'visit', swap))]]
    all_to_all x2, waiting for transfers between devices: 121 us -> 129 us  [send(): lax.all_to_all(blocks, EVERY, split_axis=0, concat_axis=0, tiled=True)]
    ppermute x4, waiting for transfers between devices: 0.01 us -> 5.01 us  [the longest x2 5.01 us: spread(): return [(coadd, beyond), (other, lax.ppermute(beyond, 'visit', swap))]]
    pallas_call x4, Pallas kernels: 23.5 us -> 27.3 us  [the longest x2 17.8 us: warp(): pl.pallas_call(functools.partial(warp_kernel, tiles, share, noted), out_s...]
  transfers between devices with their start and end apart: 16 -> 12, of which waited for: 5 -> 5; matrix products, arithmetic and copies ran while one was open for 1% -> 1% of each run, Pallas kernels for 9% -> 12%
where the time goes in v3:
time: 269 us; the launch traced here: 268 us
  waiting for transfers between devices  157 us (58%)
  Pallas kernels  55.5 us (21%)
  starting transfers between devices  49.9 us (19%)
  local copies, waits for them, and re-layouts  4.56 us (2%)
    all_to_all x2, waiting for transfers between devices, send(): lax.all_to_all(blocks, EVERY, split_axis=0, concat_axis=0, tiled=True)  129 us
    pallas_call x2, Pallas kernels, stage(): pl.pallas_call(functools.partial(stage_kernel, plan, lots), out_shape=(sh...  28.2 us
    ppermute x4, waiting for transfers between devices, neighbours(): return (lax.ppermute(last, axis, up), lax.ppermute(first, axis, down))  23.3 us
    ppermute x4, starting transfers between devices, neighbours(): return (lax.ppermute(last, axis, up), lax.ppermute(first, axis, down))  22.8 us
    pallas_call x2, Pallas kernels, warp(): pl.pallas_call(functools.partial(warp_kernel, tiles, share, noted), out_s...  17.8 us
    all_to_all x2, starting transfers between devices, send(): lax.all_to_all(blocks, EVERY, split_axis=0, concat_axis=0, tiled=True)  16.3 us
    pallas_call x2, Pallas kernels, place(): pl.pallas_call(functools.partial(place_kernel, 2 * lot), grid_spec=pltpu....  9.47 us
  transfers between devices with their start and end apart: 12, of which 5 were waited for; matrix products, arithmetic and copies ran while one was open for 1% of the time, Pallas kernels for 12%

profile of v3, /device:TPU:0, one launch (start us, length us, event | category | flops | bytes accessed | tf_op | source)
XLA Modules:
  0.0 268.4 jit_solution(4199968352169473136)
XLA Ops:
  0.6 0.8 copy.16
  1.4 0.6 reshape.16.offset_ref
  2.0 9.3 %warp.2 = bf16[32,784,128]{2,1,0:T(8,128)(2,1)} custom-call(s32[24]{0:T(128)} %visit_ref.3, s32[24]{0:T(128)} %bitcast.4, s32[48]{0:T(128)} %reshape.16.offset_ref, s32[8,256]{1,0:T(8,128)} %good_ref.3, bf16[8,256,256]{2,1,0:T(8,128)(2,1)} %rows_hbm.3, bf16[8,256,256]{2,1,0:T(8,128)(2,1)} %cols_hbm.3, bf16[24,256,256]{2,1,0:T(8,128)(2,1)} %var_hbm.3, ...), custom_call_target="tpu_custom_call" | custom-call | flops 3221225472 | bytes 12582912 | tf_op jit(solution)/shard_map/warp/pallas_call | solution.py:157
  11.3 7.4 %all-to-all-start = ((bf16[32,784,128]{2,1,0:T(8,128)(2,1)}), bf16[32,784,128]{2,1,0:T(8,128)(2,1)}, u32[]{:S(2)}, u32[]{:S(2)}) async-start(bf16[32,784,128]{2,1,0:T(8,128)(2,1)} %warp.2), calls=%async_computation | async-start | bytes 12845056 | tf_op jit(solution)/shard_map/all_to_all | solution.py:497
  18.8 8.5 %warp.3 = bf16[32,256,128]{2,1,0:T(8,128)(2,1)} custom-call(s32[24]{0:T(128)} %visit_ref.3, s32[24]{0:T(128)} %bitcast.5, s32[48]{0:T(128)} %reshape.16.offset_ref, s32[8,256]{1,0:T(8,128)} %good_ref.3, bf16[8,256,256]{2,1,0:T(8,128)(2,1)} %rows_hbm.3, bf16[8,256,256]{2,1,0:T(8,128)(2,1)} %cols_hbm.3, bf16[24,256,256]{2,1,0:T(8,128)(2,1)} %var_hbm.3, ...), custom_call_target="tpu_custom_call" | custom-call | flops 3221225472 | bytes 12582912 | tf_op jit(solution)/shard_map/warp/pallas_call | solution.py:157
  27.3 128.6 %all-to-all-done.blocks_ref = bf16[32,784,128]{2,1,0:T(8,128)(2,1)} async-done(((bf16[32,784,128]{2,1,0:T(8,128)(2,1)}), bf16[32,784,128]{2,1,0:T(8,128)(2,1)}, u32[]{:S(2)}, u32[]{:S(2)}) %all-to-all-start) | async-done | bytes 6422560 | tf_op jit(solution)/shard_map/all_to_all | solution.py:497
  155.9 8.9 %all-to-all-start.1 = ((bf16[32,256,128]{2,1,0:T(8,128)(2,1)}), bf16[32,256,128]{2,1,0:T(8,128)(2,1)S(1)}, u32[]{:S(2)}, u32[]{:S(2)}) async-start(bf16[32,256,128]{2,1,0:T(8,128)(2,1)} %warp.3), calls=%async_computation.1 | async-start | bytes 4194304 | tf_op jit(solution)/shard_map/all_to_all | solution.py:497
  164.8 1.0 slice.33
  165.8 0.1 convert_element_type.14.code_ref
  165.9 6.9 %place.2 = (bf16[384,1024]{1,0:T(8,128)(2,1)S(1)}, f32[16,384]{1,0:T(8,128)S(1)}, f32[16,1024]{1,0:T(8,128)S(1)}) custom-call(s32[64]{0:T(128)S(1)} %convert_element_type.14.code_ref, bf16[32,784,128]{2,1,0:T(8,128)(2,1)} %all-to-all-done.blocks_ref), custom_call_target="tpu_custom_call" | custom-call | flops 3211264 | bytes 6422528 | tf_op jit(solution)/shard_map/place/pallas_call | solution.py:226
  172.9 1.3 collective-permute-start.1
  174.2 4.5 %collective-permute-start = (f32[8,384]{1,0:T(8,128)S(1)}, f32[8,384]{1,0:T(8,128)S(1)}, u32[]{:S(2)}, u32[]{:S(2)}) collective-permute-start(f32[8,384]{1,0:T(8,128)S(1)} %get-tuple-element.29), channel_id=1, source_target_pairs={{0,1},{1,2},{2,3},{4,5},{5,6},{6,7},{8,9},{9,10},{10,11},{12,13},{... | collective-permute-start | bytes 36872 | tf_op jit(solution)/shard_map/ppermute | solution.py:252
  178.7 1.8 collective-permute-start.4
  180.5 19.1 %collective-permute-done = f32[8,384]{1,0:T(8,128)S(1)} collective-permute-done((f32[8,384]{1,0:T(8,128)S(1)}, f32[8,384]{1,0:T(8,128)S(1)}, u32[]{:S(2)}, u32[]{:S(2)}) %collective-permute-start) | collective-permute-done | bytes 12320 | tf_op jit(solution)/shard_map/ppermute | solution.py:252
  199.9 0.1 concatenate.13
  200.0 1.3 collective-permute-start.3
  201.3 0.7 collective-permute-start.2
  201.9 4.1 %collective-permute-start.5 = (f32[16,384]{1,0:T(8,128)S(1)}, f32[16,384]{1,0:T(8,128)S(1)}, u32[]{:S(2)}, u32[]{:S(2)}) collective-permute-start(f32[16,384]{1,0:T(8,128)S(1)} %constant_dynamic-update-slice_fusion.refs_4_), channel_id=1, source_target_pairs={{0,16},{16,0},{1,17},{17,1},{2,18},{18,2},{3,19},{19,3},{4,20},{20... | collective-permute-start | bytes 73736 | tf_op jit(solution)/shard_map/ppermute | solution.py:261
  206.0 0.7 pad_maximum_fusion.refs_2_
  206.7 1.9 collective-permute-done.5.refs_6_
  208.6 0.6 copy-done.4
  209.2 17.0 %stage.2 = (f32[1024,1024]{1,0:T(8,128)}, f32[1024,1024]{1,0:T(8,128)}) custom-call(s32[1]{0:T(128)} %bitcast.refs_0_, f32[7]{0:T(128)} %refs_1_.3, f32[16,1152]{1,0:T(8,128)} %pad_maximum_fusion.refs_2_, bf16[384,1024]{1,0:T(8,128)(2,1)} %copy-done, f32[16,384]{1,0:T(8,128)} %copy-done.3, bf16[384,1024]{1,0:T(8,128)(2,1)} %collective-permute-done.4.refs_5_, ...), custom_call_target="tpu_custom_call" | custom-call | flops 79626240 | bytes 11943936 | tf_op jit(solution)/shard_map/stage/pallas_call | solution.py:424
  226.2 2.6 place.3
  228.7 2.4 collective-permute-start.8
  231.1 15.7 %collective-permute-start.6 = (f32[8,128]{1,0:T(8,128)S(1)}, f32[8,128]{1,0:T(8,128)S(1)}, u32[]{:S(2)}, u32[]{:S(2)}) collective-permute-start(f32[8,128]{1,0:T(8,128)S(1)} %get-tuple-element.31), channel_id=1, source_target_pairs={{0,1},{1,2},{2,3},{4,5},{5,6},{6,7},{8,9},{9,10},{10,11},{12,13},{... | collective-permute-start | bytes 12296 | tf_op jit(solution)/shard_map/ppermute | solution.py:252
  246.8 1.3 collective-permute-start.7
  248.1 4.2 %collective-permute-done.7 = f32[8,128]{1,0:T(8,128)S(1)} collective-permute-done((f32[8,128]{1,0:T(8,128)S(1)}, f32[8,128]{1,0:T(8,128)S(1)}, u32[]{:S(2)}, u32[]{:S(2)}) %collective-permute-start.7) | collective-permute-done | bytes 4128 | tf_op jit(solution)/shard_map/ppermute | solution.py:252
  252.3 0.5 collective-permute-start.9
  252.8 3.1 %collective-permute-done.9.refs_10_ = f32[16,128]{1,0:T(8,128)S(1)} collective-permute-done((f32[16,128]{1,0:T(8,128)S(1)}, f32[16,128]{1,0:T(8,128)S(1)}, u32[]{:S(2)}, u32[]{:S(2)}) %collective-permute-start.9) | collective-permute-done | bytes 8224 | tf_op jit(solution)/shard_map/ppermute | solution.py:261
  255.9 0.6 copy-done.6
  256.5 0.7 copy-done.2
  257.2 11.2 %stage.3 = (f32[1024,1024]{1,0:T(8,128)}, f32[1024,1024]{1,0:T(8,128)}) custom-call(s32[1]{0:T(128)} %bitcast.refs_0_, f32[7]{0:T(128)} %refs_1_.3, f32[16,1152]{1,0:T(8,128)} %pad_maximum_fusion.refs_2_, bf16[384,1024]{1,0:T(8,128)(2,1)} %copy-done, f32[16,384]{1,0:T(8,128)} %copy-done.3, ...), custom_call_target="tpu_custom_call", output_to_operand_aliasing={{0}: (11, {}), {1}: (12, {})} | custom-call | flops 47185920 | bytes 7077888 | tf_op jit(solution)/shard_map/stage/pallas_call | solution.py:424
  (32 shorter events, 0.4 us)
Async XLA Ops:
  11.3 144.5 %all-to-all-start = ((bf16[32,784,128]{2,1,0:T(8,128)(2,1)}), bf16[32,784,128]{2,1,0:T(8,128)(2,1)}, u32[]{:S(2)}, u32[]{:S(2)}) async-start(bf16[32,784,128]{2,1,0:T(8,128)(2,1)} %warp.2), calls=%async_computation | async-start | bytes 12845056 | tf_op jit(solution)/shard_map/all_to_all | solution.py:497
  155.9 70.3 %all-to-all-start.1 = ((bf16[32,256,128]{2,1,0:T(8,128)(2,1)}), bf16[32,256,128]{2,1,0:T(8,128)(2,1)S(1)}, u32[]{:S(2)}, u32[]{:S(2)}) async-start(bf16[32,256,128]{2,1,0:T(8,128)(2,1)} %warp.3), calls=%async_computation.1 | async-start | bytes 4194304 | tf_op jit(solution)/shard_map/all_to_all | solution.py:497
  172.8 35.7 %copy-start = (bf16[384,1024]{1,0:T(8,128)(2,1)}, bf16[384,1024]{1,0:T(8,128)(2,1)S(1)}, u32[]{:S(2)}) copy-start(bf16[384,1024]{1,0:T(8,128)(2,1)S(1)} %get-tuple-element.17.refs_3_) | copy-start | bytes 2359300
  172.9 26.8 %collective-permute-start.1 = (f32[8,384]{1,0:T(8,128)S(1)}, f32[8,384]{1,0:T(8,128)S(1)}, u32[]{:S(2)}, u32[]{:S(2)}) collective-permute-start(f32[8,384]{1,0:T(8,128)S(1)} %get-tuple-element.28), channel_id=1, source_target_pairs={{1,0},{2,1},{3,2},{5,4},{6,5},{7,6},{9,8},{10,9},{11,10},{13,12},{... | collective-permute-start | bytes 36872 | tf_op jit(solution)/shard_map/ppermute | solution.py:252
  174.2 25.5 %collective-permute-start = (f32[8,384]{1,0:T(8,128)S(1)}, f32[8,384]{1,0:T(8,128)S(1)}, u32[]{:S(2)}, u32[]{:S(2)}) collective-permute-start(f32[8,384]{1,0:T(8,128)S(1)} %get-tuple-element.29), channel_id=1, source_target_pairs={{0,1},{1,2},{2,3},{4,5},{5,6},{6,7},{8,9},{9,10},{10,11},{12,13},{... | collective-permute-start | bytes 36872 | tf_op jit(solution)/shard_map/ppermute | solution.py:252
  178.7 29.9 %collective-permute-start.4 = (bf16[384,1024]{1,0:T(8,128)(2,1)S(1)}, bf16[384,1024]{1,0:T(8,128)(2,1)}, u32[]{:S(2)}, u32[]{:S(2)}) collective-permute-start(bf16[384,1024]{1,0:T(8,128)(2,1)S(1)} %get-tuple-element.17.refs_3_), channel_id=1, source_target_pairs={{0,16},{16,0},{1,17},{17,1},{2,18},{18,2},{3,19},{19,3},{4,20},{20... | collective-permute-start | bytes 2359304 | tf_op jit(solution)/shard_map/ppermute | solution.py:259
  199.7 8.9 %copy-start.3 = (f32[16,384]{1,0:T(8,128)}, f32[16,384]{1,0:T(8,128)S(1)}, u32[]{:S(2)}) copy-start(f32[16,384]{1,0:T(8,128)S(1)} %constant_dynamic-update-slice_fusion.refs_4_) | copy-start | bytes 73732
  200.0 6.0 %collective-permute-start.3 = (f32[8,1152]{1,0:T(8,128)S(1)}, f32[8,1152]{1,0:T(8,128)S(1)}, u32[]{:S(2)}, u32[]{:S(2)}) collective-permute-start(f32[8,1152]{1,0:T(8,128)S(1)} %concatenate.13), channel_id=1, source_target_pairs={{4,0},{8,4},{12,8},{16,20},{20,24},{24,28},{5,1},{9,5},{13,9},{17,... | collective-permute-start | bytes 110600 | tf_op jit(solution)/shard_map/ppermute | solution.py:297
  201.3 4.7 %collective-permute-start.2 = (f32[8,1152]{1,0:T(8,128)S(1)}, f32[8,1152]{1,0:T(8,128)S(1)}, u32[]{:S(2)}, u32[]{:S(2)}) collective-permute-start(f32[8,1152]{1,0:T(8,128)S(1)} %concatenate.13), channel_id=1, source_target_pairs={{4,16},{8,20},{12,24},{16,4},{20,8},{24,12},{5,17},{9,21},{13,25},... | collective-permute-start | bytes 110600 | tf_op jit(solution)/shard_map/ppermute | solution.py:298
  201.9 6.6 %collective-permute-start.5 = (f32[16,384]{1,0:T(8,128)S(1)}, f32[16,384]{1,0:T(8,128)S(1)}, u32[]{:S(2)}, u32[]{:S(2)}) collective-permute-start(f32[16,384]{1,0:T(8,128)S(1)} %constant_dynamic-update-slice_fusion.refs_4_), channel_id=1, source_target_pairs={{0,16},{16,0},{1,17},{17,1},{2,18},{18,2},{3,19},{19,3},{4,20},{20... | collective-permute-start | bytes 73736 | tf_op jit(solution)/shard_map/ppermute | solution.py:261
  208.6 0.6 copy-start.4
  228.7 27.2 %copy-start.1 = (bf16[128,1024]{1,0:T(8,128)(2,1)}, bf16[128,1024]{1,0:T(8,128)(2,1)S(1)}, u32[]{:S(2)}) copy-start(bf16[128,1024]{1,0:T(8,128)(2,1)S(1)} %get-tuple-element.22.refs_7_) | copy-start | bytes 786436
  228.7 27.2 %collective-permute-start.8 = (bf16[128,1024]{1,0:T(8,128)(2,1)S(1)}, bf16[128,1024]{1,0:T(8,128)(2,1)S(1)}, u32[]{:S(2)}, u32[]{:S(2)}) collective-permute-start(bf16[128,1024]{1,0:T(8,128)(2,1)S(1)} %get-tuple-element.22.refs_7_), channel_id=1, source_target_pairs={{0,16},{16,0},{1,17},{17,1},{2,18},{18,2},{3,19},{19,3},{4,20},{20... | collective-permute-start | bytes 786440 | tf_op jit(solution)/shard_map/ppermute | solution.py:259
  231.1 17.0 %collective-permute-start.6 = (f32[8,128]{1,0:T(8,128)S(1)}, f32[8,128]{1,0:T(8,128)S(1)}, u32[]{:S(2)}, u32[]{:S(2)}) collective-permute-start(f32[8,128]{1,0:T(8,128)S(1)} %get-tuple-element.31), channel_id=1, source_target_pairs={{0,1},{1,2},{2,3},{4,5},{5,6},{6,7},{8,9},{9,10},{10,11},{12,13},{... | collective-permute-start | bytes 12296 | tf_op jit(solution)/shard_map/ppermute | solution.py:252
  246.8 5.5 %collective-permute-start.7 = (f32[8,128]{1,0:T(8,128)S(1)}, f32[8,128]{1,0:T(8,128)S(1)}, u32[]{:S(2)}, u32[]{:S(2)}) collective-permute-start(f32[8,128]{1,0:T(8,128)S(1)} %get-tuple-element.30), channel_id=1, source_target_pairs={{1,0},{2,1},{3,2},{5,4},{6,5},{7,6},{9,8},{10,9},{11,10},{13,12},{... | collective-permute-start | bytes 12296 | tf_op jit(solution)/shard_map/ppermute | solution.py:252
  252.3 3.7 %copy-start.5 = (f32[16,128]{1,0:T(8,128)}, f32[16,128]{1,0:T(8,128)S(1)}, u32[]{:S(2)}) copy-start(f32[16,128]{1,0:T(8,128)S(1)} %constant_dynamic-update-slice_fusion.2.refs_8_) | copy-start | bytes 24580
  252.3 3.7 %collective-permute-start.9 = (f32[16,128]{1,0:T(8,128)S(1)}, f32[16,128]{1,0:T(8,128)S(1)}, u32[]{:S(2)}, u32[]{:S(2)}) collective-permute-start(f32[16,128]{1,0:T(8,128)S(1)} %constant_dynamic-update-slice_fusion.2.refs_8_), channel_id=1, source_target_pairs={{0,16},{16,0},{1,17},{17,1},{2,18},{18,2},{3,19},{19,3},{4,20},{20... | collective-permute-start | bytes 24584 | tf_op jit(solution)/shard_map/ppermute | solution.py:261
  255.9 0.6 copy-start.6
  256.5 0.7 copy-start.2

commit v4 on v3

--- a/solution.py
+++ b/solution.py
@@ -13,6 +13,7 @@
 CAP = 2
 UNITS = TY // STEP
 HALO = 8
+EDGE = 16
 SIDE = 128
 WIDE = TX + SIDE
 GROUP = 4
@@ -127,7 +128,7 @@
                     out_sems.at[block, visit],
                 ).start()
                 if noted:
-                    code = offset_ref[2 * block] * 8 + offset_ref[2 * block + 1]
+                    code = offset_ref[0, block] * 8 + offset_ref[1, block]
                     note[target] = jnp.where(
                         slot_of_lane == rank, code.astype(jnp.float32), note[target].astype(jnp.float32)
                     ).astype(jnp.bfloat16)
@@ -218,11 +219,11 @@
         edge_ref[HALO:] = coadd[height - HALO :]
 
 
-def place(code, blocks, lot, dtype):
+def place(code, blocks, lot):
     count, tall, side = blocks.shape
     some = 4
     height = lot * UNITS
-    shapes = [((height, TX), dtype), ((2 * HALO, height), jnp.float32), ((2 * HALO, TX), jnp.float32)]
+    shapes = [((height, TX), jnp.bfloat16), ((2 * HALO, height), jnp.float32), ((2 * HALO, TX), jnp.float32)]
     return pl.pallas_call(
         functools.partial(place_kernel, 2 * lot),
         grid_spec=pltpu.PrefetchScalarGridSpec(
@@ -254,37 +255,44 @@
 
 def spread(coadd, strip):
     visits = lax.axis_size("visit")
+    first, last = strip[:HALO], strip[HALO:]
     if visits == 2:
-        swap = [(0, 1), (1, 0)]
-        other = lax.ppermute(coadd, "visit", swap)
-        beyond = jnp.concatenate(neighbours(strip[:HALO], strip[HALO:], "px"), axis=0)
-        return [(coadd, beyond), (other, lax.ppermute(beyond, "visit", swap))]
-    beyond = jnp.concatenate(neighbours(strip[:HALO], strip[HALO:], "px"), axis=0)
+        other = lax.ppermute(coadd, "visit", [(0, 1), (1, 0)])
+        count = lax.axis_size("px")
+        up, down = beside("px")
+
+        def crossed(pairs):
+            return [(v * count + i, (1 - v) * count + j) for v in range(2) for i, j in pairs]
+
+        left, right = neighbours(first, last, "px")
+        other_left = lax.ppermute(last, ("visit", "px"), crossed(up))
+        other_right = lax.ppermute(first, ("visit", "px"), crossed(down))
+        return [(coadd, left, right), (other, other_left, other_right)]
+    one = (coadd, *neighbours(first, last, "px"))
     if visits == 1:
-        return [(coadd, beyond)]
-    every = [lax.all_gather(part, "visit") for part in (coadd, beyond)]
+        return [one]
+    every = [lax.all_gather(part, "visit") for part in one]
     return [tuple(part[visit] for part in every) for visit in range(visits)]
 
 
-def widened(rows, beyond):
-    corner = beyond.T
+def widened(rows, left, right):
     gap = jnp.zeros((HALO, SIDE - 2 * HALO), jnp.float32)
-    return jnp.concatenate([rows, corner[:, HALO:], gap, corner[:, :HALO]], axis=1)
+    return jnp.concatenate([rows, right.T, gap, left.T], axis=1)
 
 
 def rows_between(edge, parts):
     visits = len(parts)
     height = parts[0][1].shape[1]
+    none = jnp.zeros((EDGE - HALO, WIDE), jnp.float32)
     if visits != 2:
-        last = widened(edge[0][HALO:], parts[-1][1][:, height - HALO :])
-        first = widened(edge[1][:HALO], parts[0][1][:, :HALO])
+        last = widened(edge[0][HALO:], *[side[:, height - HALO :] for side in parts[-1][1:]])
+        first = widened(edge[1][:HALO], *[side[:, :HALO] for side in parts[0][1:]])
         above, below = neighbours(first, last, "py")
-        return jnp.concatenate([above, below], axis=0)
+        return jnp.concatenate([none, above, below, none], axis=0).astype(jnp.bfloat16)
     lower = lax.axis_index("visit") == 0
-    beyond = parts[0][1]
     mine = widened(
         jnp.where(lower, edge[:HALO], edge[HALO:]),
-        jnp.where(lower, beyond[:, :HALO], beyond[:, height - HALO :]),
+        *[jnp.where(lower, side[:, :HALO], side[:, height - HALO :]) for side in parts[0][1:]],
     )
     count = lax.axis_size("py")
     up, down = beside("py")
@@ -296,47 +304,60 @@
 
     straight = lax.ppermute(mine, ("visit", "py"), pairs(0))
     crossed = lax.ppermute(mine, ("visit", "py"), pairs(1))
-    return jnp.concatenate(
-        [jnp.where(lower, crossed, straight), jnp.where(lower, straight, crossed)], axis=0
-    )
+    above, below = jnp.where(lower, crossed, straight), jnp.where(lower, straight, crossed)
+    return jnp.concatenate([none, above, below, none], axis=0).astype(jnp.bfloat16)
+
+
+def bands(plan, taps):
+    fields = plan[0]
+    tall, margin = fields["tall"], fields["margin"]
+    row = jnp.arange(tall, dtype=jnp.int32)
+    out = jnp.arange(tall - 2 * margin, dtype=jnp.int32) + margin
+    three = (jnp.abs(row[:, None] - row[None, :]) <= 1).astype(jnp.bfloat16)
+    nine = (jnp.abs(out[:, None] - row[None, :]) <= 4).astype(jnp.bfloat16)
+    count = taps.shape[0]
+    ahead = row[None, :] - out[:, None] + count // 2
+    blur = sum(jnp.where(ahead == tap, taps[tap], 0.0) for tap in range(count))
+    coarse = blur.astype(jnp.bfloat16)
+    fine = (blur - coarse.astype(jnp.float32)).astype(jnp.bfloat16)
+    return jnp.concatenate([three, coarse, fine], axis=0), nine
 
 
 def stage_kernel(plan, lots, *refs):
-    mine_ref, taps_ref, between_ref = refs[:3]
+    mine_ref, taps_ref, between_ref, sums_ref, nine_ref = refs[:5]
     fields, copies, outs = plan
-    visits = fields["visits"]
-    at = 3
+    visits, margin = fields["visits"], fields["margin"]
+    at = 5
     chunks = []
     for lot in lots:
         parts = []
         for _ in range(visits):
-            parts.append(refs[at : at + 2])
-            at += 2
+            parts.append(refs[at : at + 3])
+            at += 3
         chunks.append(parts)
     at += fields["aliased"]
     detection_hbm, variance_hbm = refs[at : at + 2]
     field, detection, variance, sems = refs[at + 2 : at + 6]
     sides = refs[at + 6 :]
     spans, tall, _ = field.shape
+    short = tall - 2 * margin
 
     which = 0
     held = []
     for parts in chunks:
         group = []
-        for cells, beyond in parts:
+        for cells, left, right in parts:
             side = sides[which]
             which += 1
             height = cells.shape[0]
             side[...] = jnp.concatenate(
-                [
-                    beyond[HALO:, :],
-                    jnp.zeros((SIDE - 2 * HALO, height), jnp.float32),
-                    beyond[:HALO, :],
-                ],
-                axis=0,
-            ).T
+                [right[...], jnp.zeros((SIDE - 2 * HALO, height), jnp.float32), left[...]], axis=0
+            ).T.astype(jnp.bfloat16)
             group.append((cells, side))
         held.append(group)
+
+    for span, first, rows in fields["blank"]:
+        field[span, first : first + rows, :] = jnp.zeros((rows, WIDE), jnp.bfloat16)
 
     def assemble(order):
         for chunk, visit, first, rows, at_row, begin, end, shift in copies:
@@ -345,9 +366,9 @@
 
             @pl.loop(begin, end)
             def _(unit):
-                start = pl.multiple_of(unit * lot + first, HALO)
+                start = pl.multiple_of(unit * lot + first, EDGE)
                 into = pl.ds(at_row, rows)
-                field[unit + shift, into, :TX] = cells[pl.ds(start, rows), :].astype(jnp.float32)
+                field[unit + shift, into, :TX] = cells[pl.ds(start, rows), :]
                 field[unit + shift, into, TX:] = side[pl.ds(start, rows), :]
 
     if visits == 2:
@@ -361,19 +382,16 @@
         assemble(tuple(range(visits)))
     if fields["between"]:
         above_at, below_at = fields["between"]
-        field[0, above_at : above_at + HALO, :] = between_ref[:HALO, :]
-        field[spans - 1, below_at : below_at + HALO, :] = between_ref[HALO:, :]
+        field[0, above_at : above_at + EDGE, :] = between_ref[:EDGE, :]
+        field[spans - 1, below_at : below_at + EDGE, :] = between_ref[EDGE:, :]
 
     taps = [taps_ref[tap] for tap in range(7)]
-
-    def down(value, by):
-        return value if by == 0 else pltpu.roll(value, by % tall, 0)
 
     def across(value, by):
         return value if by == 0 else pltpu.roll(value, by % WIDE, 1)
 
-    def three(value, shift, by):
-        return value + shift(value, by) + shift(value, -by)
+    def three(value, by):
+        return value + across(value, by) + across(value, -by)
 
     def stores(unit, source, rows, target):
         return [
@@ -388,12 +406,16 @@
     @pl.loop(0, spans)
     def _(unit):
         value = field[unit]
-        resid = value - three(three(value, down, 1), across, 1) * (1.0 / 9.0)
+        sums = jnp.dot(sums_ref[...], value, preferred_element_type=jnp.float32)
+        resid = value.astype(jnp.float32) - three(sums[:tall], 1) * (1.0 / 9.0)
         square = resid * resid
-        tower = three(three(square, down, 1), down, 3)[HALO : tall - HALO]
-        box = three(three(tower, across, 1), across, 3)
-        local = box[:, :TX] * (1.0 / 81.0) + 1e-05
-        rowwise = sum(taps[tap] * down(value, 3 - tap) for tap in range(7))[HALO : tall - HALO]
+        coarse = square.astype(jnp.bfloat16)
+        fine = (square - coarse.astype(jnp.float32)).astype(jnp.bfloat16)
+        tower = jnp.dot(nine_ref[...], coarse, preferred_element_type=jnp.float32) + jnp.dot(
+            nine_ref[...], fine, preferred_element_type=jnp.float32
+        )
+        local = three(three(tower, 1), 3)[:, :TX] * (1.0 / 81.0) + 1e-05
+        rowwise = sums[tall : tall + short] + sums[tall + short :]
         blurred = sum(taps[tap] * across(rowwise, 3 - tap) for tap in range(7))
         variance[unit] = local
         detection[unit] = blurred[:, :TX] * lax.rsqrt(local)
@@ -415,35 +437,39 @@
                     store.wait()
 
 
-def stage(plan, mine, taps, between, chunks, lots, held=()):
+def stage(plan, mine, taps, between, tables, chunks, lots, held=()):
     fields, _, _ = plan
     spans, tall = fields["spans"], fields["tall"]
     shape = jax.ShapeDtypeStruct((TY, TX), jnp.float32)
     flat = [array for parts in chunks for part in parts for array in part]
-    first = 3 + len(flat)
+    first = 5 + len(flat)
+    out = pltpu.VMEM((spans, tall - 2 * fields["margin"], TX), jnp.float32)
     return pl.pallas_call(
         functools.partial(stage_kernel, plan, lots),
         out_shape=(shape, shape),
-        in_specs=[SMEM, SMEM, VMEM] + [VMEM] * len(flat) + [HBM] * len(held),
+        in_specs=[SMEM, SMEM, VMEM, VMEM, VMEM] + [VMEM] * len(flat) + [HBM] * len(held),
         out_specs=(HBM, HBM),
         input_output_aliases={first + at: at for at in range(len(held))},
         scratch_shapes=[
-            pltpu.VMEM((spans, tall, WIDE), jnp.float32),
-            pltpu.VMEM((spans, tall - 2 * HALO, TX), jnp.float32),
-            pltpu.VMEM((spans, tall - 2 * HALO, TX), jnp.float32),
+            pltpu.VMEM((spans, tall, WIDE), jnp.bfloat16),
+            out,
+            out,
             pltpu.SemaphoreType.DMA((spans, 2)),
         ]
-        + [pltpu.VMEM((part[0].shape[0], SIDE), jnp.float32) for parts in chunks for part in parts],
+        + [pltpu.VMEM((part[0].shape[0], SIDE), jnp.bfloat16) for parts in chunks for part in parts],
         compiler_params=pltpu.CompilerParams(vmem_limit_bytes=56 * MIB),
         cost_estimate=pl.CostEstimate(
             flops=80 * spans * tall * WIDE, bytes_accessed=12 * spans * tall * WIDE, transcendentals=0
         ),
         name="stage",
-    )(mine, taps, between, *flat, *held)
+    )(mine, taps, between, *tables, *flat, *held)
 
 
 def outer_plan(lot):
-    fields = dict(visits=2, aliased=0, spans=UNITS + 1, tall=2 * lot, between=(lot - HALO, lot))
+    fields = dict(
+        visits=2, aliased=0, spans=UNITS + 1, tall=2 * lot, margin=HALO, between=(lot - EDGE, lot),
+        blank=[(0, 0, lot - EDGE), (UNITS, lot + EDGE, lot - EDGE)],
+    )
     copies = [(0, 1, 0, lot, 0, 0, UNITS, 1), (0, 0, 0, lot, lot, 0, UNITS, 0)]
     rows = lot - HALO
     outs = [
@@ -455,25 +481,27 @@
 
 
 def inner_plan(lot, inner):
-    edge = 2 * HALO
-    tall = 2 * inner + 2 * edge
-    fields = dict(visits=2, aliased=2, spans=UNITS, tall=tall, between=None)
+    tall = 2 * inner + 2 * EDGE
+    fields = dict(
+        visits=2, aliased=2, spans=UNITS, tall=tall, margin=HALO, between=None, blank=[]
+    )
     copies = [
-        (0, 0, lot - edge, edge, 0, 0, UNITS, 0),
-        (1, 0, 0, inner, edge, 0, UNITS, 0),
-        (1, 1, 0, inner, edge + inner, 0, UNITS, 0),
-        (0, 1, 0, edge, edge + 2 * inner, 0, UNITS, 0),
+        (0, 0, lot - EDGE, EDGE, 0, 0, UNITS, 0),
+        (1, 0, 0, inner, EDGE, 0, UNITS, 0),
+        (1, 1, 0, inner, EDGE + inner, 0, UNITS, 0),
+        (0, 1, 0, EDGE, EDGE + 2 * inner, 0, UNITS, 0),
     ]
-    return fields, copies, [(0, UNITS, 0, tall - edge, lot - HALO)]
+    return fields, copies, [(0, UNITS, 0, tall - 2 * HALO, lot - HALO)]
 
 
 def whole_plan(lot, visits):
     fields = dict(
-        visits=visits, aliased=0, spans=UNITS, tall=STEP + 2 * HALO, between=(0, HALO + STEP)
-    )
-    copies = [(0, visit, 0, lot, HALO + visit * lot, 0, UNITS, 0) for visit in range(visits)]
-    copies.append((0, visits - 1, lot - HALO, HALO, 0, 0, UNITS - 1, 1))
-    copies.append((0, 0, 0, HALO, HALO + STEP, 1, UNITS, -1))
+        visits=visits, aliased=0, spans=UNITS, tall=STEP + 2 * EDGE, margin=EDGE,
+        between=(0, EDGE + STEP), blank=[],
+    )
+    copies = [(0, visit, 0, lot, EDGE + visit * lot, 0, UNITS, 0) for visit in range(visits)]
+    copies.append((0, visits - 1, lot - EDGE, EDGE, 0, 0, UNITS - 1, 1))
+    copies.append((0, 0, 0, EDGE, EDGE + STEP, 1, UNITS, -1))
     return fields, copies, [(0, UNITS, 0, STEP, 0)]
 
 
@@ -485,21 +513,21 @@
     plan = shares(visits)
     lots = [rows for rows, _ in plan]
     mine = lax.axis_index("visit").astype(jnp.int32).reshape(1)
-    dtype = jnp.bfloat16 if visits == 2 else jnp.float32
-
-    def make(chunk):
+
+    def make(chunk, var):
         return warp(
-            tiles, plan[chunk], chunk == 0, block_visit, dest_tile[:, 0], offsets.reshape(-1),
-            good_columns, warp_rows, warp_cols, inv_var, images,
+            tiles, plan[chunk], chunk == 0, block_visit, dest_tile[:, 0], offsets.T,
+            good_columns, warp_rows, warp_cols, var, images,
         )
 
     def send(blocks):
         return lax.all_to_all(blocks, EVERY, split_axis=0, concat_axis=0, tiled=True)
 
-    arrived = send(make(0))
+    made, psf_taps = lax.optimization_barrier((make(0, inv_var), psf_taps))
+    arrived = send(made)
     if len(plan) == 1:
         code = codes(arrived)
-        coadd, strip, edge = place(code, arrived, lots[0], dtype)
+        coadd, strip, edge = place(code, arrived, lots[0])
         parts = spread(coadd, strip)
         if visits > 1:
             edges = lax.all_gather(edge, "visit")
@@ -507,20 +535,24 @@
         else:
             edge = (edge, edge)
         between = rows_between(edge, parts)
-        return stage(whole_plan(lots[0], visits), mine, psf_taps, between, [parts], lots)
-
-    later = make(1)
-    arrived, later = lax.optimization_barrier((arrived, later))
+        every = whole_plan(lots[0], visits)
+        return stage(every, mine, psf_taps, between, bands(every, psf_taps), [parts], lots)
+
+    outer, inner = outer_plan(lots[0]), inner_plan(*lots)
+    tables, inv_var = lax.optimization_barrier(
+        ([bands(part, psf_taps) for part in (outer, inner)], inv_var)
+    )
+    arrived, later = lax.optimization_barrier((arrived, make(1, inv_var)))
     second = send(later)
     code = codes(arrived)
-    coadd, strip, edge = place(code, arrived, lots[0], dtype)
+    coadd, strip, edge = place(code, arrived, lots[0])
     parts = spread(coadd, strip)
     between = rows_between(edge, parts)
-    held = stage(outer_plan(lots[0]), mine, psf_taps, between, [parts], lots[:1])
-    second, held = lax.optimization_barrier((second, held))
-    coadd, strip, _ = place(code, second, lots[1], dtype)
+    coadd, strip, _ = place(code, second, lots[1])
     more = spread(coadd, strip)
-    return stage(inner_plan(*lots), mine, psf_taps, between, [parts, more], lots, held)
+    (parts, between), _ = lax.optimization_barrier(((parts, between), coadd))
+    held = stage(outer, mine, psf_taps, between, tables[0], [parts], lots[:1])
+    return stage(inner, mine, psf_taps, between, tables[1], [parts, more], lots, held)
 
 
 def codes(arrived):

time: 269 us -> 279 us (1.037)
  waiting for transfers between devices: 157 us -> 143 us
  other arithmetic: 0.8 us -> 12.6 us
  starting transfers between devices: 49.9 us -> 60.3 us
    ppermute x4 -> x6, starting transfers between devices: 8.78 us -> 31.5 us  [the longest x2 26.9 us: spread(): other_left = lax.ppermute(last, ('visit', 'px'), crossed(up))]
    all_to_all x2, waiting for transfers between devices: 129 us -> 116 us  [send(): lax.all_to_all(blocks, EVERY, split_axis=0, concat_axis=0, tiled=True)]
    ppermute x4, starting transfers between devices: 22.8 us -> 10.6 us  [neighbours(): return (lax.ppermute(last, axis, up), lax.ppermute(first, axis, down))]
    convert_element_type x0 -> x6, other arithmetic: none -> 10.5 us  [the longest x2 9.1 us: bands(): coarse = blur.astype(jnp.bfloat16)]
    ppermute x4 -> x6, waiting for transfers between devices: 5.01 us -> 6.6 us  [the longest x2 6.59 us: spread(): other = lax.ppermute(coadd, 'visit', [(0, 1), (1, 0)])]
  transfers between devices with their start and end apart: 12 -> 14, of which waited for: 5 -> 4; matrix products, arithmetic and copies ran while one was open for 1% -> 5% of each run, Pallas kernels for 12% -> 13%
where the time goes in v4:
time: 279 us; the launch traced here: 277 us
  waiting for transfers between devices  143 us (51%)
  starting transfers between devices  60.3 us (22%)
  Pallas kernels  56.7 us (20%)
  other arithmetic  12.6 us (5%)
    all_to_all x2, waiting for transfers between devices, send(): lax.all_to_all(blocks, EVERY, split_axis=0, concat_axis=0, tiled=True)  116 us
    pallas_call x2, Pallas kernels, stage(): pl.pallas_call(functools.partial(stage_kernel, plan, lots), out_shape=(sh...  29.4 us
    ppermute x2, starting transfers between devices, spread(): other_left = lax.ppermute(last, ('visit', 'px'), crossed(up))  26.9 us
    ppermute x4, waiting for transfers between devices, neighbours(): return (lax.ppermute(last, axis, up), lax.ppermute(first, axis, down))  20.8 us
    pallas_call x2, Pallas kernels, warp(): pl.pallas_call(functools.partial(warp_kernel, tiles, share, noted), out_s...  17.8 us
    all_to_all x2, starting transfers between devices, send(): lax.all_to_all(blocks, EVERY, split_axis=0, concat_axis=0, tiled=True)  16.3 us
    ppermute x4, starting transfers between devices, neighbours(): return (lax.ppermute(last, axis, up), lax.ppermute(first, axis, down))  10.6 us
    pallas_call x2, Pallas kernels, place(): pl.pallas_call(functools.partial(place_kernel, 2 * lot), grid_spec=pltpu....  9.49 us
  transfers between devices with their start and end apart: 14, of which 4 were waited for; matrix products, arithmetic and copies ran while one was open for 5% of the time, Pallas kernels for 13%

profile of v4, /device:TPU:0, one launch (start us, length us, event | category | flops | bytes accessed | tf_op | source)
XLA Modules:
  0.0 277.0 jit_solution(4570983222880712370)
XLA Ops:
  0.6 9.4 %warp.2 = bf16[32,784,128]{2,1,0:T(8,128)(2,1)} custom-call(s32[24]{0:T(128)} %visit_ref.3, s32[24]{0:T(128)} %bitcast.16, s32[2,24]{1,0:T(2,128)} %bitcast.14, s32[8,256]{1,0:T(8,128)} %good_ref.3, bf16[8,256,256]{2,1,0:T(8,128)(2,1)} %rows_hbm.3, bf16[8,256,256]{2,1,0:T(8,128)(2,1)} %cols_hbm.3, bf16[24,256,256]{2,1,0:T(8,128)(2,1)} %var_hbm.2, ...), custom_call_target="tpu_custom_call" | custom-call | flops 3221225472 | bytes 12582912 | tf_op jit(solution)/shard_map/warp/pallas_call | solution.py:158
  10.0 7.4 %all-to-all-start = ((bf16[32,784,128]{2,1,0:T(8,128)(2,1)}), bf16[32,784,128]{2,1,0:T(8,128)(2,1)}, u32[]{:S(2)}, u32[]{:S(2)}) async-start(bf16[32,784,128]{2,1,0:T(8,128)(2,1)} %warp.2), calls=%async_computation | async-start | bytes 12845056 | tf_op jit(solution)/shard_map/all_to_all | solution.py:524
  17.4 0.7 fusion.24
  18.1 4.5 %fusion.19 = (bf16[48,64]{1,0:T(8,128)(2,1)S(1)}, bf16[48,64]{1,0:T(8,128)(2,1)S(1)}) fusion(f32[]{:T(128)} %bitcast.9, f32[]{:T(128)} %bitcast.8, f32[]{:T(128)} %bitcast.7, f32[]{:T(128)} %bitcast.6, f32[]{:T(128)} %bitcast.5, f32[]{:T(128)} %bitcast.4, f32[]{:T(128)} %bitcast.3, s32[48]{0:T(128)S(1)} %iota_add_fusion), kind=kLoop, calls=%fused_computation.36 | loop fusion | flops 79872 | bytes 12508 | tf_op jit(solution)/shard_map/convert_element_type | solution.py:321
  22.7 0.6 pad_maximum_fusion.2.refs_3_
  23.3 4.6 %fusion.18 = (bf16[80,96]{1,0:T(8,128)(2,1)S(1)}, bf16[80,96]{1,0:T(8,128)(2,1)S(1)}) fusion(f32[]{:T(128)} %bitcast.9, f32[]{:T(128)} %bitcast.8, f32[]{:T(128)} %bitcast.7, f32[]{:T(128)} %bitcast.6, f32[]{:T(128)} %bitcast.5, f32[]{:T(128)} %bitcast.4, f32[]{:T(128)} %bitcast.3, s32[80]{0:T(128)S(1)} %iota_add_fusion.1), kind=kLoop, calls=%fused_computation.34 | loop fusion | flops 199680 | bytes 31068 | tf_op jit(solution)/shard_map/convert_element_type | solution.py:321
  27.9 0.7 pad_maximum_fusion.1.refs_3_
  28.5 0.7 fusion.17.refs_4_
  29.2 0.7 fusion.8.refs_4_
  29.9 8.5 %warp.3 = bf16[32,256,128]{2,1,0:T(8,128)(2,1)} custom-call(s32[24]{0:T(128)} %visit_ref.3, s32[24]{0:T(128)} %bitcast.17, s32[2,24]{1,0:T(2,128)} %bitcast.15, s32[8,256]{1,0:T(8,128)} %good_ref.3, bf16[8,256,256]{2,1,0:T(8,128)(2,1)} %rows_hbm.3, bf16[8,256,256]{2,1,0:T(8,128)(2,1)} %cols_hbm.3, bf16[24,256,256]{2,1,0:T(8,128)(2,1)} %var_hbm.2, ...), custom_call_target="tpu_custom_call" | custom-call | flops 3221225472 | bytes 12582912 | tf_op jit(solution)/shard_map/warp/pallas_call | solution.py:158
  38.4 116.1 %all-to-all-done.blocks_ref = bf16[32,784,128]{2,1,0:T(8,128)(2,1)} async-done(((bf16[32,784,128]{2,1,0:T(8,128)(2,1)}), bf16[32,784,128]{2,1,0:T(8,128)(2,1)}, u32[]{:S(2)}, u32[]{:S(2)}) %all-to-all-start) | async-done | bytes 6422560 | tf_op jit(solution)/shard_map/all_to_all | solution.py:524
  154.5 8.9 %all-to-all-start.1 = ((bf16[32,256,128]{2,1,0:T(8,128)(2,1)}), bf16[32,256,128]{2,1,0:T(8,128)(2,1)S(1)}, u32[]{:S(2)}, u32[]{:S(2)}) async-start(bf16[32,256,128]{2,1,0:T(8,128)(2,1)} %warp.3), calls=%async_computation.1 | async-start | bytes 4194304 | tf_op jit(solution)/shard_map/all_to_all | solution.py:524
  163.4 1.0 slice.68
  164.5 6.9 %place.2 = (bf16[384,1024]{1,0:T(8,128)(2,1)S(1)}, f32[16,384]{1,0:T(8,128)S(1)}, f32[16,1024]{1,0:T(8,128)S(1)}) custom-call(s32[64]{0:T(128)S(1)} %convert_element_type.55.code_ref, bf16[32,784,128]{2,1,0:T(8,128)(2,1)} %all-to-all-done.blocks_ref), custom_call_target="tpu_custom_call" | custom-call | flops 3211264 | bytes 6422528 | tf_op jit(solution)/shard_map/place/pallas_call | solution.py:227
  171.5 1.3 collective-permute-start.1
  172.8 4.5 %collective-permute-start = (f32[8,384]{1,0:T(8,128)S(1)}, f32[8,384]{1,0:T(8,128)S(1)}, u32[]{:S(2)}, u32[]{:S(2)}) collective-permute-start(f32[8,384]{1,0:T(8,128)S(1)} %get-tuple-element.51), channel_id=1, source_target_pairs={{0,1},{1,2},{2,3},{4,5},{5,6},{6,7},{8,9},{9,10},{10,11},{12,13},{... | collective-permute-start | bytes 36872 | tf_op jit(solution)/shard_map/ppermute | solution.py:253
  177.3 10.4 %collective-permute-done.1.refs_7_ = f32[8,384]{1,0:T(8,128)S(1)} collective-permute-done((f32[8,384]{1,0:T(8,128)S(1)}, f32[8,384]{1,0:T(8,128)S(1)}, u32[]{:S(2)}, u32[]{:S(2)}) %collective-permute-start.1) | collective-permute-done | bytes 12320 | tf_op jit(solution)/shard_map/ppermute | solution.py:253
  187.9 10.4 %collective-permute-done.refs_6_ = f32[8,384]{1,0:T(8,128)S(1)} collective-permute-done((f32[8,384]{1,0:T(8,128)S(1)}, f32[8,384]{1,0:T(8,128)S(1)}, u32[]{:S(2)}, u32[]{:S(2)}) %collective-permute-start) | collective-permute-done | bytes 12320 | tf_op jit(solution)/shard_map/ppermute | solution.py:253
  198.5 1.3 collective-permute-start.6
  199.8 0.7 collective-permute-start.5
  200.5 1.3 collective-permute-start.4
  201.8 20.8 %collective-permute-start.3 = (f32[8,384]{1,0:T(8,128)S(1)}, f32[8,384]{1,0:T(8,128)S(1)}, u32[]{:S(2)}, u32[]{:S(2)}) collective-permute-start(f32[8,384]{1,0:T(8,128)S(1)} %get-tuple-element.51), channel_id=1, source_target_pairs={{0,17},{1,18},{2,19},{16,1},{17,2},{18,3},{4,21},{5,22},{6,23},{20... | collective-permute-start | bytes 36872 | tf_op jit(solution)/shard_map/ppermute | solution.py:268
  222.7 2.6 place.3
  225.3 2.0 collective-permute-start.9
  227.3 0.6 pad_maximum_fusion.refs_2_
  227.9 1.3 collective-permute-start.11
  229.3 1.3 collective-permute-start.8
  230.6 6.1 %collective-permute-start.10 = (f32[8,128]{1,0:T(8,128)S(1)}, f32[8,128]{1,0:T(8,128)S(1)}, u32[]{:S(2)}, u32[]{:S(2)}) collective-permute-start(f32[8,128]{1,0:T(8,128)S(1)} %get-tuple-element.53), channel_id=1, source_target_pairs={{0,17},{1,18},{2,19},{16,1},{17,2},{18,3},{4,21},{5,22},{6,23},{20... | collective-permute-start | bytes 12296 | tf_op jit(solution)/shard_map/ppermute | solution.py:268
  236.7 6.6 %collective-permute-done.2.refs_8_ = bf16[384,1024]{1,0:T(8,128)(2,1)} collective-permute-done((bf16[384,1024]{1,0:T(8,128)(2,1)S(1)}, bf16[384,1024]{1,0:T(8,128)(2,1)}, u32[]{:S(2)}, u32[]{:S(2)}) %collective-permute-start.2) | collective-permute-done | bytes 786464 | tf_op jit(solution)/shard_map/ppermute | solution.py:260
  243.2 3.4 %collective-permute-start.7 = (f32[8,128]{1,0:T(8,128)S(1)}, f32[8,128]{1,0:T(8,128)S(1)}, u32[]{:S(2)}, u32[]{:S(2)}) collective-permute-start(f32[8,128]{1,0:T(8,128)S(1)} %get-tuple-element.53), channel_id=1, source_target_pairs={{0,1},{1,2},{2,3},{4,5},{5,6},{6,7},{8,9},{9,10},{10,11},{12,13},{... | collective-permute-start | bytes 12296 | tf_op jit(solution)/shard_map/ppermute | solution.py:253
  246.7 18.0 %stage.2 = (f32[1024,1024]{1,0:T(8,128)}, f32[1024,1024]{1,0:T(8,128)}) custom-call(s32[1]{0:T(128)} %bitcast.refs_0_, f32[7]{0:T(128)} %refs_1_.1, bf16[32,1152]{1,0:T(8,128)(2,1)} %pad_maximum_fusion.refs_2_, bf16[256,96]{1,0:T(8,128)(2,1)} %pad_maximum_fusion.1.refs_3_, bf16[80,96]{1,0:T(8,128)(2,1)} %fusion.8.refs_4_, bf16[384,1024]{1,0:T(8,128)(2,1)} %copy-done, ...), custom_call_target="tpu_custom_call" | custom-call | flops 79626240 | bytes 11943936 | tf_op jit(solution)/shard_map/stage/pallas_call | solution.py:447
  265.5 11.4 %stage.3 = (f32[1024,1024]{1,0:T(8,128)}, f32[1024,1024]{1,0:T(8,128)}) custom-call(s32[1]{0:T(128)} %bitcast.refs_0_, f32[7]{0:T(128)} %refs_1_.1, bf16[32,1152]{1,0:T(8,128)(2,1)} %pad_maximum_fusion.refs_2_, bf16[160,64]{1,0:T(8,128)(2,1)} %pad_maximum_fusion.2.refs_3_, ...), custom_call_target="tpu_custom_call", output_to_operand_aliasing={{0}: (17, {}), {1}: (18, {})} | custom-call | flops 47185920 | bytes 7077888 | tf_op jit(solution)/shard_map/stage/pallas_call | solution.py:447
  (52 shorter events, 1.5 us)
Async XLA Ops:
  10.0 7.4 %copy-start.7 = (f32[7]{0:T(128)S(1)}, f32[7]{0:T(128)}, u32[]{:S(2)}) copy-start(f32[7]{0:T(128)} %refs_1_.1) | copy-start | bytes 88
  10.0 144.4 %all-to-all-start = ((bf16[32,784,128]{2,1,0:T(8,128)(2,1)}), bf16[32,784,128]{2,1,0:T(8,128)(2,1)}, u32[]{:S(2)}, u32[]{:S(2)}) async-start(bf16[32,784,128]{2,1,0:T(8,128)(2,1)} %warp.2), calls=%async_computation | async-start | bytes 12845056 | tf_op jit(solution)/shard_map/all_to_all | solution.py:524
  154.5 68.2 %all-to-all-start.1 = ((bf16[32,256,128]{2,1,0:T(8,128)(2,1)}), bf16[32,256,128]{2,1,0:T(8,128)(2,1)S(1)}, u32[]{:S(2)}, u32[]{:S(2)}) async-start(bf16[32,256,128]{2,1,0:T(8,128)(2,1)} %warp.3), calls=%async_computation.1 | async-start | bytes 4194304 | tf_op jit(solution)/shard_map/all_to_all | solution.py:524
  171.4 75.3 %copy-start = (bf16[384,1024]{1,0:T(8,128)(2,1)}, bf16[384,1024]{1,0:T(8,128)(2,1)S(1)}, u32[]{:S(2)}) copy-start(bf16[384,1024]{1,0:T(8,128)(2,1)S(1)} %get-tuple-element.37.refs_5_) | copy-start | bytes 2359300
  171.5 16.2 %collective-permute-start.1 = (f32[8,384]{1,0:T(8,128)S(1)}, f32[8,384]{1,0:T(8,128)S(1)}, u32[]{:S(2)}, u32[]{:S(2)}) collective-permute-start(f32[8,384]{1,0:T(8,128)S(1)} %get-tuple-element.50), channel_id=1, source_target_pairs={{1,0},{2,1},{3,2},{5,4},{6,5},{7,6},{9,8},{10,9},{11,10},{13,12},{... | collective-permute-start | bytes 36872 | tf_op jit(solution)/shard_map/ppermute | solution.py:253
  172.8 25.5 %collective-permute-start = (f32[8,384]{1,0:T(8,128)S(1)}, f32[8,384]{1,0:T(8,128)S(1)}, u32[]{:S(2)}, u32[]{:S(2)}) collective-permute-start(f32[8,384]{1,0:T(8,128)S(1)} %get-tuple-element.51), channel_id=1, source_target_pairs={{0,1},{1,2},{2,3},{4,5},{5,6},{6,7},{8,9},{9,10},{10,11},{12,13},{... | collective-permute-start | bytes 36872 | tf_op jit(solution)/shard_map/ppermute | solution.py:253
  187.7 59.0 %copy-start.3 = (f32[8,384]{1,0:T(8,128)}, f32[8,384]{1,0:T(8,128)S(1)}, u32[]{:S(2)}) copy-start(f32[8,384]{1,0:T(8,128)S(1)} %collective-permute-done.1.refs_7_) | copy-start | bytes 36868
  198.3 48.5 %copy-start.4 = (f32[8,384]{1,0:T(8,128)}, f32[8,384]{1,0:T(8,128)S(1)}, u32[]{:S(2)}) copy-start(f32[8,384]{1,0:T(8,128)S(1)} %collective-permute-done.refs_6_) | copy-start | bytes 36868
  198.5 24.1 %collective-permute-start.6 = (bf16[8,1152]{1,0:T(8,128)(2,1)S(1)}, bf16[8,1152]{1,0:T(8,128)(2,1)S(1)}, u32[]{:S(2)}, u32[]{:S(2)}) collective-permute-start(bf16[8,1152]{1,0:T(8,128)(2,1)S(1)} %concatenate.15), channel_id=1, source_target_pairs={{4,0},{8,4},{12,8},{16,20},{20,24},{24,28},{5,1},{9,5},{13,9},{17,... | collective-permute-start | bytes 55304 | tf_op jit(solution)/shard_map/ppermute | solution.py:305
  199.8 22.9 %collective-permute-start.5 = (bf16[8,1152]{1,0:T(8,128)(2,1)S(1)}, bf16[8,1152]{1,0:T(8,128)(2,1)S(1)}, u32[]{:S(2)}, u32[]{:S(2)}) collective-permute-start(bf16[8,1152]{1,0:T(8,128)(2,1)S(1)} %concatenate.15), channel_id=1, source_target_pairs={{4,16},{8,20},{12,24},{16,4},{20,8},{24,12},{5,17},{9,21},{13,25},... | collective-permute-start | bytes 55304 | tf_op jit(solution)/shard_map/ppermute | solution.py:306
  200.5 28.8 %collective-permute-start.4 = (f32[8,384]{1,0:T(8,128)S(1)}, f32[8,384]{1,0:T(8,128)S(1)}, u32[]{:S(2)}, u32[]{:S(2)}) collective-permute-start(f32[8,384]{1,0:T(8,128)S(1)} %get-tuple-element.50), channel_id=1, source_target_pairs={{1,16},{2,17},{3,18},{17,0},{18,1},{19,2},{5,20},{6,21},{7,22},{21... | collective-permute-start | bytes 36872 | tf_op jit(solution)/shard_map/ppermute | solution.py:269
  201.8 28.8 %collective-permute-start.3 = (f32[8,384]{1,0:T(8,128)S(1)}, f32[8,384]{1,0:T(8,128)S(1)}, u32[]{:S(2)}, u32[]{:S(2)}) collective-permute-start(f32[8,384]{1,0:T(8,128)S(1)} %get-tuple-element.51), channel_id=1, source_target_pairs={{0,17},{1,18},{2,19},{16,1},{17,2},{18,3},{4,21},{5,22},{6,23},{20... | collective-permute-start | bytes 36872 | tf_op jit(solution)/shard_map/ppermute | solution.py:268
  222.6 20.7 %collective-permute-start.2 = (bf16[384,1024]{1,0:T(8,128)(2,1)S(1)}, bf16[384,1024]{1,0:T(8,128)(2,1)}, u32[]{:S(2)}, u32[]{:S(2)}) collective-permute-start(bf16[384,1024]{1,0:T(8,128)(2,1)S(1)} %get-tuple-element.37.refs_5_), channel_id=1, source_target_pairs={{0,16},{16,0},{1,17},{17,1},{2,18},{18,2},{3,19},{19,3},{4,20},{20... | collective-permute-start | bytes 2359304 | tf_op jit(solution)/shard_map/ppermute | solution.py:260
  225.3 39.6 %copy-start.1 = (bf16[128,1024]{1,0:T(8,128)(2,1)}, bf16[128,1024]{1,0:T(8,128)(2,1)S(1)}, u32[]{:S(2)}) copy-start(bf16[128,1024]{1,0:T(8,128)(2,1)S(1)} %get-tuple-element.33.refs_11_) | copy-start | bytes 786436
  225.3 39.5 %collective-permute-start.9 = (bf16[128,1024]{1,0:T(8,128)(2,1)S(1)}, bf16[128,1024]{1,0:T(8,128)(2,1)S(1)}, u32[]{:S(2)}, u32[]{:S(2)}) collective-permute-start(bf16[128,1024]{1,0:T(8,128)(2,1)S(1)} %get-tuple-element.33.refs_11_), channel_id=1, source_target_pairs={{0,16},{16,0},{1,17},{17,1},{2,18},{18,2},{3,19},{19,3},{4,20},{20... | collective-permute-start | bytes 786440 | tf_op jit(solution)/shard_map/ppermute | solution.py:260
  227.9 36.8 %collective-permute-start.11 = (f32[8,128]{1,0:T(8,128)S(1)}, f32[8,128]{1,0:T(8,128)S(1)}, u32[]{:S(2)}, u32[]{:S(2)}) collective-permute-start(f32[8,128]{1,0:T(8,128)S(1)} %get-tuple-element.52), channel_id=1, source_target_pairs={{1,16},{2,17},{3,18},{17,0},{18,1},{19,2},{5,20},{6,21},{7,22},{21... | collective-permute-start | bytes 12296 | tf_op jit(solution)/shard_map/ppermute | solution.py:269
  229.2 17.5 %copy-start.5 = (f32[8,384]{1,0:T(8,128)}, f32[8,384]{1,0:T(8,128)S(1)}, u32[]{:S(2)}) copy-start(f32[8,384]{1,0:T(8,128)S(1)} %collective-permute-done.4.refs_10_) | copy-start | bytes 36868
  229.3 35.5 %collective-permute-start.8 = (f32[8,128]{1,0:T(8,128)S(1)}, f32[8,128]{1,0:T(8,128)S(1)}, u32[]{:S(2)}, u32[]{:S(2)}) collective-permute-start(f32[8,128]{1,0:T(8,128)S(1)} %get-tuple-element.52), channel_id=1, source_target_pairs={{1,0},{2,1},{3,2},{5,4},{6,5},{7,6},{9,8},{10,9},{11,10},{13,12},{... | collective-permute-start | bytes 12296 | tf_op jit(solution)/shard_map/ppermute | solution.py:253
  230.6 16.2 %copy-start.6 = (f32[8,384]{1,0:T(8,128)}, f32[8,384]{1,0:T(8,128)S(1)}, u32[]{:S(2)}) copy-start(f32[8,384]{1,0:T(8,128)S(1)} %collective-permute-done.3.refs_9_) | copy-start | bytes 36868
  230.6 34.2 %collective-permute-start.10 = (f32[8,128]{1,0:T(8,128)S(1)}, f32[8,128]{1,0:T(8,128)S(1)}, u32[]{:S(2)}, u32[]{:S(2)}) collective-permute-start(f32[8,128]{1,0:T(8,128)S(1)} %get-tuple-element.53), channel_id=1, source_target_pairs={{0,17},{1,18},{2,19},{16,1},{17,2},{18,3},{4,21},{5,22},{6,23},{20... | collective-permute-start | bytes 12296 | tf_op jit(solution)/shard_map/ppermute | solution.py:268
  243.2 21.6 %collective-permute-start.7 = (f32[8,128]{1,0:T(8,128)S(1)}, f32[8,128]{1,0:T(8,128)S(1)}, u32[]{:S(2)}, u32[]{:S(2)}) collective-permute-start(f32[8,128]{1,0:T(8,128)S(1)} %get-tuple-element.53), channel_id=1, source_target_pairs={{0,1},{1,2},{2,3},{4,5},{5,6},{6,7},{8,9},{9,10},{10,11},{12,13},{... | collective-permute-start | bytes 12296 | tf_op jit(solution)/shard_map/ppermute | solution.py:253
  264.7 0.6 copy-start.8
  264.8 0.6 copy-start.9
  264.8 0.6 copy-start.10
  264.8 0.6 copy-start.11
  264.8 0.7 copy-start.2

commit v5 on v4

--- a/solution.py
+++ b/solution.py
@@ -27,7 +27,7 @@
 
 def shares(visits):
     if visits == 2:
-        edge, inner = 48, 16
+        edge, inner = 32, 32
         return [(edge, (0, STEP - edge)), (inner, (edge, edge + inner))]
     rows = STEP // visits
     return [(rows, tuple(visit * rows for visit in range(visits)))]
@@ -257,17 +257,11 @@
     visits = lax.axis_size("visit")
     first, last = strip[:HALO], strip[HALO:]
     if visits == 2:
-        other = lax.ppermute(coadd, "visit", [(0, 1), (1, 0)])
-        count = lax.axis_size("px")
-        up, down = beside("px")
-
-        def crossed(pairs):
-            return [(v * count + i, (1 - v) * count + j) for v in range(2) for i, j in pairs]
-
+        swap = [(0, 1), (1, 0)]
+        other = lax.ppermute(coadd, "visit", swap)
         left, right = neighbours(first, last, "px")
-        other_left = lax.ppermute(last, ("visit", "px"), crossed(up))
-        other_right = lax.ppermute(first, ("visit", "px"), crossed(down))
-        return [(coadd, left, right), (other, other_left, other_right)]
+        far = lax.ppermute(jnp.concatenate([left, right], axis=0), "visit", swap)
+        return [(coadd, left, right), (other, far[:HALO], far[HALO:])]
     one = (coadd, *neighbours(first, last, "px"))
     if visits == 1:
         return [one]
@@ -548,10 +542,10 @@
     coadd, strip, edge = place(code, arrived, lots[0])
     parts = spread(coadd, strip)
     between = rows_between(edge, parts)
+    held = stage(outer, mine, psf_taps, between, tables[0], [parts], lots[:1])
+    second, held = lax.optimization_barrier((second, held))
     coadd, strip, _ = place(code, second, lots[1])
     more = spread(coadd, strip)
-    (parts, between), _ = lax.optimization_barrier(((parts, between), coadd))
-    held = stage(outer, mine, psf_taps, between, tables[0], [parts], lots[:1])
     return stage(inner, mine, psf_taps, between, tables[1], [parts, more], lots, held)
 
 

time: 279 us -> 271 us (0.971)
  waiting for transfers between devices: 143 us -> 136 us
  starting transfers between devices: 60.3 us -> 54.1 us
  Pallas kernels: 56.7 us -> 59.9 us
    all_to_all x2, waiting for transfers between devices: 116 us -> 73.5 us  [send(): lax.all_to_all(blocks, EVERY, split_axis=0, concat_axis=0, tiled=True)]
    ppermute x4, waiting for transfers between devices: 20.8 us -> 58.2 us  [neighbours(): return (lax.ppermute(last, axis, up), lax.ppermute(first, axis, down))]
    ppermute x6 -> x4, starting transfers between devices: 31.5 us -> 5.81 us  [the longest x2 4.48 us: spread(): other = lax.ppermute(coadd, 'visit', swap)]
    ppermute x4, starting transfers between devices: 10.6 us -> 32.4 us  [neighbours(): return (lax.ppermute(last, axis, up), lax.ppermute(first, axis, down))]
    pallas_call x2, Pallas kernels: 9.49 us -> 13.7 us  [place(): pl.pallas_call(functools.partial(place_kernel, 2 * lot), grid_spec=pltpu....]
    ppermute x6 -> x4, waiting for transfers between devices: 6.6 us -> 3.98 us  [the longest x2 3.97 us: spread(): far = lax.ppermute(jnp.concatenate([left, right], axis=0), 'visit', swap)]
  transfers between devices with their start and end apart: 14 -> 12, of which waited for: 4 -> 7; matrix products, arithmetic and copies ran while one was open for 5% -> 6% of each run, Pallas kernels for 13% -> 10%
where the time goes in v5:
time: 271 us; the launch traced here: 268 us
  waiting for transfers between devices  136 us (50%)
  Pallas kernels  59.9 us (22%)
  starting transfers between devices  54.1 us (20%)
  other arithmetic  12.3 us (5%)
  local copies, waits for them, and re-layouts  4.85 us (2%)
    all_to_all x2, waiting for transfers between devices, send(): lax.all_to_all(blocks, EVERY, split_axis=0, concat_axis=0, tiled=True)  73.5 us
    ppermute x4, waiting for transfers between devices, neighbours(): return (lax.ppermute(last, axis, up), lax.ppermute(first, axis, down))  58.2 us
    ppermute x4, starting transfers between devices, neighbours(): return (lax.ppermute(last, axis, up), lax.ppermute(first, axis, down))  32.4 us
    pallas_call x2, Pallas kernels, stage(): pl.pallas_call(functools.partial(stage_kernel, plan, lots), out_shape=(sh...  28.6 us
    pallas_call x2, Pallas kernels, warp(): pl.pallas_call(functools.partial(warp_kernel, tiles, share, noted), out_s...  17.7 us
    all_to_all x2, starting transfers between devices, send(): lax.all_to_all(blocks, EVERY, split_axis=0, concat_axis=0, tiled=True)  13.9 us
    pallas_call x2, Pallas kernels, place(): pl.pallas_call(functools.partial(place_kernel, 2 * lot), grid_spec=pltpu....  13.7 us
    convert_element_type x2, other arithmetic, bands(): coarse = blur.astype(jnp.bfloat16)  8.78 us
  transfers between devices with their start and end apart: 12, of which 7 were waited for; matrix products, arithmetic and copies ran while one was open for 6% of the time, Pallas kernels for 10%

profile of v5, /device:TPU:0, one launch (start us, length us, event | category | flops | bytes accessed | tf_op | source)
XLA Modules:
  0.0 268.1 jit_solution(14058375317646494682)
XLA Ops:
  0.6 8.9 %warp.2 = bf16[32,528,128]{2,1,0:T(8,128)(2,1)} custom-call(s32[24]{0:T(128)} %visit_ref.3, s32[24]{0:T(128)} %bitcast.16, s32[2,24]{1,0:T(2,128)} %bitcast.14, s32[8,256]{1,0:T(8,128)} %good_ref.3, bf16[8,256,256]{2,1,0:T(8,128)(2,1)} %rows_hbm.3, bf16[8,256,256]{2,1,0:T(8,128)(2,1)} %cols_hbm.3, bf16[24,256,256]{2,1,0:T(8,128)(2,1)} %var_hbm.2, ...), custom_call_target="tpu_custom_call" | custom-call | flops 3221225472 | bytes 12582912 | tf_op jit(solution)/shard_map/warp/pallas_call | solution.py:158
  9.6 7.4 %all-to-all-start = ((bf16[32,528,128]{2,1,0:T(8,128)(2,1)}), bf16[32,528,128]{2,1,0:T(8,128)(2,1)}, u32[]{:S(2)}, u32[]{:S(2)}) async-start(bf16[32,528,128]{2,1,0:T(8,128)(2,1)} %warp.2), calls=%async_computation | async-start | bytes 8650752 | tf_op jit(solution)/shard_map/all_to_all | solution.py:518
  17.0 0.7 fusion.26
  17.8 4.4 %fusion.19 = (bf16[48,64]{1,0:T(8,128)(2,1)S(1)}, bf16[48,64]{1,0:T(8,128)(2,1)S(1)}) fusion(f32[]{:T(128)} %bitcast.9, f32[]{:T(128)} %bitcast.8, f32[]{:T(128)} %bitcast.7, f32[]{:T(128)} %bitcast.6, f32[]{:T(128)} %bitcast.5, f32[]{:T(128)} %bitcast.4, f32[]{:T(128)} %bitcast.3, s32[48]{0:T(128)S(1)} %iota_add_fusion.1), kind=kLoop, calls=%fused_computation.38 | loop fusion | flops 79872 | bytes 12508 | tf_op jit(solution)/shard_map/convert_element_type | solution.py:315
  22.8 4.4 %fusion.18 = (bf16[80,96]{1,0:T(8,128)(2,1)S(1)}, bf16[80,96]{1,0:T(8,128)(2,1)S(1)}) fusion(f32[]{:T(128)} %bitcast.9, f32[]{:T(128)} %bitcast.8, f32[]{:T(128)} %bitcast.7, f32[]{:T(128)} %bitcast.6, f32[]{:T(128)} %bitcast.5, f32[]{:T(128)} %bitcast.4, f32[]{:T(128)} %bitcast.3, s32[80]{0:T(128)S(1)} %iota_add_fusion), kind=kLoop, calls=%fused_computation.34 | loop fusion | flops 199680 | bytes 31068 | tf_op jit(solution)/shard_map/convert_element_type | solution.py:315
  27.2 0.6 pad_maximum_fusion.1.refs_3_
  27.8 0.7 fusion.17.refs_4_
  28.5 0.7 fusion.8.refs_4_
  29.2 8.7 %warp.3 = bf16[32,512,128]{2,1,0:T(8,128)(2,1)} custom-call(s32[24]{0:T(128)} %visit_ref.3, s32[24]{0:T(128)} %bitcast.17, s32[2,24]{1,0:T(2,128)} %bitcast.15, s32[8,256]{1,0:T(8,128)} %good_ref.3, bf16[8,256,256]{2,1,0:T(8,128)(2,1)} %rows_hbm.3, bf16[8,256,256]{2,1,0:T(8,128)(2,1)} %cols_hbm.3, bf16[24,256,256]{2,1,0:T(8,128)(2,1)} %var_hbm.2, ...), custom_call_target="tpu_custom_call" | custom-call | flops 3221225472 | bytes 12582912 | tf_op jit(solution)/shard_map/warp/pallas_call | solution.py:158
  37.9 72.3 %all-to-all-done.blocks_ref = bf16[32,528,128]{2,1,0:T(8,128)(2,1)} async-done(((bf16[32,528,128]{2,1,0:T(8,128)(2,1)}), bf16[32,528,128]{2,1,0:T(8,128)(2,1)}, u32[]{:S(2)}, u32[]{:S(2)}) %all-to-all-start) | async-done | bytes 4325408 | tf_op jit(solution)/shard_map/all_to_all | solution.py:518
  110.3 6.5 %all-to-all-start.1 = ((bf16[32,512,128]{2,1,0:T(8,128)(2,1)}), bf16[32,512,128]{2,1,0:T(8,128)(2,1)}, u32[]{:S(2)}, u32[]{:S(2)}) async-start(bf16[32,512,128]{2,1,0:T(8,128)(2,1)} %warp.3), calls=%async_computation.1 | async-start | bytes 8388608 | tf_op jit(solution)/shard_map/all_to_all | solution.py:518
  116.8 1.0 slice.80
  117.9 6.5 %place.2 = (bf16[256,1024]{1,0:T(8,128)(2,1)S(1)}, f32[16,256]{1,0:T(8,128)S(1)}, f32[16,1024]{1,0:T(8,128)S(1)}) custom-call(s32[64]{0:T(128)S(1)} %convert_element_type.55.code_ref, bf16[32,528,128]{2,1,0:T(8,128)(2,1)} %all-to-all-done.blocks_ref), custom_call_target="tpu_custom_call" | custom-call | flops 2162688 | bytes 4325376 | tf_op jit(solution)/shard_map/place/pallas_call | solution.py:227
  124.5 4.0 %collective-permute-start.1 = (f32[8,256]{1,0:T(8,128)S(1)}, f32[8,256]{1,0:T(8,128)S(1)}, u32[]{:S(2)}, u32[]{:S(2)}) collective-permute-start(f32[8,256]{1,0:T(8,128)S(1)} %get-tuple-element.48), channel_id=1, source_target_pairs={{0,1},{1,2},{2,3},{4,5},{5,6},{6,7},{8,9},{9,10},{10,11},{12,13},{... | collective-permute-start | bytes 24584 | tf_op jit(solution)/shard_map/ppermute | solution.py:253
  128.5 1.3 collective-permute-start
  129.8 1.1 collective-permute-start.4
  130.9 56.9 %collective-permute-done.1.refs_6_ = f32[8,256]{1,0:T(8,128)S(1)} collective-permute-done((f32[8,256]{1,0:T(8,128)S(1)}, f32[8,256]{1,0:T(8,128)S(1)}, u32[]{:S(2)}, u32[]{:S(2)}) %collective-permute-start.1) | collective-permute-done | bytes 8224 | tf_op jit(solution)/shard_map/ppermute | solution.py:253
  187.8 1.3 collective-permute-start.5
  189.6 1.3 collective-permute-start.3
  190.9 0.7 collective-permute-start.2
  192.7 0.6 pad_maximum_fusion.refs_2_
  193.3 0.8 copy-done.2
  194.1 12.0 %stage.2 = (f32[1024,1024]{1,0:T(8,128)}, f32[1024,1024]{1,0:T(8,128)}) custom-call(s32[1]{0:T(128)} %bitcast.refs_0_, f32[7]{0:T(128)} %refs_1_.1, bf16[32,1152]{1,0:T(8,128)(2,1)} %pad_maximum_fusion.refs_2_, bf16[160,64]{1,0:T(8,128)(2,1)} %pad_maximum_fusion.2.refs_3_, bf16[48,64]{1,0:T(8,128)(2,1)} %fusion.17.refs_4_, bf16[256,1024]{1,0:T(8,128)(2,1)} %copy-done, ...), custom_call_target="tpu_custom_call" | custom-call | flops 53084160 | bytes 7962624 | tf_op jit(solution)/shard_map/stage/pallas_call | solution.py:441
  206.1 1.2 all-to-all-done.1.blocks_ref
  207.3 7.1 %place.3 = (bf16[256,1024]{1,0:T(8,128)(2,1)S(1)}, f32[16,256]{1,0:T(8,128)S(1)}, f32[16,1024]{1,0:T(8,128)}) custom-call(s32[64]{0:T(128)S(1)} %convert_element_type.55.code_ref, bf16[32,512,128]{2,1,0:T(8,128)(2,1)} %all-to-all-done.1.blocks_ref), custom_call_target="tpu_custom_call" | custom-call | flops 2097152 | bytes 4194304 | tf_op jit(solution)/shard_map/place/pallas_call | solution.py:227
  214.4 3.4 %collective-permute-start.8 = (bf16[256,1024]{1,0:T(8,128)(2,1)S(1)}, bf16[256,1024]{1,0:T(8,128)(2,1)S(1)}, u32[]{:S(2)}, u32[]{:S(2)}) collective-permute-start(bf16[256,1024]{1,0:T(8,128)(2,1)S(1)} %get-tuple-element.36.refs_11_), channel_id=1, source_target_pairs={{0,16},{16,0},{1,17},{17,1},{2,18},{18,2},{3,19},{19,3},{4,20},{20... | collective-permute-start | bytes 1572872 | tf_op jit(solution)/shard_map/ppermute | solution.py:261
  217.8 1.3 collective-permute-start.7
  219.1 25.9 %collective-permute-start.6 = (f32[8,256]{1,0:T(8,128)S(1)}, f32[8,256]{1,0:T(8,128)S(1)}, u32[]{:S(2)}, u32[]{:S(2)}) collective-permute-start(f32[8,256]{1,0:T(8,128)S(1)} %get-tuple-element.45), channel_id=1, source_target_pairs={{0,1},{1,2},{2,3},{4,5},{5,6},{6,7},{8,9},{9,10},{10,11},{12,13},{... | collective-permute-start | bytes 24584 | tf_op jit(solution)/shard_map/ppermute | solution.py:253
  245.0 1.3 collective-permute-done.6.refs_12_
  246.3 3.9 %collective-permute-done.9 = f32[16,256]{1,0:T(8,128)S(1)} collective-permute-done((f32[16,256]{1,0:T(8,128)S(1)}, f32[16,256]{1,0:T(8,128)S(1)}, u32[]{:S(2)}, u32[]{:S(2)}) %collective-permute-start.9) | collective-permute-done | bytes 16416 | tf_op jit(solution)/shard_map/ppermute | solution.py:263
  250.8 0.8 copy-done.3
  251.6 16.6 %stage.3 = (f32[1024,1024]{1,0:T(8,128)}, f32[1024,1024]{1,0:T(8,128)}) custom-call(s32[1]{0:T(128)} %bitcast.refs_0_, f32[7]{0:T(128)} %refs_1_.1, bf16[32,1152]{1,0:T(8,128)(2,1)} %pad_maximum_fusion.refs_2_, bf16[256,96]{1,0:T(8,128)(2,1)} %pad_maximum_fusion.1.refs_3_, ...), custom_call_target="tpu_custom_call", output_to_operand_aliasing={{0}: (17, {}), {1}: (18, {})} | custom-call | flops 70778880 | bytes 10616832 | tf_op jit(solution)/shard_map/stage/pallas_call | solution.py:441
  (46 shorter events, 3.0 us)
Async XLA Ops:
  9.6 7.5 %copy-start.6 = (f32[7]{0:T(128)S(1)}, f32[7]{0:T(128)}, u32[]{:S(2)}) copy-start(f32[7]{0:T(128)} %refs_1_.1) | copy-start | bytes 88
  9.6 100.7 %all-to-all-start = ((bf16[32,528,128]{2,1,0:T(8,128)(2,1)}), bf16[32,528,128]{2,1,0:T(8,128)(2,1)}, u32[]{:S(2)}, u32[]{:S(2)}) async-start(bf16[32,528,128]{2,1,0:T(8,128)(2,1)} %warp.2), calls=%async_computation | async-start | bytes 8650752 | tf_op jit(solution)/shard_map/all_to_all | solution.py:518
  110.3 97.0 %all-to-all-start.1 = ((bf16[32,512,128]{2,1,0:T(8,128)(2,1)}), bf16[32,512,128]{2,1,0:T(8,128)(2,1)}, u32[]{:S(2)}, u32[]{:S(2)}) async-start(bf16[32,512,128]{2,1,0:T(8,128)(2,1)} %warp.3), calls=%async_computation.1 | async-start | bytes 8388608 | tf_op jit(solution)/shard_map/all_to_all | solution.py:518
  124.5 68.8 %copy-start = (bf16[256,1024]{1,0:T(8,128)(2,1)}, bf16[256,1024]{1,0:T(8,128)(2,1)S(1)}, u32[]{:S(2)}) copy-start(bf16[256,1024]{1,0:T(8,128)(2,1)S(1)} %get-tuple-element.29.refs_5_) | copy-start | bytes 1572868
  124.5 63.3 %collective-permute-start.1 = (f32[8,256]{1,0:T(8,128)S(1)}, f32[8,256]{1,0:T(8,128)S(1)}, u32[]{:S(2)}, u32[]{:S(2)}) collective-permute-start(f32[8,256]{1,0:T(8,128)S(1)} %get-tuple-element.48), channel_id=1, source_target_pairs={{0,1},{1,2},{2,3},{4,5},{5,6},{6,7},{8,9},{9,10},{10,11},{12,13},{... | collective-permute-start | bytes 24584 | tf_op jit(solution)/shard_map/ppermute | solution.py:253
  128.5 59.3 %collective-permute-start = (f32[8,256]{1,0:T(8,128)S(1)}, f32[8,256]{1,0:T(8,128)S(1)}, u32[]{:S(2)}, u32[]{:S(2)}) collective-permute-start(f32[8,256]{1,0:T(8,128)S(1)} %get-tuple-element.49), channel_id=1, source_target_pairs={{1,0},{2,1},{3,2},{5,4},{6,5},{7,6},{9,8},{10,9},{11,10},{13,12},{... | collective-permute-start | bytes 24584 | tf_op jit(solution)/shard_map/ppermute | solution.py:253
  129.8 63.5 %collective-permute-start.4 = (bf16[256,1024]{1,0:T(8,128)(2,1)S(1)}, bf16[256,1024]{1,0:T(8,128)(2,1)S(1)}, u32[]{:S(2)}, u32[]{:S(2)}) collective-permute-start(bf16[256,1024]{1,0:T(8,128)(2,1)S(1)} %get-tuple-element.29.refs_5_), channel_id=1, source_target_pairs={{0,16},{16,0},{1,17},{17,1},{2,18},{18,2},{3,19},{19,3},{4,20},{20... | collective-permute-start | bytes 1572872 | tf_op jit(solution)/shard_map/ppermute | solution.py:261
  187.8 5.5 %copy-start.4 = (f32[8,256]{1,0:T(8,128)}, f32[8,256]{1,0:T(8,128)S(1)}, u32[]{:S(2)}) copy-start(f32[8,256]{1,0:T(8,128)S(1)} %collective-permute-done.1.refs_6_) | copy-start | bytes 24580
  187.8 5.5 %copy-start.5 = (f32[8,256]{1,0:T(8,128)}, f32[8,256]{1,0:T(8,128)S(1)}, u32[]{:S(2)}) copy-start(f32[8,256]{1,0:T(8,128)S(1)} %collective-permute-done.refs_7_) | copy-start | bytes 24580
  187.8 3.8 %collective-permute-start.5 = (f32[16,256]{1,0:T(8,128)S(1)}, f32[16,256]{1,0:T(8,128)S(1)}, u32[]{:S(2)}, u32[]{:S(2)}) collective-permute-start(f32[16,256]{1,0:T(8,128)S(1)} %pad_maximum_fusion.3), channel_id=1, source_target_pairs={{0,16},{16,0},{1,17},{17,1},{2,18},{18,2},{3,19},{19,3},{4,20},{20... | collective-permute-start | bytes 49160 | tf_op jit(solution)/shard_map/ppermute | solution.py:263
  189.6 3.1 %collective-permute-start.3 = (bf16[8,1152]{1,0:T(8,128)(2,1)S(1)}, bf16[8,1152]{1,0:T(8,128)(2,1)S(1)}, u32[]{:S(2)}, u32[]{:S(2)}) collective-permute-start(bf16[8,1152]{1,0:T(8,128)(2,1)S(1)} %concatenate.21), channel_id=1, source_target_pairs={{4,0},{8,4},{12,8},{16,20},{20,24},{24,28},{5,1},{9,5},{13,9},{17,... | collective-permute-start | bytes 55304 | tf_op jit(solution)/shard_map/ppermute | solution.py:299
  190.9 1.8 collective-permute-start.2
  193.3 0.8 copy-start.2
  214.4 36.4 %copy-start.1 = (bf16[256,1024]{1,0:T(8,128)(2,1)}, bf16[256,1024]{1,0:T(8,128)(2,1)S(1)}, u32[]{:S(2)}) copy-start(bf16[256,1024]{1,0:T(8,128)(2,1)S(1)} %get-tuple-element.36.refs_11_) | copy-start | bytes 1572868
  214.4 36.3 %collective-permute-start.8 = (bf16[256,1024]{1,0:T(8,128)(2,1)S(1)}, bf16[256,1024]{1,0:T(8,128)(2,1)S(1)}, u32[]{:S(2)}, u32[]{:S(2)}) collective-permute-start(bf16[256,1024]{1,0:T(8,128)(2,1)S(1)} %get-tuple-element.36.refs_11_), channel_id=1, source_target_pairs={{0,16},{16,0},{1,17},{17,1},{2,18},{18,2},{3,19},{19,3},{4,20},{20... | collective-permute-start | bytes 1572872 | tf_op jit(solution)/shard_map/ppermute | solution.py:261
  217.8 27.2 %collective-permute-start.7 = (f32[8,256]{1,0:T(8,128)S(1)}, f32[8,256]{1,0:T(8,128)S(1)}, u32[]{:S(2)}, u32[]{:S(2)}) collective-permute-start(f32[8,256]{1,0:T(8,128)S(1)} %get-tuple-element.44), channel_id=1, source_target_pairs={{1,0},{2,1},{3,2},{5,4},{6,5},{7,6},{9,8},{10,9},{11,10},{13,12},{... | collective-permute-start | bytes 24584 | tf_op jit(solution)/shard_map/ppermute | solution.py:253
  219.1 27.2 %collective-permute-start.6 = (f32[8,256]{1,0:T(8,128)S(1)}, f32[8,256]{1,0:T(8,128)S(1)}, u32[]{:S(2)}, u32[]{:S(2)}) collective-permute-start(f32[8,256]{1,0:T(8,128)S(1)} %get-tuple-element.45), channel_id=1, source_target_pairs={{0,1},{1,2},{2,3},{4,5},{5,6},{6,7},{8,9},{9,10},{10,11},{12,13},{... | collective-permute-start | bytes 24584 | tf_op jit(solution)/shard_map/ppermute | solution.py:253
  244.9 5.8 %copy-start.7 = (f32[8,256]{1,0:T(8,128)}, f32[8,256]{1,0:T(8,128)S(1)}, u32[]{:S(2)}) copy-start(f32[8,256]{1,0:T(8,128)S(1)} %collective-permute-done.7.refs_13_) | copy-start | bytes 24580
  246.3 4.5 %copy-start.8 = (f32[8,256]{1,0:T(8,128)}, f32[8,256]{1,0:T(8,128)S(1)}, u32[]{:S(2)}) copy-start(f32[8,256]{1,0:T(8,128)S(1)} %collective-permute-done.6.refs_12_) | copy-start | bytes 24580
  246.3 3.9 %collective-permute-start.9 = (f32[16,256]{1,0:T(8,128)S(1)}, f32[16,256]{1,0:T(8,128)S(1)}, u32[]{:S(2)}, u32[]{:S(2)}) collective-permute-start(f32[16,256]{1,0:T(8,128)S(1)} %pad_maximum_fusion.4), channel_id=1, source_target_pairs={{0,16},{16,0},{1,17},{17,1},{2,18},{18,2},{3,19},{19,3},{4,20},{20... | collective-permute-start | bytes 49160 | tf_op jit(solution)/shard_map/ppermute | solution.py:263
  250.8 0.8 copy-start.3

commit v6 on v4

--- a/solution.py
+++ b/solution.py
@@ -253,47 +253,34 @@
     return lax.ppermute(last, axis, up), lax.ppermute(first, axis, down)
 
 
-def spread(coadd, strip):
-    visits = lax.axis_size("visit")
+def swapped(array):
+    return lax.ppermute(array, "visit", [(0, 1), (1, 0)])
+
+
+def beyond(strips, above, below):
+    first = [strip[:HALO] for strip in strips] + [rows[:, :SIDE] for rows in (above, below)]
+    last = [strip[HALO:] for strip in strips] + [rows[:, TX - SIDE :] for rows in (above, below)]
+    return neighbours(jnp.concatenate(first, axis=1), jnp.concatenate(last, axis=1), "px")
+
+
+def straight_to_both(strip):
     first, last = strip[:HALO], strip[HALO:]
-    if visits == 2:
-        other = lax.ppermute(coadd, "visit", [(0, 1), (1, 0)])
-        count = lax.axis_size("px")
-        up, down = beside("px")
-
-        def crossed(pairs):
-            return [(v * count + i, (1 - v) * count + j) for v in range(2) for i, j in pairs]
-
-        left, right = neighbours(first, last, "px")
-        other_left = lax.ppermute(last, ("visit", "px"), crossed(up))
-        other_right = lax.ppermute(first, ("visit", "px"), crossed(down))
-        return [(coadd, left, right), (other, other_left, other_right)]
-    one = (coadd, *neighbours(first, last, "px"))
-    if visits == 1:
-        return [one]
-    every = [lax.all_gather(part, "visit") for part in one]
-    return [tuple(part[visit] for part in every) for visit in range(visits)]
-
-
-def widened(rows, left, right):
-    gap = jnp.zeros((HALO, SIDE - 2 * HALO), jnp.float32)
-    return jnp.concatenate([rows, right.T, gap, left.T], axis=1)
-
-
-def rows_between(edge, parts):
-    visits = len(parts)
-    height = parts[0][1].shape[1]
-    none = jnp.zeros((EDGE - HALO, WIDE), jnp.float32)
-    if visits != 2:
-        last = widened(edge[0][HALO:], *[side[:, height - HALO :] for side in parts[-1][1:]])
-        first = widened(edge[1][:HALO], *[side[:, :HALO] for side in parts[0][1:]])
-        above, below = neighbours(first, last, "py")
-        return jnp.concatenate([none, above, below, none], axis=0).astype(jnp.bfloat16)
+    count = lax.axis_size("px")
+    up, down = beside("px")
+
+    def crossed(pairs):
+        return [(v * count + i, (1 - v) * count + j) for v in range(2) for i, j in pairs]
+
+    own = neighbours(first, last, "px")
+    return own, (
+        lax.ppermute(last, ("visit", "px"), crossed(up)),
+        lax.ppermute(first, ("visit", "px"), crossed(down)),
+    )
+
+
+def rows_between(edge):
     lower = lax.axis_index("visit") == 0
-    mine = widened(
-        jnp.where(lower, edge[:HALO], edge[HALO:]),
-        *[jnp.where(lower, side[:, :HALO], side[:, height - HALO :]) for side in parts[0][1:]],
-    )
+    mine = jnp.where(lower, edge[:HALO], edge[HALO:])
     count = lax.axis_size("py")
     up, down = beside("py")
 
@@ -304,30 +291,70 @@
 
     straight = lax.ppermute(mine, ("visit", "py"), pairs(0))
     crossed = lax.ppermute(mine, ("visit", "py"), pairs(1))
-    above, below = jnp.where(lower, crossed, straight), jnp.where(lower, straight, crossed)
-    return jnp.concatenate([none, above, below, none], axis=0).astype(jnp.bfloat16)
+    return jnp.where(lower, crossed, straight), jnp.where(lower, straight, crossed)
 
 
 def bands(plan, taps):
-    fields = plan[0]
-    tall, margin = fields["tall"], fields["margin"]
+    tall, margin = plan[0]["tall"], plan[0]["margin"]
     row = jnp.arange(tall, dtype=jnp.int32)
     out = jnp.arange(tall - 2 * margin, dtype=jnp.int32) + margin
     three = (jnp.abs(row[:, None] - row[None, :]) <= 1).astype(jnp.bfloat16)
     nine = (jnp.abs(out[:, None] - row[None, :]) <= 4).astype(jnp.bfloat16)
     count = taps.shape[0]
     ahead = row[None, :] - out[:, None] + count // 2
-    blur = sum(jnp.where(ahead == tap, taps[tap], 0.0) for tap in range(count))
-    coarse = blur.astype(jnp.bfloat16)
-    fine = (blur - coarse.astype(jnp.float32)).astype(jnp.bfloat16)
-    return jnp.concatenate([three, coarse, fine], axis=0), nine
+    coarse, fine = split(sum(jnp.where(ahead == tap, taps[tap], 0.0) for tap in range(count)))
+    lane = jnp.arange(4 * SIDE, dtype=jnp.int32)
+    across = jnp.abs(lane[:, None] - lane[None, SIDE : 3 * SIDE]) <= 4
+    return (
+        jnp.concatenate([three] * 2, axis=1),
+        jnp.concatenate([nine] * 2, axis=1),
+        jnp.concatenate([coarse, coarse, fine], axis=1),
+        across.astype(jnp.bfloat16),
+    )
+
+
+def split(value):
+    coarse = value.astype(jnp.bfloat16)
+    return coarse, (value - coarse.astype(jnp.float32)).astype(jnp.bfloat16)
+
+
+def filtered(value, taps, tables, margin):
+    three, nine, blur, across = [table[...] for table in tables]
+    tall = value.shape[0]
+    short = tall - 2 * margin
+
+    def product(matrix, terms):
+        return jnp.dot(matrix, jnp.concatenate(terms, axis=0), preferred_element_type=jnp.float32)
+
+    moved = {
+        by: (pltpu.roll(value, -by % WIDE, 1) if by else value).astype(jnp.float32)
+        for by in range(-3, 4)
+    }
+    rowwise = sum(taps[tap] * moved[tap - 3] for tap in range(7))[:, :TX]
+    resid = moved[0] - product(three, split(moved[-1] + moved[0] + moved[1])) * (1.0 / 9.0)
+    tower = jnp.concatenate(split(product(nine, split(resid * resid))), axis=0)
+    windows = [jnp.concatenate([tower[:, TX:], tower[:, : 3 * SIDE]], axis=1)]
+    for start in range(2 * SIDE, TX, 2 * SIDE):
+        windows.append(tower[:, start - SIDE : start + 3 * SIDE])
+    boxes = jnp.dot(jnp.concatenate(windows, axis=0), across, preferred_element_type=jnp.float32)
+    box = jnp.concatenate(
+        [
+            boxes[2 * at * short : (2 * at + 1) * short] + boxes[(2 * at + 1) * short : (2 * at + 2) * short]
+            for at in range(len(windows))
+        ],
+        axis=1,
+    )
+    local = box * (1.0 / 81.0) + 1e-05
+    coarse, fine = split(rowwise)
+    return product(blur, (coarse, fine, coarse)) * lax.rsqrt(local), local
 
 
 def stage_kernel(plan, lots, *refs):
-    mine_ref, taps_ref, between_ref, sums_ref, nine_ref = refs[:5]
+    mine_ref, taps_ref, above_ref, below_ref = refs[:4]
+    tables = refs[4:8]
     fields, copies, outs = plan
     visits, margin = fields["visits"], fields["margin"]
-    at = 5
+    at = 8
     chunks = []
     for lot in lots:
         parts = []
@@ -340,19 +367,21 @@
     field, detection, variance, sems = refs[at + 2 : at + 6]
     sides = refs[at + 6 :]
     spans, tall, _ = field.shape
-    short = tall - 2 * margin
 
     which = 0
     held = []
     for parts in chunks:
         group = []
-        for cells, left, right in parts:
+        for number, (cells, left, right) in enumerate(parts):
             side = sides[which]
             which += 1
             height = cells.shape[0]
-            side[...] = jnp.concatenate(
-                [right[...], jnp.zeros((SIDE - 2 * HALO, height), jnp.float32), left[...]], axis=0
-            ).T.astype(jnp.bfloat16)
+            first = number * height if left.shape[1] > height else 0
+            here = slice(first, first + height)
+            gap = jnp.zeros((SIDE - 2 * HALO, height), jnp.float32)
+            side[...] = jnp.concatenate([right[:, here], gap, left[:, here]], axis=0).T.astype(
+                jnp.bfloat16
+            )
             group.append((cells, side))
         held.append(group)
 
@@ -380,18 +409,23 @@
 
     else:
         assemble(tuple(range(visits)))
+
     if fields["between"]:
-        above_at, below_at = fields["between"]
-        field[0, above_at : above_at + EDGE, :] = between_ref[:EDGE, :]
-        field[spans - 1, below_at : below_at + EDGE, :] = between_ref[EDGE:, :]
+        _, left, right = chunks[0][0]
+        corners = left.shape[1] - 2 * SIDE
+        from_left = lax.broadcasted_iota(jnp.int32, (HALO, SIDE), 1) >= SIDE // 2
+        none = jnp.zeros((EDGE - HALO, WIDE), jnp.float32)
+        for number, (span, first, rows) in enumerate(
+            zip((0, spans - 1), fields["between"], (above_ref, below_ref))
+        ):
+            here = slice(corners + number * SIDE, corners + (number + 1) * SIDE)
+            wide = jnp.concatenate(
+                [rows[...], jnp.where(from_left, left[:, here], right[:, here])], axis=1
+            )
+            strip = [none, wide] if number == 0 else [wide, none]
+            field[span, first : first + EDGE, :] = jnp.concatenate(strip, axis=0).astype(jnp.bfloat16)
 
     taps = [taps_ref[tap] for tap in range(7)]
-
-    def across(value, by):
-        return value if by == 0 else pltpu.roll(value, by % WIDE, 1)
-
-    def three(value, by):
-        return value + across(value, by) + across(value, -by)
 
     def stores(unit, source, rows, target):
         return [
@@ -403,29 +437,22 @@
             )
         ]
 
-    @pl.loop(0, spans)
-    def _(unit):
-        value = field[unit]
-        sums = jnp.dot(sums_ref[...], value, preferred_element_type=jnp.float32)
-        resid = value.astype(jnp.float32) - three(sums[:tall], 1) * (1.0 / 9.0)
-        square = resid * resid
-        coarse = square.astype(jnp.bfloat16)
-        fine = (square - coarse.astype(jnp.float32)).astype(jnp.bfloat16)
-        tower = jnp.dot(nine_ref[...], coarse, preferred_element_type=jnp.float32) + jnp.dot(
-            nine_ref[...], fine, preferred_element_type=jnp.float32
-        )
-        local = three(three(tower, 1), 3)[:, :TX] * (1.0 / 81.0) + 1e-05
-        rowwise = sums[tall : tall + short] + sums[tall + short :]
-        blurred = sum(taps[tap] * across(rowwise, 3 - tap) for tap in range(7))
-        variance[unit] = local
-        detection[unit] = blurred[:, :TX] * lax.rsqrt(local)
-        for begin, end, source, rows, shift in outs:
-
-            @pl.when((unit >= begin) & (unit < end))
-            def _():
-                target = pl.multiple_of(unit * STEP + shift, HALO)
-                for store in stores(unit, source, rows, target):
-                    store.start()
+    some = next(count for count in (4, 3, 2, 1) if spans % count == 0 and count * tall <= 320)
+
+    @pl.loop(0, spans, step=some)
+    def _(first):
+        for ahead in range(some):
+            unit = first + ahead
+            detection[unit], variance[unit] = filtered(field[unit], taps, tables, margin)
+        for ahead in range(some):
+            unit = first + ahead
+            for begin, end, source, rows, shift in outs:
+
+                @pl.when((unit >= begin) & (unit < end))
+                def _():
+                    target = pl.multiple_of(unit * STEP + shift, HALO)
+                    for store in stores(unit, source, rows, target):
+                        store.start()
 
     @pl.loop(0, spans)
     def _(unit):
@@ -442,12 +469,12 @@
     spans, tall = fields["spans"], fields["tall"]
     shape = jax.ShapeDtypeStruct((TY, TX), jnp.float32)
     flat = [array for parts in chunks for part in parts for array in part]
-    first = 5 + len(flat)
+    first = 8 + len(flat)
     out = pltpu.VMEM((spans, tall - 2 * fields["margin"], TX), jnp.float32)
     return pl.pallas_call(
         functools.partial(stage_kernel, plan, lots),
         out_shape=(shape, shape),
-        in_specs=[SMEM, SMEM, VMEM, VMEM, VMEM] + [VMEM] * len(flat) + [HBM] * len(held),
+        in_specs=[SMEM, SMEM] + [VMEM] * (6 + len(flat)) + [HBM] * len(held),
         out_specs=(HBM, HBM),
         input_output_aliases={first + at: at for at in range(len(held))},
         scratch_shapes=[
@@ -462,7 +489,7 @@
             flops=80 * spans * tall * WIDE, bytes_accessed=12 * spans * tall * WIDE, transcendentals=0
         ),
         name="stage",
-    )(mine, taps, between, *tables, *flat, *held)
+    )(mine, taps, *between, *tables, *flat, *held)
 
 
 def outer_plan(lot):
@@ -526,16 +553,12 @@
     made, psf_taps = lax.optimization_barrier((make(0, inv_var), psf_taps))
     arrived = send(made)
     if len(plan) == 1:
-        code = codes(arrived)
-        coadd, strip, edge = place(code, arrived, lots[0])
-        parts = spread(coadd, strip)
-        if visits > 1:
-            edges = lax.all_gather(edge, "visit")
-            edge = (edges[visits - 1], edges[0])
-        else:
-            edge = (edge, edge)
-        between = rows_between(edge, parts)
         every = whole_plan(lots[0], visits)
+        coadd, strip, edge = place(codes(arrived), arrived, lots[0])
+        all_of = [lax.all_gather(part, "visit") for part in (coadd, strip, edge)]
+        between = neighbours(all_of[2][0, :HALO], all_of[2][visits - 1, HALO:], "py")
+        sides = beyond([all_of[1][visit] for visit in range(visits)], *between)
+        parts = [(all_of[0][visit], *sides) for visit in range(visits)]
         return stage(every, mine, psf_taps, between, bands(every, psf_taps), [parts], lots)
 
     outer, inner = outer_plan(lots[0]), inner_plan(*lots)
@@ -546,10 +569,13 @@
     second = send(later)
     code = codes(arrived)
     coadd, strip, edge = place(code, arrived, lots[0])
-    parts = spread(coadd, strip)
-    between = rows_between(edge, parts)
+    other = swapped(coadd)
+    between = rows_between(edge)
+    sides = beyond([strip, swapped(strip)], *between)
+    parts = [(coadd, *sides), (other, *sides)]
     coadd, strip, _ = place(code, second, lots[1])
-    more = spread(coadd, strip)
+    own_sides, other_sides = straight_to_both(strip)
+    more = [(coadd, *own_sides), (swapped(coadd), *other_sides)]
     (parts, between), _ = lax.optimization_barrier(((parts, between), coadd))
     held = stage(outer, mine, psf_taps, between, tables[0], [parts], lots[:1])
     return stage(inner, mine, psf_taps, between, tables[1], [parts, more], lots, held)

time: 279 us -> 251 us (0.90)
  starting transfers between devices: 60.3 us -> 41.7 us
  Pallas kernels: 56.7 us -> 47.5 us
    all_to_all x2, waiting for transfers between devices: 116 us -> 140 us  [send(): lax.all_to_all(blocks, EVERY, split_axis=0, concat_axis=0, tiled=True)]
    ppermute x4, waiting for transfers between devices: 20.8 us -> 2.75 us  [neighbours(): return (lax.ppermute(last, axis, up), lax.ppermute(first, axis, down))]
    ppermute x6 -> x5, starting transfers between devices: 31.5 us -> 13.5 us  [the longest x3 7.36 us: swapped(): return lax.ppermute(array, 'visit', [(0, 1), (1, 0)])]
    pallas_call x2, Pallas kernels: 29.4 us -> 18.9 us  [stage(): pl.pallas_call(functools.partial(stage_kernel, plan, lots), out_shape=(sh...]
    ppermute x6 -> x5, waiting for transfers between devices: 6.6 us -> 0.01 us  [the longest x3 0.01 us: swapped(): return lax.ppermute(array, 'visit', [(0, 1), (1, 0)])]
    convert_element_type x6 -> x3, other arithmetic: 10.5 us -> 9.93 us  [the longest x2 9.08 us: split(): coarse = value.astype(jnp.bfloat16)]
  transfers between devices with their start and end apart: 14 -> 13, of which waited for: 4 -> 3; matrix products, arithmetic and copies ran while one was open for 5% -> 6% of each run, Pallas kernels for 13% -> 12%
where the time goes in v6:
time: 251 us; the launch traced here: 250 us
  waiting for transfers between devices  143 us (57%)
  Pallas kernels  47.5 us (19%)
  starting transfers between devices  41.7 us (17%)
  other arithmetic  14.4 us (6%)
    all_to_all x2, waiting for transfers between devices, send(): lax.all_to_all(blocks, EVERY, split_axis=0, concat_axis=0, tiled=True)  140 us
    pallas_call x2, Pallas kernels, stage(): pl.pallas_call(functools.partial(stage_kernel, plan, lots), out_shape=(sh...  18.9 us
    pallas_call x2, Pallas kernels, warp(): pl.pallas_call(functools.partial(warp_kernel, tiles, share, noted), out_s...  17.8 us
    all_to_all x2, starting transfers between devices, send(): lax.all_to_all(blocks, EVERY, split_axis=0, concat_axis=0, tiled=True)  16.3 us
    pallas_call x2, Pallas kernels, place(): pl.pallas_call(functools.partial(place_kernel, 2 * lot), grid_spec=pltpu....  10.7 us
    ppermute x4, starting transfers between devices, neighbours(): return (lax.ppermute(last, axis, up), lax.ppermute(first, axis, down))  9.87 us
    convert_element_type x2, other arithmetic, split(): coarse = value.astype(jnp.bfloat16)  9.08 us
    ppermute x3, starting transfers between devices, swapped(): return lax.ppermute(array, 'visit', [(0, 1), (1, 0)])  7.36 us
  transfers between devices with their start and end apart: 13, of which 3 were waited for; matrix products, arithmetic and copies ran while one was open for 6% of the time, Pallas kernels for 12%

profile of v6, /device:TPU:0, one launch (start us, length us, event | category | flops | bytes accessed | tf_op | source)
XLA Modules:
  0.0 250.0 jit_solution(7313892363251671581)
XLA Ops:
  0.6 9.3 %warp.2 = bf16[32,784,128]{2,1,0:T(8,128)(2,1)} custom-call(s32[24]{0:T(128)} %visit_ref.3, s32[24]{0:T(128)} %bitcast.12, s32[2,24]{1,0:T(2,128)} %bitcast.10, s32[8,256]{1,0:T(8,128)} %good_ref.3, bf16[8,256,256]{2,1,0:T(8,128)(2,1)} %rows_hbm.3, bf16[8,256,256]{2,1,0:T(8,128)(2,1)} %cols_hbm.3, bf16[24,256,256]{2,1,0:T(8,128)(2,1)} %var_hbm.2, ...), custom_call_target="tpu_custom_call" | custom-call | flops 3221225472 | bytes 12582912 | tf_op jit(solution)/shard_map/warp/pallas_call | solution.py:158
  10.0 7.4 %all-to-all-start = ((bf16[32,784,128]{2,1,0:T(8,128)(2,1)}), bf16[32,784,128]{2,1,0:T(8,128)(2,1)}, u32[]{:S(2)}, u32[]{:S(2)}) async-start(bf16[32,784,128]{2,1,0:T(8,128)(2,1)} %warp.2), calls=%async_computation | async-start | bytes 12845056 | tf_op jit(solution)/shard_map/all_to_all | solution.py:551
  17.6 0.7 add_convert_fusion.3.refs_5_
  18.3 0.7 fusion.22
  19.0 0.7 add_convert_fusion.2.refs_4_
  19.6 4.5 %fusion.16 = (bf16[48,64]{1,0:T(8,128)(2,1)S(1)}, bf16[48,64]{1,0:T(8,128)(2,1)S(1)}) fusion(f32[]{:T(128)} %bitcast.9, f32[]{:T(128)} %bitcast.8, f32[]{:T(128)} %bitcast.7, f32[]{:T(128)} %bitcast.6, f32[]{:T(128)} %bitcast.5, f32[]{:T(128)} %bitcast.4, f32[]{:T(128)} %bitcast.3, s32[48]{0:T(128)S(1)} %iota_add_fusion), kind=kLoop, calls=%fused_computation.39 | loop fusion | flops 79872 | bytes 12508 | tf_op jit(solution)/shard_map/convert_element_type | solution.py:317
  24.2 0.7 pad_maximum_fusion.3.refs_6_
  24.9 0.7 add_convert_fusion.1.refs_5_
  25.6 0.7 add_convert_fusion.refs_4_
  26.4 4.5 %fusion.15 = (bf16[80,96]{1,0:T(8,128)(2,1)S(1)}, bf16[80,96]{1,0:T(8,128)(2,1)S(1)}) fusion(f32[]{:T(128)} %bitcast.9, f32[]{:T(128)} %bitcast.8, f32[]{:T(128)} %bitcast.7, f32[]{:T(128)} %bitcast.6, f32[]{:T(128)} %bitcast.5, f32[]{:T(128)} %bitcast.4, f32[]{:T(128)} %bitcast.3, s32[80]{0:T(128)S(1)} %iota_add_fusion.1), kind=kLoop, calls=%fused_computation.35 | loop fusion | flops 199680 | bytes 31068 | tf_op jit(solution)/shard_map/convert_element_type | solution.py:317
  30.9 0.7 pad_maximum_fusion.refs_6_
  31.6 0.8 fusion.refs_7_
  32.5 8.5 %warp.3 = bf16[32,256,128]{2,1,0:T(8,128)(2,1)} custom-call(s32[24]{0:T(128)} %visit_ref.3, s32[24]{0:T(128)} %bitcast.13, s32[2,24]{1,0:T(2,128)} %bitcast.11, s32[8,256]{1,0:T(8,128)} %good_ref.3, bf16[8,256,256]{2,1,0:T(8,128)(2,1)} %rows_hbm.3, bf16[8,256,256]{2,1,0:T(8,128)(2,1)} %cols_hbm.3, bf16[24,256,256]{2,1,0:T(8,128)(2,1)} %var_hbm.2, ...), custom_call_target="tpu_custom_call" | custom-call | flops 3221225472 | bytes 12582912 | tf_op jit(solution)/shard_map/warp/pallas_call | solution.py:158
  40.9 113.5 %all-to-all-done.blocks_ref = bf16[32,784,128]{2,1,0:T(8,128)(2,1)} async-done(((bf16[32,784,128]{2,1,0:T(8,128)(2,1)}), bf16[32,784,128]{2,1,0:T(8,128)(2,1)}, u32[]{:S(2)}, u32[]{:S(2)}) %all-to-all-start) | async-done | bytes 6422560 | tf_op jit(solution)/shard_map/all_to_all | solution.py:551
  154.5 8.9 %all-to-all-start.1 = ((bf16[32,256,128]{2,1,0:T(8,128)(2,1)}), bf16[32,256,128]{2,1,0:T(8,128)(2,1)S(1)}, u32[]{:S(2)}, u32[]{:S(2)}) async-start(bf16[32,256,128]{2,1,0:T(8,128)(2,1)} %warp.3), calls=%async_computation.1 | async-start | bytes 4194304 | tf_op jit(solution)/shard_map/all_to_all | solution.py:551
  163.4 1.0 slice.81
  164.6 7.7 %place.2 = (bf16[384,1024]{1,0:T(8,128)(2,1)S(1)}, f32[16,384]{1,0:T(8,128)S(1)}, f32[16,1024]{1,0:T(8,128)S(1)}) custom-call(s32[64]{0:T(128)S(1)} %convert_element_type.49.code_ref, bf16[32,784,128]{2,1,0:T(8,128)(2,1)} %all-to-all-done.blocks_ref), custom_call_target="tpu_custom_call" | custom-call | flops 3211264 | bytes 6422528 | tf_op jit(solution)/shard_map/place/pallas_call | solution.py:227
  172.2 1.8 collective-permute-start
  174.1 1.3 collective-permute-start.2
  176.1 4.1 %collective-permute-start.5 = (bf16[384,1024]{1,0:T(8,128)(2,1)S(1)}, bf16[384,1024]{1,0:T(8,128)(2,1)}, u32[]{:S(2)}, u32[]{:S(2)}) collective-permute-start(bf16[384,1024]{1,0:T(8,128)(2,1)S(1)} %get-tuple-element.45.refs_8_), channel_id=1, source_target_pairs={{0,16},{16,0},{1,17},{17,1},{2,18},{18,2},{3,19},{19,3},{4,20},{20... | collective-permute-start | bytes 2359304 | tf_op jit(solution)/shard_map/ppermute | solution.py:257
  180.2 3.4 %collective-permute-start.3 = (f32[8,1024]{1,0:T(8,128)S(1)}, f32[8,1024]{1,0:T(8,128)S(1)}, u32[]{:S(2)}, u32[]{:S(2)}) collective-permute-start(f32[8,1024]{1,0:T(8,128)S(1)} %pad_maximum_fusion.1), channel_id=1, source_target_pairs={{0,1},{1,2},{2,3},{4,5},{5,6},{6,7},{8,9},{9,10},{10,11},{12,13},{... | collective-permute-start | bytes 98312 | tf_op jit(solution)/shard_map/ppermute | solution.py:253
  183.6 26.6 %all-to-all-done.1.blocks_ref = bf16[32,256,128]{2,1,0:T(8,128)(2,1)S(1)} async-done(((bf16[32,256,128]{2,1,0:T(8,128)(2,1)}), bf16[32,256,128]{2,1,0:T(8,128)(2,1)S(1)}, u32[]{:S(2)}, u32[]{:S(2)}) %all-to-all-start.1) | async-done | bytes 2097184 | tf_op jit(solution)/shard_map/all_to_all | solution.py:551
  210.2 3.1 %place.3 = (bf16[128,1024]{1,0:T(8,128)(2,1)S(1)}, f32[16,128]{1,0:T(8,128)S(1)}, f32[16,1024]{1,0:T(8,128)}) custom-call(s32[64]{0:T(128)S(1)} %convert_element_type.49.code_ref, bf16[32,256,128]{2,1,0:T(8,128)(2,1)S(1)} %all-to-all-done.1.blocks_ref), custom_call_target="tpu_custom_call" | custom-call | flops 1048576 | bytes 2097152 | tf_op jit(solution)/shard_map/place/pallas_call | solution.py:227
  213.3 1.5 collective-permute-start.8
  214.8 1.3 collective-permute-start.4
  216.1 1.3 collective-permute-start.10
  217.4 1.3 collective-permute-start.7
  218.7 2.7 %collective-permute-done.4.refs_10_.refs_13_ = f32[8,1024]{1,0:T(8,128)S(1)} collective-permute-done((f32[8,1024]{1,0:T(8,128)S(1)}, f32[8,1024]{1,0:T(8,128)S(1)}, u32[]{:S(2)}, u32[]{:S(2)}) %collective-permute-start.4) | collective-permute-done | bytes 32800 | tf_op jit(solution)/shard_map/ppermute | solution.py:253
  221.5 4.9 %collective-permute-start.9 = (f32[8,128]{1,0:T(8,128)S(1)}, f32[8,128]{1,0:T(8,128)S(1)}, u32[]{:S(2)}, u32[]{:S(2)}) collective-permute-start(f32[8,128]{1,0:T(8,128)S(1)} %get-tuple-element.69), channel_id=1, source_target_pairs={{0,17},{1,18},{2,19},{16,1},{17,2},{18,3},{4,21},{5,22},{6,23},{20... | collective-permute-start | bytes 12296 | tf_op jit(solution)/shard_map/ppermute | solution.py:276
  226.3 3.9 %collective-permute-start.6 = (f32[8,128]{1,0:T(8,128)S(1)}, f32[8,128]{1,0:T(8,128)S(1)}, u32[]{:S(2)}, u32[]{:S(2)}) collective-permute-start(f32[8,128]{1,0:T(8,128)S(1)} %get-tuple-element.69), channel_id=1, source_target_pairs={{0,1},{1,2},{2,3},{4,5},{5,6},{6,7},{8,9},{9,10},{10,11},{12,13},{... | collective-permute-start | bytes 12296 | tf_op jit(solution)/shard_map/ppermute | solution.py:253
  230.3 11.0 %stage.2 = (f32[1024,1024]{1,0:T(8,128)}, f32[1024,1024]{1,0:T(8,128)}) custom-call(s32[1]{0:T(128)} %bitcast.refs_0_, f32[7]{0:T(128)} %refs_1_.1, f32[8,1024]{1,0:T(8,128)} %copy-done.4, f32[8,1024]{1,0:T(8,128)} %copy-done.5, bf16[96,192]{1,0:T(8,128)(2,1)} %add_convert_fusion.refs_4_, bf16[80,192]{1,0:T(8,128)(2,1)} %add_convert_fusion.1.refs_5_, ...), custom_call_target="tpu_custom_call" | custom-call | flops 79626240 | bytes 11943936 | tf_op jit(solution)/shard_map/stage/pallas_call | solution.py:474
  242.2 7.9 %stage.3 = (f32[1024,1024]{1,0:T(8,128)}, f32[1024,1024]{1,0:T(8,128)}) custom-call(s32[1]{0:T(128)} %bitcast.refs_0_, f32[7]{0:T(128)} %refs_1_.1, f32[8,1024]{1,0:T(8,128)} %copy-done.4, f32[8,1024]{1,0:T(8,128)} %copy-done.5, bf16[64,128]{1,0:T(8,128)(2,1)} %add_convert_fusion.2.refs_4_, ...), custom_call_target="tpu_custom_call", output_to_operand_aliasing={{0}: (20, {}), {1}: (21, {})} | custom-call | flops 47185920 | bytes 7077888 | tf_op jit(solution)/shard_map/stage/pallas_call | solution.py:474
  (53 shorter events, 1.8 us)
Async XLA Ops:
  10.0 8.3 %copy-start.7 = (f32[7]{0:T(128)S(1)}, f32[7]{0:T(128)}, u32[]{:S(2)}) copy-start(f32[7]{0:T(128)} %refs_1_.1) | copy-start | bytes 88
  10.0 144.5 %all-to-all-start = ((bf16[32,784,128]{2,1,0:T(8,128)(2,1)}), bf16[32,784,128]{2,1,0:T(8,128)(2,1)}, u32[]{:S(2)}, u32[]{:S(2)}) async-start(bf16[32,784,128]{2,1,0:T(8,128)(2,1)} %warp.2), calls=%async_computation | async-start | bytes 12845056 | tf_op jit(solution)/shard_map/all_to_all | solution.py:551
  154.5 55.7 %all-to-all-start.1 = ((bf16[32,256,128]{2,1,0:T(8,128)(2,1)}), bf16[32,256,128]{2,1,0:T(8,128)(2,1)S(1)}, u32[]{:S(2)}, u32[]{:S(2)}) async-start(bf16[32,256,128]{2,1,0:T(8,128)(2,1)} %warp.3), calls=%async_computation.1 | async-start | bytes 4194304 | tf_op jit(solution)/shard_map/all_to_all | solution.py:551
  172.2 58.0 %copy-start = (bf16[384,1024]{1,0:T(8,128)(2,1)}, bf16[384,1024]{1,0:T(8,128)(2,1)S(1)}, u32[]{:S(2)}) copy-start(bf16[384,1024]{1,0:T(8,128)(2,1)S(1)} %get-tuple-element.45.refs_8_) | copy-start | bytes 2359300
  172.2 7.9 %collective-permute-start = (f32[16,384]{1,0:T(8,128)S(1)}, f32[16,384]{1,0:T(8,128)S(1)}, u32[]{:S(2)}, u32[]{:S(2)}) collective-permute-start(f32[16,384]{1,0:T(8,128)S(1)} %get-tuple-element.35), channel_id=1, source_target_pairs={{0,16},{16,0},{1,17},{17,1},{2,18},{18,2},{3,19},{19,3},{4,20},{20... | collective-permute-start | bytes 73736 | tf_op jit(solution)/shard_map/ppermute | solution.py:257
  174.1 6.0 %collective-permute-start.2 = (f32[8,1024]{1,0:T(8,128)S(1)}, f32[8,1024]{1,0:T(8,128)S(1)}, u32[]{:S(2)}, u32[]{:S(2)}) collective-permute-start(f32[8,1024]{1,0:T(8,128)S(1)} %slice_select_fusion), channel_id=1, source_target_pairs={{4,0},{8,4},{12,8},{16,20},{20,24},{24,28},{5,1},{9,5},{13,9},{17,... | collective-permute-start | bytes 98312 | tf_op jit(solution)/shard_map/ppermute | solution.py:292
  175.4 4.8 %collective-permute-start.1 = (f32[8,1024]{1,0:T(8,128)S(1)}, f32[8,1024]{1,0:T(8,128)S(1)}, u32[]{:S(2)}, u32[]{:S(2)}) collective-permute-start(f32[8,1024]{1,0:T(8,128)S(1)} %slice_select_fusion), channel_id=1, source_target_pairs={{4,16},{8,20},{12,24},{16,4},{20,8},{24,12},{5,17},{9,21},{13,25},... | collective-permute-start | bytes 98312 | tf_op jit(solution)/shard_map/ppermute | solution.py:293
  176.1 50.3 %collective-permute-start.5 = (bf16[384,1024]{1,0:T(8,128)(2,1)S(1)}, bf16[384,1024]{1,0:T(8,128)(2,1)}, u32[]{:S(2)}, u32[]{:S(2)}) collective-permute-start(bf16[384,1024]{1,0:T(8,128)(2,1)S(1)} %get-tuple-element.45.refs_8_), channel_id=1, source_target_pairs={{0,16},{16,0},{1,17},{17,1},{2,18},{18,2},{3,19},{19,3},{4,20},{20... | collective-permute-start | bytes 2359304 | tf_op jit(solution)/shard_map/ppermute | solution.py:257
  180.2 50.1 %copy-start.4 = (f32[8,1024]{1,0:T(8,128)}, f32[8,1024]{1,0:T(8,128)S(1)}, u32[]{:S(2)}) copy-start(f32[8,1024]{1,0:T(8,128)S(1)} %get-tuple-element.39.refs_2_) | copy-start | bytes 98308
  180.2 50.1 %copy-start.5 = (f32[8,1024]{1,0:T(8,128)}, f32[8,1024]{1,0:T(8,128)S(1)}, u32[]{:S(2)}) copy-start(f32[8,1024]{1,0:T(8,128)S(1)} %get-tuple-element.40.refs_3_) | copy-start | bytes 98308
  180.2 37.2 %collective-permute-start.3 = (f32[8,1024]{1,0:T(8,128)S(1)}, f32[8,1024]{1,0:T(8,128)S(1)}, u32[]{:S(2)}, u32[]{:S(2)}) collective-permute-start(f32[8,1024]{1,0:T(8,128)S(1)} %pad_maximum_fusion.1), channel_id=1, source_target_pairs={{0,1},{1,2},{2,3},{4,5},{5,6},{6,7},{8,9},{9,10},{10,11},{12,13},{... | collective-permute-start | bytes 98312 | tf_op jit(solution)/shard_map/ppermute | solution.py:253
  213.3 28.1 %copy-start.1 = (bf16[128,1024]{1,0:T(8,128)(2,1)}, bf16[128,1024]{1,0:T(8,128)(2,1)S(1)}, u32[]{:S(2)}) copy-start(bf16[128,1024]{1,0:T(8,128)(2,1)S(1)} %get-tuple-element.38.refs_14_) | copy-start | bytes 786436
  213.3 28.1 %collective-permute-start.8 = (bf16[128,1024]{1,0:T(8,128)(2,1)S(1)}, bf16[128,1024]{1,0:T(8,128)(2,1)S(1)}, u32[]{:S(2)}, u32[]{:S(2)}) collective-permute-start(bf16[128,1024]{1,0:T(8,128)(2,1)S(1)} %get-tuple-element.38.refs_14_), channel_id=1, source_target_pairs={{0,16},{16,0},{1,17},{17,1},{2,18},{18,2},{3,19},{19,3},{4,20},{20... | collective-permute-start | bytes 786440 | tf_op jit(solution)/shard_map/ppermute | solution.py:257
  214.8 6.7 %collective-permute-start.4 = (f32[8,1024]{1,0:T(8,128)S(1)}, f32[8,1024]{1,0:T(8,128)S(1)}, u32[]{:S(2)}, u32[]{:S(2)}) collective-permute-start(f32[8,1024]{1,0:T(8,128)S(1)} %pad_maximum_fusion.2), channel_id=1, source_target_pairs={{1,0},{2,1},{3,2},{5,4},{6,5},{7,6},{9,8},{10,9},{11,10},{13,12},{... | collective-permute-start | bytes 98312 | tf_op jit(solution)/shard_map/ppermute | solution.py:253
  216.1 25.3 %collective-permute-start.10 = (f32[8,128]{1,0:T(8,128)S(1)}, f32[8,128]{1,0:T(8,128)S(1)}, u32[]{:S(2)}, u32[]{:S(2)}) collective-permute-start(f32[8,128]{1,0:T(8,128)S(1)} %get-tuple-element.68), channel_id=1, source_target_pairs={{1,16},{2,17},{3,18},{17,0},{18,1},{19,2},{5,20},{6,21},{7,22},{21... | collective-permute-start | bytes 12296 | tf_op jit(solution)/shard_map/ppermute | solution.py:277
  217.4 12.9 %copy-start.2 = (f32[8,1024]{1,0:T(8,128)}, f32[8,1024]{1,0:T(8,128)S(1)}, u32[]{:S(2)}) copy-start(f32[8,1024]{1,0:T(8,128)S(1)} %collective-permute-done.3.refs_9_.refs_12_) | copy-start | bytes 98308
  217.4 24.0 %collective-permute-start.7 = (f32[8,128]{1,0:T(8,128)S(1)}, f32[8,128]{1,0:T(8,128)S(1)}, u32[]{:S(2)}, u32[]{:S(2)}) collective-permute-start(f32[8,128]{1,0:T(8,128)S(1)} %get-tuple-element.68), channel_id=1, source_target_pairs={{1,0},{2,1},{3,2},{5,4},{6,5},{7,6},{9,8},{10,9},{11,10},{13,12},{... | collective-permute-start | bytes 12296 | tf_op jit(solution)/shard_map/ppermute | solution.py:253
  221.5 8.9 %copy-start.3 = (f32[8,1024]{1,0:T(8,128)}, f32[8,1024]{1,0:T(8,128)S(1)}, u32[]{:S(2)}) copy-start(f32[8,1024]{1,0:T(8,128)S(1)} %collective-permute-done.4.refs_10_.refs_13_) | copy-start | bytes 98308
  221.5 20.0 %collective-permute-start.9 = (f32[8,128]{1,0:T(8,128)S(1)}, f32[8,128]{1,0:T(8,128)S(1)}, u32[]{:S(2)}, u32[]{:S(2)}) collective-permute-start(f32[8,128]{1,0:T(8,128)S(1)} %get-tuple-element.69), channel_id=1, source_target_pairs={{0,17},{1,18},{2,19},{16,1},{17,2},{18,3},{4,21},{5,22},{6,23},{20... | collective-permute-start | bytes 12296 | tf_op jit(solution)/shard_map/ppermute | solution.py:276
  226.3 15.1 %collective-permute-start.6 = (f32[8,128]{1,0:T(8,128)S(1)}, f32[8,128]{1,0:T(8,128)S(1)}, u32[]{:S(2)}, u32[]{:S(2)}) collective-permute-start(f32[8,128]{1,0:T(8,128)S(1)} %get-tuple-element.69), channel_id=1, source_target_pairs={{0,1},{1,2},{2,3},{4,5},{5,6},{6,7},{8,9},{9,10},{10,11},{12,13},{... | collective-permute-start | bytes 12296 | tf_op jit(solution)/shard_map/ppermute | solution.py:253
  241.4 0.6 copy-start.8
  241.4 0.6 copy-start.9
  241.4 0.6 copy-start.10
  241.4 0.6 copy-start.11
  241.5 0.7 copy-start.6

commit v7 on v6

--- a/solution.py
+++ b/solution.py
@@ -349,92 +349,171 @@
     return product(blur, (coarse, fine, coarse)) * lax.rsqrt(local), local
 
 
-def stage_kernel(plan, lots, *refs):
+def stage_kernel(plan, mend, lots, *refs):
     mine_ref, taps_ref, above_ref, below_ref = refs[:4]
-    tables = refs[4:8]
     fields, copies, outs = plan
-    visits, margin = fields["visits"], fields["margin"]
-    at = 8
+    visits, bare = fields["visits"], fields["bare"]
+    tables, at = refs[4:8], 8
+    if mend:
+        mend_tables, at = refs[8:12], 12
     chunks = []
     for lot in lots:
         parts = []
         for _ in range(visits):
-            parts.append(refs[at : at + 3])
-            at += 3
+            parts.append(refs[at : at + (1 if bare else 3)])
+            at += len(parts[-1])
         chunks.append(parts)
-    at += fields["aliased"]
-    detection_hbm, variance_hbm = refs[at : at + 2]
+    held_hbm = refs[at : at + (2 if mend else 0)]
+    at += len(held_hbm)
+    out_hbm = refs[at : at + 2]
     field, detection, variance, sems = refs[at + 2 : at + 6]
-    sides = refs[at + 6 :]
+    at += 6
+    if mend:
+        rim, columns, column_sems = refs[at : at + 3]
+        at += 3
+    sides = refs[at:]
+    results = (detection, variance)
     spans, tall, _ = field.shape
+
+    def column_copies(hbm, back):
+        found = []
+        for number, ref in enumerate(hbm):
+            for edge in range(2):
+                far = ref.at[:, pl.ds(edge * (TX - SIDE), SIDE)]
+                near = columns.at[number, edge]
+                source, target = (near, far) if back else (far, near)
+                found.append(pltpu.make_async_copy(source, target, column_sems.at[number, edge]))
+        return found
+
+    if mend:
+        for copy in column_copies(held_hbm, False):
+            copy.start()
 
     which = 0
     held = []
     for parts in chunks:
         group = []
-        for number, (cells, left, right) in enumerate(parts):
-            side = sides[which]
-            which += 1
-            height = cells.shape[0]
-            first = number * height if left.shape[1] > height else 0
-            here = slice(first, first + height)
-            gap = jnp.zeros((SIDE - 2 * HALO, height), jnp.float32)
-            side[...] = jnp.concatenate([right[:, here], gap, left[:, here]], axis=0).T.astype(
-                jnp.bfloat16
-            )
+        for number, part in enumerate(parts):
+            cells, side = part[0], None
+            if not bare:
+                _, left, right = part
+                side = sides[which]
+                which += 1
+                height = cells.shape[0]
+                first = number * height if left.shape[1] > height else 0
+                here = slice(first, first + height)
+                gap = jnp.zeros((SIDE - 2 * HALO, height), jnp.float32)
+                side[...] = jnp.concatenate([right[:, here], gap, left[:, here]], axis=0).T.astype(
+                    jnp.bfloat16
+                )
             group.append((cells, side))
         held.append(group)
 
+    def whole_rows(span, into, cells, side, rows):
+        field[span, into, :TX] = cells[rows, :]
+        if not bare:
+            field[span, into, TX:] = side[rows, :]
+
+    def rim_rows(span, into, cells, side, rows):
+        rim[span, into, :SIDE] = cells[rows, :SIDE]
+        rim[span, into, SIDE : 2 * SIDE] = cells[rows, TX - SIDE :]
+        rim[span, into, 2 * SIDE :] = side[rows, :]
+
+    def assemble(order, copies, put):
+        for chunk, visit, first, rows, at_row, begin, end, shift in copies:
+            cells, side = held[chunk][order[visit]]
+
+            @pl.loop(begin, end)
+            def _(unit):
+                start = pl.multiple_of(unit * lots[chunk] + first, EDGE)
+                put(unit + shift, pl.ds(at_row, rows), cells, side, pl.ds(start, rows))
+
+    def assemble_all(order):
+        assemble(order, copies, whole_rows)
+        if mend:
+            assemble(order, mend[1], rim_rows)
+
+    if bare:
+        field[:, :, TX:] = jnp.zeros((spans, tall, SIDE), jnp.bfloat16)
     for span, first, rows in fields["blank"]:
         field[span, first : first + rows, :] = jnp.zeros((rows, WIDE), jnp.bfloat16)
-
-    def assemble(order):
-        for chunk, visit, first, rows, at_row, begin, end, shift in copies:
-            cells, side = held[chunk][order[visit]]
-            lot = lots[chunk]
-
-            @pl.loop(begin, end)
-            def _(unit):
-                start = pl.multiple_of(unit * lot + first, EDGE)
-                into = pl.ds(at_row, rows)
-                field[unit + shift, into, :TX] = cells[pl.ds(start, rows), :]
-                field[unit + shift, into, TX:] = side[pl.ds(start, rows), :]
-
+    if mend:
+        for span, first, rows in mend[0]["blank"]:
+            rim[span, first : first + rows, :] = jnp.zeros((rows, 3 * SIDE), jnp.bfloat16)
     if visits == 2:
         for flip in range(2):
 
             @pl.when(mine_ref[0] == flip)
             def _():
-                assemble((0, 1) if flip == 0 else (1, 0))
+                assemble_all((0, 1) if flip == 0 else (1, 0))
 
     else:
-        assemble(tuple(range(visits)))
-
-    if fields["between"]:
-        _, left, right = chunks[0][0]
-        corners = left.shape[1] - 2 * SIDE
+        assemble_all(tuple(range(visits)))
+
+    between = (mend or plan)[0]["between"]
+    if between:
         from_left = lax.broadcasted_iota(jnp.int32, (HALO, SIDE), 1) >= SIDE // 2
-        none = jnp.zeros((EDGE - HALO, WIDE), jnp.float32)
-        for number, (span, first, rows) in enumerate(
-            zip((0, spans - 1), fields["between"], (above_ref, below_ref))
-        ):
-            here = slice(corners + number * SIDE, corners + (number + 1) * SIDE)
-            wide = jnp.concatenate(
-                [rows[...], jnp.where(from_left, left[:, here], right[:, here])], axis=1
-            )
-            strip = [none, wide] if number == 0 else [wide, none]
-            field[span, first : first + EDGE, :] = jnp.concatenate(strip, axis=0).astype(jnp.bfloat16)
+        for number, rows in enumerate((above_ref, below_ref)):
+            corner = jnp.zeros((HALO, SIDE), jnp.float32)
+            if not bare:
+                _, left, right = chunks[0][0]
+                first = left.shape[1] + (number - 2) * SIDE
+                here = slice(first, first + SIDE)
+                corner = jnp.where(from_left, left[:, here], right[:, here])
+            if mend:
+                wide = jnp.concatenate([rows[:, :SIDE], rows[:, TX - SIDE :], corner], axis=1)
+            else:
+                wide = jnp.concatenate([rows[...], corner], axis=1)
+            strip = [jnp.zeros_like(wide), wide] if number == 0 else [wide, jnp.zeros_like(wide)]
+            strip = jnp.concatenate(strip, axis=0).astype(jnp.bfloat16)
+            into = slice(between[number], between[number] + EDGE)
+            if mend:
+                rim[number * (rim.shape[0] - 1), into, :] = strip
+            else:
+                field[number * (spans - 1), into, :] = strip
 
     taps = [taps_ref[tap] for tap in range(7)]
+    lane = lax.broadcasted_iota(jnp.int32, (1, SIDE), 1)
+
+    if mend:
+        for copy in column_copies(held_hbm, False):
+            copy.wait()
+        count = rim.shape[0]
+        tiles = []
+        for tile in range(WIDE // SIDE):
+            pair = jnp.zeros(rim.shape[1:2] + (SIDE,), jnp.bfloat16)
+            for span in range(2 * tile, min(2 * tile + 2, count)):
+                base = (span % 2) * (SIDE // 2)
+                near, far, halo = (rim[span, :, at * SIDE : (at + 1) * SIDE] for at in range(3))
+                for value, first, last, by in (
+                    (halo, 0, 8, 8), (near, 8, 32, 8), (far, 32, 56, 56), (halo, 56, 64, 56),
+                ):
+                    inside = (lane >= base + first) & (lane < base + last)
+                    pair = jnp.where(inside, pltpu.roll(value, (base + by) % SIDE, 1), pair)
+            tiles.append(pair)
+        mended = filtered(jnp.concatenate(tiles, axis=1), taps, mend_tables, mend[0]["margin"])
+        for begin, end, source, rows, shift in mend[2]:
+            for span in range(begin, end):
+                base = (span % 2) * (SIDE // 2)
+                tile = slice((span // 2) * SIDE, (span // 2 + 1) * SIDE)
+                target = slice(span * STEP + shift, span * STEP + shift + rows)
+                for number in range(2):
+                    value = mended[number][source : source + rows, tile]
+                    for edge, by, good in ((0, -base - 8, lane < 8), (1, 72 - base, lane >= 120)):
+                        columns[number, edge, target, :] = jnp.where(
+                            good, pltpu.roll(value, by % SIDE, 1), columns[number, edge, target, :]
+                        )
+
+    lanes = pl.ds(SIDE, TX - 2 * SIDE) if mend else pl.ds(0, TX)
 
     def stores(unit, source, rows, target):
         return [
             pltpu.make_async_copy(
-                scratch.at[unit, pl.ds(source, rows)], hbm.at[pl.ds(target, rows)], sems.at[unit, at]
+                scratch.at[unit, pl.ds(source, rows), lanes],
+                hbm.at[pl.ds(target, rows), lanes],
+                sems.at[unit, at],
             )
-            for at, (scratch, hbm) in enumerate(
-                ((detection, detection_hbm), (variance, variance_hbm))
-            )
+            for at, (scratch, hbm) in enumerate(zip(results, out_hbm))
         ]
 
     some = next(count for count in (4, 3, 2, 1) if spans % count == 0 and count * tall <= 320)
@@ -443,7 +522,7 @@
     def _(first):
         for ahead in range(some):
             unit = first + ahead
-            detection[unit], variance[unit] = filtered(field[unit], taps, tables, margin)
+            detection[unit], variance[unit] = filtered(field[unit], taps, tables, fields["margin"])
         for ahead in range(some):
             unit = first + ahead
             for begin, end, source, rows, shift in outs:
@@ -453,6 +532,16 @@
                     target = pl.multiple_of(unit * STEP + shift, HALO)
                     for store in stores(unit, source, rows, target):
                         store.start()
+                    if mend:
+                        for number in range(2):
+                            for edge in range(2):
+                                columns[number, edge, pl.ds(target, rows), :] = results[number][
+                                    unit, source : source + rows, pl.ds(edge * (TX - SIDE), SIDE)
+                                ]
+
+    if mend:
+        for copy in column_copies(out_hbm, True):
+            copy.start()
 
     @pl.loop(0, spans)
     def _(unit):
@@ -463,38 +552,47 @@
                 for store in stores(unit, source, rows, 0):
                     store.wait()
 
-
-def stage(plan, mine, taps, between, tables, chunks, lots, held=()):
-    fields, _, _ = plan
+    if mend:
+        for copy in column_copies(out_hbm, True):
+            copy.wait()
+
+
+def stage(plan, mine, taps, between, tables, chunks, lots, mend=None, mend_tables=(), held=()):
+    fields = plan[0]
     spans, tall = fields["spans"], fields["tall"]
     shape = jax.ShapeDtypeStruct((TY, TX), jnp.float32)
     flat = [array for parts in chunks for part in parts for array in part]
-    first = 8 + len(flat)
+    vmems = [*between, *tables, *mend_tables, *flat]
     out = pltpu.VMEM((spans, tall - 2 * fields["margin"], TX), jnp.float32)
+    scratch = [pltpu.VMEM((spans, tall, WIDE), jnp.bfloat16), out, out, pltpu.SemaphoreType.DMA((spans, 2))]
+    if mend:
+        scratch += [
+            pltpu.VMEM((mend[0]["spans"], mend[0]["tall"], 3 * SIDE), jnp.bfloat16),
+            pltpu.VMEM((2, 2, TY, SIDE), jnp.float32),
+            pltpu.SemaphoreType.DMA((2, 2)),
+        ]
+    if not fields["bare"]:
+        scratch += [
+            pltpu.VMEM((part[0].shape[0], SIDE), jnp.bfloat16) for parts in chunks for part in parts
+        ]
     return pl.pallas_call(
-        functools.partial(stage_kernel, plan, lots),
+        functools.partial(stage_kernel, plan, mend, lots),
         out_shape=(shape, shape),
-        in_specs=[SMEM, SMEM] + [VMEM] * (6 + len(flat)) + [HBM] * len(held),
+        in_specs=[SMEM, SMEM] + [VMEM] * len(vmems) + [HBM] * len(held),
         out_specs=(HBM, HBM),
-        input_output_aliases={first + at: at for at in range(len(held))},
-        scratch_shapes=[
-            pltpu.VMEM((spans, tall, WIDE), jnp.bfloat16),
-            out,
-            out,
-            pltpu.SemaphoreType.DMA((spans, 2)),
-        ]
-        + [pltpu.VMEM((part[0].shape[0], SIDE), jnp.bfloat16) for parts in chunks for part in parts],
+        input_output_aliases={2 + len(vmems) + at: at for at in range(len(held))},
+        scratch_shapes=scratch,
         compiler_params=pltpu.CompilerParams(vmem_limit_bytes=56 * MIB),
         cost_estimate=pl.CostEstimate(
             flops=80 * spans * tall * WIDE, bytes_accessed=12 * spans * tall * WIDE, transcendentals=0
         ),
         name="stage",
-    )(mine, taps, *between, *tables, *flat, *held)
+    )(mine, taps, *vmems, *held)
 
 
 def outer_plan(lot):
     fields = dict(
-        visits=2, aliased=0, spans=UNITS + 1, tall=2 * lot, margin=HALO, between=(lot - EDGE, lot),
+        visits=2, bare=True, spans=UNITS + 1, tall=2 * lot, margin=HALO, between=(lot - EDGE, lot),
         blank=[(0, 0, lot - EDGE), (UNITS, lot + EDGE, lot - EDGE)],
     )
     copies = [(0, 1, 0, lot, 0, 0, UNITS, 1), (0, 0, 0, lot, lot, 0, UNITS, 0)]
@@ -510,7 +608,7 @@
 def inner_plan(lot, inner):
     tall = 2 * inner + 2 * EDGE
     fields = dict(
-        visits=2, aliased=2, spans=UNITS, tall=tall, margin=HALO, between=None, blank=[]
+        visits=2, bare=False, spans=UNITS, tall=tall, margin=HALO, between=None, blank=[]
     )
     copies = [
         (0, 0, lot - EDGE, EDGE, 0, 0, UNITS, 0),
@@ -523,7 +621,7 @@
 
 def whole_plan(lot, visits):
     fields = dict(
-        visits=visits, aliased=0, spans=UNITS, tall=STEP + 2 * EDGE, margin=EDGE,
+        visits=visits, bare=False, spans=UNITS, tall=STEP + 2 * EDGE, margin=EDGE,
         between=(0, EDGE + STEP), blank=[],
     )
     copies = [(0, visit, 0, lot, EDGE + visit * lot, 0, UNITS, 0) for visit in range(visits)]
@@ -573,12 +671,14 @@
     between = rows_between(edge)
     sides = beyond([strip, swapped(strip)], *between)
     parts = [(coadd, *sides), (other, *sides)]
+    held = stage(outer, mine, psf_taps, between, tables[0], [[(coadd,), (other,)]], lots[:1])
+    second, held = lax.optimization_barrier((second, held))
     coadd, strip, _ = place(code, second, lots[1])
     own_sides, other_sides = straight_to_both(strip)
     more = [(coadd, *own_sides), (swapped(coadd), *other_sides)]
-    (parts, between), _ = lax.optimization_barrier(((parts, between), coadd))
-    held = stage(outer, mine, psf_taps, between, tables[0], [parts], lots[:1])
-    return stage(inner, mine, psf_taps, between, tables[1], [parts, more], lots, held)
+    return stage(
+        inner, mine, psf_taps, between, tables[1], [parts, more], lots, outer, tables[0], held
+    )
 
 
 def codes(arrived):

time: 251 us -> 253 us (level)
  Pallas kernels: 47.5 us -> 50.8 us
  waiting for transfers between devices: 143 us -> 140 us
    all_to_all x2, waiting for transfers between devices: 140 us -> 114 us  [send(): lax.all_to_all(blocks, EVERY, split_axis=0, concat_axis=0, tiled=True)]
    ppermute x3, waiting for transfers between devices: 0.01 us -> 24.6 us  [swapped(): return lax.ppermute(array, 'visit', [(0, 1), (1, 0)])]
    pallas_call x2, Pallas kernels: 18.9 us -> 22.2 us  [stage(): pl.pallas_call(functools.partial(stage_kernel, plan, mend, lots), out_sha...]
    ppermute x1, starting transfers between devices: 4.86 us -> 7.62 us  [straight_to_both(): lax.ppermute(last, ('visit', 'px'), crossed(up))]
where the time goes in v7:
time: 253 us; the launch traced here: 252 us
  waiting for transfers between devices  140 us (55%)
  Pallas kernels  50.8 us (20%)
  starting transfers between devices  42.2 us (17%)
  other arithmetic  14.3 us (6%)
  local copies, waits for them, and re-layouts  3.91 us (2%)
    all_to_all x2, waiting for transfers between devices, send(): lax.all_to_all(blocks, EVERY, split_axis=0, concat_axis=0, tiled=True)  114 us
    ppermute x3, waiting for transfers between devices, swapped(): return lax.ppermute(array, 'visit', [(0, 1), (1, 0)])  24.6 us
    pallas_call x2, Pallas kernels, stage(): pl.pallas_call(functools.partial(stage_kernel, plan, mend, lots), out_sha...  22.2 us
    pallas_call x2, Pallas kernels, warp(): pl.pallas_call(functools.partial(warp_kernel, tiles, share, noted), out_s...  17.9 us
    all_to_all x2, starting transfers between devices, send(): lax.all_to_all(blocks, EVERY, split_axis=0, concat_axis=0, tiled=True)  16.3 us
    pallas_call x2, Pallas kernels, place(): pl.pallas_call(functools.partial(place_kernel, 2 * lot), grid_spec=pltpu....  10.7 us
    ppermute x4, starting transfers between devices, neighbours(): return (lax.ppermute(last, axis, up), lax.ppermute(first, axis, down))  9.12 us
    convert_element_type x2, other arithmetic, split(): coarse = value.astype(jnp.bfloat16)  8.98 us
  transfers between devices with their start and end apart: 13, of which 3 were waited for; matrix products, arithmetic and copies ran while one was open for 6% of the time, Pallas kernels for 12%

profile of v7, /device:TPU:0, one launch (start us, length us, event | category | flops | bytes accessed | tf_op | source)
XLA Modules:
  0.0 251.8 jit_solution(3576483677404498527)
XLA Ops:
  0.6 9.3 %warp.2 = bf16[32,784,128]{2,1,0:T(8,128)(2,1)} custom-call(s32[24]{0:T(128)} %visit_ref.3, s32[24]{0:T(128)} %bitcast.12, s32[2,24]{1,0:T(2,128)} %bitcast.10, s32[8,256]{1,0:T(8,128)} %good_ref.3, bf16[8,256,256]{2,1,0:T(8,128)(2,1)} %rows_hbm.3, bf16[8,256,256]{2,1,0:T(8,128)(2,1)} %cols_hbm.3, bf16[24,256,256]{2,1,0:T(8,128)(2,1)} %var_hbm.2, ...), custom_call_target="tpu_custom_call" | custom-call | flops 3221225472 | bytes 12582912 | tf_op jit(solution)/shard_map/warp/pallas_call | solution.py:158
  10.0 7.4 %all-to-all-start = ((bf16[32,784,128]{2,1,0:T(8,128)(2,1)}), bf16[32,784,128]{2,1,0:T(8,128)(2,1)}, u32[]{:S(2)}, u32[]{:S(2)}) async-start(bf16[32,784,128]{2,1,0:T(8,128)(2,1)} %warp.2), calls=%async_computation | async-start | bytes 12845056 | tf_op jit(solution)/shard_map/all_to_all | solution.py:649
  17.6 0.7 add_convert_fusion.3.refs_5_
  19.0 0.7 add_convert_fusion.2.refs_4_
  19.6 4.5 %fusion.16 = (bf16[48,64]{1,0:T(8,128)(2,1)S(1)}, bf16[48,64]{1,0:T(8,128)(2,1)S(1)}) fusion(f32[]{:T(128)} %bitcast.9, f32[]{:T(128)} %bitcast.8, f32[]{:T(128)} %bitcast.7, f32[]{:T(128)} %bitcast.6, f32[]{:T(128)} %bitcast.5, f32[]{:T(128)} %bitcast.4, f32[]{:T(128)} %bitcast.3, s32[48]{0:T(128)S(1)} %iota_add_fusion), kind=kLoop, calls=%fused_computation.39 | loop fusion | flops 79872 | bytes 12508 | tf_op jit(solution)/shard_map/convert_element_type | solution.py:317
  24.1 0.7 pad_maximum_fusion.3.refs_6_
  24.9 0.7 add_convert_fusion.1.refs_5_.refs_9_
  25.6 0.7 add_convert_fusion.refs_4_.refs_8_
  26.3 4.5 %fusion.15 = (bf16[80,96]{1,0:T(8,128)(2,1)S(1)}, bf16[80,96]{1,0:T(8,128)(2,1)S(1)}) fusion(f32[]{:T(128)} %bitcast.9, f32[]{:T(128)} %bitcast.8, f32[]{:T(128)} %bitcast.7, f32[]{:T(128)} %bitcast.6, f32[]{:T(128)} %bitcast.5, f32[]{:T(128)} %bitcast.4, f32[]{:T(128)} %bitcast.3, s32[80]{0:T(128)S(1)} %iota_add_fusion.1), kind=kLoop, calls=%fused_computation.35 | loop fusion | flops 199680 | bytes 31068 | tf_op jit(solution)/shard_map/convert_element_type | solution.py:317
  30.8 0.7 pad_maximum_fusion.refs_6_.refs_10_
  31.5 0.8 fusion.refs_7_.refs_11_
  32.4 8.5 %warp.3 = bf16[32,256,128]{2,1,0:T(8,128)(2,1)} custom-call(s32[24]{0:T(128)} %visit_ref.3, s32[24]{0:T(128)} %bitcast.13, s32[2,24]{1,0:T(2,128)} %bitcast.11, s32[8,256]{1,0:T(8,128)} %good_ref.3, bf16[8,256,256]{2,1,0:T(8,128)(2,1)} %rows_hbm.3, bf16[8,256,256]{2,1,0:T(8,128)(2,1)} %cols_hbm.3, bf16[24,256,256]{2,1,0:T(8,128)(2,1)} %var_hbm.2, ...), custom_call_target="tpu_custom_call" | custom-call | flops 3221225472 | bytes 12582912 | tf_op jit(solution)/shard_map/warp/pallas_call | solution.py:158
  40.9 113.6 %all-to-all-done.blocks_ref = bf16[32,784,128]{2,1,0:T(8,128)(2,1)} async-done(((bf16[32,784,128]{2,1,0:T(8,128)(2,1)}), bf16[32,784,128]{2,1,0:T(8,128)(2,1)}, u32[]{:S(2)}, u32[]{:S(2)}) %all-to-all-start) | async-done | bytes 6422560 | tf_op jit(solution)/shard_map/all_to_all | solution.py:649
  154.5 8.9 %all-to-all-start.1 = ((bf16[32,256,128]{2,1,0:T(8,128)(2,1)}), bf16[32,256,128]{2,1,0:T(8,128)(2,1)S(1)}, u32[]{:S(2)}, u32[]{:S(2)}) async-start(bf16[32,256,128]{2,1,0:T(8,128)(2,1)} %warp.3), calls=%async_computation.1 | async-start | bytes 4194304 | tf_op jit(solution)/shard_map/all_to_all | solution.py:649
  163.4 1.0 slice.81
  164.6 7.7 %place.2 = (bf16[384,1024]{1,0:T(8,128)(2,1)S(1)}, f32[16,384]{1,0:T(8,128)S(1)}, f32[16,1024]{1,0:T(8,128)S(1)}) custom-call(s32[64]{0:T(128)S(1)} %convert_element_type.49.code_ref, bf16[32,784,128]{2,1,0:T(8,128)(2,1)} %all-to-all-done.blocks_ref), custom_call_target="tpu_custom_call" | custom-call | flops 3211264 | bytes 6422528 | tf_op jit(solution)/shard_map/place/pallas_call | solution.py:227
  172.2 1.8 collective-permute-start.2
  174.1 1.3 collective-permute-start.1
  176.1 4.1 %collective-permute-start.5 = (bf16[384,1024]{1,0:T(8,128)(2,1)S(1)}, bf16[384,1024]{1,0:T(8,128)(2,1)S(1)}, u32[]{:S(2)}, u32[]{:S(2)}) collective-permute-start(bf16[384,1024]{1,0:T(8,128)(2,1)S(1)} %get-tuple-element.38.refs_8_.refs_12_), channel_id=1, source_target_pairs={{0,16},{16,0},{1,17},{17,1},{2,18},{18,2},{3,19},{19,3},{4,20},{20... | collective-permute-start | bytes 2359304 | tf_op jit(solution)/shard_map/ppermute | solution.py:257
  180.2 2.6 %collective-permute-start.3 = (f32[8,1024]{1,0:T(8,128)S(1)}, f32[8,1024]{1,0:T(8,128)S(1)}, u32[]{:S(2)}, u32[]{:S(2)}) collective-permute-start(f32[8,1024]{1,0:T(8,128)S(1)} %pad_maximum_fusion.1), channel_id=1, source_target_pairs={{0,1},{1,2},{2,3},{4,5},{5,6},{6,7},{8,9},{9,10},{10,11},{12,13},{... | collective-permute-start | bytes 98312 | tf_op jit(solution)/shard_map/ppermute | solution.py:253
  182.8 24.6 %collective-permute-done.5.refs_9_.refs_15_ = bf16[384,1024]{1,0:T(8,128)(2,1)S(1)} collective-permute-done((bf16[384,1024]{1,0:T(8,128)(2,1)S(1)}, bf16[384,1024]{1,0:T(8,128)(2,1)S(1)}, u32[]{:S(2)}, u32[]{:S(2)}) %collective-permute-start.5) | collective-permute-done | bytes 786464 | tf_op jit(solution)/shard_map/ppermute | solution.py:257
  207.5 0.9 copy-done.2
  208.4 10.9 %stage.2 = (f32[1024,1024]{1,0:T(8,128)}, f32[1024,1024]{1,0:T(8,128)}) custom-call(s32[1]{0:T(128)} %bitcast.refs_0_, f32[7]{0:T(128)} %refs_1_.1, f32[8,1024]{1,0:T(8,128)} %copy-done.4, f32[8,1024]{1,0:T(8,128)} %copy-done.3, bf16[96,192]{1,0:T(8,128)(2,1)} %add_convert_fusion.refs_4_.refs_8_, bf16[80,192]{1,0:T(8,128)(2,1)} %add_convert_fusion.1.refs_5_.refs_9_, ...), custom_call_target="tpu_custom_call" | custom-call | flops 79626240 | bytes 11943936 | tf_op jit(solution)/shard_map/stage/pallas_call | solution.py:578
  219.3 3.1 %place.3 = (bf16[128,1024]{1,0:T(8,128)(2,1)S(1)}, f32[16,128]{1,0:T(8,128)S(1)}, f32[16,1024]{1,0:T(8,128)}) custom-call(s32[64]{0:T(128)S(1)} %convert_element_type.49.code_ref, bf16[32,256,128]{2,1,0:T(8,128)(2,1)S(1)} %all-to-all-done.1.blocks_ref), custom_call_target="tpu_custom_call" | custom-call | flops 1048576 | bytes 2097152 | tf_op jit(solution)/shard_map/place/pallas_call | solution.py:227
  222.4 1.3 collective-permute-start.4
  223.7 1.3 collective-permute-start.10
  225.0 1.3 collective-permute-start.7
  226.3 7.6 %collective-permute-start.9 = (f32[8,128]{1,0:T(8,128)S(1)}, f32[8,128]{1,0:T(8,128)S(1)}, u32[]{:S(2)}, u32[]{:S(2)}) collective-permute-start(f32[8,128]{1,0:T(8,128)S(1)} %get-tuple-element.59), channel_id=1, source_target_pairs={{0,17},{1,18},{2,19},{16,1},{17,2},{18,3},{4,21},{5,22},{6,23},{20... | collective-permute-start | bytes 12296 | tf_op jit(solution)/shard_map/ppermute | solution.py:276
  234.0 3.9 %collective-permute-start.6 = (f32[8,128]{1,0:T(8,128)S(1)}, f32[8,128]{1,0:T(8,128)S(1)}, u32[]{:S(2)}, u32[]{:S(2)}) collective-permute-start(f32[8,128]{1,0:T(8,128)S(1)} %get-tuple-element.59), channel_id=1, source_target_pairs={{0,1},{1,2},{2,3},{4,5},{5,6},{6,7},{8,9},{9,10},{10,11},{12,13},{... | collective-permute-start | bytes 12296 | tf_op jit(solution)/shard_map/ppermute | solution.py:253
  238.0 1.2 collective-permute-done.6.refs_19_
  239.8 0.7 copy-done.5
  240.5 11.3 %stage.3 = (f32[1024,1024]{1,0:T(8,128)}, f32[1024,1024]{1,0:T(8,128)}) custom-call(s32[1]{0:T(128)} %bitcast.refs_0_, f32[7]{0:T(128)} %refs_1_.1, f32[8,1024]{1,0:T(8,128)} %copy-done.4, f32[8,1024]{1,0:T(8,128)} %copy-done.3, bf16[64,128]{1,0:T(8,128)(2,1)} %add_convert_fusion.2.refs_4_, ...), custom_call_target="tpu_custom_call", output_to_operand_aliasing={{0}: (24, {}), {1}: (25, {})} | custom-call | flops 47185920 | bytes 7077888 | tf_op jit(solution)/shard_map/stage/pallas_call | solution.py:578
  (55 shorter events, 2.3 us)
Async XLA Ops:
  10.0 8.3 %copy-start.8 = (f32[7]{0:T(128)S(1)}, f32[7]{0:T(128)}, u32[]{:S(2)}) copy-start(f32[7]{0:T(128)} %refs_1_.1) | copy-start | bytes 88
  10.0 144.5 %all-to-all-start = ((bf16[32,784,128]{2,1,0:T(8,128)(2,1)}), bf16[32,784,128]{2,1,0:T(8,128)(2,1)}, u32[]{:S(2)}, u32[]{:S(2)}) async-start(bf16[32,784,128]{2,1,0:T(8,128)(2,1)} %warp.2), calls=%async_computation | async-start | bytes 12845056 | tf_op jit(solution)/shard_map/all_to_all | solution.py:649
  154.5 64.8 %all-to-all-start.1 = ((bf16[32,256,128]{2,1,0:T(8,128)(2,1)}), bf16[32,256,128]{2,1,0:T(8,128)(2,1)S(1)}, u32[]{:S(2)}, u32[]{:S(2)}) async-start(bf16[32,256,128]{2,1,0:T(8,128)(2,1)} %warp.3), calls=%async_computation.1 | async-start | bytes 4194304 | tf_op jit(solution)/shard_map/all_to_all | solution.py:649
  172.2 35.2 %copy-start = (bf16[384,1024]{1,0:T(8,128)(2,1)}, bf16[384,1024]{1,0:T(8,128)(2,1)S(1)}, u32[]{:S(2)}) copy-start(bf16[384,1024]{1,0:T(8,128)(2,1)S(1)} %get-tuple-element.38.refs_8_.refs_12_) | copy-start | bytes 2359300
  172.2 7.9 %collective-permute-start.2 = (f32[16,384]{1,0:T(8,128)S(1)}, f32[16,384]{1,0:T(8,128)S(1)}, u32[]{:S(2)}, u32[]{:S(2)}) collective-permute-start(f32[16,384]{1,0:T(8,128)S(1)} %get-tuple-element.39), channel_id=1, source_target_pairs={{0,16},{16,0},{1,17},{17,1},{2,18},{18,2},{3,19},{19,3},{4,20},{20... | collective-permute-start | bytes 73736 | tf_op jit(solution)/shard_map/ppermute | solution.py:257
  174.1 6.0 %collective-permute-start.1 = (f32[8,1024]{1,0:T(8,128)S(1)}, f32[8,1024]{1,0:T(8,128)S(1)}, u32[]{:S(2)}, u32[]{:S(2)}) collective-permute-start(f32[8,1024]{1,0:T(8,128)S(1)} %slice_select_fusion), channel_id=1, source_target_pairs={{4,0},{8,4},{12,8},{16,20},{20,24},{24,28},{5,1},{9,5},{13,9},{17,... | collective-permute-start | bytes 98312 | tf_op jit(solution)/shard_map/ppermute | solution.py:292
  175.4 4.8 %collective-permute-start = (f32[8,1024]{1,0:T(8,128)S(1)}, f32[8,1024]{1,0:T(8,128)S(1)}, u32[]{:S(2)}, u32[]{:S(2)}) collective-permute-start(f32[8,1024]{1,0:T(8,128)S(1)} %slice_select_fusion), channel_id=1, source_target_pairs={{4,16},{8,20},{12,24},{16,4},{20,8},{24,12},{5,17},{9,21},{13,25},... | collective-permute-start | bytes 98312 | tf_op jit(solution)/shard_map/ppermute | solution.py:293
  176.1 31.4 %collective-permute-start.5 = (bf16[384,1024]{1,0:T(8,128)(2,1)S(1)}, bf16[384,1024]{1,0:T(8,128)(2,1)S(1)}, u32[]{:S(2)}, u32[]{:S(2)}) collective-permute-start(bf16[384,1024]{1,0:T(8,128)(2,1)S(1)} %get-tuple-element.38.refs_8_.refs_12_), channel_id=1, source_target_pairs={{0,16},{16,0},{1,17},{17,1},{2,18},{18,2},{3,19},{19,3},{4,20},{20... | collective-permute-start | bytes 2359304 | tf_op jit(solution)/shard_map/ppermute | solution.py:257
  180.2 27.3 %copy-start.3 = (f32[8,1024]{1,0:T(8,128)}, f32[8,1024]{1,0:T(8,128)S(1)}, u32[]{:S(2)}) copy-start(f32[8,1024]{1,0:T(8,128)S(1)} %get-tuple-element.48.refs_3_) | copy-start | bytes 98308
  180.2 27.3 %copy-start.4 = (f32[8,1024]{1,0:T(8,128)}, f32[8,1024]{1,0:T(8,128)S(1)}, u32[]{:S(2)}) copy-start(f32[8,1024]{1,0:T(8,128)S(1)} %get-tuple-element.49.refs_2_) | copy-start | bytes 98308
  180.2 46.1 %collective-permute-start.3 = (f32[8,1024]{1,0:T(8,128)S(1)}, f32[8,1024]{1,0:T(8,128)S(1)}, u32[]{:S(2)}, u32[]{:S(2)}) collective-permute-start(f32[8,1024]{1,0:T(8,128)S(1)} %pad_maximum_fusion.1), channel_id=1, source_target_pairs={{0,1},{1,2},{2,3},{4,5},{5,6},{6,7},{8,9},{9,10},{10,11},{12,13},{... | collective-permute-start | bytes 98312 | tf_op jit(solution)/shard_map/ppermute | solution.py:253
  207.5 0.9 copy-start.2
  222.4 16.8 %copy-start.1 = (bf16[128,1024]{1,0:T(8,128)(2,1)}, bf16[128,1024]{1,0:T(8,128)(2,1)S(1)}, u32[]{:S(2)}) copy-start(bf16[128,1024]{1,0:T(8,128)(2,1)S(1)} %get-tuple-element.44.refs_18_) | copy-start | bytes 786436
  222.4 16.8 %collective-permute-start.8 = (bf16[128,1024]{1,0:T(8,128)(2,1)S(1)}, bf16[128,1024]{1,0:T(8,128)(2,1)S(1)}, u32[]{:S(2)}, u32[]{:S(2)}) collective-permute-start(bf16[128,1024]{1,0:T(8,128)(2,1)S(1)} %get-tuple-element.44.refs_18_), channel_id=1, source_target_pairs={{0,16},{16,0},{1,17},{17,1},{2,18},{18,2},{3,19},{19,3},{4,20},{20... | collective-permute-start | bytes 786440 | tf_op jit(solution)/shard_map/ppermute | solution.py:257
  222.4 11.6 %collective-permute-start.4 = (f32[8,1024]{1,0:T(8,128)S(1)}, f32[8,1024]{1,0:T(8,128)S(1)}, u32[]{:S(2)}, u32[]{:S(2)}) collective-permute-start(f32[8,1024]{1,0:T(8,128)S(1)} %pad_maximum_fusion.2), channel_id=1, source_target_pairs={{1,0},{2,1},{3,2},{5,4},{6,5},{7,6},{9,8},{10,9},{11,10},{13,12},{... | collective-permute-start | bytes 98312 | tf_op jit(solution)/shard_map/ppermute | solution.py:253
  223.7 14.2 %collective-permute-start.10 = (f32[8,128]{1,0:T(8,128)S(1)}, f32[8,128]{1,0:T(8,128)S(1)}, u32[]{:S(2)}, u32[]{:S(2)}) collective-permute-start(f32[8,128]{1,0:T(8,128)S(1)} %get-tuple-element.58), channel_id=1, source_target_pairs={{1,16},{2,17},{3,18},{17,0},{18,1},{19,2},{5,20},{6,21},{7,22},{21... | collective-permute-start | bytes 12296 | tf_op jit(solution)/shard_map/ppermute | solution.py:277
  225.0 12.9 %collective-permute-start.7 = (f32[8,128]{1,0:T(8,128)S(1)}, f32[8,128]{1,0:T(8,128)S(1)}, u32[]{:S(2)}, u32[]{:S(2)}) collective-permute-start(f32[8,128]{1,0:T(8,128)S(1)} %get-tuple-element.58), channel_id=1, source_target_pairs={{1,0},{2,1},{3,2},{5,4},{6,5},{7,6},{9,8},{10,9},{11,10},{13,12},{... | collective-permute-start | bytes 12296 | tf_op jit(solution)/shard_map/ppermute | solution.py:253
  226.3 12.9 %copy-start.6 = (f32[8,1024]{1,0:T(8,128)}, f32[8,1024]{1,0:T(8,128)S(1)}, u32[]{:S(2)}) copy-start(f32[8,1024]{1,0:T(8,128)S(1)} %collective-permute-done.3.refs_13_.refs_16_) | copy-start | bytes 98308
  226.3 11.6 %collective-permute-start.9 = (f32[8,128]{1,0:T(8,128)S(1)}, f32[8,128]{1,0:T(8,128)S(1)}, u32[]{:S(2)}, u32[]{:S(2)}) collective-permute-start(f32[8,128]{1,0:T(8,128)S(1)} %get-tuple-element.59), channel_id=1, source_target_pairs={{0,17},{1,18},{2,19},{16,1},{17,2},{18,3},{4,21},{5,22},{6,23},{20... | collective-permute-start | bytes 12296 | tf_op jit(solution)/shard_map/ppermute | solution.py:276
  234.0 5.3 %copy-start.7 = (f32[8,1024]{1,0:T(8,128)}, f32[8,1024]{1,0:T(8,128)S(1)}, u32[]{:S(2)}) copy-start(f32[8,1024]{1,0:T(8,128)S(1)} %collective-permute-done.4.refs_14_.refs_17_) | copy-start | bytes 98308
  234.0 5.2 %collective-permute-start.6 = (f32[8,128]{1,0:T(8,128)S(1)}, f32[8,128]{1,0:T(8,128)S(1)}, u32[]{:S(2)}, u32[]{:S(2)}) collective-permute-start(f32[8,128]{1,0:T(8,128)S(1)} %get-tuple-element.59), channel_id=1, source_target_pairs={{0,1},{1,2},{2,3},{4,5},{5,6},{6,7},{8,9},{9,10},{10,11},{12,13},{... | collective-permute-start | bytes 12296 | tf_op jit(solution)/shard_map/ppermute | solution.py:253
  237.9 1.3 copy-start.9
  237.9 1.3 copy-start.10
  238.0 1.3 copy-start.11
  239.2 0.6 copy-start.12
  239.8 0.7 copy-start.5

commit v8 on v7

--- a/solution.py
+++ b/solution.py
@@ -17,6 +17,7 @@
 SIDE = 128
 WIDE = TX + SIDE
 GROUP = 4
+CUT = 6
 NOTE = 16
 MIB = 1 << 20
 EVERY = ("visit", "py", "px")
@@ -182,7 +183,8 @@
     )(visit, tile, offset, good, rows, cols, var, image)
 
 
-def place_kernel(part, code_ref, blocks_ref, coadd_ref, strip_ref, edge_ref, data, weight):
+def place_kernel(part, pieces, code_ref, blocks_ref, *refs):
+    coadd_refs, (strip_ref, edge_ref, data, weight) = refs[: len(pieces)], refs[len(pieces) :]
     step = pl.program_id(0)
     some = blocks_ref.shape[0]
     height = data.shape[0]
@@ -212,20 +214,21 @@
     @pl.when(step == pl.num_programs(0) - 1)
     def _():
         coadd = data[...] / jnp.maximum(weight[...], 1.0)
-        coadd_ref[...] = coadd.astype(coadd_ref.dtype)
+        for (first, last), coadd_ref in zip(pieces, coadd_refs):
+            coadd_ref[...] = coadd[first * lot : last * lot].astype(jnp.bfloat16)
         strip_ref[:HALO] = coadd[:, :SIDE].T[:HALO]
         strip_ref[HALO:] = coadd[:, TX - SIDE :].T[SIDE - HALO :]
         edge_ref[:HALO] = coadd[:HALO]
         edge_ref[HALO:] = coadd[height - HALO :]
 
 
-def place(code, blocks, lot):
+def place(code, blocks, lot, pieces=((0, UNITS),)):
     count, tall, side = blocks.shape
     some = 4
     height = lot * UNITS
-    shapes = [((height, TX), jnp.bfloat16), ((2 * HALO, height), jnp.float32), ((2 * HALO, TX), jnp.float32)]
+    shapes = [(((last - first) * lot, TX), jnp.bfloat16) for first, last in pieces] + [((2 * HALO, height), jnp.float32), ((2 * HALO, TX), jnp.float32)]
     return pl.pallas_call(
-        functools.partial(place_kernel, 2 * lot),
+        functools.partial(place_kernel, 2 * lot, pieces),
         grid_spec=pltpu.PrefetchScalarGridSpec(
             num_scalar_prefetch=1,
             grid=(count // some,),
@@ -261,21 +264,6 @@
     first = [strip[:HALO] for strip in strips] + [rows[:, :SIDE] for rows in (above, below)]
     last = [strip[HALO:] for strip in strips] + [rows[:, TX - SIDE :] for rows in (above, below)]
     return neighbours(jnp.concatenate(first, axis=1), jnp.concatenate(last, axis=1), "px")
-
-
-def straight_to_both(strip):
-    first, last = strip[:HALO], strip[HALO:]
-    count = lax.axis_size("px")
-    up, down = beside("px")
-
-    def crossed(pairs):
-        return [(v * count + i, (1 - v) * count + j) for v in range(2) for i, j in pairs]
-
-    own = neighbours(first, last, "px")
-    return own, (
-        lax.ppermute(last, ("visit", "px"), crossed(up)),
-        lax.ppermute(first, ("visit", "px"), crossed(down)),
-    )
 
 
 def rows_between(edge):
@@ -349,22 +337,20 @@
     return product(blur, (coarse, fine, coarse)) * lax.rsqrt(local), local
 
 
-def stage_kernel(plan, mend, lots, *refs):
+def stage_kernel(plan, mend, chunks, heights, *refs):
     mine_ref, taps_ref, above_ref, below_ref = refs[:4]
     fields, copies, outs = plan
-    visits, bare = fields["visits"], fields["bare"]
+    visits = fields["visits"]
+    bare = not heights
     tables, at = refs[4:8], 8
     if mend:
         mend_tables, at = refs[8:12], 12
-    chunks = []
-    for lot in lots:
-        parts = []
-        for _ in range(visits):
-            parts.append(refs[at : at + (1 if bare else 3)])
-            at += len(parts[-1])
-        chunks.append(parts)
-    held_hbm = refs[at : at + (2 if mend else 0)]
-    at += len(held_hbm)
+    if not bare:
+        left, right = refs[at : at + 2]
+        at += 2
+    cells_of = [refs[at + visits * chunk : at + visits * (chunk + 1)] for chunk in range(len(chunks))]
+    at += visits * len(chunks) + fields["held"]
+    held_hbm = refs[at - 2 : at] if mend else ()
     out_hbm = refs[at : at + 2]
     field, detection, variance, sems = refs[at + 2 : at + 6]
     at += 6
@@ -389,44 +375,41 @@
         for copy in column_copies(held_hbm, False):
             copy.start()
 
-    which = 0
-    held = []
-    for parts in chunks:
-        group = []
-        for number, part in enumerate(parts):
-            cells, side = part[0], None
-            if not bare:
-                _, left, right = part
-                side = sides[which]
-                which += 1
-                height = cells.shape[0]
-                first = number * height if left.shape[1] > height else 0
-                here = slice(first, first + height)
-                gap = jnp.zeros((SIDE - 2 * HALO, height), jnp.float32)
-                side[...] = jnp.concatenate([right[:, here], gap, left[:, here]], axis=0).T.astype(
-                    jnp.bfloat16
-                )
-            group.append((cells, side))
-        held.append(group)
-
-    def whole_rows(span, into, cells, side, rows):
+    first = 0
+    for lot, height in enumerate(heights):
+        for visit in range(visits):
+            here = slice(first, first + height)
+            first += height
+            gap = jnp.zeros((SIDE - 2 * HALO, height), jnp.float32)
+            sides[lot * visits + visit][...] = jnp.concatenate(
+                [right[:, here], gap, left[:, here]], axis=0
+            ).T.astype(jnp.bfloat16)
+    corners = first
+
+    def whole_rows(span, into, cells, rows, side, side_rows):
         field[span, into, :TX] = cells[rows, :]
         if not bare:
-            field[span, into, TX:] = side[rows, :]
-
-    def rim_rows(span, into, cells, side, rows):
+            field[span, into, TX:] = side[side_rows, :]
+
+    def rim_rows(span, into, cells, rows, side, side_rows):
         rim[span, into, :SIDE] = cells[rows, :SIDE]
         rim[span, into, SIDE : 2 * SIDE] = cells[rows, TX - SIDE :]
-        rim[span, into, 2 * SIDE :] = side[rows, :]
+        rim[span, into, 2 * SIDE :] = side[side_rows, :]
 
     def assemble(order, copies, put):
         for chunk, visit, first, rows, at_row, begin, end, shift in copies:
-            cells, side = held[chunk][order[visit]]
+            tall_of, base, lot = chunks[chunk]
+            cells = cells_of[chunk][order[visit]]
+            side = None if bare else sides[lot * visits + order[visit]]
 
             @pl.loop(begin, end)
             def _(unit):
-                start = pl.multiple_of(unit * lots[chunk] + first, EDGE)
-                put(unit + shift, pl.ds(at_row, rows), cells, side, pl.ds(start, rows))
+                start = pl.multiple_of((unit - base) * tall_of + first, EDGE)
+                beside = pl.multiple_of(unit * tall_of + first, EDGE)
+                put(
+                    unit + shift, pl.ds(at_row, rows), cells, pl.ds(start, rows), side,
+                    pl.ds(beside, rows),
+                )
 
     def assemble_all(order):
         assemble(order, copies, whole_rows)
@@ -454,11 +437,11 @@
     if between:
         from_left = lax.broadcasted_iota(jnp.int32, (HALO, SIDE), 1) >= SIDE // 2
         for number, rows in enumerate((above_ref, below_ref)):
+            if between[number] is None:
+                continue
             corner = jnp.zeros((HALO, SIDE), jnp.float32)
             if not bare:
-                _, left, right = chunks[0][0]
-                first = left.shape[1] + (number - 2) * SIDE
-                here = slice(first, first + SIDE)
+                here = slice(corners + number * SIDE, corners + (number + 1) * SIDE)
                 corner = jnp.where(from_left, left[:, here], right[:, here])
             if mend:
                 wide = jnp.concatenate([rows[:, :SIDE], rows[:, TX - SIDE :], corner], axis=1)
@@ -557,12 +540,11 @@
             copy.wait()
 
 
-def stage(plan, mine, taps, between, tables, chunks, lots, mend=None, mend_tables=(), held=()):
+def stage(plan, mine, taps, between, tables, chunks, cells, beside=(), heights=(), mend=None, mend_tables=(), held=()):
     fields = plan[0]
     spans, tall = fields["spans"], fields["tall"]
     shape = jax.ShapeDtypeStruct((TY, TX), jnp.float32)
-    flat = [array for parts in chunks for part in parts for array in part]
-    vmems = [*between, *tables, *mend_tables, *flat]
+    vmems = [*between, *tables, *mend_tables, *beside, *[array for parts in cells for array in parts]]
     out = pltpu.VMEM((spans, tall - 2 * fields["margin"], TX), jnp.float32)
     scratch = [pltpu.VMEM((spans, tall, WIDE), jnp.bfloat16), out, out, pltpu.SemaphoreType.DMA((spans, 2))]
     if mend:
@@ -571,12 +553,10 @@
             pltpu.VMEM((2, 2, TY, SIDE), jnp.float32),
             pltpu.SemaphoreType.DMA((2, 2)),
         ]
-    if not fields["bare"]:
-        scratch += [
-            pltpu.VMEM((part[0].shape[0], SIDE), jnp.bfloat16) for parts in chunks for part in parts
-        ]
+    for height in heights:
+        scratch += [pltpu.VMEM((height, SIDE), jnp.bfloat16)] * fields["visits"]
     return pl.pallas_call(
-        functools.partial(stage_kernel, plan, mend, lots),
+        functools.partial(stage_kernel, plan, mend, chunks, heights),
         out_shape=(shape, shape),
         in_specs=[SMEM, SMEM] + [VMEM] * len(vmems) + [HBM] * len(held),
         out_specs=(HBM, HBM),
@@ -590,38 +570,43 @@
     )(mine, taps, *vmems, *held)
 
 
-def outer_plan(lot):
+def outer_plan(lot, begin, end, pieces):
     fields = dict(
-        visits=2, bare=True, spans=UNITS + 1, tall=2 * lot, margin=HALO, between=(lot - EDGE, lot),
-        blank=[(0, 0, lot - EDGE), (UNITS, lot + EDGE, lot - EDGE)],
-    )
-    copies = [(0, 1, 0, lot, 0, 0, UNITS, 1), (0, 0, 0, lot, lot, 0, UNITS, 0)]
+        visits=2, spans=end - begin, tall=2 * lot, margin=HALO, held=0 if begin == 0 else 2,
+        between=(lot - EDGE if begin == 0 else None, lot if end == UNITS + 1 else None),
+        blank=([(0, 0, lot - EDGE)] if begin == 0 else [])
+        + ([(end - begin - 1, lot + EDGE, lot - EDGE)] if end == UNITS + 1 else []),
+    )
+    copies = []
+    for chunk, first, last in pieces:
+        copies.append((chunk, 1, 0, lot, 0, max(first, begin - 1), min(last, end - 1), 1 - begin))
+        copies.append((chunk, 0, 0, lot, lot, max(first, begin), min(last, end), -begin))
     rows = lot - HALO
-    outs = [
-        (0, 1, rows, rows, 0),
-        (1, UNITS, 0, 2 * rows, -rows),
-        (UNITS, UNITS + 1, 0, rows, -rows),
+    outs = []
+    if begin == 0:
+        outs.append((0, 1, rows, rows, 0))
+    outs.append((max(begin, 1) - begin, min(end, UNITS) - begin, 0, 2 * rows, begin * STEP - rows))
+    if end == UNITS + 1:
+        outs.append((UNITS - begin, end - begin, 0, rows, begin * STEP - rows))
+    return fields, [copy for copy in copies if copy[5] < copy[6]], outs
+
+
+def inner_plan(lot, inner, pieces):
+    tall = 2 * inner + 2 * EDGE
+    fields = dict(visits=2, spans=UNITS, tall=tall, margin=HALO, between=None, blank=[], held=2)
+    copies = [
+        (len(pieces), 0, 0, inner, EDGE, 0, UNITS, 0),
+        (len(pieces), 1, 0, inner, EDGE + inner, 0, UNITS, 0),
     ]
-    return fields, copies, outs
-
-
-def inner_plan(lot, inner):
-    tall = 2 * inner + 2 * EDGE
-    fields = dict(
-        visits=2, bare=False, spans=UNITS, tall=tall, margin=HALO, between=None, blank=[]
-    )
-    copies = [
-        (0, 0, lot - EDGE, EDGE, 0, 0, UNITS, 0),
-        (1, 0, 0, inner, EDGE, 0, UNITS, 0),
-        (1, 1, 0, inner, EDGE + inner, 0, UNITS, 0),
-        (0, 1, 0, EDGE, EDGE + 2 * inner, 0, UNITS, 0),
-    ]
+    for chunk, first, last in pieces:
+        copies.append((chunk, 0, lot - EDGE, EDGE, 0, first, last, 0))
+        copies.append((chunk, 1, 0, EDGE, EDGE + 2 * inner, first, last, 0))
     return fields, copies, [(0, UNITS, 0, tall - 2 * HALO, lot - HALO)]
 
 
 def whole_plan(lot, visits):
     fields = dict(
-        visits=visits, bare=False, spans=UNITS, tall=STEP + 2 * EDGE, margin=EDGE,
+        visits=visits, spans=UNITS, tall=STEP + 2 * EDGE, margin=EDGE, held=0,
         between=(0, EDGE + STEP), blank=[],
     )
     copies = [(0, visit, 0, lot, EDGE + visit * lot, 0, UNITS, 0) for visit in range(visits)]
@@ -656,28 +641,38 @@
         all_of = [lax.all_gather(part, "visit") for part in (coadd, strip, edge)]
         between = neighbours(all_of[2][0, :HALO], all_of[2][visits - 1, HALO:], "py")
         sides = beyond([all_of[1][visit] for visit in range(visits)], *between)
-        parts = [(all_of[0][visit], *sides) for visit in range(visits)]
-        return stage(every, mine, psf_taps, between, bands(every, psf_taps), [parts], lots)
-
-    outer, inner = outer_plan(lots[0]), inner_plan(*lots)
+        cells = [all_of[0][visit] for visit in range(visits)]
+        height = lots[0] * UNITS
+        return stage(
+            every, mine, psf_taps, between, bands(every, psf_taps), [(lots[0], 0, 0)], [cells], sides, [height]
+        )
+
+    lot, inner_lot = lots
+    ranges = [(0, CUT), (CUT - 1, UNITS)]
+    first_part = outer_plan(lot, 0, CUT, [(0, 0, CUT)])
+    second_part = outer_plan(lot, CUT, UNITS + 1, [(0, CUT - 1, UNITS)])
+    pieces = [(0, 0, CUT), (1, CUT, UNITS)]
+    outer, inner = outer_plan(lot, 0, UNITS + 1, pieces), inner_plan(lot, inner_lot, pieces)
     tables, inv_var = lax.optimization_barrier(
         ([bands(part, psf_taps) for part in (outer, inner)], inv_var)
     )
     arrived, later = lax.optimization_barrier((arrived, make(1, inv_var)))
     second = send(later)
     code = codes(arrived)
-    coadd, strip, edge = place(code, arrived, lots[0])
-    other = swapped(coadd)
+    *cells, strip, edge = place(code, arrived, lot, ranges)
+    cells = [(piece, swapped(piece)) for piece in cells]
+    strips = [strip, swapped(strip)]
     between = rows_between(edge)
-    sides = beyond([strip, swapped(strip)], *between)
-    parts = [(coadd, *sides), (other, *sides)]
-    held = stage(outer, mine, psf_taps, between, tables[0], [[(coadd,), (other,)]], lots[:1])
+    held = stage(first_part, mine, psf_taps, between, tables[0], [(lot, 0, 0)], cells[:1])
+    held = stage(
+        second_part, mine, psf_taps, between, tables[0], [(lot, CUT - 1, 0)], cells[1:], held=held
+    )
     second, held = lax.optimization_barrier((second, held))
-    coadd, strip, _ = place(code, second, lots[1])
-    own_sides, other_sides = straight_to_both(strip)
-    more = [(coadd, *own_sides), (swapped(coadd), *other_sides)]
+    coadd, strip, _ = place(code, second, inner_lot)
+    sides = beyond([*strips, strip, swapped(strip)], *between)
     return stage(
-        inner, mine, psf_taps, between, tables[1], [parts, more], lots, outer, tables[0], held
+        inner, mine, psf_taps, between, tables[1], [(lot, 0, 0), (lot, CUT - 1, 0), (inner_lot, 0, 1)],
+        [*cells, (coadd, swapped(coadd))], sides, [lot * UNITS, inner_lot * UNITS], outer, tables[0], held,
     )
 
 

time: 253 us -> 249 us (0.984)
  starting transfers between devices: 42.2 us -> 32.3 us
    ppermute x2 -> x0, starting transfers between devices: 8.91 us -> none  [the longest x1 7.62 us: straight_to_both(): lax.ppermute(last, ('visit', 'px'), crossed(up))]
    ppermute x4 -> x2, waiting for transfers between devices: 1.26 us -> 6.12 us  [neighbours(): return (lax.ppermute(last, axis, up), lax.ppermute(first, axis, down))]
    ppermute x4 -> x2, starting transfers between devices: 9.12 us -> 4.71 us  [neighbours(): return (lax.ppermute(last, axis, up), lax.ppermute(first, axis, down))]
    ppermute x3 -> x5, starting transfers between devices: 5.9 us -> 9.32 us  [swapped(): return lax.ppermute(array, 'visit', [(0, 1), (1, 0)])]
    ppermute x3 -> x5, waiting for transfers between devices: 24.6 us -> 22.7 us  [swapped(): return lax.ppermute(array, 'visit', [(0, 1), (1, 0)])]
    pallas_call x4 -> x5, Pallas kernels: 32.9 us -> 34.1 us  [the longest x3 24.6 us: stage(): pl.pallas_call(functools.partial(stage_kernel, plan, mend, chunks, height...]
  transfers between devices with their start and end apart: 13 -> 11, of which waited for: 3 -> 5; matrix products, arithmetic and copies ran while one was open for 6% -> 7% of each run, Pallas kernels for 12% -> 12%
where the time goes in v8:
time: 249 us
  waiting for transfers between devices  142 us (57%)
  Pallas kernels  52 us (21%)
  starting transfers between devices  32.3 us (13%)
  other arithmetic  15 us (6%)
  local copies, waits for them, and re-layouts  5.97 us (2%)
    all_to_all x2, waiting for transfers between devices, send(): lax.all_to_all(blocks, EVERY, split_axis=0, concat_axis=0, tiled=True)  114 us
    pallas_call x3, Pallas kernels, stage(): pl.pallas_call(functools.partial(stage_kernel, plan, mend, chunks, height...  24.6 us
    ppermute x5, waiting for transfers between devices, swapped(): return lax.ppermute(array, 'visit', [(0, 1), (1, 0)])  22.7 us
    pallas_call x2, Pallas kernels, warp(): pl.pallas_call(functools.partial(warp_kernel, tiles, share, noted), out_s...  17.9 us
    all_to_all x2, starting transfers between devices, send(): lax.all_to_all(blocks, EVERY, split_axis=0, concat_axis=0, tiled=True)  16.3 us
    pallas_call x2, Pallas kernels, place(): pl.pallas_call(functools.partial(place_kernel, 2 * lot, pieces), grid_spe...  9.49 us
    ppermute x5, starting transfers between devices, swapped(): return lax.ppermute(array, 'visit', [(0, 1), (1, 0)])  9.32 us
    convert_element_type x2, other arithmetic, split(): coarse = value.astype(jnp.bfloat16)  9.11 us
  transfers between devices with their start and end apart: 11, of which 5 were waited for; matrix products, arithmetic and copies ran while one was open for 7% of the time, Pallas kernels for 12%

profile of v8, /device:TPU:0, one launch (start us, length us, event | category | flops | bytes accessed | tf_op | source)
XLA Modules:
  0.0 248.6 jit_solution(3294442498105500579)
XLA Ops:
  0.6 9.4 %warp.2 = bf16[32,784,128]{2,1,0:T(8,128)(2,1)} custom-call(s32[24]{0:T(128)} %visit_ref.3, s32[24]{0:T(128)} %bitcast.12, s32[2,24]{1,0:T(2,128)} %bitcast.10, s32[8,256]{1,0:T(8,128)} %good_ref.3, bf16[8,256,256]{2,1,0:T(8,128)(2,1)} %rows_hbm.3, bf16[8,256,256]{2,1,0:T(8,128)(2,1)} %cols_hbm.3, bf16[24,256,256]{2,1,0:T(8,128)(2,1)} %var_hbm.2, ...), custom_call_target="tpu_custom_call" | custom-call | flops 3221225472 | bytes 12582912 | tf_op jit(solution)/shard_map/warp/pallas_call | solution.py:159
  10.1 7.4 %all-to-all-start = ((bf16[32,784,128]{2,1,0:T(8,128)(2,1)}), bf16[32,784,128]{2,1,0:T(8,128)(2,1)}, u32[]{:S(2)}, u32[]{:S(2)}) async-start(bf16[32,784,128]{2,1,0:T(8,128)(2,1)} %warp.2), calls=%async_computation | async-start | bytes 12845056 | tf_op jit(solution)/shard_map/all_to_all | solution.py:634
  19.0 0.7 add_convert_fusion.2.refs_4_
  19.7 4.5 %fusion.16 = (bf16[48,64]{1,0:T(8,128)(2,1)S(1)}, bf16[48,64]{1,0:T(8,128)(2,1)S(1)}) fusion(f32[]{:T(128)} %bitcast.9, f32[]{:T(128)} %bitcast.8, f32[]{:T(128)} %bitcast.7, f32[]{:T(128)} %bitcast.6, f32[]{:T(128)} %bitcast.5, f32[]{:T(128)} %bitcast.4, f32[]{:T(128)} %bitcast.3, s32[48]{0:T(128)S(1)} %iota_add_fusion), kind=kLoop, calls=%fused_computation.49 | loop fusion | flops 79872 | bytes 12508 | tf_op jit(solution)/shard_map/convert_element_type | solution.py:305
  25.0 0.7 add_convert_fusion.1.refs_5_.refs_9_
  25.7 0.7 add_convert_fusion.refs_4_.refs_8_
  26.4 4.6 %fusion.15 = (bf16[80,96]{1,0:T(8,128)(2,1)S(1)}, bf16[80,96]{1,0:T(8,128)(2,1)S(1)}) fusion(f32[]{:T(128)} %bitcast.9, f32[]{:T(128)} %bitcast.8, f32[]{:T(128)} %bitcast.7, f32[]{:T(128)} %bitcast.6, f32[]{:T(128)} %bitcast.5, f32[]{:T(128)} %bitcast.4, f32[]{:T(128)} %bitcast.3, s32[80]{0:T(128)S(1)} %iota_add_fusion.1), kind=kLoop, calls=%fused_computation.45 | loop fusion | flops 199680 | bytes 31068 | tf_op jit(solution)/shard_map/convert_element_type | solution.py:305
  30.9 0.7 pad_maximum_fusion.refs_6_.refs_10_
  31.7 0.8 fusion.refs_7_.refs_11_
  32.5 8.5 %warp.3 = bf16[32,256,128]{2,1,0:T(8,128)(2,1)} custom-call(s32[24]{0:T(128)} %visit_ref.3, s32[24]{0:T(128)} %bitcast.13, s32[2,24]{1,0:T(2,128)} %bitcast.11, s32[8,256]{1,0:T(8,128)} %good_ref.3, bf16[8,256,256]{2,1,0:T(8,128)(2,1)} %rows_hbm.3, bf16[8,256,256]{2,1,0:T(8,128)(2,1)} %cols_hbm.3, bf16[24,256,256]{2,1,0:T(8,128)(2,1)} %var_hbm.2, ...), custom_call_target="tpu_custom_call" | custom-call | flops 3221225472 | bytes 12582912 | tf_op jit(solution)/shard_map/warp/pallas_call | solution.py:159
  41.0 113.5 %all-to-all-done.blocks_ref = bf16[32,784,128]{2,1,0:T(8,128)(2,1)} async-done(((bf16[32,784,128]{2,1,0:T(8,128)(2,1)}), bf16[32,784,128]{2,1,0:T(8,128)(2,1)}, u32[]{:S(2)}, u32[]{:S(2)}) %all-to-all-start) | async-done | bytes 6422560 | tf_op jit(solution)/shard_map/all_to_all | solution.py:634
  154.5 8.9 %all-to-all-start.1 = ((bf16[32,256,128]{2,1,0:T(8,128)(2,1)}), bf16[32,256,128]{2,1,0:T(8,128)(2,1)S(1)}, u32[]{:S(2)}, u32[]{:S(2)}) async-start(bf16[32,256,128]{2,1,0:T(8,128)(2,1)} %warp.3), calls=%async_computation.1 | async-start | bytes 4194304 | tf_op jit(solution)/shard_map/all_to_all | solution.py:634
  163.4 1.0 slice.87
  164.6 6.9 %place.2 = (bf16[288,1024]{1,0:T(8,128)(2,1)S(1)}, bf16[144,1024]{1,0:T(8,128)(2,1)S(1)}, f32[16,384]{1,0:T(8,128)S(1)}, f32[16,1024]{1,0:T(8,128)S(1)}) custom-call(s32[64]{0:T(128)S(1)} %convert_element_type.49.code_ref, bf16[32,784,128]{2,1,0:T(8,128)(2,1)} %all-to-all-done.blocks_ref), custom_call_target="tpu_custom_call" | custom-call | flops 3211264 | bytes 6422528 | tf_op jit(solution)/shard_map/place/pallas_call | solution.py:230
  172.2 1.3 collective-permute-start.1
  173.5 5.3 %collective-permute-start.4 = (bf16[288,1024]{1,0:T(8,128)(2,1)S(1)}, bf16[288,1024]{1,0:T(8,128)(2,1)S(1)}, u32[]{:S(2)}, u32[]{:S(2)}) collective-permute-start(bf16[288,1024]{1,0:T(8,128)(2,1)S(1)} %get-tuple-element.44.refs_8_.refs_14_), channel_id=1, source_target_pairs={{0,16},{16,0},{1,17},{17,1},{2,18},{18,2},{3,19},{19,3},{4,20},{20... | collective-permute-start | bytes 1769480 | tf_op jit(solution)/shard_map/ppermute | solution.py:260
  178.9 1.9 collective-permute-start.3
  180.8 21.0 %collective-permute-done.2 = f32[16,384]{1,0:T(8,128)S(1)} collective-permute-done((f32[16,384]{1,0:T(8,128)S(1)}, f32[16,384]{1,0:T(8,128)S(1)}, u32[]{:S(2)}, u32[]{:S(2)}) %collective-permute-start.2) | collective-permute-done | bytes 24608 | tf_op jit(solution)/shard_map/ppermute | solution.py:260
  202.4 0.8 copy-done.3
  203.2 8.2 %stage.3 = (f32[1024,1024]{1,0:T(8,128)}, f32[1024,1024]{1,0:T(8,128)}) custom-call(s32[1]{0:T(128)} %bitcast.refs_0_, f32[7]{0:T(128)} %refs_1_.2, f32[8,1024]{1,0:T(8,128)} %get-tuple-element.55.refs_2_, f32[8,1024]{1,0:T(8,128)} %get-tuple-element.54.refs_3_, bf16[96,192]{1,0:T(8,128)(2,1)} %add_convert_fusion.refs_4_.refs_8_, ...), custom_call_target="tpu_custom_call" | custom-call | flops 53084160 | bytes 7962624 | tf_op jit(solution)/shard_map/stage/pallas_call | solution.py:558
  211.5 0.7 copy-done.4
  212.2 5.1 %stage.4 = (f32[1024,1024]{1,0:T(8,128)}, f32[1024,1024]{1,0:T(8,128)}) custom-call(s32[1]{0:T(128)} %bitcast.refs_0_, f32[7]{0:T(128)} %refs_1_.2, f32[8,1024]{1,0:T(8,128)} %get-tuple-element.55.refs_2_, f32[8,1024]{1,0:T(8,128)} %get-tuple-element.54.refs_3_, ...), custom_call_target="tpu_custom_call", output_to_operand_aliasing={{0}: (10, {}), {1}: (11, {})} | custom-call | flops 26542080 | bytes 3981312 | tf_op jit(solution)/shard_map/stage/pallas_call | solution.py:558
  217.3 2.6 %place.3 = (bf16[128,1024]{1,0:T(8,128)(2,1)S(1)}, f32[16,128]{1,0:T(8,128)S(1)}, f32[16,1024]{1,0:T(8,128)}) custom-call(s32[64]{0:T(128)S(1)} %convert_element_type.49.code_ref, bf16[32,256,128]{2,1,0:T(8,128)(2,1)S(1)} %all-to-all-done.1.blocks_ref), custom_call_target="tpu_custom_call" | custom-call | flops 1048576 | bytes 2097152 | tf_op jit(solution)/shard_map/place/pallas_call | solution.py:230
  219.9 1.0 collective-permute-start.5
  220.9 1.0 collective-permute-start.8
  221.9 1.7 collective-permute-done.5
  223.6 0.7 constant_dynamic-update-slice_fusion.7
  225.0 3.4 %collective-permute-start.6 = (f32[8,1280]{1,0:T(8,128)S(1)}, f32[8,1280]{1,0:T(8,128)S(1)}, u32[]{:S(2)}, u32[]{:S(2)}) collective-permute-start(f32[8,1280]{1,0:T(8,128)S(1)} %get-tuple-element.57), channel_id=1, source_target_pairs={{0,1},{1,2},{2,3},{4,5},{5,6},{6,7},{8,9},{9,10},{10,11},{12,13},{... | collective-permute-start | bytes 122888 | tf_op jit(solution)/shard_map/ppermute | solution.py:256
  228.4 1.3 collective-permute-start.7
  230.1 5.8 %collective-permute-done.7.refs_13_ = f32[8,1280]{1,0:T(8,128)S(1)} collective-permute-done((f32[8,1280]{1,0:T(8,128)S(1)}, f32[8,1280]{1,0:T(8,128)S(1)}, u32[]{:S(2)}, u32[]{:S(2)}) %collective-permute-start.7) | collective-permute-done | bytes 40992 | tf_op jit(solution)/shard_map/ppermute | solution.py:256
  236.5 0.7 copy-done.5
  237.2 11.3 %stage.5 = (f32[1024,1024]{1,0:T(8,128)}, f32[1024,1024]{1,0:T(8,128)}) custom-call(s32[1]{0:T(128)} %bitcast.refs_0_, f32[7]{0:T(128)} %refs_1_.2, f32[8,1024]{1,0:T(8,128)} %get-tuple-element.55.refs_2_, f32[8,1024]{1,0:T(8,128)} %get-tuple-element.54.refs_3_, ...), custom_call_target="tpu_custom_call", output_to_operand_aliasing={{0}: (20, {}), {1}: (21, {})} | custom-call | flops 47185920 | bytes 7077888 | tf_op jit(solution)/shard_map/stage/pallas_call | solution.py:558
  (44 shorter events, 5.4 us)
Async XLA Ops:
  10.0 8.3 %copy-start.6 = (f32[7]{0:T(128)S(1)}, f32[7]{0:T(128)}, u32[]{:S(2)}) copy-start(f32[7]{0:T(128)} %refs_1_.2) | copy-start | bytes 88
  10.1 144.5 %all-to-all-start = ((bf16[32,784,128]{2,1,0:T(8,128)(2,1)}), bf16[32,784,128]{2,1,0:T(8,128)(2,1)}, u32[]{:S(2)}, u32[]{:S(2)}) async-start(bf16[32,784,128]{2,1,0:T(8,128)(2,1)} %warp.2), calls=%async_computation | async-start | bytes 12845056 | tf_op jit(solution)/shard_map/all_to_all | solution.py:634
  154.5 62.8 %all-to-all-start.1 = ((bf16[32,256,128]{2,1,0:T(8,128)(2,1)}), bf16[32,256,128]{2,1,0:T(8,128)(2,1)S(1)}, u32[]{:S(2)}, u32[]{:S(2)}) async-start(bf16[32,256,128]{2,1,0:T(8,128)(2,1)} %warp.3), calls=%async_computation.1 | async-start | bytes 4194304 | tf_op jit(solution)/shard_map/all_to_all | solution.py:634
  171.5 30.9 %copy-start = (bf16[288,1024]{1,0:T(8,128)(2,1)}, bf16[288,1024]{1,0:T(8,128)(2,1)S(1)}, u32[]{:S(2)}) copy-start(bf16[288,1024]{1,0:T(8,128)(2,1)S(1)} %get-tuple-element.44.refs_8_.refs_14_) | copy-start | bytes 1769476
  171.5 39.9 %copy-start.1 = (bf16[144,1024]{1,0:T(8,128)(2,1)}, bf16[144,1024]{1,0:T(8,128)(2,1)S(1)}, u32[]{:S(2)}) copy-start(bf16[144,1024]{1,0:T(8,128)(2,1)S(1)} %get-tuple-element.43.refs_8_.refs_16_) | copy-start | bytes 884740
  171.5 30.2 %collective-permute-start = (f32[8,1024]{1,0:T(8,128)S(1)}, f32[8,1024]{1,0:T(8,128)S(1)}, u32[]{:S(2)}, u32[]{:S(2)}) collective-permute-start(f32[8,1024]{1,0:T(8,128)S(1)} %slice_select_fusion), channel_id=1, source_target_pairs={{4,16},{8,20},{12,24},{16,4},{20,8},{24,12},{5,17},{9,21},{13,25},... | collective-permute-start | bytes 98312 | tf_op jit(solution)/shard_map/ppermute | solution.py:281
  172.2 29.6 %collective-permute-start.1 = (f32[8,1024]{1,0:T(8,128)S(1)}, f32[8,1024]{1,0:T(8,128)S(1)}, u32[]{:S(2)}, u32[]{:S(2)}) collective-permute-start(f32[8,1024]{1,0:T(8,128)S(1)} %slice_select_fusion), channel_id=1, source_target_pairs={{4,0},{8,4},{12,8},{16,20},{20,24},{24,28},{5,1},{9,5},{13,9},{17,... | collective-permute-start | bytes 98312 | tf_op jit(solution)/shard_map/ppermute | solution.py:280
  173.5 28.9 %collective-permute-start.4 = (bf16[288,1024]{1,0:T(8,128)(2,1)S(1)}, bf16[288,1024]{1,0:T(8,128)(2,1)S(1)}, u32[]{:S(2)}, u32[]{:S(2)}) collective-permute-start(bf16[288,1024]{1,0:T(8,128)(2,1)S(1)} %get-tuple-element.44.refs_8_.refs_14_), channel_id=1, source_target_pairs={{0,16},{16,0},{1,17},{17,1},{2,18},{18,2},{3,19},{19,3},{4,20},{20... | collective-permute-start | bytes 1769480 | tf_op jit(solution)/shard_map/ppermute | solution.py:260
  178.8 23.0 %collective-permute-start.2 = (f32[16,384]{1,0:T(8,128)S(1)}, f32[16,384]{1,0:T(8,128)S(1)}, u32[]{:S(2)}, u32[]{:S(2)}) collective-permute-start(f32[16,384]{1,0:T(8,128)S(1)} %get-tuple-element.41), channel_id=1, source_target_pairs={{0,16},{16,0},{1,17},{17,1},{2,18},{18,2},{3,19},{19,3},{4,20},{20... | collective-permute-start | bytes 73736 | tf_op jit(solution)/shard_map/ppermute | solution.py:260
  178.9 32.6 %collective-permute-start.3 = (bf16[144,1024]{1,0:T(8,128)(2,1)S(1)}, bf16[144,1024]{1,0:T(8,128)(2,1)S(1)}, u32[]{:S(2)}, u32[]{:S(2)}) collective-permute-start(bf16[144,1024]{1,0:T(8,128)(2,1)S(1)} %get-tuple-element.43.refs_8_.refs_16_), channel_id=1, source_target_pairs={{0,16},{16,0},{1,17},{17,1},{2,18},{18,2},{3,19},{19,3},{4,20},{20... | collective-permute-start | bytes 884744 | tf_op jit(solution)/shard_map/ppermute | solution.py:260
  202.4 0.8 copy-start.3
  211.4 0.7 copy-start.4
  219.9 16.0 %copy-start.2 = (bf16[128,1024]{1,0:T(8,128)(2,1)}, bf16[128,1024]{1,0:T(8,128)(2,1)S(1)}, u32[]{:S(2)}) copy-start(bf16[128,1024]{1,0:T(8,128)(2,1)S(1)} %get-tuple-element.51.refs_18_) | copy-start | bytes 786436
  219.9 3.7 %collective-permute-start.5 = (f32[16,128]{1,0:T(8,128)S(1)}, f32[16,128]{1,0:T(8,128)S(1)}, u32[]{:S(2)}, u32[]{:S(2)}) collective-permute-start(f32[16,128]{1,0:T(8,128)S(1)} %get-tuple-element.50), channel_id=1, source_target_pairs={{0,16},{16,0},{1,17},{17,1},{2,18},{18,2},{3,19},{19,3},{4,20},{20... | collective-permute-start | bytes 24584 | tf_op jit(solution)/shard_map/ppermute | solution.py:260
  220.9 15.0 %collective-permute-start.8 = (bf16[128,1024]{1,0:T(8,128)(2,1)S(1)}, bf16[128,1024]{1,0:T(8,128)(2,1)S(1)}, u32[]{:S(2)}, u32[]{:S(2)}) collective-permute-start(bf16[128,1024]{1,0:T(8,128)(2,1)S(1)} %get-tuple-element.51.refs_18_), channel_id=1, source_target_pairs={{0,16},{16,0},{1,17},{17,1},{2,18},{18,2},{3,19},{19,3},{4,20},{20... | collective-permute-start | bytes 786440 | tf_op jit(solution)/shard_map/ppermute | solution.py:260
  225.0 5.1 %collective-permute-start.6 = (f32[8,1280]{1,0:T(8,128)S(1)}, f32[8,1280]{1,0:T(8,128)S(1)}, u32[]{:S(2)}, u32[]{:S(2)}) collective-permute-start(f32[8,1280]{1,0:T(8,128)S(1)} %get-tuple-element.57), channel_id=1, source_target_pairs={{0,1},{1,2},{2,3},{4,5},{5,6},{6,7},{8,9},{9,10},{10,11},{12,13},{... | collective-permute-start | bytes 122888 | tf_op jit(solution)/shard_map/ppermute | solution.py:256
  228.4 7.4 %collective-permute-start.7 = (f32[8,1280]{1,0:T(8,128)S(1)}, f32[8,1280]{1,0:T(8,128)S(1)}, u32[]{:S(2)}, u32[]{:S(2)}) collective-permute-start(f32[8,1280]{1,0:T(8,128)S(1)} %get-tuple-element.56), channel_id=1, source_target_pairs={{1,0},{2,1},{3,2},{5,4},{6,5},{7,6},{9,8},{10,9},{11,10},{13,12},{... | collective-permute-start | bytes 122888 | tf_op jit(solution)/shard_map/ppermute | solution.py:256
  230.1 5.8 %copy-start.7 = (f32[8,1280]{1,0:T(8,128)}, f32[8,1280]{1,0:T(8,128)S(1)}, u32[]{:S(2)}) copy-start(f32[8,1280]{1,0:T(8,128)S(1)} %collective-permute-done.6.refs_12_) | copy-start | bytes 122884
  235.8 0.6 copy-start.8
  236.5 0.7 copy-start.5

commit v9 on v8

--- a/solution.py
+++ b/solution.py
@@ -661,7 +661,7 @@
     code = codes(arrived)
     *cells, strip, edge = place(code, arrived, lot, ranges)
     cells = [(piece, swapped(piece)) for piece in cells]
-    strips = [strip, swapped(strip)]
+    outer_strip = strip
     between = rows_between(edge)
     held = stage(first_part, mine, psf_taps, between, tables[0], [(lot, 0, 0)], cells[:1])
     held = stage(
@@ -669,7 +669,11 @@
     )
     second, held = lax.optimization_barrier((second, held))
     coadd, strip, _ = place(code, second, inner_lot)
-    sides = beyond([*strips, strip, swapped(strip)], *between)
+    height = lot * UNITS
+    strip = jnp.concatenate([outer_strip, strip], axis=1)
+    other = swapped(strip)
+    strips = [half[:, span] for span in (slice(height), slice(height, None)) for half in (strip, other)]
+    sides = beyond(strips, *between)
     return stage(
         inner, mine, psf_taps, between, tables[1], [(lot, 0, 0), (lot, CUT - 1, 0), (inner_lot, 0, 1)],
         [*cells, (coadd, swapped(coadd))], sides, [lot * UNITS, inner_lot * UNITS], outer, tables[0], held,

time: 249 us -> 254 us (1.020)
  starting transfers between devices: 32.3 us -> 37.5 us
    ppermute x1, waiting for transfers between devices: 0.01 us -> 4.42 us  [rows_between(): straight = lax.ppermute(mine, ('visit', 'py'), pairs(0))]
    ppermute x5 -> x4, starting transfers between devices: 9.32 us -> 13.5 us  [swapped(): return lax.ppermute(array, 'visit', [(0, 1), (1, 0)])]
    ppermute x5 -> x4, waiting for transfers between devices: 22.7 us -> 19 us  [swapped(): return lax.ppermute(array, 'visit', [(0, 1), (1, 0)])]
  transfers between devices with their start and end apart: 11 -> 10, of which waited for: 5 -> 7; matrix products, arithmetic and copies ran while one was open for 7% -> 7% of each run, Pallas kernels for 12% -> 11%
where the time goes in v9:
time: 254 us; the launch traced here: 252 us
  waiting for transfers between devices  142 us (56%)
  Pallas kernels  51.9 us (20%)
  starting transfers between devices  37.5 us (15%)
  other arithmetic  14.9 us (6%)
  local copies, waits for them, and re-layouts  5.15 us (2%)
    all_to_all x2, waiting for transfers between devices, send(): lax.all_to_all(blocks, EVERY, split_axis=0, concat_axis=0, tiled=True)  114 us
    pallas_call x3, Pallas kernels, stage(): pl.pallas_call(functools.partial(stage_kernel, plan, mend, chunks, height...  24.6 us
    ppermute x4, waiting for transfers between devices, swapped(): return lax.ppermute(array, 'visit', [(0, 1), (1, 0)])  19 us
    pallas_call x2, Pallas kernels, warp(): pl.pallas_call(functools.partial(warp_kernel, tiles, share, noted), out_s...  17.8 us
    all_to_all x2, starting transfers between devices, send(): lax.all_to_all(blocks, EVERY, split_axis=0, concat_axis=0, tiled=True)  16.3 us
    ppermute x4, starting transfers between devices, swapped(): return lax.ppermute(array, 'visit', [(0, 1), (1, 0)])  13.5 us
    pallas_call x2, Pallas kernels, place(): pl.pallas_call(functools.partial(place_kernel, 2 * lot, pieces), grid_spe...  9.47 us
    convert_element_type x2, other arithmetic, split(): coarse = value.astype(jnp.bfloat16)  8.98 us
  transfers between devices with their start and end apart: 10, of which 7 were waited for; matrix products, arithmetic and copies ran while one was open for 7% of the time, Pallas kernels for 11%

profile of v9, /device:TPU:0, one launch (start us, length us, event | category | flops | bytes accessed | tf_op | source)
XLA Modules:
  0.0 252.1 jit_solution(11626366687960842428)
XLA Ops:
  0.6 9.3 %warp.2 = bf16[32,784,128]{2,1,0:T(8,128)(2,1)} custom-call(s32[24]{0:T(128)} %visit_ref.3, s32[24]{0:T(128)} %bitcast.12, s32[2,24]{1,0:T(2,128)} %bitcast.10, s32[8,256]{1,0:T(8,128)} %good_ref.3, bf16[8,256,256]{2,1,0:T(8,128)(2,1)} %rows_hbm.3, bf16[8,256,256]{2,1,0:T(8,128)(2,1)} %cols_hbm.3, bf16[24,256,256]{2,1,0:T(8,128)(2,1)} %var_hbm.2, ...), custom_call_target="tpu_custom_call" | custom-call | flops 3221225472 | bytes 12582912 | tf_op jit(solution)/shard_map/warp/pallas_call | solution.py:159
  10.0 7.4 %all-to-all-start = ((bf16[32,784,128]{2,1,0:T(8,128)(2,1)}), bf16[32,784,128]{2,1,0:T(8,128)(2,1)}, u32[]{:S(2)}, u32[]{:S(2)}) async-start(bf16[32,784,128]{2,1,0:T(8,128)(2,1)} %warp.2), calls=%async_computation | async-start | bytes 12845056 | tf_op jit(solution)/shard_map/all_to_all | solution.py:634
  19.6 4.5 %fusion.16 = (bf16[48,64]{1,0:T(8,128)(2,1)S(1)}, bf16[48,64]{1,0:T(8,128)(2,1)S(1)}) fusion(f32[]{:T(128)} %bitcast.9, f32[]{:T(128)} %bitcast.8, f32[]{:T(128)} %bitcast.7, f32[]{:T(128)} %bitcast.6, f32[]{:T(128)} %bitcast.5, f32[]{:T(128)} %bitcast.4, f32[]{:T(128)} %bitcast.3, s32[48]{0:T(128)S(1)} %iota_add_fusion), kind=kLoop, calls=%fused_computation.50 | loop fusion | flops 79872 | bytes 12508 | tf_op jit(solution)/shard_map/convert_element_type | solution.py:305
  24.1 0.7 pad_maximum_fusion.2.refs_6_
  24.9 0.7 add_convert_fusion.1.refs_5_.refs_9_
  25.6 0.7 add_convert_fusion.refs_4_.refs_8_
  26.3 4.5 %fusion.15 = (bf16[80,96]{1,0:T(8,128)(2,1)S(1)}, bf16[80,96]{1,0:T(8,128)(2,1)S(1)}) fusion(f32[]{:T(128)} %bitcast.9, f32[]{:T(128)} %bitcast.8, f32[]{:T(128)} %bitcast.7, f32[]{:T(128)} %bitcast.6, f32[]{:T(128)} %bitcast.5, f32[]{:T(128)} %bitcast.4, f32[]{:T(128)} %bitcast.3, s32[80]{0:T(128)S(1)} %iota_add_fusion.1), kind=kLoop, calls=%fused_computation.46 | loop fusion | flops 199680 | bytes 31068 | tf_op jit(solution)/shard_map/convert_element_type | solution.py:305
  30.8 0.7 pad_maximum_fusion.refs_6_.refs_10_
  31.5 0.8 fusion.refs_7_.refs_11_
  32.3 8.5 %warp.3 = bf16[32,256,128]{2,1,0:T(8,128)(2,1)} custom-call(s32[24]{0:T(128)} %visit_ref.3, s32[24]{0:T(128)} %bitcast.13, s32[2,24]{1,0:T(2,128)} %bitcast.11, s32[8,256]{1,0:T(8,128)} %good_ref.3, bf16[8,256,256]{2,1,0:T(8,128)(2,1)} %rows_hbm.3, bf16[8,256,256]{2,1,0:T(8,128)(2,1)} %cols_hbm.3, bf16[24,256,256]{2,1,0:T(8,128)(2,1)} %var_hbm.2, ...), custom_call_target="tpu_custom_call" | custom-call | flops 3221225472 | bytes 12582912 | tf_op jit(solution)/shard_map/warp/pallas_call | solution.py:159
  40.8 113.6 %all-to-all-done.blocks_ref = bf16[32,784,128]{2,1,0:T(8,128)(2,1)} async-done(((bf16[32,784,128]{2,1,0:T(8,128)(2,1)}), bf16[32,784,128]{2,1,0:T(8,128)(2,1)}, u32[]{:S(2)}, u32[]{:S(2)}) %all-to-all-start) | async-done | bytes 6422560 | tf_op jit(solution)/shard_map/all_to_all | solution.py:634
  154.5 8.9 %all-to-all-start.1 = ((bf16[32,256,128]{2,1,0:T(8,128)(2,1)}), bf16[32,256,128]{2,1,0:T(8,128)(2,1)S(1)}, u32[]{:S(2)}, u32[]{:S(2)}) async-start(bf16[32,256,128]{2,1,0:T(8,128)(2,1)} %warp.3), calls=%async_computation.1 | async-start | bytes 4194304 | tf_op jit(solution)/shard_map/all_to_all | solution.py:634
  163.4 1.0 slice.93
  164.5 6.9 %place.2 = (bf16[288,1024]{1,0:T(8,128)(2,1)S(1)}, bf16[144,1024]{1,0:T(8,128)(2,1)S(1)}, f32[16,384]{1,0:T(8,128)S(1)}, f32[16,1024]{1,0:T(8,128)S(1)}) custom-call(s32[64]{0:T(128)S(1)} %convert_element_type.49.code_ref, bf16[32,784,128]{2,1,0:T(8,128)(2,1)} %all-to-all-done.blocks_ref), custom_call_target="tpu_custom_call" | custom-call | flops 3211264 | bytes 6422528 | tf_op jit(solution)/shard_map/place/pallas_call | solution.py:230
  171.5 1.8 collective-permute-start.3
  174.2 1.3 collective-permute-start.1
  175.5 4.4 %collective-permute-done.1 = f32[8,1024]{1,0:T(8,128)S(1)} collective-permute-done((f32[8,1024]{1,0:T(8,128)S(1)}, f32[8,1024]{1,0:T(8,128)S(1)}, u32[]{:S(2)}, u32[]{:S(2)}) %collective-permute-start.1) | collective-permute-done | bytes 32800 | tf_op jit(solution)/shard_map/ppermute | solution.py:280
  180.6 15.6 %collective-permute-done.3.refs_9_.refs_15_ = bf16[288,1024]{1,0:T(8,128)(2,1)} collective-permute-done((bf16[288,1024]{1,0:T(8,128)(2,1)S(1)}, bf16[288,1024]{1,0:T(8,128)(2,1)}, u32[]{:S(2)}, u32[]{:S(2)}) %collective-permute-start.3) | collective-permute-done | bytes 589856 | tf_op jit(solution)/shard_map/ppermute | solution.py:260
  196.2 8.2 %stage.3 = (f32[1024,1024]{1,0:T(8,128)}, f32[1024,1024]{1,0:T(8,128)}) custom-call(s32[1]{0:T(128)} %bitcast.refs_0_, f32[7]{0:T(128)} %refs_1_.2, f32[8,1024]{1,0:T(8,128)} %get-tuple-element.55.refs_2_, f32[8,1024]{1,0:T(8,128)} %get-tuple-element.54.refs_3_, bf16[96,192]{1,0:T(8,128)(2,1)} %add_convert_fusion.refs_4_.refs_8_, ...), custom_call_target="tpu_custom_call" | custom-call | flops 53084160 | bytes 7962624 | tf_op jit(solution)/shard_map/stage/pallas_call | solution.py:558
  204.4 1.5 collective-permute-done.2.refs_9_.refs_17_
  205.9 0.7 copy-done.3
  206.7 5.1 %stage.4 = (f32[1024,1024]{1,0:T(8,128)}, f32[1024,1024]{1,0:T(8,128)}) custom-call(s32[1]{0:T(128)} %bitcast.refs_0_, f32[7]{0:T(128)} %refs_1_.2, f32[8,1024]{1,0:T(8,128)} %get-tuple-element.55.refs_2_, f32[8,1024]{1,0:T(8,128)} %get-tuple-element.54.refs_3_, ...), custom_call_target="tpu_custom_call", output_to_operand_aliasing={{0}: (10, {}), {1}: (11, {})} | custom-call | flops 26542080 | bytes 3981312 | tf_op jit(solution)/shard_map/stage/pallas_call | solution.py:558
  211.8 2.6 %place.3 = (bf16[128,1024]{1,0:T(8,128)(2,1)S(1)}, f32[16,128]{1,0:T(8,128)S(1)}, f32[16,1024]{1,0:T(8,128)}) custom-call(s32[64]{0:T(128)S(1)} %convert_element_type.49.code_ref, bf16[32,256,128]{2,1,0:T(8,128)(2,1)S(1)} %all-to-all-done.1.blocks_ref), custom_call_target="tpu_custom_call" | custom-call | flops 1048576 | bytes 2097152 | tf_op jit(solution)/shard_map/place/pallas_call | solution.py:230
  214.4 11.3 %collective-permute-start.4 = (f32[16,512]{1,0:T(8,128)S(1)}, f32[16,512]{1,0:T(8,128)S(1)}, u32[]{:S(2)}, u32[]{:S(2)}) collective-permute-start(f32[16,512]{1,0:T(8,128)S(1)} %pad_maximum_fusion.1), channel_id=1, source_target_pairs={{0,16},{16,0},{1,17},{17,1},{2,18},{18,2},{3,19},{19,3},{4,20},{20... | collective-permute-start | bytes 98312 | tf_op jit(solution)/shard_map/ppermute | solution.py:260
  225.8 1.8 collective-permute-done.4
  227.6 0.7 constant_dynamic-update-slice_fusion.7
  228.3 0.7 constant_dynamic-update-slice_fusion.6
  229.0 4.5 %collective-permute-start.5 = (f32[8,1280]{1,0:T(8,128)S(1)}, f32[8,1280]{1,0:T(8,128)S(1)}, u32[]{:S(2)}, u32[]{:S(2)}) collective-permute-start(f32[8,1280]{1,0:T(8,128)S(1)} %get-tuple-element.57), channel_id=1, source_target_pairs={{0,1},{1,2},{2,3},{4,5},{5,6},{6,7},{8,9},{9,10},{10,11},{12,13},{... | collective-permute-start | bytes 122888 | tf_op jit(solution)/shard_map/ppermute | solution.py:256
  233.5 1.3 collective-permute-start.6
  235.2 4.1 %collective-permute-done.6.refs_13_ = f32[8,1280]{1,0:T(8,128)S(1)} collective-permute-done((f32[8,1280]{1,0:T(8,128)S(1)}, f32[8,1280]{1,0:T(8,128)S(1)}, u32[]{:S(2)}, u32[]{:S(2)}) %collective-permute-start.6) | collective-permute-done | bytes 40992 | tf_op jit(solution)/shard_map/ppermute | solution.py:256
  240.0 0.7 copy-done.4
  240.7 11.3 %stage.5 = (f32[1024,1024]{1,0:T(8,128)}, f32[1024,1024]{1,0:T(8,128)}) custom-call(s32[1]{0:T(128)} %bitcast.refs_0_, f32[7]{0:T(128)} %refs_1_.2, f32[8,1024]{1,0:T(8,128)} %get-tuple-element.55.refs_2_, f32[8,1024]{1,0:T(8,128)} %get-tuple-element.54.refs_3_, ...), custom_call_target="tpu_custom_call", output_to_operand_aliasing={{0}: (20, {}), {1}: (21, {})} | custom-call | flops 47185920 | bytes 7077888 | tf_op jit(solution)/shard_map/stage/pallas_call | solution.py:558
  (41 shorter events, 5.1 us)
Async XLA Ops:
  10.0 8.3 %copy-start.5 = (f32[7]{0:T(128)S(1)}, f32[7]{0:T(128)}, u32[]{:S(2)}) copy-start(f32[7]{0:T(128)} %refs_1_.2) | copy-start | bytes 88
  10.0 144.5 %all-to-all-start = ((bf16[32,784,128]{2,1,0:T(8,128)(2,1)}), bf16[32,784,128]{2,1,0:T(8,128)(2,1)}, u32[]{:S(2)}, u32[]{:S(2)}) async-start(bf16[32,784,128]{2,1,0:T(8,128)(2,1)} %warp.2), calls=%async_computation | async-start | bytes 12845056 | tf_op jit(solution)/shard_map/all_to_all | solution.py:634
  154.5 57.3 %all-to-all-start.1 = ((bf16[32,256,128]{2,1,0:T(8,128)(2,1)}), bf16[32,256,128]{2,1,0:T(8,128)(2,1)S(1)}, u32[]{:S(2)}, u32[]{:S(2)}) async-start(bf16[32,256,128]{2,1,0:T(8,128)(2,1)} %warp.3), calls=%async_computation.1 | async-start | bytes 4194304 | tf_op jit(solution)/shard_map/all_to_all | solution.py:634
  171.4 24.8 %copy-start = (bf16[288,1024]{1,0:T(8,128)(2,1)}, bf16[288,1024]{1,0:T(8,128)(2,1)S(1)}, u32[]{:S(2)}) copy-start(bf16[288,1024]{1,0:T(8,128)(2,1)S(1)} %get-tuple-element.44.refs_8_.refs_14_) | copy-start | bytes 1769476
  171.4 34.5 %copy-start.1 = (bf16[144,1024]{1,0:T(8,128)(2,1)}, bf16[144,1024]{1,0:T(8,128)(2,1)S(1)}, u32[]{:S(2)}) copy-start(bf16[144,1024]{1,0:T(8,128)(2,1)S(1)} %get-tuple-element.43.refs_8_.refs_16_) | copy-start | bytes 884740
  171.5 24.8 %collective-permute-start.3 = (bf16[288,1024]{1,0:T(8,128)(2,1)S(1)}, bf16[288,1024]{1,0:T(8,128)(2,1)}, u32[]{:S(2)}, u32[]{:S(2)}) collective-permute-start(bf16[288,1024]{1,0:T(8,128)(2,1)S(1)} %get-tuple-element.44.refs_8_.refs_14_), channel_id=1, source_target_pairs={{0,16},{16,0},{1,17},{17,1},{2,18},{18,2},{3,19},{19,3},{4,20},{20... | collective-permute-start | bytes 1769480 | tf_op jit(solution)/shard_map/ppermute | solution.py:260
  173.3 32.6 %collective-permute-start.2 = (bf16[144,1024]{1,0:T(8,128)(2,1)S(1)}, bf16[144,1024]{1,0:T(8,128)(2,1)S(1)}, u32[]{:S(2)}, u32[]{:S(2)}) collective-permute-start(bf16[144,1024]{1,0:T(8,128)(2,1)S(1)} %get-tuple-element.43.refs_8_.refs_16_), channel_id=1, source_target_pairs={{0,16},{16,0},{1,17},{17,1},{2,18},{18,2},{3,19},{19,3},{4,20},{20... | collective-permute-start | bytes 884744 | tf_op jit(solution)/shard_map/ppermute | solution.py:260
  173.6 2.0 collective-permute-start
  174.2 5.7 %collective-permute-start.1 = (f32[8,1024]{1,0:T(8,128)S(1)}, f32[8,1024]{1,0:T(8,128)S(1)}, u32[]{:S(2)}, u32[]{:S(2)}) collective-permute-start(f32[8,1024]{1,0:T(8,128)S(1)} %slice_select_fusion), channel_id=1, source_target_pairs={{4,0},{8,4},{12,8},{16,20},{20,24},{24,28},{5,1},{9,5},{13,9},{17,... | collective-permute-start | bytes 98312 | tf_op jit(solution)/shard_map/ppermute | solution.py:280
  205.9 0.7 copy-start.3
  214.4 25.0 %copy-start.2 = (bf16[128,1024]{1,0:T(8,128)(2,1)}, bf16[128,1024]{1,0:T(8,128)(2,1)S(1)}, u32[]{:S(2)}) copy-start(bf16[128,1024]{1,0:T(8,128)(2,1)S(1)} %get-tuple-element.51.refs_18_) | copy-start | bytes 786436
  214.4 13.2 %collective-permute-start.4 = (f32[16,512]{1,0:T(8,128)S(1)}, f32[16,512]{1,0:T(8,128)S(1)}, u32[]{:S(2)}, u32[]{:S(2)}) collective-permute-start(f32[16,512]{1,0:T(8,128)S(1)} %pad_maximum_fusion.1), channel_id=1, source_target_pairs={{0,16},{16,0},{1,17},{17,1},{2,18},{18,2},{3,19},{19,3},{4,20},{20... | collective-permute-start | bytes 98312 | tf_op jit(solution)/shard_map/ppermute | solution.py:260
  225.7 13.6 %collective-permute-start.7 = (bf16[128,1024]{1,0:T(8,128)(2,1)S(1)}, bf16[128,1024]{1,0:T(8,128)(2,1)S(1)}, u32[]{:S(2)}, u32[]{:S(2)}) collective-permute-start(bf16[128,1024]{1,0:T(8,128)(2,1)S(1)} %get-tuple-element.51.refs_18_), channel_id=1, source_target_pairs={{0,16},{16,0},{1,17},{17,1},{2,18},{18,2},{3,19},{19,3},{4,20},{20... | collective-permute-start | bytes 786440 | tf_op jit(solution)/shard_map/ppermute | solution.py:260
  229.0 6.2 %collective-permute-start.5 = (f32[8,1280]{1,0:T(8,128)S(1)}, f32[8,1280]{1,0:T(8,128)S(1)}, u32[]{:S(2)}, u32[]{:S(2)}) collective-permute-start(f32[8,1280]{1,0:T(8,128)S(1)} %get-tuple-element.57), channel_id=1, source_target_pairs={{0,1},{1,2},{2,3},{4,5},{5,6},{6,7},{8,9},{9,10},{10,11},{12,13},{... | collective-permute-start | bytes 122888 | tf_op jit(solution)/shard_map/ppermute | solution.py:256
  233.5 5.9 %collective-permute-start.6 = (f32[8,1280]{1,0:T(8,128)S(1)}, f32[8,1280]{1,0:T(8,128)S(1)}, u32[]{:S(2)}, u32[]{:S(2)}) collective-permute-start(f32[8,1280]{1,0:T(8,128)S(1)} %get-tuple-element.56), channel_id=1, source_target_pairs={{1,0},{2,1},{3,2},{5,4},{6,5},{7,6},{9,8},{10,9},{11,10},{13,12},{... | collective-permute-start | bytes 122888 | tf_op jit(solution)/shard_map/ppermute | solution.py:256
  235.2 4.2 %copy-start.6 = (f32[8,1280]{1,0:T(8,128)}, f32[8,1280]{1,0:T(8,128)S(1)}, u32[]{:S(2)}) copy-start(f32[8,1280]{1,0:T(8,128)S(1)} %collective-permute-done.5.refs_12_) | copy-start | bytes 122884
  239.4 0.6 copy-start.7
  240.0 0.7 copy-start.4

commit v10 on v6

--- a/solution.py
+++ b/solution.py
@@ -263,21 +263,6 @@
     return neighbours(jnp.concatenate(first, axis=1), jnp.concatenate(last, axis=1), "px")
 
 
-def straight_to_both(strip):
-    first, last = strip[:HALO], strip[HALO:]
-    count = lax.axis_size("px")
-    up, down = beside("px")
-
-    def crossed(pairs):
-        return [(v * count + i, (1 - v) * count + j) for v in range(2) for i, j in pairs]
-
-    own = neighbours(first, last, "px")
-    return own, (
-        lax.ppermute(last, ("visit", "px"), crossed(up)),
-        lax.ppermute(first, ("visit", "px"), crossed(down)),
-    )
-
-
 def rows_between(edge):
     lower = lax.axis_index("visit") == 0
     mine = jnp.where(lower, edge[:HALO], edge[HALO:])
@@ -379,9 +364,9 @@
             first = number * height if left.shape[1] > height else 0
             here = slice(first, first + height)
             gap = jnp.zeros((SIDE - 2 * HALO, height), jnp.float32)
-            side[...] = jnp.concatenate([right[:, here], gap, left[:, here]], axis=0).T.astype(
-                jnp.bfloat16
-            )
+            side[...] = jnp.concatenate(
+                [right[right.shape[0] - HALO :, here], gap, left[:HALO, here]], axis=0
+            ).T.astype(jnp.bfloat16)
             group.append((cells, side))
         held.append(group)
 
@@ -569,15 +554,19 @@
     second = send(later)
     code = codes(arrived)
     coadd, strip, edge = place(code, arrived, lots[0])
+    between, other_strip = rows_between(edge), swapped(strip)
+    coadd, between, other_strip = lax.optimization_barrier((coadd, between, other_strip))
+    sides = beyond([strip, other_strip], *between)
     other = swapped(coadd)
-    between = rows_between(edge)
-    sides = beyond([strip, swapped(strip)], *between)
+    second, sides, other = lax.optimization_barrier((second, sides, other))
     parts = [(coadd, *sides), (other, *sides)]
     coadd, strip, _ = place(code, second, lots[1])
-    own_sides, other_sides = straight_to_both(strip)
-    more = [(coadd, *own_sides), (swapped(coadd), *other_sides)]
+    other = swapped(coadd)
+    near = neighbours(strip[:HALO], strip[HALO:], "px")
     (parts, between), _ = lax.optimization_barrier(((parts, between), coadd))
     held = stage(outer, mine, psf_taps, between, tables[0], [parts], lots[:1])
+    far = swapped(jnp.concatenate(near, axis=0))
+    more = [(coadd, *near), (other, far, far)]
     return stage(inner, mine, psf_taps, between, tables[1], [parts, more], lots, held)
 
 

time: 251 us -> 245 us (0.976)
  starting transfers between devices: 41.7 us -> 36.8 us
    all_to_all x2, waiting for transfers between devices: 140 us -> 114 us  [send(): lax.all_to_all(blocks, EVERY, split_axis=0, concat_axis=0, tiled=True)]
    ppermute x3 -> x4, waiting for transfers between devices: 0.01 us -> 17.9 us  [swapped(): return lax.ppermute(array, 'visit', [(0, 1), (1, 0)])]
    ppermute x4, waiting for transfers between devices: 2.75 us -> 11.1 us  [neighbours(): return (lax.ppermute(last, axis, up), lax.ppermute(first, axis, down))]
    ppermute x2 -> x0, starting transfers between devices: 6.15 us -> none  [the longest x1 4.86 us: straight_to_both(): lax.ppermute(last, ('visit', 'px'), crossed(up))]
    ppermute x3 -> x4, starting transfers between devices: 7.36 us -> 6.73 us  [swapped(): return lax.ppermute(array, 'visit', [(0, 1), (1, 0)])]
  transfers between devices with their start and end apart: 13 -> 12, of which waited for: 3 -> 6; matrix products, arithmetic and copies ran while one was open for 6% -> 7% of each run, Pallas kernels for 12% -> 11%
where the time goes in v10:
time: 245 us; the launch traced here: 243 us
  waiting for transfers between devices  143 us (58%)
  Pallas kernels  46.3 us (19%)
  starting transfers between devices  36.8 us (15%)
  other arithmetic  14.4 us (6%)
  local copies, waits for them, and re-layouts  2.46 us (1%)
    all_to_all x2, waiting for transfers between devices, send(): lax.all_to_all(blocks, EVERY, split_axis=0, concat_axis=0, tiled=True)  114 us
    pallas_call x2, Pallas kernels, stage(): pl.pallas_call(functools.partial(stage_kernel, plan, lots), out_shape=(sh...  18.9 us
    ppermute x4, waiting for transfers between devices, swapped(): return lax.ppermute(array, 'visit', [(0, 1), (1, 0)])  17.9 us
    pallas_call x2, Pallas kernels, warp(): pl.pallas_call(functools.partial(warp_kernel, tiles, share, noted), out_s...  17.9 us
    all_to_all x2, starting transfers between devices, send(): lax.all_to_all(blocks, EVERY, split_axis=0, concat_axis=0, tiled=True)  16.3 us
    ppermute x4, starting transfers between devices, neighbours(): return (lax.ppermute(last, axis, up), lax.ppermute(first, axis, down))  11.8 us
    ppermute x4, waiting for transfers between devices, neighbours(): return (lax.ppermute(last, axis, up), lax.ppermute(first, axis, down))  11.1 us
    pallas_call x2, Pallas kernels, place(): pl.pallas_call(functools.partial(place_kernel, 2 * lot), grid_spec=pltpu....  9.49 us
  transfers between devices with their start and end apart: 12, of which 6 were waited for; matrix products, arithmetic and copies ran while one was open for 7% of the time, Pallas kernels for 11%

profile of v10, /device:TPU:0, one launch (start us, length us, event | category | flops | bytes accessed | tf_op | source)
XLA Modules:
  0.0 243.5 jit_solution(15799724706014700042)
XLA Ops:
  0.6 9.4 %warp.2 = bf16[32,784,128]{2,1,0:T(8,128)(2,1)} custom-call(s32[24]{0:T(128)} %visit_ref.3, s32[24]{0:T(128)} %bitcast.12, s32[2,24]{1,0:T(2,128)} %bitcast.10, s32[8,256]{1,0:T(8,128)} %good_ref.3, bf16[8,256,256]{2,1,0:T(8,128)(2,1)} %rows_hbm.3, bf16[8,256,256]{2,1,0:T(8,128)(2,1)} %cols_hbm.3, bf16[24,256,256]{2,1,0:T(8,128)(2,1)} %var_hbm.2, ...), custom_call_target="tpu_custom_call" | custom-call | flops 3221225472 | bytes 12582912 | tf_op jit(solution)/shard_map/warp/pallas_call | solution.py:158
  10.1 7.4 %all-to-all-start = ((bf16[32,784,128]{2,1,0:T(8,128)(2,1)}), bf16[32,784,128]{2,1,0:T(8,128)(2,1)}, u32[]{:S(2)}, u32[]{:S(2)}) async-start(bf16[32,784,128]{2,1,0:T(8,128)(2,1)} %warp.2), calls=%async_computation | async-start | bytes 12845056 | tf_op jit(solution)/shard_map/all_to_all | solution.py:536
  17.6 0.7 add_convert_fusion.3.refs_5_
  19.0 0.7 add_convert_fusion.2.refs_4_
  19.6 4.5 %fusion.16 = (bf16[48,64]{1,0:T(8,128)(2,1)S(1)}, bf16[48,64]{1,0:T(8,128)(2,1)S(1)}) fusion(f32[]{:T(128)} %bitcast.9, f32[]{:T(128)} %bitcast.8, f32[]{:T(128)} %bitcast.7, f32[]{:T(128)} %bitcast.6, f32[]{:T(128)} %bitcast.5, f32[]{:T(128)} %bitcast.4, f32[]{:T(128)} %bitcast.3, s32[48]{0:T(128)S(1)} %iota_add_fusion), kind=kLoop, calls=%fused_computation.39 | loop fusion | flops 79872 | bytes 12508 | tf_op jit(solution)/shard_map/convert_element_type | solution.py:302
  24.2 0.7 pad_maximum_fusion.3.refs_6_
  25.0 0.7 add_convert_fusion.1.refs_5_
  25.7 0.7 add_convert_fusion.refs_4_
  26.4 4.6 %fusion.15 = (bf16[80,96]{1,0:T(8,128)(2,1)S(1)}, bf16[80,96]{1,0:T(8,128)(2,1)S(1)}) fusion(f32[]{:T(128)} %bitcast.9, f32[]{:T(128)} %bitcast.8, f32[]{:T(128)} %bitcast.7, f32[]{:T(128)} %bitcast.6, f32[]{:T(128)} %bitcast.5, f32[]{:T(128)} %bitcast.4, f32[]{:T(128)} %bitcast.3, s32[80]{0:T(128)S(1)} %iota_add_fusion.1), kind=kLoop, calls=%fused_computation.35 | loop fusion | flops 199680 | bytes 31068 | tf_op jit(solution)/shard_map/convert_element_type | solution.py:302
  30.9 0.7 pad_maximum_fusion.refs_6_
  31.7 0.8 fusion.refs_7_
  32.5 8.5 %warp.3 = bf16[32,256,128]{2,1,0:T(8,128)(2,1)} custom-call(s32[24]{0:T(128)} %visit_ref.3, s32[24]{0:T(128)} %bitcast.13, s32[2,24]{1,0:T(2,128)} %bitcast.11, s32[8,256]{1,0:T(8,128)} %good_ref.3, bf16[8,256,256]{2,1,0:T(8,128)(2,1)} %rows_hbm.3, bf16[8,256,256]{2,1,0:T(8,128)(2,1)} %cols_hbm.3, bf16[24,256,256]{2,1,0:T(8,128)(2,1)} %var_hbm.2, ...), custom_call_target="tpu_custom_call" | custom-call | flops 3221225472 | bytes 12582912 | tf_op jit(solution)/shard_map/warp/pallas_call | solution.py:158
  41.0 113.5 %all-to-all-done.blocks_ref = bf16[32,784,128]{2,1,0:T(8,128)(2,1)} async-done(((bf16[32,784,128]{2,1,0:T(8,128)(2,1)}), bf16[32,784,128]{2,1,0:T(8,128)(2,1)}, u32[]{:S(2)}, u32[]{:S(2)}) %all-to-all-start) | async-done | bytes 6422560 | tf_op jit(solution)/shard_map/all_to_all | solution.py:536
  154.5 8.9 %all-to-all-start.1 = ((bf16[32,256,128]{2,1,0:T(8,128)(2,1)}), bf16[32,256,128]{2,1,0:T(8,128)(2,1)S(1)}, u32[]{:S(2)}, u32[]{:S(2)}) async-start(bf16[32,256,128]{2,1,0:T(8,128)(2,1)} %warp.3), calls=%async_computation.1 | async-start | bytes 4194304 | tf_op jit(solution)/shard_map/all_to_all | solution.py:536
  163.4 1.0 slice.81
  164.6 6.9 %place.2 = (bf16[384,1024]{1,0:T(8,128)(2,1)S(1)}, f32[16,384]{1,0:T(8,128)S(1)}, f32[16,1024]{1,0:T(8,128)S(1)}) custom-call(s32[64]{0:T(128)S(1)} %convert_element_type.49.code_ref, bf16[32,784,128]{2,1,0:T(8,128)(2,1)} %all-to-all-done.blocks_ref), custom_call_target="tpu_custom_call" | custom-call | flops 3211264 | bytes 6422528 | tf_op jit(solution)/shard_map/place/pallas_call | solution.py:227
  171.5 1.3 collective-permute-start.1
  172.8 0.7 collective-permute-start
  173.5 4.1 %collective-permute-start.2 = (f32[16,384]{1,0:T(8,128)S(1)}, f32[16,384]{1,0:T(8,128)S(1)}, u32[]{:S(2)}, u32[]{:S(2)}) collective-permute-start(f32[16,384]{1,0:T(8,128)S(1)} %get-tuple-element.44), channel_id=1, source_target_pairs={{0,16},{16,0},{1,17},{17,1},{2,18},{18,2},{3,19},{19,3},{4,20},{20... | collective-permute-start | bytes 73736 | tf_op jit(solution)/shard_map/ppermute | solution.py:257
  177.6 6.5 %collective-permute-done.2 = f32[16,384]{1,0:T(8,128)S(1)} collective-permute-done((f32[16,384]{1,0:T(8,128)S(1)}, f32[16,384]{1,0:T(8,128)S(1)}, u32[]{:S(2)}, u32[]{:S(2)}) %collective-permute-start.2) | collective-permute-done | bytes 24608 | tf_op jit(solution)/shard_map/ppermute | solution.py:257
  184.1 3.5 %collective-permute-start.3 = (f32[8,1024]{1,0:T(8,128)S(1)}, f32[8,1024]{1,0:T(8,128)S(1)}, u32[]{:S(2)}, u32[]{:S(2)}) collective-permute-start(f32[8,1024]{1,0:T(8,128)S(1)} %pad_maximum_fusion.1), channel_id=1, source_target_pairs={{0,1},{1,2},{2,3},{4,5},{5,6},{6,7},{8,9},{9,10},{10,11},{12,13},{... | collective-permute-start | bytes 98312 | tf_op jit(solution)/shard_map/ppermute | solution.py:253
  187.7 1.3 collective-permute-start.4
  189.0 9.8 %collective-permute-done.3.refs_9_.refs_12_ = f32[8,1024]{1,0:T(8,128)S(1)} collective-permute-done((f32[8,1024]{1,0:T(8,128)S(1)}, f32[8,1024]{1,0:T(8,128)S(1)}, u32[]{:S(2)}, u32[]{:S(2)}) %collective-permute-start.3) | collective-permute-done | bytes 32800 | tf_op jit(solution)/shard_map/ppermute | solution.py:253
  198.8 11.4 %collective-permute-done.5.refs_11_ = bf16[384,1024]{1,0:T(8,128)(2,1)} collective-permute-done((bf16[384,1024]{1,0:T(8,128)(2,1)S(1)}, bf16[384,1024]{1,0:T(8,128)(2,1)}, u32[]{:S(2)}, u32[]{:S(2)}) %collective-permute-start.5) | collective-permute-done | bytes 786464 | tf_op jit(solution)/shard_map/ppermute | solution.py:257
  210.3 2.6 %place.3 = (bf16[128,1024]{1,0:T(8,128)(2,1)S(1)}, f32[16,128]{1,0:T(8,128)S(1)}, f32[16,1024]{1,0:T(8,128)}) custom-call(s32[64]{0:T(128)S(1)} %convert_element_type.49.code_ref, bf16[32,256,128]{2,1,0:T(8,128)(2,1)S(1)} %all-to-all-done.1.blocks_ref), custom_call_target="tpu_custom_call" | custom-call | flops 1048576 | bytes 2097152 | tf_op jit(solution)/shard_map/place/pallas_call | solution.py:227
  212.8 1.5 collective-permute-start.8
  214.3 1.3 collective-permute-start.7
  215.6 5.7 %collective-permute-start.6 = (f32[8,128]{1,0:T(8,128)S(1)}, f32[8,128]{1,0:T(8,128)S(1)}, u32[]{:S(2)}, u32[]{:S(2)}) collective-permute-start(f32[8,128]{1,0:T(8,128)S(1)} %get-tuple-element.85), channel_id=1, source_target_pairs={{0,1},{1,2},{2,3},{4,5},{5,6},{6,7},{8,9},{9,10},{10,11},{12,13},{... | collective-permute-start | bytes 12296 | tf_op jit(solution)/shard_map/ppermute | solution.py:253
  221.3 1.3 collective-permute-done.6.refs_15_
  222.6 1.2 collective-permute-start.9
  223.8 11.0 %stage.2 = (f32[1024,1024]{1,0:T(8,128)}, f32[1024,1024]{1,0:T(8,128)}) custom-call(s32[1]{0:T(128)} %bitcast.refs_0_, f32[7]{0:T(128)} %refs_1_.1, f32[8,1024]{1,0:T(8,128)} %copy-done.5, f32[8,1024]{1,0:T(8,128)} %copy-done.4, bf16[96,192]{1,0:T(8,128)(2,1)} %add_convert_fusion.refs_4_, bf16[80,192]{1,0:T(8,128)(2,1)} %add_convert_fusion.1.refs_5_, ...), custom_call_target="tpu_custom_call" | custom-call | flops 79626240 | bytes 11943936 | tf_op jit(solution)/shard_map/stage/pallas_call | solution.py:459
  235.6 7.9 %stage.3 = (f32[1024,1024]{1,0:T(8,128)}, f32[1024,1024]{1,0:T(8,128)}) custom-call(s32[1]{0:T(128)} %bitcast.refs_0_, f32[7]{0:T(128)} %refs_1_.1, f32[8,1024]{1,0:T(8,128)} %copy-done.5, f32[8,1024]{1,0:T(8,128)} %copy-done.4, bf16[64,128]{1,0:T(8,128)(2,1)} %add_convert_fusion.2.refs_4_, ...), custom_call_target="tpu_custom_call", output_to_operand_aliasing={{0}: (20, {}), {1}: (21, {})} | custom-call | flops 47185920 | bytes 7077888 | tf_op jit(solution)/shard_map/stage/pallas_call | solution.py:459
  (50 shorter events, 1.9 us)
Async XLA Ops:
  10.0 8.3 %copy-start.7 = (f32[7]{0:T(128)S(1)}, f32[7]{0:T(128)}, u32[]{:S(2)}) copy-start(f32[7]{0:T(128)} %refs_1_.1) | copy-start | bytes 88
  10.1 144.4 %all-to-all-start = ((bf16[32,784,128]{2,1,0:T(8,128)(2,1)}), bf16[32,784,128]{2,1,0:T(8,128)(2,1)}, u32[]{:S(2)}, u32[]{:S(2)}) async-start(bf16[32,784,128]{2,1,0:T(8,128)(2,1)} %warp.2), calls=%async_computation | async-start | bytes 12845056 | tf_op jit(solution)/shard_map/all_to_all | solution.py:536
  154.5 55.7 %all-to-all-start.1 = ((bf16[32,256,128]{2,1,0:T(8,128)(2,1)}), bf16[32,256,128]{2,1,0:T(8,128)(2,1)S(1)}, u32[]{:S(2)}, u32[]{:S(2)}) async-start(bf16[32,256,128]{2,1,0:T(8,128)(2,1)} %warp.3), calls=%async_computation.1 | async-start | bytes 4194304 | tf_op jit(solution)/shard_map/all_to_all | solution.py:536
  171.5 52.3 %copy-start = (bf16[384,1024]{1,0:T(8,128)(2,1)}, bf16[384,1024]{1,0:T(8,128)(2,1)S(1)}, u32[]{:S(2)}) copy-start(bf16[384,1024]{1,0:T(8,128)(2,1)S(1)} %get-tuple-element.61.refs_8_) | copy-start | bytes 2359300
  171.5 6.0 %collective-permute-start.1 = (f32[8,1024]{1,0:T(8,128)S(1)}, f32[8,1024]{1,0:T(8,128)S(1)}, u32[]{:S(2)}, u32[]{:S(2)}) collective-permute-start(f32[8,1024]{1,0:T(8,128)S(1)} %slice_select_fusion), channel_id=1, source_target_pairs={{4,0},{8,4},{12,8},{16,20},{20,24},{24,28},{5,1},{9,5},{13,9},{17,... | collective-permute-start | bytes 98312 | tf_op jit(solution)/shard_map/ppermute | solution.py:277
  172.8 4.7 %collective-permute-start = (f32[8,1024]{1,0:T(8,128)S(1)}, f32[8,1024]{1,0:T(8,128)S(1)}, u32[]{:S(2)}, u32[]{:S(2)}) collective-permute-start(f32[8,1024]{1,0:T(8,128)S(1)} %slice_select_fusion), channel_id=1, source_target_pairs={{4,16},{8,20},{12,24},{16,4},{20,8},{24,12},{5,17},{9,21},{13,25},... | collective-permute-start | bytes 98312 | tf_op jit(solution)/shard_map/ppermute | solution.py:278
  173.5 10.6 %collective-permute-start.2 = (f32[16,384]{1,0:T(8,128)S(1)}, f32[16,384]{1,0:T(8,128)S(1)}, u32[]{:S(2)}, u32[]{:S(2)}) collective-permute-start(f32[16,384]{1,0:T(8,128)S(1)} %get-tuple-element.44), channel_id=1, source_target_pairs={{0,16},{16,0},{1,17},{17,1},{2,18},{18,2},{3,19},{19,3},{4,20},{20... | collective-permute-start | bytes 73736 | tf_op jit(solution)/shard_map/ppermute | solution.py:257
  177.6 46.2 %copy-start.4 = (f32[8,1024]{1,0:T(8,128)}, f32[8,1024]{1,0:T(8,128)S(1)}, u32[]{:S(2)}) copy-start(f32[8,1024]{1,0:T(8,128)S(1)} %get-tuple-element.56.refs_3_) | copy-start | bytes 98308
  177.6 46.2 %copy-start.5 = (f32[8,1024]{1,0:T(8,128)}, f32[8,1024]{1,0:T(8,128)S(1)}, u32[]{:S(2)}) copy-start(f32[8,1024]{1,0:T(8,128)S(1)} %get-tuple-element.55.refs_2_) | copy-start | bytes 98308
  184.1 26.1 %collective-permute-start.5 = (bf16[384,1024]{1,0:T(8,128)(2,1)S(1)}, bf16[384,1024]{1,0:T(8,128)(2,1)}, u32[]{:S(2)}, u32[]{:S(2)}) collective-permute-start(bf16[384,1024]{1,0:T(8,128)(2,1)S(1)} %get-tuple-element.61.refs_8_), channel_id=1, source_target_pairs={{0,16},{16,0},{1,17},{17,1},{2,18},{18,2},{3,19},{19,3},{4,20},{20... | collective-permute-start | bytes 2359304 | tf_op jit(solution)/shard_map/ppermute | solution.py:257
  184.1 14.6 %collective-permute-start.3 = (f32[8,1024]{1,0:T(8,128)S(1)}, f32[8,1024]{1,0:T(8,128)S(1)}, u32[]{:S(2)}, u32[]{:S(2)}) collective-permute-start(f32[8,1024]{1,0:T(8,128)S(1)} %pad_maximum_fusion.1), channel_id=1, source_target_pairs={{0,1},{1,2},{2,3},{4,5},{5,6},{6,7},{8,9},{9,10},{10,11},{12,13},{... | collective-permute-start | bytes 98312 | tf_op jit(solution)/shard_map/ppermute | solution.py:253
  187.7 11.1 %collective-permute-start.4 = (f32[8,1024]{1,0:T(8,128)S(1)}, f32[8,1024]{1,0:T(8,128)S(1)}, u32[]{:S(2)}, u32[]{:S(2)}) collective-permute-start(f32[8,1024]{1,0:T(8,128)S(1)} %pad_maximum_fusion.2), channel_id=1, source_target_pairs={{1,0},{2,1},{3,2},{5,4},{6,5},{7,6},{9,8},{10,9},{11,10},{13,12},{... | collective-permute-start | bytes 98312 | tf_op jit(solution)/shard_map/ppermute | solution.py:253
  198.8 25.1 %copy-start.2 = (f32[8,1024]{1,0:T(8,128)}, f32[8,1024]{1,0:T(8,128)S(1)}, u32[]{:S(2)}) copy-start(f32[8,1024]{1,0:T(8,128)S(1)} %collective-permute-done.3.refs_9_.refs_12_) | copy-start | bytes 98308
  198.8 25.1 %copy-start.3 = (f32[8,1024]{1,0:T(8,128)}, f32[8,1024]{1,0:T(8,128)S(1)}, u32[]{:S(2)}) copy-start(f32[8,1024]{1,0:T(8,128)S(1)} %collective-permute-done.4.refs_10_.refs_13_) | copy-start | bytes 98308
  212.8 22.1 %copy-start.1 = (bf16[128,1024]{1,0:T(8,128)(2,1)}, bf16[128,1024]{1,0:T(8,128)(2,1)S(1)}, u32[]{:S(2)}) copy-start(bf16[128,1024]{1,0:T(8,128)(2,1)S(1)} %get-tuple-element.54.refs_14_) | copy-start | bytes 786436
  212.8 22.1 %collective-permute-start.8 = (bf16[128,1024]{1,0:T(8,128)(2,1)S(1)}, bf16[128,1024]{1,0:T(8,128)(2,1)S(1)}, u32[]{:S(2)}, u32[]{:S(2)}) collective-permute-start(bf16[128,1024]{1,0:T(8,128)(2,1)S(1)} %get-tuple-element.54.refs_14_), channel_id=1, source_target_pairs={{0,16},{16,0},{1,17},{17,1},{2,18},{18,2},{3,19},{19,3},{4,20},{20... | collective-permute-start | bytes 786440 | tf_op jit(solution)/shard_map/ppermute | solution.py:257
  214.3 7.0 %collective-permute-start.7 = (f32[8,128]{1,0:T(8,128)S(1)}, f32[8,128]{1,0:T(8,128)S(1)}, u32[]{:S(2)}, u32[]{:S(2)}) collective-permute-start(f32[8,128]{1,0:T(8,128)S(1)} %get-tuple-element.84), channel_id=1, source_target_pairs={{1,0},{2,1},{3,2},{5,4},{6,5},{7,6},{9,8},{10,9},{11,10},{13,12},{... | collective-permute-start | bytes 12296 | tf_op jit(solution)/shard_map/ppermute | solution.py:253
  215.6 7.0 %collective-permute-start.6 = (f32[8,128]{1,0:T(8,128)S(1)}, f32[8,128]{1,0:T(8,128)S(1)}, u32[]{:S(2)}, u32[]{:S(2)}) collective-permute-start(f32[8,128]{1,0:T(8,128)S(1)} %get-tuple-element.85), channel_id=1, source_target_pairs={{0,1},{1,2},{2,3},{4,5},{5,6},{6,7},{8,9},{9,10},{10,11},{12,13},{... | collective-permute-start | bytes 12296 | tf_op jit(solution)/shard_map/ppermute | solution.py:253
  221.3 13.6 %copy-start.9 = (f32[8,128]{1,0:T(8,128)}, f32[8,128]{1,0:T(8,128)S(1)}, u32[]{:S(2)}) copy-start(f32[8,128]{1,0:T(8,128)S(1)} %collective-permute-done.7.refs_16_) | copy-start | bytes 12292
  222.6 12.3 %copy-start.10 = (f32[8,128]{1,0:T(8,128)}, f32[8,128]{1,0:T(8,128)S(1)}, u32[]{:S(2)}) copy-start(f32[8,128]{1,0:T(8,128)S(1)} %collective-permute-done.6.refs_15_) | copy-start | bytes 12292
  222.6 12.3 %collective-permute-start.9 = (f32[16,128]{1,0:T(8,128)S(1)}, f32[16,128]{1,0:T(8,128)S(1)}, u32[]{:S(2)}, u32[]{:S(2)}) collective-permute-start(f32[16,128]{1,0:T(8,128)S(1)} %pad_maximum_fusion.4), channel_id=1, source_target_pairs={{0,16},{16,0},{1,17},{17,1},{2,18},{18,2},{3,19},{19,3},{4,20},{20... | collective-permute-start | bytes 24584 | tf_op jit(solution)/shard_map/ppermute | solution.py:257
  234.9 0.6 copy-start.8
  234.9 0.7 copy-start.6

commit v11 on v10

--- a/solution.py
+++ b/solution.py
@@ -16,7 +16,7 @@
 EDGE = 16
 SIDE = 128
 WIDE = TX + SIDE
-GROUP = 4
+GROUP = 8
 NOTE = 16
 MIB = 1 << 20
 EVERY = ("visit", "py", "px")
@@ -291,8 +291,8 @@
     lane = jnp.arange(4 * SIDE, dtype=jnp.int32)
     across = jnp.abs(lane[:, None] - lane[None, SIDE : 3 * SIDE]) <= 4
     return (
-        jnp.concatenate([three] * 2, axis=1),
-        jnp.concatenate([nine] * 2, axis=1),
+        three,
+        nine,
         jnp.concatenate([coarse, coarse, fine], axis=1),
         across.astype(jnp.bfloat16),
     )
@@ -316,18 +316,14 @@
         for by in range(-3, 4)
     }
     rowwise = sum(taps[tap] * moved[tap - 3] for tap in range(7))[:, :TX]
-    resid = moved[0] - product(three, split(moved[-1] + moved[0] + moved[1])) * (1.0 / 9.0)
-    tower = jnp.concatenate(split(product(nine, split(resid * resid))), axis=0)
+    resid = moved[0] - product(three, [(moved[-1] + moved[0] + moved[1]).astype(jnp.bfloat16)]) * (1.0 / 9.0)
+    tower = product(nine, [(resid * resid).astype(jnp.bfloat16)]).astype(jnp.bfloat16)
     windows = [jnp.concatenate([tower[:, TX:], tower[:, : 3 * SIDE]], axis=1)]
     for start in range(2 * SIDE, TX, 2 * SIDE):
         windows.append(tower[:, start - SIDE : start + 3 * SIDE])
     boxes = jnp.dot(jnp.concatenate(windows, axis=0), across, preferred_element_type=jnp.float32)
     box = jnp.concatenate(
-        [
-            boxes[2 * at * short : (2 * at + 1) * short] + boxes[(2 * at + 1) * short : (2 * at + 2) * short]
-            for at in range(len(windows))
-        ],
-        axis=1,
+        [boxes[at * short : (at + 1) * short] for at in range(len(windows))], axis=1
     )
     local = box * (1.0 / 81.0) + 1e-05
     coarse, fine = split(rowwise)
@@ -469,7 +465,7 @@
             pltpu.SemaphoreType.DMA((spans, 2)),
         ]
         + [pltpu.VMEM((part[0].shape[0], SIDE), jnp.bfloat16) for parts in chunks for part in parts],
-        compiler_params=pltpu.CompilerParams(vmem_limit_bytes=56 * MIB),
+        compiler_params=pltpu.CompilerParams(vmem_limit_bytes=32 * MIB),
         cost_estimate=pl.CostEstimate(
             flops=80 * spans * tall * WIDE, bytes_accessed=12 * spans * tall * WIDE, transcendentals=0
         ),

time: 245 us -> 241 us (0.984)
  Pallas kernels: 46.3 us -> 41.2 us
  waiting for transfers between devices: 143 us -> 148 us
  other arithmetic: 14.4 us -> 9.47 us
    all_to_all x2, waiting for transfers between devices: 114 us -> 119 us  [send(): lax.all_to_all(blocks, EVERY, split_axis=0, concat_axis=0, tiled=True)]
    pallas_call x2, Pallas kernels: 18.9 us -> 15.1 us  [stage(): pl.pallas_call(functools.partial(stage_kernel, plan, lots), out_shape=(sh...]
    concatenate x4 -> x0, other arithmetic: 2.77 us -> none  [the longest x2 1.39 us: bands(): jnp.concatenate([three] * 2, axis=1)]
  transfers between devices with their start and end apart: 12 -> 12, of which waited for: 6 -> 5; matrix products, arithmetic and copies ran while one was open for 7% -> 5% of each run, Pallas kernels for 11% -> 10%
where the time goes in v11:
time: 241 us; the launch traced here: 240 us
  waiting for transfers between devices  148 us (61%)
  Pallas kernels  41.2 us (17%)
  starting transfers between devices  36.9 us (15%)
  other arithmetic  9.47 us (4%)
  local copies, waits for them, and re-layouts  3.78 us (2%)
    all_to_all x2, waiting for transfers between devices, send(): lax.all_to_all(blocks, EVERY, split_axis=0, concat_axis=0, tiled=True)  119 us
    ppermute x4, waiting for transfers between devices, swapped(): return lax.ppermute(array, 'visit', [(0, 1), (1, 0)])  17.8 us
    pallas_call x2, Pallas kernels, warp(): pl.pallas_call(functools.partial(warp_kernel, tiles, share, noted), out_s...  16.6 us
    all_to_all x2, starting transfers between devices, send(): lax.all_to_all(blocks, EVERY, split_axis=0, concat_axis=0, tiled=True)  16.4 us
    pallas_call x2, Pallas kernels, stage(): pl.pallas_call(functools.partial(stage_kernel, plan, lots), out_shape=(sh...  15.1 us
    ppermute x4, starting transfers between devices, neighbours(): return (lax.ppermute(last, axis, up), lax.ppermute(first, axis, down))  13.2 us
    ppermute x4, waiting for transfers between devices, neighbours(): return (lax.ppermute(last, axis, up), lax.ppermute(first, axis, down))  11.1 us
    pallas_call x2, Pallas kernels, place(): pl.pallas_call(functools.partial(place_kernel, 2 * lot), grid_spec=pltpu....  9.48 us
  transfers between devices with their start and end apart: 12, of which 5 were waited for; matrix products, arithmetic and copies ran while one was open for 5% of the time, Pallas kernels for 10%

profile of v11, /device:TPU:0, one launch (start us, length us, event | category | flops | bytes accessed | tf_op | source)
XLA Modules:
  0.0 240.2 jit_solution(5606378310150354048)
XLA Ops:
  0.6 8.7 %warp.2 = bf16[32,784,128]{2,1,0:T(8,128)(2,1)} custom-call(s32[24]{0:T(128)} %visit_ref.3, s32[24]{0:T(128)} %bitcast.12, s32[2,24]{1,0:T(2,128)} %bitcast.10, s32[8,256]{1,0:T(8,128)} %good_ref.3, bf16[8,256,256]{2,1,0:T(8,128)(2,1)} %rows_hbm.3, bf16[8,256,256]{2,1,0:T(8,128)(2,1)} %cols_hbm.3, bf16[24,256,256]{2,1,0:T(8,128)(2,1)} %var_hbm.2, ...), custom_call_target="tpu_custom_call" | custom-call | flops 3221225472 | bytes 12582912 | tf_op jit(solution)/shard_map/warp/pallas_call | solution.py:158
  9.3 7.5 %all-to-all-start = ((bf16[32,784,128]{2,1,0:T(8,128)(2,1)}), bf16[32,784,128]{2,1,0:T(8,128)(2,1)}, u32[]{:S(2)}, u32[]{:S(2)}) async-start(bf16[32,784,128]{2,1,0:T(8,128)(2,1)} %warp.2), calls=%async_computation | async-start | bytes 12845056 | tf_op jit(solution)/shard_map/all_to_all | solution.py:532
  16.9 0.7 fusion.26
  17.6 4.4 %fusion.20 = (bf16[48,64]{1,0:T(8,128)(2,1)S(1)}, bf16[48,64]{1,0:T(8,128)(2,1)S(1)}) fusion(f32[]{:T(128)} %bitcast.9, f32[]{:T(128)} %bitcast.8, f32[]{:T(128)} %bitcast.7, f32[]{:T(128)} %bitcast.6, f32[]{:T(128)} %bitcast.5, f32[]{:T(128)} %bitcast.4, f32[]{:T(128)} %bitcast.3, s32[48]{0:T(128)S(1)} %iota_add_fusion), kind=kLoop, calls=%fused_computation.39 | loop fusion | flops 79872 | bytes 12508 | tf_op jit(solution)/shard_map/convert_element_type | solution.py:302
  22.0 0.1 pad_maximum_fusion.3.refs_6_
  22.1 4.4 %fusion.19 = (bf16[80,96]{1,0:T(8,128)(2,1)S(1)}, bf16[80,96]{1,0:T(8,128)(2,1)S(1)}) fusion(f32[]{:T(128)} %bitcast.9, f32[]{:T(128)} %bitcast.8, f32[]{:T(128)} %bitcast.7, f32[]{:T(128)} %bitcast.6, f32[]{:T(128)} %bitcast.5, f32[]{:T(128)} %bitcast.4, f32[]{:T(128)} %bitcast.3, s32[80]{0:T(128)S(1)} %iota_add_fusion.1), kind=kLoop, calls=%fused_computation.35 | loop fusion | flops 199680 | bytes 31068 | tf_op jit(solution)/shard_map/convert_element_type | solution.py:302
  26.6 0.1 pad_maximum_fusion.refs_6_
  26.8 0.1 fusion.refs_7_
  27.0 7.9 %warp.3 = bf16[32,256,128]{2,1,0:T(8,128)(2,1)} custom-call(s32[24]{0:T(128)} %visit_ref.3, s32[24]{0:T(128)} %bitcast.13, s32[2,24]{1,0:T(2,128)} %bitcast.11, s32[8,256]{1,0:T(8,128)} %good_ref.3, bf16[8,256,256]{2,1,0:T(8,128)(2,1)} %rows_hbm.3, bf16[8,256,256]{2,1,0:T(8,128)(2,1)} %cols_hbm.3, bf16[24,256,256]{2,1,0:T(8,128)(2,1)} %var_hbm.2, ...), custom_call_target="tpu_custom_call" | custom-call | flops 3221225472 | bytes 12582912 | tf_op jit(solution)/shard_map/warp/pallas_call | solution.py:158
  34.9 119.0 %all-to-all-done.blocks_ref = bf16[32,784,128]{2,1,0:T(8,128)(2,1)} async-done(((bf16[32,784,128]{2,1,0:T(8,128)(2,1)}), bf16[32,784,128]{2,1,0:T(8,128)(2,1)}, u32[]{:S(2)}, u32[]{:S(2)}) %all-to-all-start) | async-done | bytes 6422560 | tf_op jit(solution)/shard_map/all_to_all | solution.py:532
  153.9 8.9 %all-to-all-start.1 = ((bf16[32,256,128]{2,1,0:T(8,128)(2,1)}), bf16[32,256,128]{2,1,0:T(8,128)(2,1)S(1)}, u32[]{:S(2)}, u32[]{:S(2)}) async-start(bf16[32,256,128]{2,1,0:T(8,128)(2,1)} %warp.3), calls=%async_computation.1 | async-start | bytes 4194304 | tf_op jit(solution)/shard_map/all_to_all | solution.py:532
  162.8 1.0 slice.81
  163.9 0.1 convert_element_type.61.code_ref
  164.0 6.9 %place.2 = (bf16[384,1024]{1,0:T(8,128)(2,1)S(1)}, f32[16,384]{1,0:T(8,128)S(1)}, f32[16,1024]{1,0:T(8,128)S(1)}) custom-call(s32[64]{0:T(128)S(1)} %convert_element_type.61.code_ref, bf16[32,784,128]{2,1,0:T(8,128)(2,1)} %all-to-all-done.blocks_ref), custom_call_target="tpu_custom_call" | custom-call | flops 3211264 | bytes 6422528 | tf_op jit(solution)/shard_map/place/pallas_call | solution.py:227
  170.9 1.3 collective-permute-start.1
  172.2 0.7 collective-permute-start
  172.9 4.1 %collective-permute-start.2 = (f32[16,384]{1,0:T(8,128)S(1)}, f32[16,384]{1,0:T(8,128)S(1)}, u32[]{:S(2)}, u32[]{:S(2)}) collective-permute-start(f32[16,384]{1,0:T(8,128)S(1)} %get-tuple-element.44), channel_id=1, source_target_pairs={{0,16},{16,0},{1,17},{17,1},{2,18},{18,2},{3,19},{19,3},{4,20},{20... | collective-permute-start | bytes 73736 | tf_op jit(solution)/shard_map/ppermute | solution.py:257
  176.9 6.5 %collective-permute-done.2 = f32[16,384]{1,0:T(8,128)S(1)} collective-permute-done((f32[16,384]{1,0:T(8,128)S(1)}, f32[16,384]{1,0:T(8,128)S(1)}, u32[]{:S(2)}, u32[]{:S(2)}) %collective-permute-start.2) | collective-permute-done | bytes 24608 | tf_op jit(solution)/shard_map/ppermute | solution.py:257
  183.5 3.5 %collective-permute-start.3 = (f32[8,1024]{1,0:T(8,128)S(1)}, f32[8,1024]{1,0:T(8,128)S(1)}, u32[]{:S(2)}, u32[]{:S(2)}) collective-permute-start(f32[8,1024]{1,0:T(8,128)S(1)} %pad_maximum_fusion.1), channel_id=1, source_target_pairs={{0,1},{1,2},{2,3},{4,5},{5,6},{6,7},{8,9},{9,10},{10,11},{12,13},{... | collective-permute-start | bytes 98312 | tf_op jit(solution)/shard_map/ppermute | solution.py:253
  187.1 1.3 collective-permute-start.4
  188.4 9.8 %collective-permute-done.3.refs_9_.refs_12_ = f32[8,1024]{1,0:T(8,128)S(1)} collective-permute-done((f32[8,1024]{1,0:T(8,128)S(1)}, f32[8,1024]{1,0:T(8,128)S(1)}, u32[]{:S(2)}, u32[]{:S(2)}) %collective-permute-start.3) | collective-permute-done | bytes 32800 | tf_op jit(solution)/shard_map/ppermute | solution.py:253
  198.1 11.3 %collective-permute-done.5.refs_11_ = bf16[384,1024]{1,0:T(8,128)(2,1)S(1)} collective-permute-done((bf16[384,1024]{1,0:T(8,128)(2,1)S(1)}, bf16[384,1024]{1,0:T(8,128)(2,1)S(1)}, u32[]{:S(2)}, u32[]{:S(2)}) %collective-permute-start.5) | collective-permute-done | bytes 786464 | tf_op jit(solution)/shard_map/ppermute | solution.py:257
  209.4 0.9 copy-done
  210.3 2.6 %place.3 = (bf16[128,1024]{1,0:T(8,128)(2,1)S(1)}, f32[16,128]{1,0:T(8,128)S(1)}, f32[16,1024]{1,0:T(8,128)}) custom-call(s32[64]{0:T(128)S(1)} %convert_element_type.61.code_ref, bf16[32,256,128]{2,1,0:T(8,128)(2,1)S(1)} %all-to-all-done.1.blocks_ref), custom_call_target="tpu_custom_call" | custom-call | flops 1048576 | bytes 2097152 | tf_op jit(solution)/shard_map/place/pallas_call | solution.py:227
  212.9 0.8 collective-permute-start.8
  213.7 1.3 collective-permute-start.7
  215.0 7.1 %collective-permute-start.6 = (f32[8,128]{1,0:T(8,128)S(1)}, f32[8,128]{1,0:T(8,128)S(1)}, u32[]{:S(2)}, u32[]{:S(2)}) collective-permute-start(f32[8,128]{1,0:T(8,128)S(1)} %get-tuple-element.85), channel_id=1, source_target_pairs={{0,1},{1,2},{2,3},{4,5},{5,6},{6,7},{8,9},{9,10},{10,11},{12,13},{... | collective-permute-start | bytes 12296 | tf_op jit(solution)/shard_map/ppermute | solution.py:253
  222.1 1.3 collective-permute-done.6.refs_15_
  223.4 0.6 collective-permute-start.9
  223.9 1.1 copy-done.1
  225.1 8.9 %stage.2 = (f32[1024,1024]{1,0:T(8,128)}, f32[1024,1024]{1,0:T(8,128)}) custom-call(s32[1]{0:T(128)} %bitcast.refs_0_, f32[7]{0:T(128)S(1)} %copy-done.2, f32[8,1024]{1,0:T(8,128)S(1)} %get-tuple-element.55.refs_2_, f32[8,1024]{1,0:T(8,128)S(1)} %get-tuple-element.56.refs_3_, bf16[96,96]{1,0:T(8,128)(2,1)S(1)} %fusion.1.refs_4_, ...), custom_call_target="tpu_custom_call" | custom-call | flops 79626240 | bytes 11943936 | tf_op jit(solution)/shard_map/stage/pallas_call | solution.py:455
  234.0 6.2 %stage.3 = (f32[1024,1024]{1,0:T(8,128)}, f32[1024,1024]{1,0:T(8,128)}) custom-call(s32[1]{0:T(128)} %bitcast.refs_0_, f32[7]{0:T(128)S(1)} %copy-done.2, f32[8,1024]{1,0:T(8,128)S(1)} %get-tuple-element.55.refs_2_, f32[8,1024]{1,0:T(8,128)S(1)} %get-tuple-element.56.refs_3_, ...), custom_call_target="tpu_custom_call", output_to_operand_aliasing={{0}: (20, {}), {1}: (21, {})} | custom-call | flops 47185920 | bytes 7077888 | tf_op jit(solution)/shard_map/stage/pallas_call | solution.py:455
  (30 shorter events, 0.3 us)
Async XLA Ops:
  9.3 7.5 %copy-start.2 = (f32[7]{0:T(128)S(1)}, f32[7]{0:T(128)}, u32[]{:S(2)}) copy-start(f32[7]{0:T(128)} %refs_1_.1) | copy-start | bytes 88
  9.3 144.5 %all-to-all-start = ((bf16[32,784,128]{2,1,0:T(8,128)(2,1)}), bf16[32,784,128]{2,1,0:T(8,128)(2,1)}, u32[]{:S(2)}, u32[]{:S(2)}) async-start(bf16[32,784,128]{2,1,0:T(8,128)(2,1)} %warp.2), calls=%async_computation | async-start | bytes 12845056 | tf_op jit(solution)/shard_map/all_to_all | solution.py:532
  153.9 56.4 %all-to-all-start.1 = ((bf16[32,256,128]{2,1,0:T(8,128)(2,1)}), bf16[32,256,128]{2,1,0:T(8,128)(2,1)S(1)}, u32[]{:S(2)}, u32[]{:S(2)}) async-start(bf16[32,256,128]{2,1,0:T(8,128)(2,1)} %warp.3), calls=%async_computation.1 | async-start | bytes 4194304 | tf_op jit(solution)/shard_map/all_to_all | solution.py:532
  170.9 6.0 %collective-permute-start.1 = (f32[8,1024]{1,0:T(8,128)S(1)}, f32[8,1024]{1,0:T(8,128)S(1)}, u32[]{:S(2)}, u32[]{:S(2)}) collective-permute-start(f32[8,1024]{1,0:T(8,128)S(1)} %slice_select_fusion), channel_id=1, source_target_pairs={{4,0},{8,4},{12,8},{16,20},{20,24},{24,28},{5,1},{9,5},{13,9},{17,... | collective-permute-start | bytes 98312 | tf_op jit(solution)/shard_map/ppermute | solution.py:277
  172.2 4.7 %collective-permute-start = (f32[8,1024]{1,0:T(8,128)S(1)}, f32[8,1024]{1,0:T(8,128)S(1)}, u32[]{:S(2)}, u32[]{:S(2)}) collective-permute-start(f32[8,1024]{1,0:T(8,128)S(1)} %slice_select_fusion), channel_id=1, source_target_pairs={{4,16},{8,20},{12,24},{16,4},{20,8},{24,12},{5,17},{9,21},{13,25},... | collective-permute-start | bytes 98312 | tf_op jit(solution)/shard_map/ppermute | solution.py:278
  172.9 10.6 %collective-permute-start.2 = (f32[16,384]{1,0:T(8,128)S(1)}, f32[16,384]{1,0:T(8,128)S(1)}, u32[]{:S(2)}, u32[]{:S(2)}) collective-permute-start(f32[16,384]{1,0:T(8,128)S(1)} %get-tuple-element.44), channel_id=1, source_target_pairs={{0,16},{16,0},{1,17},{17,1},{2,18},{18,2},{3,19},{19,3},{4,20},{20... | collective-permute-start | bytes 73736 | tf_op jit(solution)/shard_map/ppermute | solution.py:257
  183.5 26.0 %collective-permute-start.5 = (bf16[384,1024]{1,0:T(8,128)(2,1)S(1)}, bf16[384,1024]{1,0:T(8,128)(2,1)S(1)}, u32[]{:S(2)}, u32[]{:S(2)}) collective-permute-start(bf16[384,1024]{1,0:T(8,128)(2,1)S(1)} %get-tuple-element.61.refs_8_), channel_id=1, source_target_pairs={{0,16},{16,0},{1,17},{17,1},{2,18},{18,2},{3,19},{19,3},{4,20},{20... | collective-permute-start | bytes 2359304 | tf_op jit(solution)/shard_map/ppermute | solution.py:257
  183.5 14.6 %collective-permute-start.3 = (f32[8,1024]{1,0:T(8,128)S(1)}, f32[8,1024]{1,0:T(8,128)S(1)}, u32[]{:S(2)}, u32[]{:S(2)}) collective-permute-start(f32[8,1024]{1,0:T(8,128)S(1)} %pad_maximum_fusion.1), channel_id=1, source_target_pairs={{0,1},{1,2},{2,3},{4,5},{5,6},{6,7},{8,9},{9,10},{10,11},{12,13},{... | collective-permute-start | bytes 98312 | tf_op jit(solution)/shard_map/ppermute | solution.py:253
  187.1 11.1 %collective-permute-start.4 = (f32[8,1024]{1,0:T(8,128)S(1)}, f32[8,1024]{1,0:T(8,128)S(1)}, u32[]{:S(2)}, u32[]{:S(2)}) collective-permute-start(f32[8,1024]{1,0:T(8,128)S(1)} %pad_maximum_fusion.2), channel_id=1, source_target_pairs={{1,0},{2,1},{3,2},{5,4},{6,5},{7,6},{9,8},{10,9},{11,10},{13,12},{... | collective-permute-start | bytes 98312 | tf_op jit(solution)/shard_map/ppermute | solution.py:253
  209.4 0.9 copy-start
  212.9 21.1 %collective-permute-start.8 = (bf16[128,1024]{1,0:T(8,128)(2,1)S(1)}, bf16[128,1024]{1,0:T(8,128)(2,1)S(1)}, u32[]{:S(2)}, u32[]{:S(2)}) collective-permute-start(bf16[128,1024]{1,0:T(8,128)(2,1)S(1)} %get-tuple-element.54.refs_14_), channel_id=1, source_target_pairs={{0,16},{16,0},{1,17},{17,1},{2,18},{18,2},{3,19},{19,3},{4,20},{20... | collective-permute-start | bytes 786440 | tf_op jit(solution)/shard_map/ppermute | solution.py:257
  213.7 8.4 %collective-permute-start.7 = (f32[8,128]{1,0:T(8,128)S(1)}, f32[8,128]{1,0:T(8,128)S(1)}, u32[]{:S(2)}, u32[]{:S(2)}) collective-permute-start(f32[8,128]{1,0:T(8,128)S(1)} %get-tuple-element.84), channel_id=1, source_target_pairs={{1,0},{2,1},{3,2},{5,4},{6,5},{7,6},{9,8},{10,9},{11,10},{13,12},{... | collective-permute-start | bytes 12296 | tf_op jit(solution)/shard_map/ppermute | solution.py:253
  215.0 8.4 %collective-permute-start.6 = (f32[8,128]{1,0:T(8,128)S(1)}, f32[8,128]{1,0:T(8,128)S(1)}, u32[]{:S(2)}, u32[]{:S(2)}) collective-permute-start(f32[8,128]{1,0:T(8,128)S(1)} %get-tuple-element.85), channel_id=1, source_target_pairs={{0,1},{1,2},{2,3},{4,5},{5,6},{6,7},{8,9},{9,10},{10,11},{12,13},{... | collective-permute-start | bytes 12296 | tf_op jit(solution)/shard_map/ppermute | solution.py:253
  223.4 10.6 %collective-permute-start.9 = (f32[16,128]{1,0:T(8,128)S(1)}, f32[16,128]{1,0:T(8,128)S(1)}, u32[]{:S(2)}, u32[]{:S(2)}) collective-permute-start(f32[16,128]{1,0:T(8,128)S(1)} %pad_maximum_fusion.4), channel_id=1, source_target_pairs={{0,16},{16,0},{1,17},{17,1},{2,18},{18,2},{3,19},{19,3},{4,20},{20... | collective-permute-start | bytes 24584 | tf_op jit(solution)/shard_map/ppermute | solution.py:257
  223.9 1.1 copy-start.1

commit v12 on v11

--- a/solution.py
+++ b/solution.py
@@ -554,7 +554,7 @@
     coadd, between, other_strip = lax.optimization_barrier((coadd, between, other_strip))
     sides = beyond([strip, other_strip], *between)
     other = swapped(coadd)
-    second, sides, other = lax.optimization_barrier((second, sides, other))
+    second, sides = lax.optimization_barrier((second, sides))
     parts = [(coadd, *sides), (other, *sides)]
     coadd, strip, _ = place(code, second, lots[1])
     other = swapped(coadd)

time: 241 us -> 240 us (level)
    ppermute x4, waiting for transfers between devices: 17.8 us -> 4.95 us  [swapped(): return lax.ppermute(array, 'visit', [(0, 1), (1, 0)])]
    all_to_all x2, waiting for transfers between devices: 119 us -> 131 us  [send(): lax.all_to_all(blocks, EVERY, split_axis=0, concat_axis=0, tiled=True)]
    ppermute x4, starting transfers between devices: 5.4 us -> 9.04 us  [swapped(): return lax.ppermute(array, 'visit', [(0, 1), (1, 0)])]
  transfers between devices with their start and end apart: 12 -> 12, of which waited for: 5 -> 5; matrix products, arithmetic and copies ran while one was open for 5% -> 5% of each run, Pallas kernels for 10% -> 11%
where the time goes in v12:
time: 240 us
  waiting for transfers between devices  147 us (61%)
  Pallas kernels  42.4 us (18%)
  starting transfers between devices  38.4 us (16%)
  other arithmetic  9.48 us (4%)
    all_to_all x2, waiting for transfers between devices, send(): lax.all_to_all(blocks, EVERY, split_axis=0, concat_axis=0, tiled=True)  131 us
    pallas_call x2, Pallas kernels, warp(): pl.pallas_call(functools.partial(warp_kernel, tiles, share, noted), out_s...  16.6 us
    all_to_all x2, starting transfers between devices, send(): lax.all_to_all(blocks, EVERY, split_axis=0, concat_axis=0, tiled=True)  16.3 us
    pallas_call x2, Pallas kernels, stage(): pl.pallas_call(functools.partial(stage_kernel, plan, lots), out_shape=(sh...  16.3 us
    ppermute x4, waiting for transfers between devices, neighbours(): return (lax.ppermute(last, axis, up), lax.ppermute(first, axis, down))  11.1 us
    ppermute x4, starting transfers between devices, neighbours(): return (lax.ppermute(last, axis, up), lax.ppermute(first, axis, down))  11 us
    pallas_call x2, Pallas kernels, place(): pl.pallas_call(functools.partial(place_kernel, 2 * lot), grid_spec=pltpu....  9.48 us
    ppermute x4, starting transfers between devices, swapped(): return lax.ppermute(array, 'visit', [(0, 1), (1, 0)])  9.04 us
  transfers between devices with their start and end apart: 12, of which 5 were waited for; matrix products, arithmetic and copies ran while one was open for 5% of the time, Pallas kernels for 11%

profile of v12, /device:TPU:0, one launch (start us, length us, event | category | flops | bytes accessed | tf_op | source)
XLA Modules:
  0.0 239.5 jit_solution(13292021176547586233)
XLA Ops:
  0.6 8.7 %warp.2 = bf16[32,784,128]{2,1,0:T(8,128)(2,1)} custom-call(s32[24]{0:T(128)} %visit_ref.3, s32[24]{0:T(128)} %bitcast.12, s32[2,24]{1,0:T(2,128)} %bitcast.10, s32[8,256]{1,0:T(8,128)} %good_ref.3, bf16[8,256,256]{2,1,0:T(8,128)(2,1)} %rows_hbm.3, bf16[8,256,256]{2,1,0:T(8,128)(2,1)} %cols_hbm.3, bf16[24,256,256]{2,1,0:T(8,128)(2,1)} %var_hbm.2, ...), custom_call_target="tpu_custom_call" | custom-call | flops 3221225472 | bytes 12582912 | tf_op jit(solution)/shard_map/warp/pallas_call | solution.py:158
  9.4 7.4 %all-to-all-start = ((bf16[32,784,128]{2,1,0:T(8,128)(2,1)}), bf16[32,784,128]{2,1,0:T(8,128)(2,1)}, u32[]{:S(2)}, u32[]{:S(2)}) async-start(bf16[32,784,128]{2,1,0:T(8,128)(2,1)} %warp.2), calls=%async_computation | async-start | bytes 12845056 | tf_op jit(solution)/shard_map/all_to_all | solution.py:532
  16.9 0.6 fusion.26
  17.5 4.4 %fusion.20 = (bf16[48,64]{1,0:T(8,128)(2,1)S(1)}, bf16[48,64]{1,0:T(8,128)(2,1)S(1)}) fusion(f32[]{:T(128)} %bitcast.9, f32[]{:T(128)} %bitcast.8, f32[]{:T(128)} %bitcast.7, f32[]{:T(128)} %bitcast.6, f32[]{:T(128)} %bitcast.5, f32[]{:T(128)} %bitcast.4, f32[]{:T(128)} %bitcast.3, s32[48]{0:T(128)S(1)} %iota_add_fusion), kind=kLoop, calls=%fused_computation.39 | loop fusion | flops 79872 | bytes 12508 | tf_op jit(solution)/shard_map/convert_element_type | solution.py:302
  22.0 0.1 pad_maximum_fusion.3.refs_6_
  22.1 4.5 %fusion.19 = (bf16[80,96]{1,0:T(8,128)(2,1)S(1)}, bf16[80,96]{1,0:T(8,128)(2,1)S(1)}) fusion(f32[]{:T(128)} %bitcast.9, f32[]{:T(128)} %bitcast.8, f32[]{:T(128)} %bitcast.7, f32[]{:T(128)} %bitcast.6, f32[]{:T(128)} %bitcast.5, f32[]{:T(128)} %bitcast.4, f32[]{:T(128)} %bitcast.3, s32[80]{0:T(128)S(1)} %iota_add_fusion.1), kind=kLoop, calls=%fused_computation.35 | loop fusion | flops 199680 | bytes 31068 | tf_op jit(solution)/shard_map/convert_element_type | solution.py:302
  26.5 0.1 pad_maximum_fusion.refs_6_
  26.7 0.1 fusion.9.refs_5_
  26.8 0.1 fusion.refs_7_
  26.9 7.9 %warp.3 = bf16[32,256,128]{2,1,0:T(8,128)(2,1)} custom-call(s32[24]{0:T(128)} %visit_ref.3, s32[24]{0:T(128)} %bitcast.13, s32[2,24]{1,0:T(2,128)} %bitcast.11, s32[8,256]{1,0:T(8,128)} %good_ref.3, bf16[8,256,256]{2,1,0:T(8,128)(2,1)} %rows_hbm.3, bf16[8,256,256]{2,1,0:T(8,128)(2,1)} %cols_hbm.3, bf16[24,256,256]{2,1,0:T(8,128)(2,1)} %var_hbm.2, ...), custom_call_target="tpu_custom_call" | custom-call | flops 3221225472 | bytes 12582912 | tf_op jit(solution)/shard_map/warp/pallas_call | solution.py:158
  34.8 119.0 %all-to-all-done.blocks_ref = bf16[32,784,128]{2,1,0:T(8,128)(2,1)} async-done(((bf16[32,784,128]{2,1,0:T(8,128)(2,1)}), bf16[32,784,128]{2,1,0:T(8,128)(2,1)}, u32[]{:S(2)}, u32[]{:S(2)}) %all-to-all-start) | async-done | bytes 6422560 | tf_op jit(solution)/shard_map/all_to_all | solution.py:532
  153.9 8.9 %all-to-all-start.1 = ((bf16[32,256,128]{2,1,0:T(8,128)(2,1)}), bf16[32,256,128]{2,1,0:T(8,128)(2,1)S(1)}, u32[]{:S(2)}, u32[]{:S(2)}) async-start(bf16[32,256,128]{2,1,0:T(8,128)(2,1)} %warp.3), calls=%async_computation.1 | async-start | bytes 4194304 | tf_op jit(solution)/shard_map/all_to_all | solution.py:532
  162.8 1.0 slice.81
  163.8 0.1 convert_element_type.61.code_ref
  164.0 6.9 %place.2 = (bf16[384,1024]{1,0:T(8,128)(2,1)S(1)}, f32[16,384]{1,0:T(8,128)S(1)}, f32[16,1024]{1,0:T(8,128)S(1)}) custom-call(s32[64]{0:T(128)S(1)} %convert_element_type.61.code_ref, bf16[32,784,128]{2,1,0:T(8,128)(2,1)} %all-to-all-done.blocks_ref), custom_call_target="tpu_custom_call" | custom-call | flops 3211264 | bytes 6422528 | tf_op jit(solution)/shard_map/place/pallas_call | solution.py:227
  170.9 1.3 collective-permute-start.1
  172.2 0.7 collective-permute-start
  172.9 4.6 %collective-permute-start.2 = (f32[16,384]{1,0:T(8,128)S(1)}, f32[16,384]{1,0:T(8,128)S(1)}, u32[]{:S(2)}, u32[]{:S(2)}) collective-permute-start(f32[16,384]{1,0:T(8,128)S(1)} %get-tuple-element.43), channel_id=1, source_target_pairs={{0,16},{16,0},{1,17},{17,1},{2,18},{18,2},{3,19},{19,3},{4,20},{20... | collective-permute-start | bytes 73736 | tf_op jit(solution)/shard_map/ppermute | solution.py:257
  177.5 4.9 %collective-permute-done.2 = f32[16,384]{1,0:T(8,128)S(1)} collective-permute-done((f32[16,384]{1,0:T(8,128)S(1)}, f32[16,384]{1,0:T(8,128)S(1)}, u32[]{:S(2)}, u32[]{:S(2)}) %collective-permute-start.2) | collective-permute-done | bytes 24608 | tf_op jit(solution)/shard_map/ppermute | solution.py:257
  182.4 1.8 collective-permute-start.5
  184.2 2.8 %collective-permute-start.3 = (f32[8,1024]{1,0:T(8,128)S(1)}, f32[8,1024]{1,0:T(8,128)S(1)}, u32[]{:S(2)}, u32[]{:S(2)}) collective-permute-start(f32[8,1024]{1,0:T(8,128)S(1)} %pad_maximum_fusion.1), channel_id=1, source_target_pairs={{0,1},{1,2},{2,3},{4,5},{5,6},{6,7},{8,9},{9,10},{10,11},{12,13},{... | collective-permute-start | bytes 98312 | tf_op jit(solution)/shard_map/ppermute | solution.py:253
  187.0 1.3 collective-permute-start.4
  188.3 9.8 %collective-permute-done.3.refs_9_.refs_12_ = f32[8,1024]{1,0:T(8,128)S(1)} collective-permute-done((f32[8,1024]{1,0:T(8,128)S(1)}, f32[8,1024]{1,0:T(8,128)S(1)}, u32[]{:S(2)}, u32[]{:S(2)}) %collective-permute-start.3) | collective-permute-done | bytes 32800 | tf_op jit(solution)/shard_map/ppermute | solution.py:253
  198.1 11.5 %all-to-all-done.1.blocks_ref = bf16[32,256,128]{2,1,0:T(8,128)(2,1)S(1)} async-done(((bf16[32,256,128]{2,1,0:T(8,128)(2,1)}), bf16[32,256,128]{2,1,0:T(8,128)(2,1)S(1)}, u32[]{:S(2)}, u32[]{:S(2)}) %all-to-all-start.1) | async-done | bytes 2097184 | tf_op jit(solution)/shard_map/all_to_all | solution.py:532
  209.6 2.6 %place.3 = (bf16[128,1024]{1,0:T(8,128)(2,1)S(1)}, f32[16,128]{1,0:T(8,128)S(1)}, f32[16,1024]{1,0:T(8,128)}) custom-call(s32[64]{0:T(128)S(1)} %convert_element_type.61.code_ref, bf16[32,256,128]{2,1,0:T(8,128)(2,1)S(1)} %all-to-all-done.1.blocks_ref), custom_call_target="tpu_custom_call" | custom-call | flops 1048576 | bytes 2097152 | tf_op jit(solution)/shard_map/place/pallas_call | solution.py:227
  212.2 1.5 collective-permute-start.8
  213.7 1.3 collective-permute-start.7
  215.0 5.7 %collective-permute-start.6 = (f32[8,128]{1,0:T(8,128)S(1)}, f32[8,128]{1,0:T(8,128)S(1)}, u32[]{:S(2)}, u32[]{:S(2)}) collective-permute-start(f32[8,128]{1,0:T(8,128)S(1)} %get-tuple-element.83), channel_id=1, source_target_pairs={{0,1},{1,2},{2,3},{4,5},{5,6},{6,7},{8,9},{9,10},{10,11},{12,13},{... | collective-permute-start | bytes 12296 | tf_op jit(solution)/shard_map/ppermute | solution.py:253
  220.7 1.3 collective-permute-done.6.refs_15_
  222.0 1.2 collective-permute-start.9
  223.2 9.5 %stage.2 = (f32[1024,1024]{1,0:T(8,128)}, f32[1024,1024]{1,0:T(8,128)}) custom-call(s32[1]{0:T(128)} %bitcast.refs_0_, f32[7]{0:T(128)S(1)} %copy-done, f32[8,1024]{1,0:T(8,128)S(1)} %get-tuple-element.53.refs_2_, f32[8,1024]{1,0:T(8,128)S(1)} %get-tuple-element.54.refs_3_, bf16[96,96]{1,0:T(8,128)(2,1)S(1)} %fusion.1.refs_4_, ...), custom_call_target="tpu_custom_call" | custom-call | flops 79626240 | bytes 11943936 | tf_op jit(solution)/shard_map/stage/pallas_call | solution.py:455
  232.7 6.8 %stage.3 = (f32[1024,1024]{1,0:T(8,128)}, f32[1024,1024]{1,0:T(8,128)}) custom-call(s32[1]{0:T(128)} %bitcast.refs_0_, f32[7]{0:T(128)S(1)} %copy-done, f32[8,1024]{1,0:T(8,128)S(1)} %get-tuple-element.53.refs_2_, f32[8,1024]{1,0:T(8,128)S(1)} %get-tuple-element.54.refs_3_, ...), custom_call_target="tpu_custom_call", output_to_operand_aliasing={{0}: (20, {}), {1}: (21, {})} | custom-call | flops 47185920 | bytes 7077888 | tf_op jit(solution)/shard_map/stage/pallas_call | solution.py:455
  (26 shorter events, 0.2 us)
Async XLA Ops:
  9.4 7.5 %copy-start = (f32[7]{0:T(128)S(1)}, f32[7]{0:T(128)}, u32[]{:S(2)}) copy-start(f32[7]{0:T(128)} %refs_1_.1) | copy-start | bytes 88
  9.4 144.5 %all-to-all-start = ((bf16[32,784,128]{2,1,0:T(8,128)(2,1)}), bf16[32,784,128]{2,1,0:T(8,128)(2,1)}, u32[]{:S(2)}, u32[]{:S(2)}) async-start(bf16[32,784,128]{2,1,0:T(8,128)(2,1)} %warp.2), calls=%async_computation | async-start | bytes 12845056 | tf_op jit(solution)/shard_map/all_to_all | solution.py:532
  153.9 55.7 %all-to-all-start.1 = ((bf16[32,256,128]{2,1,0:T(8,128)(2,1)}), bf16[32,256,128]{2,1,0:T(8,128)(2,1)S(1)}, u32[]{:S(2)}, u32[]{:S(2)}) async-start(bf16[32,256,128]{2,1,0:T(8,128)(2,1)} %warp.3), calls=%async_computation.1 | async-start | bytes 4194304 | tf_op jit(solution)/shard_map/all_to_all | solution.py:532
  170.9 6.6 %collective-permute-start.1 = (f32[8,1024]{1,0:T(8,128)S(1)}, f32[8,1024]{1,0:T(8,128)S(1)}, u32[]{:S(2)}, u32[]{:S(2)}) collective-permute-start(f32[8,1024]{1,0:T(8,128)S(1)} %slice_select_fusion), channel_id=1, source_target_pairs={{4,0},{8,4},{12,8},{16,20},{20,24},{24,28},{5,1},{9,5},{13,9},{17,... | collective-permute-start | bytes 98312 | tf_op jit(solution)/shard_map/ppermute | solution.py:277
  172.2 5.3 %collective-permute-start = (f32[8,1024]{1,0:T(8,128)S(1)}, f32[8,1024]{1,0:T(8,128)S(1)}, u32[]{:S(2)}, u32[]{:S(2)}) collective-permute-start(f32[8,1024]{1,0:T(8,128)S(1)} %slice_select_fusion), channel_id=1, source_target_pairs={{4,16},{8,20},{12,24},{16,4},{20,8},{24,12},{5,17},{9,21},{13,25},... | collective-permute-start | bytes 98312 | tf_op jit(solution)/shard_map/ppermute | solution.py:278
  172.9 9.6 %collective-permute-start.2 = (f32[16,384]{1,0:T(8,128)S(1)}, f32[16,384]{1,0:T(8,128)S(1)}, u32[]{:S(2)}, u32[]{:S(2)}) collective-permute-start(f32[16,384]{1,0:T(8,128)S(1)} %get-tuple-element.43), channel_id=1, source_target_pairs={{0,16},{16,0},{1,17},{17,1},{2,18},{18,2},{3,19},{19,3},{4,20},{20... | collective-permute-start | bytes 73736 | tf_op jit(solution)/shard_map/ppermute | solution.py:257
  182.4 38.2 %collective-permute-start.5 = (bf16[384,1024]{1,0:T(8,128)(2,1)S(1)}, bf16[384,1024]{1,0:T(8,128)(2,1)}, u32[]{:S(2)}, u32[]{:S(2)}) collective-permute-start(bf16[384,1024]{1,0:T(8,128)(2,1)S(1)} %get-tuple-element.59.refs_8_), channel_id=1, source_target_pairs={{0,16},{16,0},{1,17},{17,1},{2,18},{18,2},{3,19},{19,3},{4,20},{20... | collective-permute-start | bytes 2359304 | tf_op jit(solution)/shard_map/ppermute | solution.py:257
  184.2 13.9 %collective-permute-start.3 = (f32[8,1024]{1,0:T(8,128)S(1)}, f32[8,1024]{1,0:T(8,128)S(1)}, u32[]{:S(2)}, u32[]{:S(2)}) collective-permute-start(f32[8,1024]{1,0:T(8,128)S(1)} %pad_maximum_fusion.1), channel_id=1, source_target_pairs={{0,1},{1,2},{2,3},{4,5},{5,6},{6,7},{8,9},{9,10},{10,11},{12,13},{... | collective-permute-start | bytes 98312 | tf_op jit(solution)/shard_map/ppermute | solution.py:253
  187.0 11.1 %collective-permute-start.4 = (f32[8,1024]{1,0:T(8,128)S(1)}, f32[8,1024]{1,0:T(8,128)S(1)}, u32[]{:S(2)}, u32[]{:S(2)}) collective-permute-start(f32[8,1024]{1,0:T(8,128)S(1)} %pad_maximum_fusion.2), channel_id=1, source_target_pairs={{1,0},{2,1},{3,2},{5,4},{6,5},{7,6},{9,8},{10,9},{11,10},{13,12},{... | collective-permute-start | bytes 98312 | tf_op jit(solution)/shard_map/ppermute | solution.py:253
  212.2 20.5 %collective-permute-start.8 = (bf16[128,1024]{1,0:T(8,128)(2,1)S(1)}, bf16[128,1024]{1,0:T(8,128)(2,1)S(1)}, u32[]{:S(2)}, u32[]{:S(2)}) collective-permute-start(bf16[128,1024]{1,0:T(8,128)(2,1)S(1)} %get-tuple-element.52.refs_14_), channel_id=1, source_target_pairs={{0,16},{16,0},{1,17},{17,1},{2,18},{18,2},{3,19},{19,3},{4,20},{20... | collective-permute-start | bytes 786440 | tf_op jit(solution)/shard_map/ppermute | solution.py:257
  213.7 7.0 %collective-permute-start.7 = (f32[8,128]{1,0:T(8,128)S(1)}, f32[8,128]{1,0:T(8,128)S(1)}, u32[]{:S(2)}, u32[]{:S(2)}) collective-permute-start(f32[8,128]{1,0:T(8,128)S(1)} %get-tuple-element.82), channel_id=1, source_target_pairs={{1,0},{2,1},{3,2},{5,4},{6,5},{7,6},{9,8},{10,9},{11,10},{13,12},{... | collective-permute-start | bytes 12296 | tf_op jit(solution)/shard_map/ppermute | solution.py:253
  215.0 7.0 %collective-permute-start.6 = (f32[8,128]{1,0:T(8,128)S(1)}, f32[8,128]{1,0:T(8,128)S(1)}, u32[]{:S(2)}, u32[]{:S(2)}) collective-permute-start(f32[8,128]{1,0:T(8,128)S(1)} %get-tuple-element.83), channel_id=1, source_target_pairs={{0,1},{1,2},{2,3},{4,5},{5,6},{6,7},{8,9},{9,10},{10,11},{12,13},{... | collective-permute-start | bytes 12296 | tf_op jit(solution)/shard_map/ppermute | solution.py:253
  222.0 10.7 %collective-permute-start.9 = (f32[16,128]{1,0:T(8,128)S(1)}, f32[16,128]{1,0:T(8,128)S(1)}, u32[]{:S(2)}, u32[]{:S(2)}) collective-permute-start(f32[16,128]{1,0:T(8,128)S(1)} %pad_maximum_fusion.4), channel_id=1, source_target_pairs={{0,16},{16,0},{1,17},{17,1},{2,18},{18,2},{3,19},{19,3},{4,20},{20... | collective-permute-start | bytes 24584 | tf_op jit(solution)/shard_map/ppermute | solution.py:257

commit v13 on v12

--- a/solution.py
+++ b/solution.py
@@ -557,11 +557,12 @@
     second, sides = lax.optimization_barrier((second, sides))
     parts = [(coadd, *sides), (other, *sides)]
     coadd, strip, _ = place(code, second, lots[1])
+    near = neighbours(strip[:HALO], strip[HALO:], "px")
+    coadd, near = lax.optimization_barrier((coadd, near))
+    far = swapped(jnp.concatenate(near, axis=0))
     other = swapped(coadd)
-    near = neighbours(strip[:HALO], strip[HALO:], "px")
     (parts, between), _ = lax.optimization_barrier(((parts, between), coadd))
     held = stage(outer, mine, psf_taps, between, tables[0], [parts], lots[:1])
-    far = swapped(jnp.concatenate(near, axis=0))
     more = [(coadd, *near), (other, far, far)]
     return stage(inner, mine, psf_taps, between, tables[1], [parts, more], lots, held)
 

time: 240 us -> 241 us (level)
  transfers between devices with their start and end apart: 12 -> 12, of which waited for: 5 -> 5; matrix products, arithmetic and copies ran while one was open for 5% -> 5% of each run, Pallas kernels for 11% -> 12%
where the time goes in v13:
time: 241 us; the launch traced here: 240 us
  waiting for transfers between devices  147 us (61%)
  Pallas kernels  43.7 us (18%)
  starting transfers between devices  37.1 us (15%)
  other arithmetic  9.48 us (4%)
    all_to_all x2, waiting for transfers between devices, send(): lax.all_to_all(blocks, EVERY, split_axis=0, concat_axis=0, tiled=True)  131 us
    pallas_call x2, Pallas kernels, warp(): pl.pallas_call(functools.partial(warp_kernel, tiles, share, noted), out_s...  16.6 us
    pallas_call x2, Pallas kernels, stage(): pl.pallas_call(functools.partial(stage_kernel, plan, lots), out_shape=(sh...  16.3 us
    all_to_all x2, starting transfers between devices, send(): lax.all_to_all(blocks, EVERY, split_axis=0, concat_axis=0, tiled=True)  16.3 us
    ppermute x4, starting transfers between devices, neighbours(): return (lax.ppermute(last, axis, up), lax.ppermute(first, axis, down))  11.7 us
    ppermute x4, waiting for transfers between devices, neighbours(): return (lax.ppermute(last, axis, up), lax.ppermute(first, axis, down))  11.1 us
    pallas_call x2, Pallas kernels, place(): pl.pallas_call(functools.partial(place_kernel, 2 * lot), grid_spec=pltpu....  10.8 us
    convert_element_type x2, other arithmetic, split(): coarse = value.astype(jnp.bfloat16)  8.89 us
  transfers between devices with their start and end apart: 12, of which 5 were waited for; matrix products, arithmetic and copies ran while one was open for 5% of the time, Pallas kernels for 12%

profile of v13, /device:TPU:0, one launch (start us, length us, event | category | flops | bytes accessed | tf_op | source)
XLA Modules:
  0.0 240.0 jit_solution(3060790063312696641)
XLA Ops:
  0.6 8.7 %warp.2 = bf16[32,784,128]{2,1,0:T(8,128)(2,1)} custom-call(s32[24]{0:T(128)} %visit_ref.3, s32[24]{0:T(128)} %bitcast.12, s32[2,24]{1,0:T(2,128)} %bitcast.10, s32[8,256]{1,0:T(8,128)} %good_ref.3, bf16[8,256,256]{2,1,0:T(8,128)(2,1)} %rows_hbm.3, bf16[8,256,256]{2,1,0:T(8,128)(2,1)} %cols_hbm.3, bf16[24,256,256]{2,1,0:T(8,128)(2,1)} %var_hbm.2, ...), custom_call_target="tpu_custom_call" | custom-call | flops 3221225472 | bytes 12582912 | tf_op jit(solution)/shard_map/warp/pallas_call | solution.py:158
  9.4 7.4 %all-to-all-start = ((bf16[32,784,128]{2,1,0:T(8,128)(2,1)}), bf16[32,784,128]{2,1,0:T(8,128)(2,1)}, u32[]{:S(2)}, u32[]{:S(2)}) async-start(bf16[32,784,128]{2,1,0:T(8,128)(2,1)} %warp.2), calls=%async_computation | async-start | bytes 12845056 | tf_op jit(solution)/shard_map/all_to_all | solution.py:532
  16.8 0.6 fusion.26
  17.5 4.4 %fusion.20 = (bf16[48,64]{1,0:T(8,128)(2,1)S(1)}, bf16[48,64]{1,0:T(8,128)(2,1)S(1)}) fusion(f32[]{:T(128)} %bitcast.9, f32[]{:T(128)} %bitcast.8, f32[]{:T(128)} %bitcast.7, f32[]{:T(128)} %bitcast.6, f32[]{:T(128)} %bitcast.5, f32[]{:T(128)} %bitcast.4, f32[]{:T(128)} %bitcast.3, s32[48]{0:T(128)S(1)} %iota_add_fusion), kind=kLoop, calls=%fused_computation.39 | loop fusion | flops 79872 | bytes 12508 | tf_op jit(solution)/shard_map/convert_element_type | solution.py:302
  21.9 0.1 pad_maximum_fusion.3.refs_6_
  22.0 4.5 %fusion.19 = (bf16[80,96]{1,0:T(8,128)(2,1)S(1)}, bf16[80,96]{1,0:T(8,128)(2,1)S(1)}) fusion(f32[]{:T(128)} %bitcast.9, f32[]{:T(128)} %bitcast.8, f32[]{:T(128)} %bitcast.7, f32[]{:T(128)} %bitcast.6, f32[]{:T(128)} %bitcast.5, f32[]{:T(128)} %bitcast.4, f32[]{:T(128)} %bitcast.3, s32[80]{0:T(128)S(1)} %iota_add_fusion.1), kind=kLoop, calls=%fused_computation.35 | loop fusion | flops 199680 | bytes 31068 | tf_op jit(solution)/shard_map/convert_element_type | solution.py:302
  26.5 0.1 pad_maximum_fusion.refs_6_
  26.7 0.1 fusion.9.refs_5_
  26.7 0.1 fusion.refs_7_
  26.9 7.9 %warp.3 = bf16[32,256,128]{2,1,0:T(8,128)(2,1)} custom-call(s32[24]{0:T(128)} %visit_ref.3, s32[24]{0:T(128)} %bitcast.13, s32[2,24]{1,0:T(2,128)} %bitcast.11, s32[8,256]{1,0:T(8,128)} %good_ref.3, bf16[8,256,256]{2,1,0:T(8,128)(2,1)} %rows_hbm.3, bf16[8,256,256]{2,1,0:T(8,128)(2,1)} %cols_hbm.3, bf16[24,256,256]{2,1,0:T(8,128)(2,1)} %var_hbm.2, ...), custom_call_target="tpu_custom_call" | custom-call | flops 3221225472 | bytes 12582912 | tf_op jit(solution)/shard_map/warp/pallas_call | solution.py:158
  34.8 119.0 %all-to-all-done.blocks_ref = bf16[32,784,128]{2,1,0:T(8,128)(2,1)} async-done(((bf16[32,784,128]{2,1,0:T(8,128)(2,1)}), bf16[32,784,128]{2,1,0:T(8,128)(2,1)}, u32[]{:S(2)}, u32[]{:S(2)}) %all-to-all-start) | async-done | bytes 6422560 | tf_op jit(solution)/shard_map/all_to_all | solution.py:532
  153.8 8.9 %all-to-all-start.1 = ((bf16[32,256,128]{2,1,0:T(8,128)(2,1)}), bf16[32,256,128]{2,1,0:T(8,128)(2,1)S(1)}, u32[]{:S(2)}, u32[]{:S(2)}) async-start(bf16[32,256,128]{2,1,0:T(8,128)(2,1)} %warp.3), calls=%async_computation.1 | async-start | bytes 4194304 | tf_op jit(solution)/shard_map/all_to_all | solution.py:532
  162.8 1.0 slice.81
  163.8 0.1 convert_element_type.61.code_ref
  163.9 7.7 %place.2 = (bf16[384,1024]{1,0:T(8,128)(2,1)S(1)}, f32[16,384]{1,0:T(8,128)S(1)}, f32[16,1024]{1,0:T(8,128)S(1)}) custom-call(s32[64]{0:T(128)S(1)} %convert_element_type.61.code_ref, bf16[32,784,128]{2,1,0:T(8,128)(2,1)} %all-to-all-done.blocks_ref), custom_call_target="tpu_custom_call" | custom-call | flops 3211264 | bytes 6422528 | tf_op jit(solution)/shard_map/place/pallas_call | solution.py:227
  171.6 1.3 collective-permute-start.1
  172.9 0.7 collective-permute-start
  173.6 4.1 %collective-permute-start.2 = (f32[16,384]{1,0:T(8,128)S(1)}, f32[16,384]{1,0:T(8,128)S(1)}, u32[]{:S(2)}, u32[]{:S(2)}) collective-permute-start(f32[16,384]{1,0:T(8,128)S(1)} %get-tuple-element.46), channel_id=1, source_target_pairs={{0,16},{16,0},{1,17},{17,1},{2,18},{18,2},{3,19},{19,3},{4,20},{20... | collective-permute-start | bytes 73736 | tf_op jit(solution)/shard_map/ppermute | solution.py:257
  177.7 5.5 %collective-permute-done.2 = f32[16,384]{1,0:T(8,128)S(1)} collective-permute-done((f32[16,384]{1,0:T(8,128)S(1)}, f32[16,384]{1,0:T(8,128)S(1)}, u32[]{:S(2)}, u32[]{:S(2)}) %collective-permute-start.2) | collective-permute-done | bytes 24608 | tf_op jit(solution)/shard_map/ppermute | solution.py:257
  183.1 1.0 collective-permute-start.5
  184.2 2.8 %collective-permute-start.3 = (f32[8,1024]{1,0:T(8,128)S(1)}, f32[8,1024]{1,0:T(8,128)S(1)}, u32[]{:S(2)}, u32[]{:S(2)}) collective-permute-start(f32[8,1024]{1,0:T(8,128)S(1)} %pad_maximum_fusion.1), channel_id=1, source_target_pairs={{0,1},{1,2},{2,3},{4,5},{5,6},{6,7},{8,9},{9,10},{10,11},{12,13},{... | collective-permute-start | bytes 98312 | tf_op jit(solution)/shard_map/ppermute | solution.py:253
  187.0 1.3 collective-permute-start.4
  188.3 9.8 %collective-permute-done.3.refs_9_.refs_12_ = f32[8,1024]{1,0:T(8,128)S(1)} collective-permute-done((f32[8,1024]{1,0:T(8,128)S(1)}, f32[8,1024]{1,0:T(8,128)S(1)}, u32[]{:S(2)}, u32[]{:S(2)}) %collective-permute-start.3) | collective-permute-done | bytes 32800 | tf_op jit(solution)/shard_map/ppermute | solution.py:253
  198.1 11.5 %all-to-all-done.1.blocks_ref = bf16[32,256,128]{2,1,0:T(8,128)(2,1)S(1)} async-done(((bf16[32,256,128]{2,1,0:T(8,128)(2,1)}), bf16[32,256,128]{2,1,0:T(8,128)(2,1)S(1)}, u32[]{:S(2)}, u32[]{:S(2)}) %all-to-all-start.1) | async-done | bytes 2097184 | tf_op jit(solution)/shard_map/all_to_all | solution.py:532
  209.6 3.1 %place.3 = (bf16[128,1024]{1,0:T(8,128)(2,1)S(1)}, f32[16,128]{1,0:T(8,128)S(1)}, f32[16,1024]{1,0:T(8,128)}) custom-call(s32[64]{0:T(128)S(1)} %convert_element_type.61.code_ref, bf16[32,256,128]{2,1,0:T(8,128)(2,1)S(1)} %all-to-all-done.1.blocks_ref), custom_call_target="tpu_custom_call" | custom-call | flops 1048576 | bytes 2097152 | tf_op jit(solution)/shard_map/place/pallas_call | solution.py:227
  212.7 1.3 collective-permute-start.7
  214.0 6.3 %collective-permute-start.6 = (f32[8,128]{1,0:T(8,128)S(1)}, f32[8,128]{1,0:T(8,128)S(1)}, u32[]{:S(2)}, u32[]{:S(2)}) collective-permute-start(f32[8,128]{1,0:T(8,128)S(1)} %get-tuple-element.89), channel_id=1, source_target_pairs={{0,1},{1,2},{2,3},{4,5},{5,6},{6,7},{8,9},{9,10},{10,11},{12,13},{... | collective-permute-start | bytes 12296 | tf_op jit(solution)/shard_map/ppermute | solution.py:253
  220.3 1.3 collective-permute-done.6.refs_15_
  221.6 0.8 collective-permute-start.8
  222.4 1.2 collective-permute-start.9
  223.6 9.5 %stage.2 = (f32[1024,1024]{1,0:T(8,128)}, f32[1024,1024]{1,0:T(8,128)}) custom-call(s32[1]{0:T(128)} %bitcast.refs_0_, f32[7]{0:T(128)S(1)} %copy-done, f32[8,1024]{1,0:T(8,128)S(1)} %get-tuple-element.58.refs_2_, f32[8,1024]{1,0:T(8,128)S(1)} %get-tuple-element.59.refs_3_, bf16[96,96]{1,0:T(8,128)(2,1)S(1)} %fusion.1.refs_4_, ...), custom_call_target="tpu_custom_call" | custom-call | flops 79626240 | bytes 11943936 | tf_op jit(solution)/shard_map/stage/pallas_call | solution.py:455
  233.2 6.8 %stage.3 = (f32[1024,1024]{1,0:T(8,128)}, f32[1024,1024]{1,0:T(8,128)}) custom-call(s32[1]{0:T(128)} %bitcast.refs_0_, f32[7]{0:T(128)S(1)} %copy-done, f32[8,1024]{1,0:T(8,128)S(1)} %get-tuple-element.58.refs_2_, f32[8,1024]{1,0:T(8,128)S(1)} %get-tuple-element.59.refs_3_, ...), custom_call_target="tpu_custom_call", output_to_operand_aliasing={{0}: (20, {}), {1}: (21, {})} | custom-call | flops 47185920 | bytes 7077888 | tf_op jit(solution)/shard_map/stage/pallas_call | solution.py:455
  (26 shorter events, 0.2 us)
Async XLA Ops:
  9.4 7.5 %copy-start = (f32[7]{0:T(128)S(1)}, f32[7]{0:T(128)}, u32[]{:S(2)}) copy-start(f32[7]{0:T(128)} %refs_1_.1) | copy-start | bytes 88
  9.4 144.5 %all-to-all-start = ((bf16[32,784,128]{2,1,0:T(8,128)(2,1)}), bf16[32,784,128]{2,1,0:T(8,128)(2,1)}, u32[]{:S(2)}, u32[]{:S(2)}) async-start(bf16[32,784,128]{2,1,0:T(8,128)(2,1)} %warp.2), calls=%async_computation | async-start | bytes 12845056 | tf_op jit(solution)/shard_map/all_to_all | solution.py:532
  153.8 55.7 %all-to-all-start.1 = ((bf16[32,256,128]{2,1,0:T(8,128)(2,1)}), bf16[32,256,128]{2,1,0:T(8,128)(2,1)S(1)}, u32[]{:S(2)}, u32[]{:S(2)}) async-start(bf16[32,256,128]{2,1,0:T(8,128)(2,1)} %warp.3), calls=%async_computation.1 | async-start | bytes 4194304 | tf_op jit(solution)/shard_map/all_to_all | solution.py:532
  171.6 6.1 %collective-permute-start.1 = (f32[8,1024]{1,0:T(8,128)S(1)}, f32[8,1024]{1,0:T(8,128)S(1)}, u32[]{:S(2)}, u32[]{:S(2)}) collective-permute-start(f32[8,1024]{1,0:T(8,128)S(1)} %slice_select_fusion), channel_id=1, source_target_pairs={{4,0},{8,4},{12,8},{16,20},{20,24},{24,28},{5,1},{9,5},{13,9},{17,... | collective-permute-start | bytes 98312 | tf_op jit(solution)/shard_map/ppermute | solution.py:277
  172.9 4.8 %collective-permute-start = (f32[8,1024]{1,0:T(8,128)S(1)}, f32[8,1024]{1,0:T(8,128)S(1)}, u32[]{:S(2)}, u32[]{:S(2)}) collective-permute-start(f32[8,1024]{1,0:T(8,128)S(1)} %slice_select_fusion), channel_id=1, source_target_pairs={{4,16},{8,20},{12,24},{16,4},{20,8},{24,12},{5,17},{9,21},{13,25},... | collective-permute-start | bytes 98312 | tf_op jit(solution)/shard_map/ppermute | solution.py:278
  173.6 9.5 %collective-permute-start.2 = (f32[16,384]{1,0:T(8,128)S(1)}, f32[16,384]{1,0:T(8,128)S(1)}, u32[]{:S(2)}, u32[]{:S(2)}) collective-permute-start(f32[16,384]{1,0:T(8,128)S(1)} %get-tuple-element.46), channel_id=1, source_target_pairs={{0,16},{16,0},{1,17},{17,1},{2,18},{18,2},{3,19},{19,3},{4,20},{20... | collective-permute-start | bytes 73736 | tf_op jit(solution)/shard_map/ppermute | solution.py:257
  183.1 40.5 %collective-permute-start.5 = (bf16[384,1024]{1,0:T(8,128)(2,1)S(1)}, bf16[384,1024]{1,0:T(8,128)(2,1)}, u32[]{:S(2)}, u32[]{:S(2)}) collective-permute-start(bf16[384,1024]{1,0:T(8,128)(2,1)S(1)} %get-tuple-element.64.refs_8_), channel_id=1, source_target_pairs={{0,16},{16,0},{1,17},{17,1},{2,18},{18,2},{3,19},{19,3},{4,20},{20... | collective-permute-start | bytes 2359304 | tf_op jit(solution)/shard_map/ppermute | solution.py:257
  184.2 13.9 %collective-permute-start.3 = (f32[8,1024]{1,0:T(8,128)S(1)}, f32[8,1024]{1,0:T(8,128)S(1)}, u32[]{:S(2)}, u32[]{:S(2)}) collective-permute-start(f32[8,1024]{1,0:T(8,128)S(1)} %pad_maximum_fusion.1), channel_id=1, source_target_pairs={{0,1},{1,2},{2,3},{4,5},{5,6},{6,7},{8,9},{9,10},{10,11},{12,13},{... | collective-permute-start | bytes 98312 | tf_op jit(solution)/shard_map/ppermute | solution.py:253
  187.0 11.1 %collective-permute-start.4 = (f32[8,1024]{1,0:T(8,128)S(1)}, f32[8,1024]{1,0:T(8,128)S(1)}, u32[]{:S(2)}, u32[]{:S(2)}) collective-permute-start(f32[8,1024]{1,0:T(8,128)S(1)} %pad_maximum_fusion.2), channel_id=1, source_target_pairs={{1,0},{2,1},{3,2},{5,4},{6,5},{7,6},{9,8},{10,9},{11,10},{13,12},{... | collective-permute-start | bytes 98312 | tf_op jit(solution)/shard_map/ppermute | solution.py:253
  212.7 7.6 %collective-permute-start.7 = (f32[8,128]{1,0:T(8,128)S(1)}, f32[8,128]{1,0:T(8,128)S(1)}, u32[]{:S(2)}, u32[]{:S(2)}) collective-permute-start(f32[8,128]{1,0:T(8,128)S(1)} %get-tuple-element.88), channel_id=1, source_target_pairs={{1,0},{2,1},{3,2},{5,4},{6,5},{7,6},{9,8},{10,9},{11,10},{13,12},{... | collective-permute-start | bytes 12296 | tf_op jit(solution)/shard_map/ppermute | solution.py:253
  214.0 7.6 %collective-permute-start.6 = (f32[8,128]{1,0:T(8,128)S(1)}, f32[8,128]{1,0:T(8,128)S(1)}, u32[]{:S(2)}, u32[]{:S(2)}) collective-permute-start(f32[8,128]{1,0:T(8,128)S(1)} %get-tuple-element.89), channel_id=1, source_target_pairs={{0,1},{1,2},{2,3},{4,5},{5,6},{6,7},{8,9},{9,10},{10,11},{12,13},{... | collective-permute-start | bytes 12296 | tf_op jit(solution)/shard_map/ppermute | solution.py:253
  221.6 11.6 %collective-permute-start.8 = (bf16[128,1024]{1,0:T(8,128)(2,1)S(1)}, bf16[128,1024]{1,0:T(8,128)(2,1)S(1)}, u32[]{:S(2)}, u32[]{:S(2)}) collective-permute-start(bf16[128,1024]{1,0:T(8,128)(2,1)S(1)} %get-tuple-element.57.refs_14_), channel_id=1, source_target_pairs={{0,16},{16,0},{1,17},{17,1},{2,18},{18,2},{3,19},{19,3},{4,20},{20... | collective-permute-start | bytes 786440 | tf_op jit(solution)/shard_map/ppermute | solution.py:257
  222.4 10.7 %collective-permute-start.9 = (f32[16,128]{1,0:T(8,128)S(1)}, f32[16,128]{1,0:T(8,128)S(1)}, u32[]{:S(2)}, u32[]{:S(2)}) collective-permute-start(f32[16,128]{1,0:T(8,128)S(1)} %pad_maximum_fusion.4), channel_id=1, source_target_pairs={{0,16},{16,0},{1,17},{17,1},{2,18},{18,2},{3,19},{19,3},{4,20},{20... | collective-permute-start | bytes 24584 | tf_op jit(solution)/shard_map/ppermute | solution.py:257

commit v14 on v12

--- a/solution.py
+++ b/solution.py
@@ -558,9 +558,10 @@
     parts = [(coadd, *sides), (other, *sides)]
     coadd, strip, _ = place(code, second, lots[1])
     other = swapped(coadd)
-    near = neighbours(strip[:HALO], strip[HALO:], "px")
     (parts, between), _ = lax.optimization_barrier(((parts, between), coadd))
     held = stage(outer, mine, psf_taps, between, tables[0], [parts], lots[:1])
+    strip, held = lax.optimization_barrier((strip, held))
+    near = neighbours(strip[:HALO], strip[HALO:], "px")
     far = swapped(jnp.concatenate(near, axis=0))
     more = [(coadd, *near), (other, far, far)]
     return stage(inner, mine, psf_taps, between, tables[1], [parts, more], lots, held)

time: 240 us -> 243 us (1.012)
    ppermute x4, waiting for transfers between devices: 4.95 us -> 7.41 us  [swapped(): return lax.ppermute(array, 'visit', [(0, 1), (1, 0)])]
  transfers between devices with their start and end apart: 12 -> 12, of which waited for: 5 -> 6; matrix products, arithmetic and copies ran while one was open for 5% -> 5% of each run, Pallas kernels for 11% -> 11%
where the time goes in v14:
time: 243 us; the launch traced here: 242 us
  waiting for transfers between devices  149 us (61%)
  Pallas kernels  42.5 us (17%)
  starting transfers between devices  38.8 us (16%)
  other arithmetic  9.48 us (4%)
    all_to_all x2, waiting for transfers between devices, send(): lax.all_to_all(blocks, EVERY, split_axis=0, concat_axis=0, tiled=True)  131 us
    pallas_call x2, Pallas kernels, warp(): pl.pallas_call(functools.partial(warp_kernel, tiles, share, noted), out_s...  16.7 us
    pallas_call x2, Pallas kernels, stage(): pl.pallas_call(functools.partial(stage_kernel, plan, lots), out_shape=(sh...  16.3 us
    all_to_all x2, starting transfers between devices, send(): lax.all_to_all(blocks, EVERY, split_axis=0, concat_axis=0, tiled=True)  16.3 us
    ppermute x4, starting transfers between devices, neighbours(): return (lax.ppermute(last, axis, up), lax.ppermute(first, axis, down))  11.6 us
    ppermute x4, waiting for transfers between devices, neighbours(): return (lax.ppermute(last, axis, up), lax.ppermute(first, axis, down))  11.1 us
    pallas_call x2, Pallas kernels, place(): pl.pallas_call(functools.partial(place_kernel, 2 * lot), grid_spec=pltpu....  9.48 us
    ppermute x4, starting transfers between devices, swapped(): return lax.ppermute(array, 'visit', [(0, 1), (1, 0)])  9.04 us
  transfers between devices with their start and end apart: 12, of which 6 were waited for; matrix products, arithmetic and copies ran while one was open for 5% of the time, Pallas kernels for 11%

profile of v14, /device:TPU:0, one launch (start us, length us, event | category | flops | bytes accessed | tf_op | source)
XLA Modules:
  0.0 242.5 jit_solution(2378698418632010600)
XLA Ops:
  0.6 8.8 %warp.2 = bf16[32,784,128]{2,1,0:T(8,128)(2,1)} custom-call(s32[24]{0:T(128)} %visit_ref.3, s32[24]{0:T(128)} %bitcast.12, s32[2,24]{1,0:T(2,128)} %bitcast.10, s32[8,256]{1,0:T(8,128)} %good_ref.3, bf16[8,256,256]{2,1,0:T(8,128)(2,1)} %rows_hbm.3, bf16[8,256,256]{2,1,0:T(8,128)(2,1)} %cols_hbm.3, bf16[24,256,256]{2,1,0:T(8,128)(2,1)} %var_hbm.2, ...), custom_call_target="tpu_custom_call" | custom-call | flops 3221225472 | bytes 12582912 | tf_op jit(solution)/shard_map/warp/pallas_call | solution.py:158
  9.4 7.4 %all-to-all-start = ((bf16[32,784,128]{2,1,0:T(8,128)(2,1)}), bf16[32,784,128]{2,1,0:T(8,128)(2,1)}, u32[]{:S(2)}, u32[]{:S(2)}) async-start(bf16[32,784,128]{2,1,0:T(8,128)(2,1)} %warp.2), calls=%async_computation | async-start | bytes 12845056 | tf_op jit(solution)/shard_map/all_to_all | solution.py:532
  16.9 0.6 fusion.26
  17.5 4.4 %fusion.20 = (bf16[48,64]{1,0:T(8,128)(2,1)S(1)}, bf16[48,64]{1,0:T(8,128)(2,1)S(1)}) fusion(f32[]{:T(128)} %bitcast.9, f32[]{:T(128)} %bitcast.8, f32[]{:T(128)} %bitcast.7, f32[]{:T(128)} %bitcast.6, f32[]{:T(128)} %bitcast.5, f32[]{:T(128)} %bitcast.4, f32[]{:T(128)} %bitcast.3, s32[48]{0:T(128)S(1)} %iota_add_fusion), kind=kLoop, calls=%fused_computation.39 | loop fusion | flops 79872 | bytes 12508 | tf_op jit(solution)/shard_map/convert_element_type | solution.py:302
  22.0 0.1 pad_maximum_fusion.3.refs_6_
  22.1 4.5 %fusion.19 = (bf16[80,96]{1,0:T(8,128)(2,1)S(1)}, bf16[80,96]{1,0:T(8,128)(2,1)S(1)}) fusion(f32[]{:T(128)} %bitcast.9, f32[]{:T(128)} %bitcast.8, f32[]{:T(128)} %bitcast.7, f32[]{:T(128)} %bitcast.6, f32[]{:T(128)} %bitcast.5, f32[]{:T(128)} %bitcast.4, f32[]{:T(128)} %bitcast.3, s32[80]{0:T(128)S(1)} %iota_add_fusion.1), kind=kLoop, calls=%fused_computation.35 | loop fusion | flops 199680 | bytes 31068 | tf_op jit(solution)/shard_map/convert_element_type | solution.py:302
  26.5 0.1 pad_maximum_fusion.refs_6_
  26.8 0.1 fusion.refs_7_
  26.9 7.9 %warp.3 = bf16[32,256,128]{2,1,0:T(8,128)(2,1)} custom-call(s32[24]{0:T(128)} %visit_ref.3, s32[24]{0:T(128)} %bitcast.13, s32[2,24]{1,0:T(2,128)} %bitcast.11, s32[8,256]{1,0:T(8,128)} %good_ref.3, bf16[8,256,256]{2,1,0:T(8,128)(2,1)} %rows_hbm.3, bf16[8,256,256]{2,1,0:T(8,128)(2,1)} %cols_hbm.3, bf16[24,256,256]{2,1,0:T(8,128)(2,1)} %var_hbm.2, ...), custom_call_target="tpu_custom_call" | custom-call | flops 3221225472 | bytes 12582912 | tf_op jit(solution)/shard_map/warp/pallas_call | solution.py:158
  34.8 119.0 %all-to-all-done.blocks_ref = bf16[32,784,128]{2,1,0:T(8,128)(2,1)} async-done(((bf16[32,784,128]{2,1,0:T(8,128)(2,1)}), bf16[32,784,128]{2,1,0:T(8,128)(2,1)}, u32[]{:S(2)}, u32[]{:S(2)}) %all-to-all-start) | async-done | bytes 6422560 | tf_op jit(solution)/shard_map/all_to_all | solution.py:532
  153.9 8.9 %all-to-all-start.1 = ((bf16[32,256,128]{2,1,0:T(8,128)(2,1)}), bf16[32,256,128]{2,1,0:T(8,128)(2,1)S(1)}, u32[]{:S(2)}, u32[]{:S(2)}) async-start(bf16[32,256,128]{2,1,0:T(8,128)(2,1)} %warp.3), calls=%async_computation.1 | async-start | bytes 4194304 | tf_op jit(solution)/shard_map/all_to_all | solution.py:532
  162.8 1.0 slice.81
  163.8 0.1 convert_element_type.61.code_ref
  164.0 6.9 %place.2 = (bf16[384,1024]{1,0:T(8,128)(2,1)S(1)}, f32[16,384]{1,0:T(8,128)S(1)}, f32[16,1024]{1,0:T(8,128)S(1)}) custom-call(s32[64]{0:T(128)S(1)} %convert_element_type.61.code_ref, bf16[32,784,128]{2,1,0:T(8,128)(2,1)} %all-to-all-done.blocks_ref), custom_call_target="tpu_custom_call" | custom-call | flops 3211264 | bytes 6422528 | tf_op jit(solution)/shard_map/place/pallas_call | solution.py:227
  170.9 1.3 collective-permute-start.1
  172.2 0.7 collective-permute-start
  172.8 4.6 %collective-permute-start.2 = (f32[16,384]{1,0:T(8,128)S(1)}, f32[16,384]{1,0:T(8,128)S(1)}, u32[]{:S(2)}, u32[]{:S(2)}) collective-permute-start(f32[16,384]{1,0:T(8,128)S(1)} %get-tuple-element.46), channel_id=1, source_target_pairs={{0,16},{16,0},{1,17},{17,1},{2,18},{18,2},{3,19},{19,3},{4,20},{20... | collective-permute-start | bytes 73736 | tf_op jit(solution)/shard_map/ppermute | solution.py:257
  177.5 5.0 %collective-permute-done.2 = f32[16,384]{1,0:T(8,128)S(1)} collective-permute-done((f32[16,384]{1,0:T(8,128)S(1)}, f32[16,384]{1,0:T(8,128)S(1)}, u32[]{:S(2)}, u32[]{:S(2)}) %collective-permute-start.2) | collective-permute-done | bytes 24608 | tf_op jit(solution)/shard_map/ppermute | solution.py:257
  182.4 1.8 collective-permute-start.5
  184.2 2.8 %collective-permute-start.3 = (f32[8,1024]{1,0:T(8,128)S(1)}, f32[8,1024]{1,0:T(8,128)S(1)}, u32[]{:S(2)}, u32[]{:S(2)}) collective-permute-start(f32[8,1024]{1,0:T(8,128)S(1)} %pad_maximum_fusion.1), channel_id=1, source_target_pairs={{0,1},{1,2},{2,3},{4,5},{5,6},{6,7},{8,9},{9,10},{10,11},{12,13},{... | collective-permute-start | bytes 98312 | tf_op jit(solution)/shard_map/ppermute | solution.py:253
  187.0 1.3 collective-permute-start.4
  188.3 9.8 %collective-permute-done.3.refs_9_.refs_12_ = f32[8,1024]{1,0:T(8,128)S(1)} collective-permute-done((f32[8,1024]{1,0:T(8,128)S(1)}, f32[8,1024]{1,0:T(8,128)S(1)}, u32[]{:S(2)}, u32[]{:S(2)}) %collective-permute-start.3) | collective-permute-done | bytes 32800 | tf_op jit(solution)/shard_map/ppermute | solution.py:253
  198.1 11.5 %all-to-all-done.1.blocks_ref = bf16[32,256,128]{2,1,0:T(8,128)(2,1)S(1)} async-done(((bf16[32,256,128]{2,1,0:T(8,128)(2,1)}), bf16[32,256,128]{2,1,0:T(8,128)(2,1)S(1)}, u32[]{:S(2)}, u32[]{:S(2)}) %all-to-all-start.1) | async-done | bytes 2097184 | tf_op jit(solution)/shard_map/all_to_all | solution.py:532
  209.6 2.6 %place.3 = (bf16[128,1024]{1,0:T(8,128)(2,1)S(1)}, f32[16,128]{1,0:T(8,128)S(1)}, f32[16,1024]{1,0:T(8,128)}) custom-call(s32[64]{0:T(128)S(1)} %convert_element_type.61.code_ref, bf16[32,256,128]{2,1,0:T(8,128)(2,1)S(1)} %all-to-all-done.1.blocks_ref), custom_call_target="tpu_custom_call" | custom-call | flops 1048576 | bytes 2097152 | tf_op jit(solution)/shard_map/place/pallas_call | solution.py:227
  212.2 1.5 collective-permute-start.8
  213.7 9.5 %stage.2 = (f32[1024,1024]{1,0:T(8,128)}, f32[1024,1024]{1,0:T(8,128)}) custom-call(s32[1]{0:T(128)} %bitcast.refs_0_, f32[7]{0:T(128)S(1)} %copy-done, f32[8,1024]{1,0:T(8,128)S(1)} %get-tuple-element.56.refs_2_, f32[8,1024]{1,0:T(8,128)S(1)} %get-tuple-element.57.refs_3_, bf16[96,96]{1,0:T(8,128)(2,1)S(1)} %fusion.1.refs_4_, ...), custom_call_target="tpu_custom_call" | custom-call | flops 79626240 | bytes 11943936 | tf_op jit(solution)/shard_map/stage/pallas_call | solution.py:455
  223.2 1.3 collective-permute-start.7
  224.5 6.2 %collective-permute-start.6 = (f32[8,128]{1,0:T(8,128)S(1)}, f32[8,128]{1,0:T(8,128)S(1)}, u32[]{:S(2)}, u32[]{:S(2)}) collective-permute-start(f32[8,128]{1,0:T(8,128)S(1)} %get-tuple-element.89), channel_id=1, source_target_pairs={{0,1},{1,2},{2,3},{4,5},{5,6},{6,7},{8,9},{9,10},{10,11},{12,13},{... | collective-permute-start | bytes 12296 | tf_op jit(solution)/shard_map/ppermute | solution.py:253
  230.7 1.3 collective-permute-done.6.refs_15_
  232.0 1.2 collective-permute-start.9
  233.2 2.4 %collective-permute-done.9.refs_18_.refs_19_ = f32[16,128]{1,0:T(8,128)S(1)} collective-permute-done((f32[16,128]{1,0:T(8,128)S(1)}, f32[16,128]{1,0:T(8,128)S(1)}, u32[]{:S(2)}, u32[]{:S(2)}) %collective-permute-start.9) | collective-permute-done | bytes 8224 | tf_op jit(solution)/shard_map/ppermute | solution.py:257
  235.7 6.8 %stage.3 = (f32[1024,1024]{1,0:T(8,128)}, f32[1024,1024]{1,0:T(8,128)}) custom-call(s32[1]{0:T(128)} %bitcast.refs_0_, f32[7]{0:T(128)S(1)} %copy-done, f32[8,1024]{1,0:T(8,128)S(1)} %get-tuple-element.56.refs_2_, f32[8,1024]{1,0:T(8,128)S(1)} %get-tuple-element.57.refs_3_, ...), custom_call_target="tpu_custom_call", output_to_operand_aliasing={{0}: (20, {}), {1}: (21, {})} | custom-call | flops 47185920 | bytes 7077888 | tf_op jit(solution)/shard_map/stage/pallas_call | solution.py:455
  (26 shorter events, 0.3 us)
Async XLA Ops:
  9.4 7.4 %copy-start = (f32[7]{0:T(128)S(1)}, f32[7]{0:T(128)}, u32[]{:S(2)}) copy-start(f32[7]{0:T(128)} %refs_1_.1) | copy-start | bytes 88
  9.4 144.4 %all-to-all-start = ((bf16[32,784,128]{2,1,0:T(8,128)(2,1)}), bf16[32,784,128]{2,1,0:T(8,128)(2,1)}, u32[]{:S(2)}, u32[]{:S(2)}) async-start(bf16[32,784,128]{2,1,0:T(8,128)(2,1)} %warp.2), calls=%async_computation | async-start | bytes 12845056 | tf_op jit(solution)/shard_map/all_to_all | solution.py:532
  153.9 55.7 %all-to-all-start.1 = ((bf16[32,256,128]{2,1,0:T(8,128)(2,1)}), bf16[32,256,128]{2,1,0:T(8,128)(2,1)S(1)}, u32[]{:S(2)}, u32[]{:S(2)}) async-start(bf16[32,256,128]{2,1,0:T(8,128)(2,1)} %warp.3), calls=%async_computation.1 | async-start | bytes 4194304 | tf_op jit(solution)/shard_map/all_to_all | solution.py:532
  170.9 6.6 %collective-permute-start.1 = (f32[8,1024]{1,0:T(8,128)S(1)}, f32[8,1024]{1,0:T(8,128)S(1)}, u32[]{:S(2)}, u32[]{:S(2)}) collective-permute-start(f32[8,1024]{1,0:T(8,128)S(1)} %slice_select_fusion), channel_id=1, source_target_pairs={{4,0},{8,4},{12,8},{16,20},{20,24},{24,28},{5,1},{9,5},{13,9},{17,... | collective-permute-start | bytes 98312 | tf_op jit(solution)/shard_map/ppermute | solution.py:277
  172.2 5.3 %collective-permute-start = (f32[8,1024]{1,0:T(8,128)S(1)}, f32[8,1024]{1,0:T(8,128)S(1)}, u32[]{:S(2)}, u32[]{:S(2)}) collective-permute-start(f32[8,1024]{1,0:T(8,128)S(1)} %slice_select_fusion), channel_id=1, source_target_pairs={{4,16},{8,20},{12,24},{16,4},{20,8},{24,12},{5,17},{9,21},{13,25},... | collective-permute-start | bytes 98312 | tf_op jit(solution)/shard_map/ppermute | solution.py:278
  172.8 9.6 %collective-permute-start.2 = (f32[16,384]{1,0:T(8,128)S(1)}, f32[16,384]{1,0:T(8,128)S(1)}, u32[]{:S(2)}, u32[]{:S(2)}) collective-permute-start(f32[16,384]{1,0:T(8,128)S(1)} %get-tuple-element.46), channel_id=1, source_target_pairs={{0,16},{16,0},{1,17},{17,1},{2,18},{18,2},{3,19},{19,3},{4,20},{20... | collective-permute-start | bytes 73736 | tf_op jit(solution)/shard_map/ppermute | solution.py:257
  182.4 31.2 %collective-permute-start.5 = (bf16[384,1024]{1,0:T(8,128)(2,1)S(1)}, bf16[384,1024]{1,0:T(8,128)(2,1)}, u32[]{:S(2)}, u32[]{:S(2)}) collective-permute-start(bf16[384,1024]{1,0:T(8,128)(2,1)S(1)} %get-tuple-element.62.refs_8_), channel_id=1, source_target_pairs={{0,16},{16,0},{1,17},{17,1},{2,18},{18,2},{3,19},{19,3},{4,20},{20... | collective-permute-start | bytes 2359304 | tf_op jit(solution)/shard_map/ppermute | solution.py:257
  184.2 13.9 %collective-permute-start.3 = (f32[8,1024]{1,0:T(8,128)S(1)}, f32[8,1024]{1,0:T(8,128)S(1)}, u32[]{:S(2)}, u32[]{:S(2)}) collective-permute-start(f32[8,1024]{1,0:T(8,128)S(1)} %pad_maximum_fusion.1), channel_id=1, source_target_pairs={{0,1},{1,2},{2,3},{4,5},{5,6},{6,7},{8,9},{9,10},{10,11},{12,13},{... | collective-permute-start | bytes 98312 | tf_op jit(solution)/shard_map/ppermute | solution.py:253
  187.0 11.1 %collective-permute-start.4 = (f32[8,1024]{1,0:T(8,128)S(1)}, f32[8,1024]{1,0:T(8,128)S(1)}, u32[]{:S(2)}, u32[]{:S(2)}) collective-permute-start(f32[8,1024]{1,0:T(8,128)S(1)} %pad_maximum_fusion.2), channel_id=1, source_target_pairs={{1,0},{2,1},{3,2},{5,4},{6,5},{7,6},{9,8},{10,9},{11,10},{13,12},{... | collective-permute-start | bytes 98312 | tf_op jit(solution)/shard_map/ppermute | solution.py:253
  212.2 23.5 %collective-permute-start.8 = (bf16[128,1024]{1,0:T(8,128)(2,1)S(1)}, bf16[128,1024]{1,0:T(8,128)(2,1)S(1)}, u32[]{:S(2)}, u32[]{:S(2)}) collective-permute-start(bf16[128,1024]{1,0:T(8,128)(2,1)S(1)} %get-tuple-element.55.refs_14_), channel_id=1, source_target_pairs={{0,16},{16,0},{1,17},{17,1},{2,18},{18,2},{3,19},{19,3},{4,20},{20... | collective-permute-start | bytes 786440 | tf_op jit(solution)/shard_map/ppermute | solution.py:257
  223.2 7.5 %collective-permute-start.7 = (f32[8,128]{1,0:T(8,128)S(1)}, f32[8,128]{1,0:T(8,128)S(1)}, u32[]{:S(2)}, u32[]{:S(2)}) collective-permute-start(f32[8,128]{1,0:T(8,128)S(1)} %get-tuple-element.88), channel_id=1, source_target_pairs={{1,0},{2,1},{3,2},{5,4},{6,5},{7,6},{9,8},{10,9},{11,10},{13,12},{... | collective-permute-start | bytes 12296 | tf_op jit(solution)/shard_map/ppermute | solution.py:253
  224.5 7.5 %collective-permute-start.6 = (f32[8,128]{1,0:T(8,128)S(1)}, f32[8,128]{1,0:T(8,128)S(1)}, u32[]{:S(2)}, u32[]{:S(2)}) collective-permute-start(f32[8,128]{1,0:T(8,128)S(1)} %get-tuple-element.89), channel_id=1, source_target_pairs={{0,1},{1,2},{2,3},{4,5},{5,6},{6,7},{8,9},{9,10},{10,11},{12,13},{... | collective-permute-start | bytes 12296 | tf_op jit(solution)/shard_map/ppermute | solution.py:253
  232.0 3.7 %collective-permute-start.9 = (f32[16,128]{1,0:T(8,128)S(1)}, f32[16,128]{1,0:T(8,128)S(1)}, u32[]{:S(2)}, u32[]{:S(2)}) collective-permute-start(f32[16,128]{1,0:T(8,128)S(1)} %pad_maximum_fusion.4), channel_id=1, source_target_pairs={{0,16},{16,0},{1,17},{17,1},{2,18},{18,2},{3,19},{19,3},{4,20},{20... | collective-permute-start | bytes 24584 | tf_op jit(solution)/shard_map/ppermute | solution.py:257

commit v15 on v12

--- a/solution.py
+++ b/solution.py
@@ -221,7 +221,7 @@
 
 def place(code, blocks, lot):
     count, tall, side = blocks.shape
-    some = 4
+    some = next(some for some in (16, 8, 4, 2, 1) if count % some == 0 and some * tall <= 4096)
     height = lot * UNITS
     shapes = [((height, TX), jnp.bfloat16), ((2 * HALO, height), jnp.float32), ((2 * HALO, TX), jnp.float32)]
     return pl.pallas_call(

time: 240 us -> 240 us (level)
  transfers between devices with their start and end apart: 12 -> 12, of which waited for: 5 -> 5; matrix products, arithmetic and copies ran while one was open for 5% -> 5% of each run, Pallas kernels for 11% -> 12%
where the time goes in v15:
time: 240 us; the launch traced here: 239 us
  waiting for transfers between devices  147 us (61%)
  Pallas kernels  43.6 us (18%)
  starting transfers between devices  36.6 us (15%)
  other arithmetic  9.48 us (4%)
    all_to_all x2, waiting for transfers between devices, send(): lax.all_to_all(blocks, EVERY, split_axis=0, concat_axis=0, tiled=True)  131 us
    pallas_call x2, Pallas kernels, warp(): pl.pallas_call(functools.partial(warp_kernel, tiles, share, noted), out_s...  16.6 us
    pallas_call x2, Pallas kernels, stage(): pl.pallas_call(functools.partial(stage_kernel, plan, lots), out_shape=(sh...  16.3 us
    all_to_all x2, starting transfers between devices, send(): lax.all_to_all(blocks, EVERY, split_axis=0, concat_axis=0, tiled=True)  16.3 us
    ppermute x4, waiting for transfers between devices, neighbours(): return (lax.ppermute(last, axis, up), lax.ppermute(first, axis, down))  11.1 us
    pallas_call x2, Pallas kernels, place(): pl.pallas_call(functools.partial(place_kernel, 2 * lot), grid_spec=pltpu....  10.6 us
    ppermute x4, starting transfers between devices, neighbours(): return (lax.ppermute(last, axis, up), lax.ppermute(first, axis, down))  10.5 us
    convert_element_type x2, other arithmetic, split(): coarse = value.astype(jnp.bfloat16)  8.89 us
  transfers between devices with their start and end apart: 12, of which 5 were waited for; matrix products, arithmetic and copies ran while one was open for 5% of the time, Pallas kernels for 12%

profile of v15, /device:TPU:0, one launch (start us, length us, event | category | flops | bytes accessed | tf_op | source)
XLA Modules:
  0.0 239.4 jit_solution(1910277549021982131)
XLA Ops:
  0.6 8.7 %warp.2 = bf16[32,784,128]{2,1,0:T(8,128)(2,1)} custom-call(s32[24]{0:T(128)} %visit_ref.3, s32[24]{0:T(128)} %bitcast.12, s32[2,24]{1,0:T(2,128)} %bitcast.10, s32[8,256]{1,0:T(8,128)} %good_ref.3, bf16[8,256,256]{2,1,0:T(8,128)(2,1)} %rows_hbm.3, bf16[8,256,256]{2,1,0:T(8,128)(2,1)} %cols_hbm.3, bf16[24,256,256]{2,1,0:T(8,128)(2,1)} %var_hbm.2, ...), custom_call_target="tpu_custom_call" | custom-call | flops 3221225472 | bytes 12582912 | tf_op jit(solution)/shard_map/warp/pallas_call | solution.py:158
  9.4 7.4 %all-to-all-start = ((bf16[32,784,128]{2,1,0:T(8,128)(2,1)}), bf16[32,784,128]{2,1,0:T(8,128)(2,1)}, u32[]{:S(2)}, u32[]{:S(2)}) async-start(bf16[32,784,128]{2,1,0:T(8,128)(2,1)} %warp.2), calls=%async_computation | async-start | bytes 12845056 | tf_op jit(solution)/shard_map/all_to_all | solution.py:532
  16.9 0.6 fusion.26
  17.5 4.4 %fusion.20 = (bf16[48,64]{1,0:T(8,128)(2,1)S(1)}, bf16[48,64]{1,0:T(8,128)(2,1)S(1)}) fusion(f32[]{:T(128)} %bitcast.9, f32[]{:T(128)} %bitcast.8, f32[]{:T(128)} %bitcast.7, f32[]{:T(128)} %bitcast.6, f32[]{:T(128)} %bitcast.5, f32[]{:T(128)} %bitcast.4, f32[]{:T(128)} %bitcast.3, s32[48]{0:T(128)S(1)} %iota_add_fusion), kind=kLoop, calls=%fused_computation.39 | loop fusion | flops 79872 | bytes 12508 | tf_op jit(solution)/shard_map/convert_element_type | solution.py:302
  22.0 0.1 pad_maximum_fusion.3.refs_6_
  22.1 4.5 %fusion.19 = (bf16[80,96]{1,0:T(8,128)(2,1)S(1)}, bf16[80,96]{1,0:T(8,128)(2,1)S(1)}) fusion(f32[]{:T(128)} %bitcast.9, f32[]{:T(128)} %bitcast.8, f32[]{:T(128)} %bitcast.7, f32[]{:T(128)} %bitcast.6, f32[]{:T(128)} %bitcast.5, f32[]{:T(128)} %bitcast.4, f32[]{:T(128)} %bitcast.3, s32[80]{0:T(128)S(1)} %iota_add_fusion.1), kind=kLoop, calls=%fused_computation.35 | loop fusion | flops 199680 | bytes 31068 | tf_op jit(solution)/shard_map/convert_element_type | solution.py:302
  26.5 0.1 pad_maximum_fusion.refs_6_
  26.7 0.1 fusion.9.refs_5_
  26.8 0.1 fusion.refs_7_
  26.9 7.9 %warp.3 = bf16[32,256,128]{2,1,0:T(8,128)(2,1)} custom-call(s32[24]{0:T(128)} %visit_ref.3, s32[24]{0:T(128)} %bitcast.13, s32[2,24]{1,0:T(2,128)} %bitcast.11, s32[8,256]{1,0:T(8,128)} %good_ref.3, bf16[8,256,256]{2,1,0:T(8,128)(2,1)} %rows_hbm.3, bf16[8,256,256]{2,1,0:T(8,128)(2,1)} %cols_hbm.3, bf16[24,256,256]{2,1,0:T(8,128)(2,1)} %var_hbm.2, ...), custom_call_target="tpu_custom_call" | custom-call | flops 3221225472 | bytes 12582912 | tf_op jit(solution)/shard_map/warp/pallas_call | solution.py:158
  34.8 119.0 %all-to-all-done.blocks_ref = bf16[32,784,128]{2,1,0:T(8,128)(2,1)} async-done(((bf16[32,784,128]{2,1,0:T(8,128)(2,1)}), bf16[32,784,128]{2,1,0:T(8,128)(2,1)}, u32[]{:S(2)}, u32[]{:S(2)}) %all-to-all-start) | async-done | bytes 6422560 | tf_op jit(solution)/shard_map/all_to_all | solution.py:532
  153.9 8.9 %all-to-all-start.1 = ((bf16[32,256,128]{2,1,0:T(8,128)(2,1)}), bf16[32,256,128]{2,1,0:T(8,128)(2,1)S(1)}, u32[]{:S(2)}, u32[]{:S(2)}) async-start(bf16[32,256,128]{2,1,0:T(8,128)(2,1)} %warp.3), calls=%async_computation.1 | async-start | bytes 4194304 | tf_op jit(solution)/shard_map/all_to_all | solution.py:532
  162.8 1.0 slice.81
  163.8 0.1 convert_element_type.61.code_ref
  163.9 7.7 %place.2 = (bf16[384,1024]{1,0:T(8,128)(2,1)S(1)}, f32[16,384]{1,0:T(8,128)S(1)}, f32[16,1024]{1,0:T(8,128)S(1)}) custom-call(s32[64]{0:T(128)S(1)} %convert_element_type.61.code_ref, bf16[32,784,128]{2,1,0:T(8,128)(2,1)} %all-to-all-done.blocks_ref), custom_call_target="tpu_custom_call" | custom-call | flops 3211264 | bytes 6422528 | tf_op jit(solution)/shard_map/place/pallas_call | solution.py:227
  171.6 1.3 collective-permute-start.1
  172.9 0.7 collective-permute-start
  173.6 4.1 %collective-permute-start.2 = (f32[16,384]{1,0:T(8,128)S(1)}, f32[16,384]{1,0:T(8,128)S(1)}, u32[]{:S(2)}, u32[]{:S(2)}) collective-permute-start(f32[16,384]{1,0:T(8,128)S(1)} %get-tuple-element.43), channel_id=1, source_target_pairs={{0,16},{16,0},{1,17},{17,1},{2,18},{18,2},{3,19},{19,3},{4,20},{20... | collective-permute-start | bytes 73736 | tf_op jit(solution)/shard_map/ppermute | solution.py:257
  177.7 5.5 %collective-permute-done.2 = f32[16,384]{1,0:T(8,128)S(1)} collective-permute-done((f32[16,384]{1,0:T(8,128)S(1)}, f32[16,384]{1,0:T(8,128)S(1)}, u32[]{:S(2)}, u32[]{:S(2)}) %collective-permute-start.2) | collective-permute-done | bytes 24608 | tf_op jit(solution)/shard_map/ppermute | solution.py:257
  183.1 1.1 collective-permute-start.5
  184.2 2.8 %collective-permute-start.3 = (f32[8,1024]{1,0:T(8,128)S(1)}, f32[8,1024]{1,0:T(8,128)S(1)}, u32[]{:S(2)}, u32[]{:S(2)}) collective-permute-start(f32[8,1024]{1,0:T(8,128)S(1)} %pad_maximum_fusion.1), channel_id=1, source_target_pairs={{0,1},{1,2},{2,3},{4,5},{5,6},{6,7},{8,9},{9,10},{10,11},{12,13},{... | collective-permute-start | bytes 98312 | tf_op jit(solution)/shard_map/ppermute | solution.py:253
  187.0 1.3 collective-permute-start.4
  188.3 9.8 %collective-permute-done.3.refs_9_.refs_12_ = f32[8,1024]{1,0:T(8,128)S(1)} collective-permute-done((f32[8,1024]{1,0:T(8,128)S(1)}, f32[8,1024]{1,0:T(8,128)S(1)}, u32[]{:S(2)}, u32[]{:S(2)}) %collective-permute-start.3) | collective-permute-done | bytes 32800 | tf_op jit(solution)/shard_map/ppermute | solution.py:253
  198.1 11.5 %all-to-all-done.1.blocks_ref = bf16[32,256,128]{2,1,0:T(8,128)(2,1)S(1)} async-done(((bf16[32,256,128]{2,1,0:T(8,128)(2,1)}), bf16[32,256,128]{2,1,0:T(8,128)(2,1)S(1)}, u32[]{:S(2)}, u32[]{:S(2)}) %all-to-all-start.1) | async-done | bytes 2097184 | tf_op jit(solution)/shard_map/all_to_all | solution.py:532
  209.6 3.0 %place.3 = (bf16[128,1024]{1,0:T(8,128)(2,1)S(1)}, f32[16,128]{1,0:T(8,128)S(1)}, f32[16,1024]{1,0:T(8,128)}) custom-call(s32[64]{0:T(128)S(1)} %convert_element_type.61.code_ref, bf16[32,256,128]{2,1,0:T(8,128)(2,1)S(1)} %all-to-all-done.1.blocks_ref), custom_call_target="tpu_custom_call" | custom-call | flops 1048576 | bytes 2097152 | tf_op jit(solution)/shard_map/place/pallas_call | solution.py:227
  212.6 1.5 collective-permute-start.8
  214.0 1.3 collective-permute-start.7
  215.3 5.2 %collective-permute-start.6 = (f32[8,128]{1,0:T(8,128)S(1)}, f32[8,128]{1,0:T(8,128)S(1)}, u32[]{:S(2)}, u32[]{:S(2)}) collective-permute-start(f32[8,128]{1,0:T(8,128)S(1)} %get-tuple-element.83), channel_id=1, source_target_pairs={{0,1},{1,2},{2,3},{4,5},{5,6},{6,7},{8,9},{9,10},{10,11},{12,13},{... | collective-permute-start | bytes 12296 | tf_op jit(solution)/shard_map/ppermute | solution.py:253
  220.5 1.3 collective-permute-done.6.refs_15_
  221.8 1.2 collective-permute-start.9
  223.0 9.5 %stage.2 = (f32[1024,1024]{1,0:T(8,128)}, f32[1024,1024]{1,0:T(8,128)}) custom-call(s32[1]{0:T(128)} %bitcast.refs_0_, f32[7]{0:T(128)S(1)} %copy-done, f32[8,1024]{1,0:T(8,128)S(1)} %get-tuple-element.53.refs_2_, f32[8,1024]{1,0:T(8,128)S(1)} %get-tuple-element.54.refs_3_, bf16[96,96]{1,0:T(8,128)(2,1)S(1)} %fusion.1.refs_4_, ...), custom_call_target="tpu_custom_call" | custom-call | flops 79626240 | bytes 11943936 | tf_op jit(solution)/shard_map/stage/pallas_call | solution.py:455
  232.6 6.8 %stage.3 = (f32[1024,1024]{1,0:T(8,128)}, f32[1024,1024]{1,0:T(8,128)}) custom-call(s32[1]{0:T(128)} %bitcast.refs_0_, f32[7]{0:T(128)S(1)} %copy-done, f32[8,1024]{1,0:T(8,128)S(1)} %get-tuple-element.53.refs_2_, f32[8,1024]{1,0:T(8,128)S(1)} %get-tuple-element.54.refs_3_, ...), custom_call_target="tpu_custom_call", output_to_operand_aliasing={{0}: (20, {}), {1}: (21, {})} | custom-call | flops 47185920 | bytes 7077888 | tf_op jit(solution)/shard_map/stage/pallas_call | solution.py:455
  (26 shorter events, 0.2 us)
Async XLA Ops:
  9.4 7.5 %copy-start = (f32[7]{0:T(128)S(1)}, f32[7]{0:T(128)}, u32[]{:S(2)}) copy-start(f32[7]{0:T(128)} %refs_1_.1) | copy-start | bytes 88
  9.4 144.5 %all-to-all-start = ((bf16[32,784,128]{2,1,0:T(8,128)(2,1)}), bf16[32,784,128]{2,1,0:T(8,128)(2,1)}, u32[]{:S(2)}, u32[]{:S(2)}) async-start(bf16[32,784,128]{2,1,0:T(8,128)(2,1)} %warp.2), calls=%async_computation | async-start | bytes 12845056 | tf_op jit(solution)/shard_map/all_to_all | solution.py:532
  153.9 55.7 %all-to-all-start.1 = ((bf16[32,256,128]{2,1,0:T(8,128)(2,1)}), bf16[32,256,128]{2,1,0:T(8,128)(2,1)S(1)}, u32[]{:S(2)}, u32[]{:S(2)}) async-start(bf16[32,256,128]{2,1,0:T(8,128)(2,1)} %warp.3), calls=%async_computation.1 | async-start | bytes 4194304 | tf_op jit(solution)/shard_map/all_to_all | solution.py:532
  171.6 6.1 %collective-permute-start.1 = (f32[8,1024]{1,0:T(8,128)S(1)}, f32[8,1024]{1,0:T(8,128)S(1)}, u32[]{:S(2)}, u32[]{:S(2)}) collective-permute-start(f32[8,1024]{1,0:T(8,128)S(1)} %slice_select_fusion), channel_id=1, source_target_pairs={{4,0},{8,4},{12,8},{16,20},{20,24},{24,28},{5,1},{9,5},{13,9},{17,... | collective-permute-start | bytes 98312 | tf_op jit(solution)/shard_map/ppermute | solution.py:277
  172.9 4.8 %collective-permute-start = (f32[8,1024]{1,0:T(8,128)S(1)}, f32[8,1024]{1,0:T(8,128)S(1)}, u32[]{:S(2)}, u32[]{:S(2)}) collective-permute-start(f32[8,1024]{1,0:T(8,128)S(1)} %slice_select_fusion), channel_id=1, source_target_pairs={{4,16},{8,20},{12,24},{16,4},{20,8},{24,12},{5,17},{9,21},{13,25},... | collective-permute-start | bytes 98312 | tf_op jit(solution)/shard_map/ppermute | solution.py:278
  173.6 9.5 %collective-permute-start.2 = (f32[16,384]{1,0:T(8,128)S(1)}, f32[16,384]{1,0:T(8,128)S(1)}, u32[]{:S(2)}, u32[]{:S(2)}) collective-permute-start(f32[16,384]{1,0:T(8,128)S(1)} %get-tuple-element.43), channel_id=1, source_target_pairs={{0,16},{16,0},{1,17},{17,1},{2,18},{18,2},{3,19},{19,3},{4,20},{20... | collective-permute-start | bytes 73736 | tf_op jit(solution)/shard_map/ppermute | solution.py:257
  183.1 37.4 %collective-permute-start.5 = (bf16[384,1024]{1,0:T(8,128)(2,1)S(1)}, bf16[384,1024]{1,0:T(8,128)(2,1)}, u32[]{:S(2)}, u32[]{:S(2)}) collective-permute-start(bf16[384,1024]{1,0:T(8,128)(2,1)S(1)} %get-tuple-element.59.refs_8_), channel_id=1, source_target_pairs={{0,16},{16,0},{1,17},{17,1},{2,18},{18,2},{3,19},{19,3},{4,20},{20... | collective-permute-start | bytes 2359304 | tf_op jit(solution)/shard_map/ppermute | solution.py:257
  184.2 13.9 %collective-permute-start.3 = (f32[8,1024]{1,0:T(8,128)S(1)}, f32[8,1024]{1,0:T(8,128)S(1)}, u32[]{:S(2)}, u32[]{:S(2)}) collective-permute-start(f32[8,1024]{1,0:T(8,128)S(1)} %pad_maximum_fusion.1), channel_id=1, source_target_pairs={{0,1},{1,2},{2,3},{4,5},{5,6},{6,7},{8,9},{9,10},{10,11},{12,13},{... | collective-permute-start | bytes 98312 | tf_op jit(solution)/shard_map/ppermute | solution.py:253
  187.0 11.1 %collective-permute-start.4 = (f32[8,1024]{1,0:T(8,128)S(1)}, f32[8,1024]{1,0:T(8,128)S(1)}, u32[]{:S(2)}, u32[]{:S(2)}) collective-permute-start(f32[8,1024]{1,0:T(8,128)S(1)} %pad_maximum_fusion.2), channel_id=1, source_target_pairs={{1,0},{2,1},{3,2},{5,4},{6,5},{7,6},{9,8},{10,9},{11,10},{13,12},{... | collective-permute-start | bytes 98312 | tf_op jit(solution)/shard_map/ppermute | solution.py:253
  212.6 20.0 %collective-permute-start.8 = (bf16[128,1024]{1,0:T(8,128)(2,1)S(1)}, bf16[128,1024]{1,0:T(8,128)(2,1)S(1)}, u32[]{:S(2)}, u32[]{:S(2)}) collective-permute-start(bf16[128,1024]{1,0:T(8,128)(2,1)S(1)} %get-tuple-element.52.refs_14_), channel_id=1, source_target_pairs={{0,16},{16,0},{1,17},{17,1},{2,18},{18,2},{3,19},{19,3},{4,20},{20... | collective-permute-start | bytes 786440 | tf_op jit(solution)/shard_map/ppermute | solution.py:257
  214.0 6.5 %collective-permute-start.7 = (f32[8,128]{1,0:T(8,128)S(1)}, f32[8,128]{1,0:T(8,128)S(1)}, u32[]{:S(2)}, u32[]{:S(2)}) collective-permute-start(f32[8,128]{1,0:T(8,128)S(1)} %get-tuple-element.82), channel_id=1, source_target_pairs={{1,0},{2,1},{3,2},{5,4},{6,5},{7,6},{9,8},{10,9},{11,10},{13,12},{... | collective-permute-start | bytes 12296 | tf_op jit(solution)/shard_map/ppermute | solution.py:253
  215.3 6.5 %collective-permute-start.6 = (f32[8,128]{1,0:T(8,128)S(1)}, f32[8,128]{1,0:T(8,128)S(1)}, u32[]{:S(2)}, u32[]{:S(2)}) collective-permute-start(f32[8,128]{1,0:T(8,128)S(1)} %get-tuple-element.83), channel_id=1, source_target_pairs={{0,1},{1,2},{2,3},{4,5},{5,6},{6,7},{8,9},{9,10},{10,11},{12,13},{... | collective-permute-start | bytes 12296 | tf_op jit(solution)/shard_map/ppermute | solution.py:253
  221.8 10.7 %collective-permute-start.9 = (f32[16,128]{1,0:T(8,128)S(1)}, f32[16,128]{1,0:T(8,128)S(1)}, u32[]{:S(2)}, u32[]{:S(2)}) collective-permute-start(f32[16,128]{1,0:T(8,128)S(1)} %pad_maximum_fusion.4), channel_id=1, source_target_pairs={{0,16},{16,0},{1,17},{17,1},{2,18},{18,2},{3,19},{19,3},{4,20},{20... | collective-permute-start | bytes 24584 | tf_op jit(solution)/shard_map/ppermute | solution.py:257
